TPU v7x, 32 devices: a whole 2x2x4 slice. The times are simulated.
32 devices in a mesh: groups: 2 (over x), slab: 8 (over z, y), dom: 2 (over core).
Axes of the slice: x: 2, y: 2, z: 4, core: 2. Of those that a mesh axis runs over, the one named last changes fastest.
Arguments:
- volume: bfloat16 [524288, 128], P(('groups', 'slab')), parts along dimension 0, may hold values from -6 to 6
- kernels: bfloat16 [4, 128, 128], replicated, may hold values from -0.5 to 0.5
- images: bfloat16 [256, 1024, 128], P(('groups', 'slab', 'dom')), parts along dimension 0, may hold values from -6 to 6
- owners: int32 [256, 1024, 1], P(('groups', 'slab', 'dom')), parts along dimension 0, may hold values from 0 to 7; in each aligned block of 8192 rows (0 to 8191, 8192 to 16383, ..., all dimensions but the last counted through in order) at most 2048 rows name the same one
- local_block: int32 [256, 1024], P(('groups', 'slab', 'dom')), parts along dimension 0, may hold values from 0 to 32767
- kinds: int32 [256, 1024], P(('groups', 'slab', 'dom')), parts along dimension 0, may hold values from 0 to 3
- counts: int32 [256], P(('groups', 'slab', 'dom')), parts along dimension 0, may hold values from 512 to 1024
- ctf_code: int32 [256], P(('groups', 'slab', 'dom')), parts along dimension 0, may hold values from 0 to 63
- ctf_table: float32 [64, 2], replicated, may hold values from 5 to 40
- scales: bfloat16 [256], P(('groups', 'slab', 'dom')), parts along dimension 0, may hold values from 0.5 to 2
Outputs:
- gradient_field: float32 [2, 512, 256, 256], P(None, ('groups', 'dom'), 'slab'), parts along dimension 1
- losses: float32 [256], P(('groups', 'slab', 'dom')), parts along dimension 0
There are 2 independent parts, one for each index of `groups`. A program takes and returns all parts, laid end to end along the dimension named above; an argument that names none is the same for every part. Nothing has to cross between parts.
Inputs may be any that keep to these rules, and one draw needn't show every extreme that they name: `owners`: in the rows of one device (aligned blocks of 8192 entries) no slab is named more than 2048 times, a bound that some block reaches.
All inputs are finite; a program needn't handle non-finite values.
Results may differ from a plain program's by a relative error of at most 0.0023.
Values may be sent and summed in bfloat16 or wider, within the bound.
No kernel may reach another device: no remote copies, remote signals or barrier semaphores. Data moves between devices by JAX's collectives and lax.ppermute only.
A program may use at most 320 MiB of HBM per device.

v0:
```python
import math

import jax
import jax.numpy as jnp
from jax import lax
from jax.sharding import PartitionSpec as P

HIGHEST = lax.Precision.HIGHEST


def pixel_factor(block_pos, scaling, defocus, phase_shift, side_cells):
    per_row = side_cells // 8
    offsets = jnp.arange(64, dtype=jnp.int32)
    vert_pos = (block_pos // per_row)[:, None] * 8 + offsets[None, :] // 8
    horiz_pos = (block_pos % per_row)[:, None] * 8 + offsets[None, :] % 8
    freq_vert = (vert_pos - side_cells // 2).astype(jnp.float32)
    freq_horiz = (horiz_pos - side_cells // 2).astype(jnp.float32)
    radius = (freq_vert * freq_vert + freq_horiz * freq_horiz) / float((side_cells // 2) ** 2)
    factor = scaling[:, None] * jnp.sin(defocus[:, None] * radius + phase_shift[:, None])
    return jnp.concatenate([factor, factor], axis=1)


def block_terms(voxel_rows, pictures, kind_ids, factor, live_mask, kernels):
    kind_count = kernels.shape[0]
    breadth = kernels.shape[1]
    select = (kind_ids[:, None] == jnp.arange(kind_count, dtype=jnp.int32)[None, :]).astype(
        jnp.bfloat16
    )
    spread = (select[:, :, None] * voxel_rows[:, None, :]).reshape(-1, kind_count * breadth)
    forward = kernels.reshape(kind_count * breadth, breadth)
    extracted = jnp.dot(spread, forward, preferred_element_type=jnp.float32)
    misfit = jnp.where(live_mask[:, None], factor * extracted - pictures.astype(jnp.float32), 0.0)
    weighted = (factor * misfit).astype(jnp.bfloat16)
    spread_back = (select[:, :, None] * weighted[:, None, :]).reshape(-1, kind_count * breadth)
    backward = jnp.transpose(kernels, (0, 2, 1)).reshape(kind_count * breadth, breadth)
    grad_terms = jnp.dot(spread_back, backward, preferred_element_type=jnp.float32)
    return (grad_terms, jnp.sum(misfit * misfit, axis=1))


def dft_tables(input_index, side_cells):
    freqs = jnp.arange(side_cells, dtype=jnp.int32)
    product = input_index[:, None] * freqs[None, :] % side_cells
    angles = product.astype(jnp.float32) * (2.0 * math.pi / side_cells)
    norming = 1.0 / math.sqrt(side_cells)
    return (jnp.cos(angles) * norming, jnp.sin(angles) * norming)


def transform(real_part, imag_part, cos_table, sin_table, pattern):
    new_real = jnp.einsum(pattern, real_part, cos_table, precision=HIGHEST) - jnp.einsum(
        pattern, imag_part, sin_table, precision=HIGHEST
    )
    new_imag = jnp.einsum(pattern, real_part, sin_table, precision=HIGHEST) + jnp.einsum(
        pattern, imag_part, cos_table, precision=HIGHEST
    )
    return (new_real, new_imag)


def body(volume, kernels, images, owners, local_block, kinds, counts, ctf_code, ctf_table, scales):
    slab_count = lax.axis_size("slab")
    particles_here = images.shape[0]
    list_length = images.shape[1]
    side_cells = math.isqrt(list_length * 64)
    per_row = side_cells // 8
    entries = particles_here * list_length
    capacity = 2 * entries // slab_count
    slot_count = slab_count * capacity
    slab_blocks = volume.shape[0]
    planes_here = slab_blocks // (per_row * per_row)
    owner_ids = owners.reshape(entries)
    local_ids = local_block.reshape(entries)
    kind_ids = kinds.reshape(entries)
    hits = (owner_ids[:, None] == jnp.arange(slab_count, dtype=jnp.int32)[None, :]).astype(
        jnp.int32
    )
    ranks = jnp.sum(hits * (jnp.cumsum(hits, axis=0) - 1), axis=1)
    targets = owner_ids * capacity + ranks
    block_pos = jnp.tile(jnp.arange(list_length, dtype=jnp.int32), particles_here)
    live_mask = block_pos < jnp.repeat(counts, list_length, total_repeat_length=entries)
    pictures = images.reshape(entries, images.shape[2])
    requests = (
        jnp.zeros((slot_count,), jnp.int32).at[targets].set(local_ids).reshape(slab_count, capacity)
    )
    received = lax.all_to_all(requests, "slab", split_axis=0, concat_axis=0, tiled=True)
    wanted_rows = jnp.take(volume, received.reshape(-1), axis=0).reshape(
        slab_count, capacity, volume.shape[1]
    )
    fetched = lax.all_to_all(wanted_rows, "slab", split_axis=0, concat_axis=0, tiled=True)
    voxel_rows = fetched.reshape(slot_count, volume.shape[1])[targets]
    table_rows = ctf_table[ctf_code]
    factor = pixel_factor(
        block_pos,
        jnp.repeat(scales.astype(jnp.float32), list_length, total_repeat_length=entries),
        jnp.repeat(table_rows[:, 0], list_length, total_repeat_length=entries),
        jnp.repeat(table_rows[:, 1], list_length, total_repeat_length=entries),
        side_cells,
    )
    grad_terms, squares = block_terms(voxel_rows, pictures, kind_ids, factor, live_mask, kernels)
    outgoing = jnp.zeros((slot_count, grad_terms.shape[1]), jnp.float32).at[targets].set(grad_terms)
    arrived = lax.all_to_all(
        outgoing.reshape(slab_count, capacity, grad_terms.shape[1]),
        "slab",
        split_axis=0,
        concat_axis=0,
        tiled=True,
    )
    partial_value = (
        jnp.zeros((slab_blocks, grad_terms.shape[1]), jnp.float32)
        .at[received.reshape(-1)]
        .add(arrived.reshape(slot_count, grad_terms.shape[1]))
    )
    losses = jnp.sum(squares.reshape(particles_here, list_length), axis=1) / (
        counts.astype(jnp.float32) * 128.0
    )
    grid = partial_value.reshape(planes_here, per_row, per_row, 2, 8, 8).transpose(3, 0, 1, 4, 2, 5)
    grid = grid.reshape(2, planes_here, side_cells, side_cells)
    cells = jnp.arange(side_cells, dtype=jnp.int32)
    cos_table, sin_table = dft_tables(cells, side_cells)
    halves = lax.psum_scatter(grid, "dom", scatter_dimension=3, tiled=True)
    real_part, imag_part = transform(halves[0], halves[1], cos_table, sin_table, "xyz,yk->xkz")
    pencil = lax.all_to_all(
        jnp.stack([real_part, imag_part]), "slab", split_axis=2, concat_axis=1, tiled=True
    )
    real_part, imag_part = transform(pencil[0], pencil[1], cos_table, sin_table, "xyz,xk->kyz")
    rows = lax.all_to_all(
        jnp.stack([real_part, imag_part]), "dom", split_axis=1, concat_axis=3, tiled=True
    )
    real_part, imag_part = transform(rows[0], rows[1], cos_table, sin_table, "xyz,zk->xyk")
    result = jnp.stack([real_part, imag_part])
    return (result, losses)


def solution(mesh):
    in_specs = (
        P(("groups", "slab"), None),
        P(),
        P(("groups", "slab", "dom"), None, None),
        P(("groups", "slab", "dom"), None, None),
        P(("groups", "slab", "dom"), None),
        P(("groups", "slab", "dom"), None),
        P(("groups", "slab", "dom")),
        P(("groups", "slab", "dom")),
        P(),
        P(("groups", "slab", "dom")),
    )
    out_specs = (P(None, ("groups", "dom"), "slab", None), P(("groups", "slab", "dom")))
    return jax.shard_map(body, mesh=mesh, in_specs=in_specs, out_specs=out_specs, check_vma=False)
```

profile of v0, /device:TPU:0, one launch (start us, length us, event | category | flops | bytes accessed | tf_op | source)
XLA Modules:
  0.0 1129.0 jit_solution(8470513400646602995)
XLA Ops:
  13.7 31.0 %scatter_custom_fusion = s32[16384]{0:T(1024)} fusion(s32[8192]{0:T(1024)S(1)} %bitcast.223, s32[8192]{0:T(1024)S(1)} %bitcast.230, s32[]{:T(128)} %constant.252.clone.1), kind=kCustom, calls=%fused_computation.105 | custom fusion | bytes 65540 | tf_op jit(solution)/shard_map/scatter | solution.py:81
  59.0 59.9 %gather_fusion.1 = bf16[16384,128]{1,0:T(8,128)(2,1)} fusion(bf16[32768,128]{1,0:T(8,128)(2,1)} %param.20, s32[16384]{0:T(1024)S(1)} %broadcast_clamp_fusion), kind=kCustom, calls=%fused_computation.1 | custom fusion | bytes 8454144 | tf_op jit(solution)/shard_map/jit(_take)/gather | solution.py:84
  118.9 7.7 broadcast_select_fusion
  162.7 8.6 sine_multiply_fusion
  171.3 52.0 %all-to-all-done.1 = bf16[8,2048,128]{2,1,0:T(8,128)(2,1)} async-done(((bf16[8,2048,128]{2,1,0:T(8,128)(2,1)}), bf16[8,2048,128]{2,1,0:T(8,128)(2,1)}, u32[]{:S(2)}, u32[]{:S(2)}) %all-to-all-start.1) | async-done | bytes 4194336 | tf_op jit(solution)/shard_map/all_to_all | solution.py:87
  223.3 24.6 %gather_fusion.2 = bf16[8192,128]{1,0:T(8,128)(2,1)S(1)} fusion(bf16[16384,128]{1,0:T(8,128)(2,1)} %bitcast.44, s32[8192]{0:T(1024)S(1)} %broadcast_clamp_fusion.1), kind=kCustom, calls=%fused_computation.2 | custom fusion | bytes 4227072 | tf_op jit(solution)/shard_map/gather | solution.py:88
  248.0 10.5 multiply_reduce_fusion
  268.6 24.7 %scatter_custom_fusion.1 = f32[16384,128]{1,0:T(8,128)} fusion(s32[8192]{0:T(1024)S(1)} %bitcast.225, f32[8192,128]{1,0:T(8,128)} %convolution_bitcast_fusion, f32[]{:T(128)} %constant.257.clone.1), kind=kCustom, calls=%fused_computation.36 | custom fusion | bytes 8389120 | tf_op jit(solution)/shard_map/scatter | solution.py:98
  293.3 187.6 %all_to_all.49 = f32[8,2048,128]{2,1,0:T(8,128)} all-to-all(f32[8,2048,128]{2,1,0:T(8,128)} %bitcast.213), channel_id=1, replica_groups=mesh['groups'=2,'slab'=8,'dom'=2] {'slab'}, dimensions={0} | all-to-all | bytes 16777216 | tf_op jit(solution)/shard_map/all_to_all | solution.py:99
  481.0 112.9 %scatter_custom_fusion.2 = f32[32768,128]{1,0:T(8,128)} fusion(s32[16384]{0:T(1024)S(1)} %bitcast.221, f32[16384,128]{1,0:T(8,128)} %bitcast.216, f32[]{:T(128)} %constant.257.clone.1), kind=kCustom, calls=%fused_computation.18 | custom fusion | flops 2097152 | bytes 16777728 | tf_op jit(solution)/shard_map/scatter-add | solution.py:109
  593.8 17.4 %copy.97 = f32[32768,128]{0,1:T(8,128)} copy(f32[32768,128]{1,0:T(8,128)} %scatter_custom_fusion.2) | data formatting | bytes 33554432 | tf_op jit(solution)/shard_map/scatter-add | solution.py:109
  611.2 31.2 %reshape.402 = f32[32,32,32,2,8,8]{2,1,0,5,4,3:T(8,128)} reshape(f32[32768,128]{0,1:T(8,128)} %copy.97) | data formatting | bytes 33554432 | tf_op jit(solution)/shard_map/reshape | solution.py:114
  642.5 76.3 %copy.98 = f32[2,32,32,8,32,8]{1,5,4,3,2,0:T(8,128)} copy(f32[2,32,32,8,32,8]{4,2,1,5,3,0:T(8,128)} %bitcast.51) | data formatting | bytes 33554432 | tf_op jit(solution)/shard_map/transpose | solution.py:114
  718.7 43.5 %copy.99 = f32[2,32,256,256]{3,2,1,0:T(8,128)} copy(f32[2,32,256,256]{1,3,2,0:T(8,128)} %bitcast.52) | data formatting | bytes 33554432 | tf_op jit(solution)/shard_map/reshape | solution.py:115
  762.3 24.9 %reduce-scatter.2.cloned.1.call-done = f32[2,32,256,128]{3,2,1,0:T(8,128)} async-done(((f32[2,32,256,256]{3,2,1,0:T(8,128)}), f32[2,32,256,128]{3,2,1,0:T(8,128)}) %reduce-scatter.2.cloned.1.call-update) | async-done | bytes 8388624 | tf_op jit(solution)/shard_map/reduce_scatter | solution.py:118
  787.2 8.0 fusion.15
  811.8 8.3 copy.104
  826.9 182.7 %all-to-all-done.3 = f32[2,32,256,128]{3,1,0,2:T(8,128)} async-done(((f32[2,32,256,128]{3,1,0,2:T(8,128)}), f32[2,32,256,128]{3,1,0,2:T(8,128)}, u32[]{:S(2)}, u32[]{:S(2)}) %all-to-all-start.3) | async-done | bytes 8388640 | tf_op jit(solution)/shard_map/all_to_all | solution.py:120
  1042.7 10.5 all_to_all.50
  1053.1 9.8 copy.165
  1062.9 7.7 fusion.113
  1077.0 8.7 fusion.24
  1099.4 8.3 subtract_bitcast_fusion
  1113.4 8.5 copy.112
  (96 shorter events, 148.9 us)
Async XLA Ops:
  7.2 240.8 %copy-start = (bf16[4,128,128]{2,1,0:T(8,128)(2,1)S(1)}, bf16[4,128,128]{2,1,0:T(8,128)(2,1)}, u32[]{:S(2)}) copy-start(bf16[4,128,128]{2,1,0:T(8,128)(2,1)} %param.21) | copy-start | bytes 393220
  44.7 14.2 %all-to-all-start = ((s32[8,1,2048]{2,1,0:T(1,128)}), s32[8,1,2048]{2,1,0:T(1,128)S(1)}, u32[]{:S(2)}, u32[]{:S(2)}) async-start(s32[8,1,2048]{2,1,0:T(1,128)} %bitcast.8), calls=%async_computation | async-start | bytes 131072 | tf_op jit(solution)/shard_map/all_to_all | solution.py:83
  126.6 4.9 copy-start.6
  126.6 96.7 %all-to-all-start.1 = ((bf16[8,2048,128]{2,1,0:T(8,128)(2,1)}), bf16[8,2048,128]{2,1,0:T(8,128)(2,1)}, u32[]{:S(2)}, u32[]{:S(2)}) async-start(bf16[8,2048,128]{2,1,0:T(8,128)(2,1)} %broadcast_select_fusion), calls=%async_computation.1 | async-start | bytes 8388608 | tf_op jit(solution)/shard_map/all_to_all | solution.py:87
  131.3 655.9 %reduce-scatter.2.cloned.1.call-start = ((), (), s32[]{:S(2)}) async-start(), calls=%async_computation.6 | async-start | bytes 25165824 | tf_op jit(solution)/shard_map/reduce_scatter | solution.py:118
  134.0 5.8 copy-start.17
  134.0 6.5 copy-start.14
  134.0 7.2 copy-start.15
  134.0 8.6 copy-start.7
  134.0 8.6 copy-start.8
  134.0 8.6 copy-start.9
  134.0 8.6 copy-start.10
  134.0 8.6 copy-start.11
  134.0 8.6 copy-start.12
  134.0 8.6 copy-start.13
  787.2 8.0 copy-start.4
  820.1 6.3 copy-start.16
  820.1 189.5 %all-to-all-start.3 = ((f32[2,32,256,128]{3,1,0,2:T(8,128)}), f32[2,32,256,128]{3,1,0,2:T(8,128)}, u32[]{:S(2)}, u32[]{:S(2)}) async-start(f32[2,32,256,128]{3,1,0,2:T(8,128)} %copy.104), calls=%async_computation.4 | async-start | bytes 16777216 | tf_op jit(solution)/shard_map/all_to_all | solution.py:120
  1077.0 8.7 copy-start.3
  1099.3 8.3 copy-start.2
  1099.4 8.3 copy-start.5
  1113.4 8.5 copy-start.1
Sparse Core Ops, SparseCore 0:
  762.4 24.7 reduce-scatter.1
where the time goes:
time: 1140 us; the launch traced here: 1130 us
  local copies, waits for them, and re-layouts  382 us (34%)
  waiting for transfers between devices  265 us (23%)
  blocking collectives  198 us (17%)
  other arithmetic  161 us (14%)
  matrix products  90.6 us (8%)
  starting transfers between devices  18.3 us (2%)
  between operations  14.8 us (1%)
    all_to_all x1, blocking collectives, body(): lax.all_to_all(outgoing.reshape(slab_count, capacity, grad_terms.shape[1]...  188 us
    all_to_all x1, waiting for transfers between devices, body(): lax.all_to_all(jnp.stack([real_part, imag_part]), 'slab', split_axis=2, c...  183 us
    scatter-add x1, other arithmetic, body(): partial_value = jnp.zeros((slab_blocks, grad_terms.shape[1]), jnp.float32...  113 us
    transpose x1, local copies, waits for them, and re-layouts, body(): partial_value.reshape(planes_here, per_row, per_row, 2, 8, 8)  76.3 us
    gather x1, local copies, waits for them, and re-layouts, body(): jnp.take(volume, received.reshape(-1), axis=0)  59.9 us
    all_to_all x1, waiting for transfers between devices, body(): lax.all_to_all(wanted_rows, 'slab', split_axis=0, concat_axis=0, tiled=True)  52 us
    reshape x1, local copies, waits for them, and re-layouts, body(): grid = grid.reshape(2, planes_here, side_cells, side_cells)  43.5 us
    reshape x1, local copies, waits for them, and re-layouts, body(): partial_value.reshape(planes_here, per_row, per_row, 2, 8, 8)  31.2 us
  transfers between devices with their start and end apart: 4, of which 4 were waited for; matrix products, arithmetic and copies ran while one was open for 4% of the time, Pallas kernels for 0%

commit v1 on v0

v1 whole, which is shorter than its diff:
```python
import functools
import math

import jax
import jax.numpy as jnp
from jax import lax
from jax.experimental import pallas as pl
from jax.experimental.pallas import tpu as pltpu
from jax.sharding import PartitionSpec as P

HIGHEST = lax.Precision.HIGHEST
LANES = 128
GROUP = 8
VMEM_LIMIT = 56 * 1024 * 1024

SMEM_SPEC = pl.BlockSpec(memory_space=pltpu.SMEM)
VMEM_SPEC = pl.BlockSpec(memory_space=pltpu.VMEM)
ANY_SPEC = pl.BlockSpec(memory_space=pl.ANY)


def params(**extra):
    return pltpu.CompilerParams(vmem_limit_bytes=VMEM_LIMIT, **extra)


def bits_of(count):
    return (count - 1).bit_length()


def route_kernel(slabs, cap, local_bits, list_length, owner_ref, local_ref, kind_ref, counts_ref, target_ref, word_ref, totals_ref):
    rows = owner_ref.shape[0]
    rows_each = list_length // LANES
    particles = rows // rows_each
    row_id = lax.broadcasted_iota(jnp.int32, (rows, LANES), 0)
    lane_id = lax.broadcasted_iota(jnp.int32, (rows, LANES), 1)
    particle = row_id // rows_each
    position = (row_id % rows_each) * LANES + lane_id
    limit = jnp.zeros((rows, LANES), jnp.int32)
    for i in range(particles):
        limit = jnp.where(particle == i, counts_ref[i], limit)
    owner = jnp.where(position < limit, owner_ref[...], -1)
    up_to = (
        lax.broadcasted_iota(jnp.int32, (LANES, LANES), 0)
        <= lax.broadcasted_iota(jnp.int32, (LANES, LANES), 1)
    ).astype(jnp.bfloat16)
    ones = jnp.ones((LANES, LANES), jnp.bfloat16)
    before = (
        lax.broadcasted_iota(jnp.int32, (rows, rows), 1)
        < lax.broadcasted_iota(jnp.int32, (rows, rows), 0)
    ).astype(jnp.bfloat16)

    def one_slab(slab, target):
        mine = owner == slab
        hits = mine.astype(jnp.float32).astype(jnp.bfloat16)
        inside = jnp.dot(hits, up_to, preferred_element_type=jnp.float32)
        row_sum = jnp.dot(hits, ones, preferred_element_type=jnp.float32)
        above = jnp.dot(before, row_sum.astype(jnp.bfloat16), preferred_element_type=jnp.float32)
        rank = (inside + above).astype(jnp.int32) - 1
        total = (above[rows - 1:rows, :] + row_sum[rows - 1:rows, :]).astype(jnp.int32)
        totals_ref[pl.ds(slab, 1), :] = total
        return jnp.where(mine, slab * cap + rank, target)

    target = lax.fori_loop(0, slabs, one_slab, jnp.full((rows, LANES), slabs * cap, jnp.int32))
    target_ref[...] = target
    kind_bits = local_bits
    word = local_ref[...] | (kind_ref[...] << kind_bits) | (position << (kind_bits + 2))
    word_ref[...] = word | (particle << (kind_bits + 2 + bits_of(list_length)))


def pack_kernel(slots, target_ref, word_ref, image_ref, out_ref, meta_ref, wide_ref, staged_ref):
    entries = image_ref.shape[0]
    step = 256

    @pl.loop(0, entries // step)
    def _(i):
        at = pl.multiple_of(i * step, step)
        wide_ref[pl.ds(at, step), :] = image_ref[pl.ds(at, step), :].astype(jnp.float32)

    @pl.loop(0, entries // 16)
    def _(i):
        first = i * 16
        targets = [target_ref[first + j] for j in range(16)]
        rows = [wide_ref[pl.ds(first + j, 1), :] for j in range(16)]
        for j in range(16):
            staged_ref[pl.ds(targets[j], 1), :] = rows[j]
        for j in range(16):
            meta_ref[targets[j]] = word_ref[first + j]

    @pl.loop(0, slots // step)
    def _(i):
        at = pl.multiple_of(i * step, step)
        out_ref[pl.ds(at, step), :] = staged_ref[pl.ds(at, step), :].astype(jnp.bfloat16)


def decode_kernel(local_bits, dummy, word_ref, live_ref, index_ref):
    rows = word_ref.shape[0]
    live = live_ref[...] != 0
    index = jnp.where(live, word_ref[...] & ((1 << local_bits) - 1), dummy)
    lane = lax.broadcasted_iota(jnp.int32, (rows, LANES), 1)
    clash = jnp.zeros((rows, LANES), jnp.int32)
    for shift in range(1, GROUP):
        earlier = pltpu.roll(index, shift, 1)
        same = (earlier == index) & (lane % GROUP >= shift) & live
        clash = clash | same.astype(jnp.int32)
    shift = 1
    while shift < GROUP:
        clash = clash | pltpu.roll(clash, LANES - shift, 1)
        shift *= 2
    index_ref[...] = index | (clash << 24)


def gather_kernel(slabs, cap, index_ref, totals_ref, volume_ref, out_ref, wide_ref, staged_ref):
    blocks = volume_ref.shape[0]
    step = 256

    @pl.loop(0, blocks // step)
    def _(i):
        at = pl.multiple_of(i * step, step)
        wide_ref[pl.ds(at, step), :] = volume_ref[pl.ds(at, step), :].astype(jnp.float32)

    @pl.loop(0, slabs)
    def _(source):
        live = totals_ref[source]

        @pl.loop(0, (live + 15) // 16)
        def _(i):
            first = source * cap + i * 16
            places = [index_ref[first + j] & 0xFFFFFF for j in range(16)]
            rows = [wide_ref[pl.ds(places[j], 1), :] for j in range(16)]
            for j in range(16):
                staged_ref[pl.ds(i * 16 + j, 1), :] = rows[j]

        width = min(step, cap)

        @pl.loop(0, (live + width - 1) // width)
        def _(i):
            at = pl.multiple_of(i * width, width)
            to = pl.multiple_of(source * cap + i * width, width)
            out_ref[pl.ds(to, width), :] = staged_ref[pl.ds(at, width), :].astype(jnp.bfloat16)


def sine(angle):
    turns = jnp.floor(angle * (1.0 / math.pi) + 0.5)
    rest = angle - turns * 3.140625
    rest = rest - turns * 9.67502593994140625e-4
    rest = rest - turns * 1.509957990978376e-7
    odd = turns - 2.0 * jnp.floor(turns * 0.5)
    square = rest * rest
    poly = 2.718121e-6
    poly = poly * square - 1.9839334e-4
    poly = poly * square + 8.3333293e-3
    poly = poly * square - 1.6666667e-1
    value = rest + rest * square * poly
    return value * (1.0 - 2.0 * odd)


def slab_kernel(
    side, local_bits, list_length, particles, tile,
    totals_ref, defocus_ref, phase_ref, scale_ref, index_ref,
    word_ref, voxel_ref, image_ref, forward_ref, backward_ref, unit_ref,
    grad_ref, square_ref,
    sum_ref, staged_ref, sem,
):
    source = pl.program_id(0)
    cap = word_ref.shape[2]
    blocks = grad_ref.shape[0]
    features = image_ref.shape[2]
    kinds = forward_ref.shape[0] // features
    position_bits = bits_of(list_length)
    per_row = side // 8
    live = totals_ref[source]

    @pl.when(source == 0)
    def _():
        @pl.loop(0, blocks // 256)
        def _(i):
            at = pl.multiple_of(i * 256, 256)
            sum_ref[pl.ds(at, 256), :] = jnp.zeros((256, features), jnp.float32)

    square_ref[...] = jnp.zeros_like(square_ref)

    @pl.loop(0, (live + tile - 1) // tile)
    def _(t):
        at = pl.multiple_of(t * tile, tile)
        word = word_ref[0, :, pl.ds(at, tile)]
        kind = (word >> local_bits) & 3
        position = (word >> (local_bits + 2)) & (list_length - 1)
        particle = (word >> (local_bits + 2 + position_bits)) & (particles - 1)
        valid = lax.broadcasted_iota(jnp.int32, (1, tile), 1) + at < live
        defocus = jnp.zeros((1, tile), jnp.float32)
        phase = jnp.zeros((1, tile), jnp.float32)
        scale = jnp.zeros((1, tile), jnp.float32)
        for j in range(particles):
            chosen = particle == j
            defocus = jnp.where(chosen, defocus_ref[source * particles + j], defocus)
            phase = jnp.where(chosen, phase_ref[source * particles + j], phase)
            scale = jnp.where(chosen, scale_ref[source * particles + j], scale)
        half = features // 2
        cell = lax.broadcasted_iota(jnp.int32, (half, tile), 0)
        vert = ((position // per_row) * 8 + cell // 8 - side // 2).astype(jnp.float32)
        horiz = ((position % per_row) * 8 + cell % 8 - side // 2).astype(jnp.float32)
        radius = (vert * vert + horiz * horiz) * (1.0 / float((side // 2) ** 2))
        factor = scale * sine(defocus * radius + phase)
        factor = jnp.concatenate([factor, factor], axis=0)
        contract_last = (((1,), (1,)), ((), ()))
        each_kind = lax.dot_general(
            forward_ref[...], voxel_ref[0, pl.ds(at, tile), :], contract_last,
            preferred_element_type=jnp.float32,
        )
        extracted = each_kind[0:features, :]
        for k in range(1, kinds):
            extracted = jnp.where(kind == k, each_kind[k * features:(k + 1) * features, :], extracted)
        picture = lax.dot_general(
            unit_ref[...], image_ref[0, pl.ds(at, tile), :], contract_last,
            preferred_element_type=jnp.float32,
        )
        misfit = jnp.where(valid, factor * extracted - picture, 0.0)
        squares = jnp.sum(misfit * misfit, axis=0, keepdims=True)
        which = lax.broadcasted_iota(jnp.int32, (particles, tile), 0)
        spread = jnp.where(valid & (particle == which), squares, 0.0)
        folded = spread[:, 0:LANES]
        for i in range(1, tile // LANES):
            folded = folded + spread[:, i * LANES:(i + 1) * LANES]
        square_ref[0] = square_ref[0] + folded
        weighted = (factor * misfit).astype(jnp.bfloat16)
        none = jnp.zeros_like(weighted)
        spread_back = jnp.concatenate(
            [jnp.where(kind == k, weighted, none) for k in range(kinds)], axis=0
        )
        terms = jnp.dot(backward_ref[...], spread_back, preferred_element_type=jnp.float32)
        staged_ref[...] = terms.T

        @pl.loop(0, (jnp.minimum(live - at, tile) + GROUP - 1) // GROUP)
        def _(g):
            base = source * cap + at + g * GROUP
            marked = index_ref[base]
            places = [index_ref[base + j] & 0xFFFFFF for j in range(GROUP)]

            @pl.when(marked < (1 << 24))
            def _():
                held = [sum_ref[pl.ds(places[j], 1), :] for j in range(GROUP)]
                new = [staged_ref[pl.ds(g * GROUP + j, 1), :] for j in range(GROUP)]
                for j in range(GROUP):
                    sum_ref[pl.ds(places[j], 1), :] = held[j] + new[j]

            @pl.when(marked >= (1 << 24))
            def _():
                for j in range(GROUP):
                    sum_ref[pl.ds(places[j], 1), :] = (
                        sum_ref[pl.ds(places[j], 1), :] + staged_ref[pl.ds(g * GROUP + j, 1), :]
                    )

    @pl.when(source == pl.num_programs(0) - 1)
    def _():
        copy = pltpu.make_async_copy(sum_ref.at[pl.ds(0, blocks)], grad_ref, sem)
        copy.start()
        copy.wait()


def dft_tables(input_index, side_cells):
    freqs = jnp.arange(side_cells, dtype=jnp.int32)
    product = input_index[:, None] * freqs[None, :] % side_cells
    angles = product.astype(jnp.float32) * (2.0 * math.pi / side_cells)
    norming = 1.0 / math.sqrt(side_cells)
    return (jnp.cos(angles) * norming, jnp.sin(angles) * norming)


def transform(real_part, imag_part, cos_table, sin_table, pattern):
    new_real = jnp.einsum(pattern, real_part, cos_table, precision=HIGHEST) - jnp.einsum(
        pattern, imag_part, sin_table, precision=HIGHEST
    )
    new_imag = jnp.einsum(pattern, real_part, sin_table, precision=HIGHEST) + jnp.einsum(
        pattern, imag_part, cos_table, precision=HIGHEST
    )
    return (new_real, new_imag)


def gradient_of_slab(volume, kernels, images, owners, local_block, kinds, counts, ctf_code, ctf_table, scales):
    slabs = lax.axis_size("slab")
    particles, list_length, features = images.shape
    side = math.isqrt(list_length * 64)
    entries = particles * list_length
    cap = 2 * entries // slabs
    slots = slabs * cap
    blocks = volume.shape[0]
    local_bits = bits_of(blocks)
    kind_count = kernels.shape[0]
    rows = entries // LANES
    int_rows = jax.ShapeDtypeStruct((rows, LANES), jnp.int32)

    target, word, totals = pl.pallas_call(
        functools.partial(route_kernel, slabs, cap, local_bits, list_length),
        out_shape=(int_rows, int_rows, jax.ShapeDtypeStruct((slabs, LANES), jnp.int32)),
        in_specs=[VMEM_SPEC, VMEM_SPEC, VMEM_SPEC, SMEM_SPEC],
        out_specs=(VMEM_SPEC, VMEM_SPEC, VMEM_SPEC),
        compiler_params=params(),
        name="route",
    )(
        owners.reshape(rows, LANES), local_block.reshape(rows, LANES), kinds.reshape(rows, LANES), counts
    )
    packed, meta = pl.pallas_call(
        functools.partial(pack_kernel, slots),
        out_shape=(
            jax.ShapeDtypeStruct((slots, features), jnp.bfloat16),
            jax.ShapeDtypeStruct((slots + 1024,), jnp.int32),
        ),
        in_specs=[SMEM_SPEC, SMEM_SPEC, VMEM_SPEC],
        out_specs=(VMEM_SPEC, SMEM_SPEC),
        scratch_shapes=[
            pltpu.VMEM((entries, features), jnp.float32),
            pltpu.VMEM((slots + 8, features), jnp.float32),
        ],
        compiler_params=params(),
        name="pack",
    )(target.reshape(entries), word.reshape(entries), images.reshape(entries, features))

    code = ctf_code | ((scales.astype(jnp.float32) * 256.0).astype(jnp.int32) << 8)
    header = jnp.concatenate(
        [
            totals[:, 0:1],
            jnp.broadcast_to(code[None, :], (slabs, particles)),
            jnp.zeros((slabs, LANES - 1 - particles), jnp.int32),
        ],
        axis=1,
    )
    sent = jnp.concatenate([meta[:slots].reshape(slabs, cap), header], axis=1)
    arrived = lax.all_to_all(sent, "slab", split_axis=0, concat_axis=0, tiled=True)
    words = arrived[:, :cap]
    totals_in = arrived[:, cap]
    codes_in = arrived[:, cap + 1:cap + 1 + particles]
    live = (jnp.arange(cap, dtype=jnp.int32)[None, :] < totals_in[:, None]).astype(jnp.int32)
    table_rows = ctf_table[(codes_in & 255).reshape(-1)]
    scale_in = (codes_in >> 8).astype(jnp.float32).reshape(-1) * (1.0 / 256.0)

    pictures = lax.all_to_all(
        packed.reshape(slabs, cap, features), "slab", split_axis=0, concat_axis=0, tiled=True
    )

    index = pl.pallas_call(
        functools.partial(decode_kernel, local_bits, blocks),
        out_shape=jax.ShapeDtypeStruct((slots // LANES, LANES), jnp.int32),
        in_specs=[VMEM_SPEC, VMEM_SPEC],
        out_specs=VMEM_SPEC,
        compiler_params=params(),
        name="decode",
    )(words.reshape(slots // LANES, LANES), live.reshape(slots // LANES, LANES))
    index = index.reshape(slots)
    voxels = pl.pallas_call(
        functools.partial(gather_kernel, slabs, cap),
        out_shape=jax.ShapeDtypeStruct((slots, features), jnp.bfloat16),
        in_specs=[SMEM_SPEC, SMEM_SPEC, VMEM_SPEC],
        out_specs=VMEM_SPEC,
        scratch_shapes=[
            pltpu.VMEM((blocks + 8, features), jnp.float32),
            pltpu.VMEM((cap, features), jnp.float32),
        ],
        compiler_params=params(),
        cost_estimate=pl.CostEstimate(flops=0, bytes_accessed=100 * 1024 * 1024, transcendentals=0),
        name="read_voxels",
    )(index, totals_in, volume)

    forward = jnp.transpose(kernels, (0, 2, 1)).reshape(kind_count * features, features)
    backward = jnp.transpose(kernels, (1, 0, 2)).reshape(features, kind_count * features)
    unit = jnp.eye(features, dtype=jnp.bfloat16)
    tile = min(512, cap)
    per_source = lambda length, width: pl.BlockSpec((1, length, width), lambda s: (s, 0, 0))
    whole = lambda shape: pl.BlockSpec(shape, lambda s: (0,) * len(shape))
    grad, squares = pl.pallas_call(
        functools.partial(slab_kernel, side, local_bits, list_length, particles, tile),
        grid=(slabs,),
        out_shape=(
            jax.ShapeDtypeStruct((blocks, features), jnp.float32),
            jax.ShapeDtypeStruct((slabs, particles, LANES), jnp.float32),
        ),
        in_specs=[SMEM_SPEC] * 5 + [
            per_source(1, cap),
            per_source(cap, features),
            per_source(cap, features),
            whole(forward.shape),
            whole(backward.shape),
            whole(unit.shape),
        ],
        out_specs=(ANY_SPEC, per_source(particles, LANES)),
        scratch_shapes=[
            pltpu.VMEM((blocks + 8, features), jnp.float32),
            pltpu.VMEM((tile, features), jnp.float32),
            pltpu.SemaphoreType.DMA(()),
        ],
        compiler_params=params(),
        name="compare_and_add",
    )(
        totals_in, table_rows[:, 0], table_rows[:, 1], scale_in, index,
        words.reshape(slabs, 1, cap), voxels.reshape(slabs, cap, features), pictures,
        forward, backward, unit,
    )
    returned = lax.all_to_all(
        jnp.sum(squares, axis=2), "slab", split_axis=0, concat_axis=0, tiled=True
    )
    losses = jnp.sum(returned, axis=0) / (counts.astype(jnp.float32) * 128.0)
    return grad, losses, side


def body(*arrays):
    grad, losses, side_cells = gradient_of_slab(*arrays)
    per_row = side_cells // 8
    planes_here = grad.shape[0] // (per_row * per_row)
    grid = grad.reshape(planes_here, per_row, per_row, 2, 8, 8).transpose(3, 0, 1, 4, 2, 5)
    grid = grid.reshape(2, planes_here, side_cells, side_cells)
    cells = jnp.arange(side_cells, dtype=jnp.int32)
    cos_table, sin_table = dft_tables(cells, side_cells)
    halves = lax.psum_scatter(grid, "dom", scatter_dimension=3, tiled=True)
    real_part, imag_part = transform(halves[0], halves[1], cos_table, sin_table, "xyz,yk->xkz")
    pencil = lax.all_to_all(
        jnp.stack([real_part, imag_part]), "slab", split_axis=2, concat_axis=1, tiled=True
    )
    real_part, imag_part = transform(pencil[0], pencil[1], cos_table, sin_table, "xyz,xk->kyz")
    rows = lax.all_to_all(
        jnp.stack([real_part, imag_part]), "dom", split_axis=1, concat_axis=3, tiled=True
    )
    real_part, imag_part = transform(rows[0], rows[1], cos_table, sin_table, "xyz,zk->xyk")
    result = jnp.stack([real_part, imag_part])
    return (result, losses)


def solution(mesh):
    in_specs = (
        P(("groups", "slab"), None),
        P(),
        P(("groups", "slab", "dom"), None, None),
        P(("groups", "slab", "dom"), None, None),
        P(("groups", "slab", "dom"), None),
        P(("groups", "slab", "dom"), None),
        P(("groups", "slab", "dom")),
        P(("groups", "slab", "dom")),
        P(),
        P(("groups", "slab", "dom")),
    )
    out_specs = (P(None, ("groups", "dom"), "slab", None), P(("groups", "slab", "dom")))
    return jax.shard_map(body, mesh=mesh, in_specs=in_specs, out_specs=out_specs, check_vma=False)
```

time: 1140 us -> 776 us (0.68)
  blocking collectives: 198 us -> 24.5 us
  other arithmetic: 161 us -> 6.36 us
  local copies, waits for them, and re-layouts: 382 us -> 237 us
  Pallas kernels: 0 us -> 84.8 us
  starting transfers between devices: 18.3 us -> 51.5 us
  matrix products: 90.6 us -> 73.1 us
    all_to_all x1, blocking collectives: 188 us -> 14 us  [gradient_of_slab(): lax.all_to_all(sent, 'slab', split_axis=0, concat_axis=0, tiled=True)]
    scatter-add x1 -> x0, other arithmetic: 113 us -> none  [body(): partial_value = jnp.zeros((slab_blocks, grad_terms.shape[1]), jnp.float32...]
    gather x6 -> x1, local copies, waits for them, and re-layouts: 87.1 us -> 0.6 us  [gradient_of_slab(): table_rows = ctf_table[(codes_in & 255).reshape(-1)]]
    pallas_call x0 -> x5, Pallas kernels: none -> 84.8 us  [the longest x1 44.2 us: gradient_of_slab(): pl.pallas_call(functools.partial(slab_kernel, side, local_bits, list_leng...]
    scatter x2 -> x0, local copies, waits for them, and re-layouts: 55.8 us -> none  [the longest x1 31 us: body(): jnp.zeros((slot_count,), jnp.int32).at[targets].set(local_ids)]
    all_to_all x2, starting transfers between devices: 12 us -> 45.3 us  [the longest x1 40.6 us: gradient_of_slab(): lax.all_to_all(jnp.sum(squares, axis=2), 'slab', split_axis=0, concat_axi...]
    dot_general x2 -> x0, matrix products: 17.4 us -> none  [the longest x1 10.5 us: block_terms(): extracted = jnp.dot(spread, forward, preferred_element_type=jnp.float32)]
    pallas_call x0 -> x1, local copies, waits for them, and re-layouts: none -> 17.4 us  [gradient_of_slab(): pl.pallas_call(functools.partial(slab_kernel, side, local_bits, list_leng...]
  transfers between devices with their start and end apart: 4 -> 4, of which waited for: 4 -> 3; matrix products, arithmetic and copies ran while one was open for 4% -> 5% of each run, Pallas kernels for 0% -> 2%
where the time goes in v1:
time: 776 us; the launch traced here: 765 us
  waiting for transfers between devices  273 us (35%)
  local copies, waits for them, and re-layouts  237 us (31%)
  Pallas kernels  84.8 us (11%)
  matrix products  73.1 us (9%)
  starting transfers between devices  51.5 us (7%)
  blocking collectives  24.5 us (3%)
  between operations  14.7 us (2%)
    all_to_all x1, waiting for transfers between devices, body(): lax.all_to_all(jnp.stack([real_part, imag_part]), 'slab', split_axis=2, c...  183 us
    transpose x1, local copies, waits for them, and re-layouts, body(): grad.reshape(planes_here, per_row, per_row, 2, 8, 8)  76.3 us
    all_to_all x1, waiting for transfers between devices, gradient_of_slab(): lax.all_to_all(packed.reshape(slabs, cap, features), 'slab', split_axis=0...  67.9 us
    pallas_call x1, Pallas kernels, gradient_of_slab(): pl.pallas_call(functools.partial(slab_kernel, side, local_bits, list_leng...  44.2 us
    reshape x1, local copies, waits for them, and re-layouts, body(): grid = grid.reshape(2, planes_here, side_cells, side_cells)  43.6 us
    all_to_all x1, starting transfers between devices, gradient_of_slab(): lax.all_to_all(jnp.sum(squares, axis=2), 'slab', split_axis=0, concat_axi...  40.6 us
    reshape x1, local copies, waits for them, and re-layouts, body(): grad.reshape(planes_here, per_row, per_row, 2, 8, 8)  31.2 us
    reduce_scatter x1, waiting for transfers between devices, body(): halves = lax.psum_scatter(grid, 'dom', scatter_dimension=3, tiled=True)  22.2 us
  transfers between devices with their start and end apart: 4, of which 3 were waited for; matrix products, arithmetic and copies ran while one was open for 5% of the time, Pallas kernels for 2%

profile of v1, /device:TPU:0, one launch (start us, length us, event | category | flops | bytes accessed | tf_op | source)
XLA Modules:
  0.0 765.1 jit_solution(12350129945661603852)
XLA Ops:
  13.7 19.4 %pack.1 = (bf16[16384,128]{1,0:T(8,128)(2,1)}, s32[17408]{0:T(1024)}) custom-call(s32[8192]{0:T(1024)} %bitcast.134, s32[8192]{0:T(1024)} %bitcast.135, bf16[8192,128]{1,0:T(8,128)(2,1)} %bitcast.125), custom_call_target="tpu_custom_call" | custom-call | tf_op jit(solution)/shard_map/pack/pallas_call | solution.py:300
  35.4 14.0 %all_to_all.56 = s32[8,1,2176]{2,1,0:T(1,128)S(1)} all-to-all(s32[8,1,2176]{2,1,0:T(1,128)S(1)} %all_to_all.39), channel_id=1, replica_groups=mesh['groups'=2,'slab'=8,'dom'=2] {'slab'}, dimensions={0} | all-to-all | bytes 139264 | tf_op jit(solution)/shard_map/all_to_all | solution.py:326
  62.2 15.4 %read_voxels.1 = bf16[16384,128]{1,0:T(8,128)(2,1)} custom-call(s32[16384]{0:T(1024)} %bitcast.126, s32[8]{0:T(128)} %copy-done.6, bf16[32768,128]{1,0:T(8,128)(2,1)} %volume_ref.1), custom_call_target="tpu_custom_call" | custom-call | bytes 104857600 | tf_op jit(solution)/shard_map/read_voxels/pallas_call | solution.py:347
  78.3 67.9 %all-to-all-done.1.image_ref = bf16[8,2048,128]{2,1,0:T(8,128)(2,1)} async-done(((bf16[8,2048,128]{2,1,0:T(8,128)(2,1)}), bf16[8,2048,128]{2,1,0:T(8,128)(2,1)}, u32[]{:S(2)}, u32[]{:S(2)}) %all-to-all-start.1) | async-done | bytes 4194336 | tf_op jit(solution)/shard_map/all_to_all | solution.py:334
  146.2 44.2 %compare_and_add.1 = (f32[32768,128]{1,0:T(8,128)}, f32[8,8,128]{2,1,0:T(8,128)}) custom-call(s32[8]{0:T(128)} %copy-done.6, f32[64]{0:T(128)} %get-tuple-element.23.defocus_ref, f32[64]{0:T(128)} %get-tuple-element.22.phase_ref, f32[64]{0:T(128)} %mul.156.scale_ref, s32[16384]{0:T(1024)} %bitcast.127, s32[8,1,2048]{2,1,0:T(1,128)} %reshape.113.word_ref, ...), custom_call_target="tpu_custom_call" | custom-call | tf_op jit(solution)/shard_map/compare_and_add/pallas_call | solution.py:367
  190.4 17.4 %copy.51 = f32[32768,128]{0,1:T(8,128)} copy(f32[32768,128]{1,0:T(8,128)} %get-tuple-element.14) | data formatting | bytes 33554432 | tf_op jit(solution)/shard_map/compare_and_add/pallas_call | solution.py:367
  207.8 31.2 %reshape.118 = f32[32,32,32,2,8,8]{2,1,0,5,4,3:T(8,128)} reshape(f32[32768,128]{0,1:T(8,128)} %copy.51) | data formatting | bytes 33554432 | tf_op jit(solution)/shard_map/reshape | solution.py:406
  239.1 76.3 %copy.52 = f32[2,32,32,8,32,8]{1,5,4,3,2,0:T(8,128)} copy(f32[2,32,32,8,32,8]{4,2,1,5,3,0:T(8,128)} %bitcast.14) | data formatting | bytes 33554432 | tf_op jit(solution)/shard_map/transpose | solution.py:406
  315.3 43.6 %copy.53 = f32[2,32,256,256]{3,2,1,0:T(8,128)} copy(f32[2,32,256,256]{1,3,2,0:T(8,128)} %bitcast.15) | data formatting | bytes 33554432 | tf_op jit(solution)/shard_map/reshape | solution.py:407
  360.3 40.6 %all-to-all-start.4 = ((f32[8,1,8]{2,1,0:T(1,128)}), f32[8,1,8]{2,1,0:T(1,128)S(1)}, u32[]{:S(2)}, u32[]{:S(2)}) async-start(f32[8,1,8]{2,1,0:T(1,128)} %bitcast.41), calls=%async_computation.5 | async-start | bytes 8192 | tf_op jit(solution)/shard_map/all_to_all | solution.py:395
  400.9 22.2 %reduce-scatter.2.cloned.1.call-done = f32[2,32,256,128]{3,2,1,0:T(8,128)} async-done(((f32[2,32,256,256]{3,2,1,0:T(8,128)}), f32[2,32,256,128]{3,2,1,0:T(8,128)}) %reduce-scatter.2.cloned.1.call-update) | async-done | bytes 8388624 | tf_op jit(solution)/shard_map/reduce_scatter | solution.py:410
  423.1 7.8 %fusion = f32[256,32,128]{2,0,1:T(8,128)S(1)} fusion(f32[2,32,256,128]{3,2,1,0:T(8,128)} %reduce-scatter.2.cloned.1.call-done), kind=kOutput, calls=%fused_computation.14 | convolution fusion | flops 3222208512 | bytes 8388608 | tf_op jit(solution)/shard_map/xyz,yk->xkz/dot_general | solution.py:271
  447.8 8.3 %copy.58 = f32[2,32,256,128]{3,1,0,2:T(8,128)} copy(f32[2,32,256,128]{3,2,1,0:T(8,128)S(1)} %pad_maximum_fusion) | data formatting | bytes 16777216 | tf_op jit(solution)/shard_map/stack | solution.py:413
  456.0 6.1 all-to-all-start.2
  462.7 182.9 %all-to-all-done.2 = f32[2,32,256,128]{3,1,0,2:T(8,128)} async-done(((f32[2,32,256,128]{3,1,0,2:T(8,128)}), f32[2,32,256,128]{3,1,0,2:T(8,128)}, u32[]{:S(2)}, u32[]{:S(2)}) %all-to-all-start.2) | async-done | bytes 8388640 | tf_op jit(solution)/shard_map/all_to_all | solution.py:412
  678.6 10.5 %all_to_all.57 = f32[2,256,32,128]{3,2,0,1:T(8,128)S(1)} all-to-all(f32[2,256,32,128]{3,2,0,1:T(8,128)S(1)} %copy.64), channel_id=1, replica_groups=mesh['groups'=2,'slab'=8,'dom'=2] {'dom'}, dimensions={1} | all-to-all | bytes 16777216 | tf_op jit(solution)/shard_map/all_to_all | solution.py:416
  689.1 9.8 %copy.90 = f32[2,2,128,32,128]{4,1,2,3,0:T(2,128)} copy(f32[2,2,128,32,128]{4,3,0,2,1:T(8,128)S(1)} %bitcast.122) | data formatting | bytes 16777216 | tf_op jit(solution)/shard_map/all_to_all | solution.py:416
  698.9 7.7 %fusion.89 = (f32[1,128,32,2,128]{4,3,1,2,0:T(2,128)}, f32[1,128,32,2,128]{4,3,1,2,0:T(2,128)}) fusion(f32[2,128,32,2,128]{4,3,1,2,0:T(2,128)} %bitcast.121), kind=kLoop, calls=%fused_computation.122 | loop fusion | bytes 16777216 | tf_op jit(solution)/shard_map/slice | solution.py:419
  706.6 6.4 squeeze.34
  713.0 8.7 %fusion.7 = f32[128,32,256]{2,0,1:T(8,128)} fusion(f32[128,32,256]{2,0,1:T(8,128)} %squeeze.34), kind=kOutput, calls=%fused_computation.24 | convolution fusion | flops 3222208512 | bytes 8388608 | tf_op jit(solution)/shard_map/xyz,zk->xyk/dot_general | solution.py:271
  721.7 6.9 fusion.16
  728.7 6.6 squeeze.35
  735.3 8.3 %subtract_bitcast_fusion = f32[1,128,32,256]{3,1,2,0:T(8,128)S(1)} fusion(f32[128,32,256]{2,0,1:T(8,128)} %fusion.16, f32[128,32,256]{2,0,1:T(8,128)} %squeeze.35), kind=kOutput, calls=%fused_computation.9 | convolution fusion | flops 3223257088 | bytes 12582912 | tf_op jit(solution)/shard_map/xyz,zk->xyk/dot_general | solution.py:268
  749.3 8.5 %copy.67 = f32[2,128,32,256]{3,2,1,0:T(8,128)} copy(f32[2,128,32,256]{3,1,2,0:T(8,128)S(1)} %pad_maximum_fusion.2) | data formatting | bytes 16777216
  (71 shorter events, 79.6 us)
Async XLA Ops:
  49.5 4.7 copy-start.7
  49.5 4.9 copy-start.4
  49.5 96.7 %all-to-all-start.1 = ((bf16[8,2048,128]{2,1,0:T(8,128)(2,1)}), bf16[8,2048,128]{2,1,0:T(8,128)(2,1)}, u32[]{:S(2)}, u32[]{:S(2)}) async-start(bf16[8,2048,128]{2,1,0:T(8,128)(2,1)} %bitcast.124), calls=%async_computation.1 | async-start | bytes 8388608 | tf_op jit(solution)/shard_map/all_to_all | solution.py:334
  54.2 369.0 %reduce-scatter.2.cloned.1.call-start = ((), (), s32[]{:S(2)}) async-start(), calls=%async_computation.6 | async-start | bytes 25165824 | tf_op jit(solution)/shard_map/reduce_scatter | solution.py:410
  57.8 4.4 copy-start.6
  358.9 0.8 copy-start.5
  360.3 95.7 %all-to-all-start.4 = ((f32[8,1,8]{2,1,0:T(1,128)}), f32[8,1,8]{2,1,0:T(1,128)S(1)}, u32[]{:S(2)}, u32[]{:S(2)}) async-start(f32[8,1,8]{2,1,0:T(1,128)} %bitcast.41), calls=%async_computation.5 | async-start | bytes 8192 | tf_op jit(solution)/shard_map/all_to_all | solution.py:395
  423.1 7.8 %copy-start.2 = (f32[2,32,256,128]{3,2,1,0:T(8,128)S(1)}, f32[2,32,256,128]{3,2,1,0:T(8,128)}, u32[]{:S(2)}) copy-start(f32[2,32,256,128]{3,2,1,0:T(8,128)} %reduce-scatter.2.cloned.1.call-done) | copy-start | bytes 25165828
  456.0 6.2 copy-start.8
  456.0 189.6 %all-to-all-start.2 = ((f32[2,32,256,128]{3,1,0,2:T(8,128)}), f32[2,32,256,128]{3,1,0,2:T(8,128)}, u32[]{:S(2)}, u32[]{:S(2)}) async-start(f32[2,32,256,128]{3,1,0,2:T(8,128)} %copy.58), calls=%async_computation.3 | async-start | bytes 16777216 | tf_op jit(solution)/shard_map/all_to_all | solution.py:412
  713.0 8.7 %copy-start.1 = (f32[128,32,256]{2,0,1:T(8,128)S(1)}, f32[128,32,256]{2,0,1:T(8,128)}, u32[]{:S(2)}) copy-start(f32[128,32,256]{2,0,1:T(8,128)} %squeeze.34) | copy-start | bytes 12582916
  735.3 8.3 %copy-start = (f32[128,32,256]{2,0,1:T(8,128)S(1)}, f32[128,32,256]{2,0,1:T(8,128)}, u32[]{:S(2)}) copy-start(f32[128,32,256]{2,0,1:T(8,128)} %squeeze.35) | copy-start | bytes 12582916
  735.3 8.3 %copy-start.3 = (f32[128,32,256]{2,0,1:T(8,128)S(1)}, f32[128,32,256]{2,0,1:T(8,128)}, u32[]{:S(2)}) copy-start(f32[128,32,256]{2,0,1:T(8,128)} %fusion.7) | copy-start | bytes 12582916
Sparse Core Ops, SparseCore 0:
  359.0 64.0 reduce-scatter.1

commit v2 on v1

--- a/solution.py
+++ b/solution.py
@@ -3,13 +3,14 @@
 
 import jax
 import jax.numpy as jnp
+import numpy as np
 from jax import lax
 from jax.experimental import pallas as pl
 from jax.experimental.pallas import tpu as pltpu
 from jax.sharding import PartitionSpec as P
 
-HIGHEST = lax.Precision.HIGHEST
 LANES = 128
+QUADS = 1
 GROUP = 8
 VMEM_LIMIT = 56 * 1024 * 1024
 
@@ -156,13 +157,13 @@
 def slab_kernel(
     side, local_bits, list_length, particles, tile,
     totals_ref, defocus_ref, phase_ref, scale_ref, index_ref,
-    word_ref, voxel_ref, image_ref, forward_ref, backward_ref, unit_ref,
-    grad_ref, square_ref,
-    sum_ref, staged_ref, sem,
+    core_ref, word_ref, voxel_ref, image_ref, forward_ref, backward_ref, unit_ref,
+    square_ref, mine_ref, *rest,
 ):
+    theirs_refs, (sum_ref, staged_ref, sems) = rest[:-3], rest[-3:]
     source = pl.program_id(0)
     cap = word_ref.shape[2]
-    blocks = grad_ref.shape[0]
+    blocks = sum_ref.shape[0] - 8
     features = image_ref.shape[2]
     kinds = forward_ref.shape[0] // features
     position_bits = bits_of(list_length)
@@ -251,27 +252,237 @@
 
     @pl.when(source == pl.num_programs(0) - 1)
     def _():
-        copy = pltpu.make_async_copy(sum_ref.at[pl.ds(0, blocks)], grad_ref, sem)
-        copy.start()
-        copy.wait()
-
-
-def dft_tables(input_index, side_cells):
-    freqs = jnp.arange(side_cells, dtype=jnp.int32)
-    product = input_index[:, None] * freqs[None, :] % side_cells
-    angles = product.astype(jnp.float32) * (2.0 * math.pi / side_cells)
-    norming = 1.0 / math.sqrt(side_cells)
-    return (jnp.cos(angles) * norming, jnp.sin(angles) * norming)
-
-
-def transform(real_part, imag_part, cos_table, sin_table, pattern):
-    new_real = jnp.einsum(pattern, real_part, cos_table, precision=HIGHEST) - jnp.einsum(
-        pattern, imag_part, sin_table, precision=HIGHEST
-    )
-    new_imag = jnp.einsum(pattern, real_part, sin_table, precision=HIGHEST) + jnp.einsum(
-        pattern, imag_part, cos_table, precision=HIGHEST
-    )
-    return (new_real, new_imag)
+        half = blocks // 2
+        length = half // len(theirs_refs)
+        copies = []
+        for i, theirs_ref in enumerate(theirs_refs):
+            at = pl.multiple_of((1 - core_ref[0]) * half + i * length, length)
+            copies.append(pltpu.make_async_copy(sum_ref.at[pl.ds(at, length)], theirs_ref, sems.at[i + 1]))
+        at = pl.multiple_of(core_ref[0] * half, half)
+        copies.append(pltpu.make_async_copy(sum_ref.at[pl.ds(at, half)], mine_ref, sems.at[0]))
+        for copy in copies:
+            copy.start()
+        for copy in copies:
+            copy.wait()
+
+
+def rotated(value, turn, length):
+    real, imag = value
+    if turn == 0:
+        return value
+    if 4 * turn == length:
+        return (-imag, real)
+    root = math.sqrt(0.5)
+    if 8 * turn == length:
+        return ((real - imag) * root, (real + imag) * root)
+    if 8 * turn == 3 * length:
+        return ((real + imag) * -root, (real - imag) * root)
+    cos, sin = math.cos(2 * math.pi * turn / length), math.sin(2 * math.pi * turn / length)
+    return (real * cos - imag * sin, real * sin + imag * cos)
+
+
+def small_dft(values):
+    length = len(values)
+    if length == 1:
+        return values
+    even, odd = small_dft(values[0::2]), small_dft(values[1::2])
+    low, high = [], []
+    for k in range(length // 2):
+        turned = rotated(odd[k], k, length)
+        low.append((even[k][0] + turned[0], even[k][1] + turned[1]))
+        high.append((even[k][0] - turned[0], even[k][1] - turned[1]))
+    return low + high
+
+
+def swap_quarters(values):
+    lane = lax.broadcasted_iota(jnp.int32, values[0].shape, 1)
+    low, even = lane < 64, (lane // 32) % 2 == 0
+    roll = lambda value, shift: pltpu.roll(value, shift, 1)
+    for first, second, shift, keep in ((0, 2, 64, low), (1, 3, 64, low), (0, 1, 32, even), (2, 3, 32, even)):
+        one, two = values[first], values[second]
+        values[first] = jnp.where(keep, one, roll(two, shift))
+        values[second] = jnp.where(keep, roll(one, LANES - shift), two)
+    return values
+
+
+def in_halves(value):
+    high = value.astype(jnp.bfloat16)
+    return high, (value - high.astype(jnp.float32)).astype(jnp.bfloat16)
+
+
+def planes_kernel(mine_ref, theirs_ref, zblock_ref, turn_ref, wide_ref, fine_ref, out_ref, high_ref, low_ref):
+    step = pl.program_id(1)
+    count = mine_ref.shape[1]
+    groups, side = out_ref.shape[0], out_ref.shape[4]
+    height = side // groups
+
+    @pl.loop(0, count)
+    def _(i):
+        block = (mine_ref[:, i] + theirs_ref[:, i]).reshape(LANES, LANES)
+        high, low = in_halves(block.T)
+        both = jnp.dot(
+            jnp.concatenate([high, low, high], axis=1), zblock_ref[...],
+            preferred_element_type=jnp.float32,
+        )
+        by_cos = both[:, :LANES].reshape(8, 2, 8, LANES)
+        by_sin = both[:, LANES:].reshape(8, 2, 8, LANES)
+        real = by_cos[:, 0] - by_sin[:, 1]
+        imag = by_sin[:, 0] + by_cos[:, 1]
+        values = []
+        for z in range(8):
+            cos, sin = turn_ref[0, z:z + 1, :], turn_ref[1, z:z + 1, :]
+            values.append((real[z] * cos - imag[z] * sin, real[z] * sin + imag[z] * cos))
+        values = [jnp.concatenate(value, axis=0) for value in small_dft(values)]
+        at = pl.ds(pl.multiple_of((step * count + i) * 16, 16), 16)
+        for half in range(2):
+            planes = swap_quarters(values[4 * half:4 * half + 4])
+            for x in range(4):
+                columns = slice((2 * x + half) * LANES, (2 * x + half + 1) * LANES)
+                high, low = in_halves(planes[x])
+                high_ref[at, columns] = high
+                low_ref[at, columns] = low
+
+    @pl.when(step == pl.num_programs(1) - 1)
+    def _():
+        @pl.loop(0, 4)
+        def _(x):
+            columns = pl.ds(pl.multiple_of(x * side, side), side)
+            product = functools.partial(jnp.dot, preferred_element_type=jnp.float32)
+            high = high_ref[:, columns]
+            result = product(wide_ref[...], high) + (
+                product(wide_ref[...], low_ref[:, columns]) + product(fine_ref[...], high)
+            )
+            for part in range(2):
+                for group in range(groups):
+                    start = part * side + group * height
+                    out_ref[group, x, part] = result[start:start + height, :].astype(jnp.bfloat16)
+
+
+def first_dimension_kernel(slabs, each, core_ref, *refs):
+    arrays, (out_ref, mid_ref) = refs[:-2], refs[-2:]
+    chunks = len(arrays) // 2
+    own, other = arrays[:chunks], arrays[chunks:]
+    held = own[0].shape[1]
+    core = core_ref[0]
+    is_first = core == 0
+    sign = (1 - 2 * core).astype(jnp.float32)
+
+    def plane(x):
+        slab, rest = x // (2 * each), x % (2 * each)
+        half, inner = rest // each, rest % each
+        loaded = []
+        for part in range(2):
+            here = own[inner // held][slab, inner % held, part].astype(jnp.float32)
+            there = other[inner // held][slab, inner % held, part].astype(jnp.float32)
+            loaded.append(jnp.where(is_first, here, there) if half == 0 else jnp.where(is_first, there, here))
+        return tuple(loaded)
+
+    for low in range(16):
+        values = small_dft([plane(low + 16 * high) for high in range(16)])
+        for k in range(16):
+            real, imag = rotated(values[k], low * k, 256)
+            if low % 2:
+                real, imag = real * sign, imag * sign
+            mid_ref[k, low, 0] = real
+            mid_ref[k, low, 1] = imag
+
+    @pl.loop(0, 16)
+    def _(k):
+        values = [(mid_ref[k, low, 0], mid_ref[k, low, 1]) for low in range(16)]
+        even, odd = small_dft(values[0::2]), small_dft(values[1::2])
+        for m in range(8):
+            turned = rotated(odd[m], m, 16)
+            out_ref[0, k + 16 * m] = even[m][0] + turned[0]
+            out_ref[1, k + 16 * m] = even[m][1] + turned[1]
+
+
+def host_halves(table):
+    high = table.astype(jnp.bfloat16)
+    return high, (table - high.astype(np.float64)).astype(jnp.bfloat16)
+
+
+def transform_tables(side):
+    per_row = side // 8
+    grid = np.arange(per_row)
+    angle = 2 * np.pi * np.outer(grid, grid) / per_row
+    zblock = np.concatenate([np.kron(np.eye(4), np.cos(angle)), np.kron(np.eye(4), np.sin(angle))], axis=1)
+    high, low = host_halves(zblock)
+    zblock = np.concatenate([high, high, low], axis=0)
+    angle = 2 * np.pi * np.outer(np.arange(8), grid) / side
+    turns = np.stack([np.tile(np.cos(angle), (1, 4)), np.tile(np.sin(angle), (1, 4))]).astype(np.float32)
+    cells = np.arange(side)
+    angle = 2 * np.pi * (np.outer(cells, cells) % side) / side
+    cos, sin = np.cos(angle).reshape(side, per_row, 1, 8), np.sin(angle).reshape(side, per_row, 1, 8)
+    matrix = np.concatenate(
+        [np.concatenate([cos, -sin], axis=2), np.concatenate([sin, cos], axis=2)], axis=0
+    ).reshape(2 * side, 2 * side) / float(side) ** 1.5
+    return (zblock, turns) + host_halves(matrix)
+
+
+def to_field(mine, theirs_sent, side):
+    slabs = lax.axis_size("slab")
+    per_row = side // 8
+    each = side // slabs // 2
+    chunks = len(theirs_sent)
+    real_planes = each // chunks
+    held = max(4, real_planes)
+    height = side // slabs
+    groups = slabs if height % 16 == 0 else 1
+    tables = [jnp.asarray(table) for table in transform_tables(side)]
+    swap = [(0, 1), (1, 0)]
+    theirs = [lax.ppermute(chunk, "dom", swap) for chunk in theirs_sent]
+    grid_shape = (-1, per_row, per_row, LANES)
+    mine = mine.reshape(grid_shape)
+    short = held - real_planes
+    if short:
+        mine = jnp.pad(mine, ((0, short), (0, 0), (0, 0), (0, 0)))
+    yblocks = 8
+    own, other = [], []
+    for chunk in range(chunks):
+        added = theirs[chunk].reshape(grid_shape)
+        if short:
+            added = jnp.pad(added, ((0, short), (0, 0), (0, 0), (0, 0)))
+        quads = held // 4
+        whole = lambda table: pl.BlockSpec(table.shape, lambda q, y: (0,) * table.ndim)
+        sent = pl.pallas_call(
+            planes_kernel,
+            grid=(quads, per_row // yblocks),
+            out_shape=jax.ShapeDtypeStruct((groups, held, 2, side // groups, side), jnp.bfloat16),
+            in_specs=[
+                pl.BlockSpec((4, yblocks, per_row, LANES), lambda q, y, at=chunk * quads: (at + q, y, 0, 0)),
+                pl.BlockSpec((4, yblocks, per_row, LANES), lambda q, y: (q, y, 0, 0)),
+            ] + [whole(table) for table in tables],
+            out_specs=pl.BlockSpec((groups, 4, 2, side // groups, side), lambda q, y: (0, q, 0, 0, 0)),
+            scratch_shapes=[
+                pltpu.VMEM((2 * side, 4 * side), jnp.bfloat16),
+                pltpu.VMEM((2 * side, 4 * side), jnp.bfloat16),
+            ],
+            compiler_params=params(),
+            cost_estimate=pl.CostEstimate(
+                flops=held * 8 * side**3, bytes_accessed=held * 4 * side**2 * 8, transcendentals=0
+            ),
+            name="transform_planes",
+        )(mine, added, *tables)
+        if groups != slabs:
+            sent = sent.reshape(held, 2, slabs, height, side).transpose(2, 0, 1, 3, 4)[:, :real_planes]
+        got = lax.all_to_all(sent, "slab", split_axis=0, concat_axis=0, tiled=True)
+        own.append(got)
+        other.append(lax.ppermute(got, "dom", swap))
+    rows = min(16, height)
+    arrays = own + other
+    return pl.pallas_call(
+        functools.partial(first_dimension_kernel, slabs, each),
+        grid=(height // rows, side // LANES),
+        out_shape=jax.ShapeDtypeStruct((2, side // 2, height, side), jnp.float32),
+        in_specs=[SMEM_SPEC] + [
+            pl.BlockSpec((slabs, real_planes, 2, rows, LANES), lambda y, z: (0, 0, 0, y, z))
+            for _ in arrays
+        ],
+        out_specs=pl.BlockSpec((2, side // 2, rows, LANES), lambda y, z: (0, 0, y, z)),
+        scratch_shapes=[pltpu.VMEM((16, 16, 2, rows, LANES), jnp.float32)],
+        compiler_params=params(),
+        name="transform_first",
+    )(lax.axis_index("dom").astype(jnp.int32).reshape(1), *arrays)
 
 
 def gradient_of_slab(volume, kernels, images, owners, local_block, kinds, counts, ctf_code, ctf_table, scales):
@@ -359,19 +570,22 @@
     )(index, totals_in, volume)
 
     forward = jnp.transpose(kernels, (0, 2, 1)).reshape(kind_count * features, features)
-    backward = jnp.transpose(kernels, (1, 0, 2)).reshape(features, kind_count * features)
+    backward = kernels.reshape(kind_count, 2, 8, 8, features).transpose(3, 1, 2, 0, 4)
+    backward = backward.reshape(features, kind_count * features)
     unit = jnp.eye(features, dtype=jnp.bfloat16)
     tile = min(512, cap)
     per_source = lambda length, width: pl.BlockSpec((1, length, width), lambda s: (s, 0, 0))
     whole = lambda shape: pl.BlockSpec(shape, lambda s: (0,) * len(shape))
-    grad, squares = pl.pallas_call(
+    planes_each = side // slabs // 2
+    chunks = max(1, planes_each // (4 * QUADS))
+    squares, mine, *theirs = pl.pallas_call(
         functools.partial(slab_kernel, side, local_bits, list_length, particles, tile),
         grid=(slabs,),
         out_shape=(
-            jax.ShapeDtypeStruct((blocks, features), jnp.float32),
             jax.ShapeDtypeStruct((slabs, particles, LANES), jnp.float32),
-        ),
-        in_specs=[SMEM_SPEC] * 5 + [
+            jax.ShapeDtypeStruct((blocks // 2, features), jnp.float32),
+        ) + (jax.ShapeDtypeStruct((blocks // 2 // chunks, features), jnp.float32),) * chunks,
+        in_specs=[SMEM_SPEC] * 6 + [
             per_source(1, cap),
             per_source(cap, features),
             per_source(cap, features),
@@ -379,16 +593,17 @@
             whole(backward.shape),
             whole(unit.shape),
         ],
-        out_specs=(ANY_SPEC, per_source(particles, LANES)),
+        out_specs=(per_source(particles, LANES),) + (ANY_SPEC,) * (1 + chunks),
         scratch_shapes=[
             pltpu.VMEM((blocks + 8, features), jnp.float32),
             pltpu.VMEM((tile, features), jnp.float32),
-            pltpu.SemaphoreType.DMA(()),
+            pltpu.SemaphoreType.DMA((1 + chunks,)),
         ],
         compiler_params=params(),
         name="compare_and_add",
     )(
         totals_in, table_rows[:, 0], table_rows[:, 1], scale_in, index,
+        lax.axis_index("dom").astype(jnp.int32).reshape(1),
         words.reshape(slabs, 1, cap), voxels.reshape(slabs, cap, features), pictures,
         forward, backward, unit,
     )
@@ -396,29 +611,12 @@
         jnp.sum(squares, axis=2), "slab", split_axis=0, concat_axis=0, tiled=True
     )
     losses = jnp.sum(returned, axis=0) / (counts.astype(jnp.float32) * 128.0)
-    return grad, losses, side
+    return mine, theirs, losses, side
 
 
 def body(*arrays):
-    grad, losses, side_cells = gradient_of_slab(*arrays)
-    per_row = side_cells // 8
-    planes_here = grad.shape[0] // (per_row * per_row)
-    grid = grad.reshape(planes_here, per_row, per_row, 2, 8, 8).transpose(3, 0, 1, 4, 2, 5)
-    grid = grid.reshape(2, planes_here, side_cells, side_cells)
-    cells = jnp.arange(side_cells, dtype=jnp.int32)
-    cos_table, sin_table = dft_tables(cells, side_cells)
-    halves = lax.psum_scatter(grid, "dom", scatter_dimension=3, tiled=True)
-    real_part, imag_part = transform(halves[0], halves[1], cos_table, sin_table, "xyz,yk->xkz")
-    pencil = lax.all_to_all(
-        jnp.stack([real_part, imag_part]), "slab", split_axis=2, concat_axis=1, tiled=True
-    )
-    real_part, imag_part = transform(pencil[0], pencil[1], cos_table, sin_table, "xyz,xk->kyz")
-    rows = lax.all_to_all(
-        jnp.stack([real_part, imag_part]), "dom", split_axis=1, concat_axis=3, tiled=True
-    )
-    real_part, imag_part = transform(rows[0], rows[1], cos_table, sin_table, "xyz,zk->xyk")
-    result = jnp.stack([real_part, imag_part])
-    return (result, losses)
+    mine, theirs, losses, side = gradient_of_slab(*arrays)
+    return to_field(mine, theirs, side), losses
 
 
 def solution(mesh):

time: 776 us -> 385 us (0.50); the launches traced: 765 us -> 382 us
  local copies, waits for them, and re-layouts: 237 us -> 11.7 us
  waiting for transfers between devices: 273 us -> 121 us
  Pallas kernels: 84.8 us -> 160 us
  matrix products: 73.1 us -> 0 us
  between operations: 14.7 us -> 0.87 us
  starting transfers between devices: 51.5 us -> 63.5 us
    all_to_all x2 -> x4, waiting for transfers between devices: 183 us -> 46.5 us  [to_field(): got = lax.all_to_all(sent, 'slab', split_axis=0, concat_axis=0, tiled=True)]
    pallas_call x0 -> x5, Pallas kernels: none -> 86.4 us  [the longest x4 73.3 us: to_field(): pl.pallas_call(planes_kernel, grid=(quads, per_row // yblocks), out_shape...]
    transpose x1 -> x0, local copies, waits for them, and re-layouts: 76.3 us -> none  [body(): grad.reshape(planes_here, per_row, per_row, 2, 8, 8)]
    reshape x3 -> x1, local copies, waits for them, and re-layouts: 75.5 us -> 0.68 us  [gradient_of_slab(): kernels.reshape(kind_count, 2, 8, 8, features).transpose(3, 1, 2, 0, 4)]
    dot_general x12 -> x0, matrix products: 73.1 us -> none  [the longest x3 21.4 us: transform(): jnp.einsum(pattern, real_part, sin_table, precision=HIGHEST)]
    reduce_scatter x1 -> x0, waiting for transfers between devices: 22.2 us -> none  [body(): halves = lax.psum_scatter(grid, 'dom', scatter_dimension=3, tiled=True)]
    pallas_call x1 -> x0, local copies, waits for them, and re-layouts: 17.4 us -> none  [gradient_of_slab(): pl.pallas_call(functools.partial(slab_kernel, side, local_bits, list_leng...]
    all_to_all x2 -> x0, local copies, waits for them, and re-layouts: 14.2 us -> none  [the longest x1 9.77 us: body(): lax.all_to_all(jnp.stack([real_part, imag_part]), 'dom', split_axis=1, co...]
  transfers between devices with their start and end apart: 4 -> 13, of which waited for: 3 -> 6; matrix products, arithmetic and copies ran while one was open for 5% -> 2% of each run, Pallas kernels for 2% -> 23%
where the time goes in v2:
time: 385 us; the launch traced here: 382 us
  Pallas kernels  160 us (42%)
  waiting for transfers between devices  121 us (31%)
  starting transfers between devices  63.5 us (16%)
  blocking collectives  23.7 us (6%)
  local copies, waits for them, and re-layouts  11.7 us (3%)
    pallas_call x4, Pallas kernels, to_field(): pl.pallas_call(planes_kernel, grid=(quads, per_row // yblocks), out_shape...  73.3 us
    all_to_all x1, waiting for transfers between devices, gradient_of_slab(): lax.all_to_all(packed.reshape(slabs, cap, features), 'slab', split_axis=0...  70.3 us
    all_to_all x4, starting transfers between devices, to_field(): got = lax.all_to_all(sent, 'slab', split_axis=0, concat_axis=0, tiled=True)  57.2 us
    all_to_all x4, waiting for transfers between devices, to_field(): got = lax.all_to_all(sent, 'slab', split_axis=0, concat_axis=0, tiled=True)  46.5 us
    pallas_call x1, Pallas kernels, gradient_of_slab(): pl.pallas_call(functools.partial(slab_kernel, side, local_bits, list_leng...  35.2 us
    pallas_call x1, Pallas kernels, gradient_of_slab(): pl.pallas_call(functools.partial(pack_kernel, slots), out_shape=(jax.Shap...  19.4 us
    all_to_all x1, blocking collectives, gradient_of_slab(): lax.all_to_all(sent, 'slab', split_axis=0, concat_axis=0, tiled=True)  14 us
    pallas_call x1, Pallas kernels, to_field(): pl.pallas_call(functools.partial(first_dimension_kernel, slabs, each), gr...  13.1 us
  transfers between devices with their start and end apart: 13, of which 6 were waited for; matrix products, arithmetic and copies ran while one was open for 2% of the time, Pallas kernels for 23%

profile of v2, /device:TPU:0, one launch (start us, length us, event | category | flops | bytes accessed | tf_op | source)
XLA Modules:
  0.0 382.3 jit_solution(10136968974098578768)
XLA Ops:
  0.7 1.4 reshape.113.local_ref
  3.4 3.7 route.1
  7.1 19.4 %pack.1 = (bf16[16384,128]{1,0:T(8,128)(2,1)}, s32[17408]{0:T(1024)}) custom-call(s32[8192]{0:T(1024)} %bitcast.51, s32[8192]{0:T(1024)} %bitcast.52, bf16[8192,128]{1,0:T(8,128)(2,1)} %bitcast.38), custom_call_target="tpu_custom_call" | custom-call | tf_op jit(solution)/shard_map/pack/pallas_call | solution.py:511
  27.6 14.0 %all_to_all.46 = s32[8,1,2176]{2,1,0:T(1,128)S(1)} all-to-all(s32[8,1,2176]{2,1,0:T(1,128)S(1)} %all_to_all.29), channel_id=1, replica_groups=mesh['groups'=2,'slab'=8,'dom'=2] {'slab'}, dimensions={0} | all-to-all | bytes 139264 | tf_op jit(solution)/shard_map/all_to_all | solution.py:537
  41.6 4.7 %all-to-all-start.1 = ((bf16[8,2048,128]{2,1,0:T(8,128)(2,1)}), bf16[8,2048,128]{2,1,0:T(8,128)(2,1)}, u32[]{:S(2)}, u32[]{:S(2)}) async-start(bf16[8,2048,128]{2,1,0:T(8,128)(2,1)} %bitcast.37), calls=%async_computation.1 | async-start | bytes 8388608 | tf_op jit(solution)/shard_map/all_to_all | solution.py:545
  52.4 2.0 decode.1
  54.4 12.9 %read_voxels.1 = bf16[16384,128]{1,0:T(8,128)(2,1)} custom-call(s32[16384]{0:T(1024)} %bitcast.41, s32[8]{0:T(128)} %copy-done.7, bf16[32768,128]{1,0:T(8,128)(2,1)} %volume_ref.1), custom_call_target="tpu_custom_call" | custom-call | bytes 104857600 | tf_op jit(solution)/shard_map/read_voxels/pallas_call | solution.py:558
  68.1 70.3 %all-to-all-done.1.image_ref = bf16[8,2048,128]{2,1,0:T(8,128)(2,1)} async-done(((bf16[8,2048,128]{2,1,0:T(8,128)(2,1)}), bf16[8,2048,128]{2,1,0:T(8,128)(2,1)}, u32[]{:S(2)}, u32[]{:S(2)}) %all-to-all-start.1) | async-done | bytes 4194336 | tf_op jit(solution)/shard_map/all_to_all | solution.py:545
  138.4 35.2 %compare_and_add.1 = (f32[8,8,128]{2,1,0:T(8,128)}, f32[16384,128]{1,0:T(8,128)}, f32[4096,128]{1,0:T(8,128)}, f32[4096,128]{1,0:T(8,128)}, f32[4096,128]{1,0:T(8,128)}, /*index=5*/f32[4096,128]{1,0:T(8,128)}) custom-call(s32[8]{0:T(128)} %copy-done.7, f32[64]{0:T(128)} %get-tuple-element.25.defocus_ref, f32[64]{0:T(128)} %get-tuple-element.24.phase_ref, ...), custom_call_target="tpu_custom_call" | custom-call | tf_op jit(solution)/shard_map/compare_and_add/pallas_call | solution.py:581
  174.5 3.9 %collective-permute-done = f32[4096,128]{1,0:T(8,128)S(1)} collective-permute-done((f32[4096,128]{1,0:T(8,128)}, f32[4096,128]{1,0:T(8,128)S(1)}, u32[]{:S(2)}, u32[]{:S(2)}) %collective-permute-start) | collective-permute-done | bytes 2097184 | tf_op jit(solution)/shard_map/ppermute | solution.py:433
  179.8 18.3 %transform_planes.4 = bf16[8,4,2,32,256]{4,3,2,1,0:T(8,128)(2,1)} custom-call(f32[16,32,32,128]{3,2,1,0:T(8,128)} %bitcast.32, f32[4,32,32,128]{3,2,1,0:T(8,128)} %bitcast.40, bf16[384,256]{1,0:T(8,128)(2,1)} %constant.32.clone.zblock_ref, f32[2,8,128]{2,1,0:T(8,128)} %constant.33.clone.turn_ref, bf16[512,512]{1,0:T(8,128)(2,1)} %constant.34.clone.wide_ref, ...), custom_call_target="tpu_custom_call" | custom-call | flops 536870912 | bytes 8388608 | tf_op jit(solution)/shard_map/transform_planes/pallas_call | solution.py:447
  198.1 45.7 %all-to-all-start.2 = ((bf16[8,4,2,32,256]{4,3,2,1,0:T(8,128)(2,1)}), bf16[8,4,2,32,256]{4,3,2,1,0:T(8,128)(2,1)S(1)}, u32[]{:S(2)}, u32[]{:S(2)}) async-start(bf16[8,4,2,32,256]{4,3,2,1,0:T(8,128)(2,1)} %transform_planes.4), calls=%async_computation.2 | async-start | bytes 2097152 | tf_op jit(solution)/shard_map/all_to_all | solution.py:468
  245.1 18.3 %transform_planes.5 = bf16[8,4,2,32,256]{4,3,2,1,0:T(8,128)(2,1)} custom-call(f32[16,32,32,128]{3,2,1,0:T(8,128)} %bitcast.33, f32[4,32,32,128]{3,2,1,0:T(8,128)} %bitcast.39, bf16[384,256]{1,0:T(8,128)(2,1)} %constant.32.clone.zblock_ref, f32[2,8,128]{2,1,0:T(8,128)} %constant.33.clone.turn_ref, bf16[512,512]{1,0:T(8,128)(2,1)} %constant.34.clone.wide_ref, ...), custom_call_target="tpu_custom_call" | custom-call | flops 536870912 | bytes 8388608 | tf_op jit(solution)/shard_map/transform_planes/pallas_call | solution.py:447
  263.4 6.4 %all-to-all-done.2.refs_0_ = bf16[8,4,2,32,256]{4,3,2,1,0:T(8,128)(2,1)S(1)} async-done(((bf16[8,4,2,32,256]{4,3,2,1,0:T(8,128)(2,1)}), bf16[8,4,2,32,256]{4,3,2,1,0:T(8,128)(2,1)S(1)}, u32[]{:S(2)}, u32[]{:S(2)}) %all-to-all-start.2) | async-done | bytes 1048608 | tf_op jit(solution)/shard_map/all_to_all | solution.py:468
  269.8 3.6 all-to-all-start.3
  273.5 18.3 %transform_planes.6 = bf16[8,4,2,32,256]{4,3,2,1,0:T(8,128)(2,1)} custom-call(f32[16,32,32,128]{3,2,1,0:T(8,128)} %bitcast.34, f32[4,32,32,128]{3,2,1,0:T(8,128)} %bitcast.18.theirs_ref, bf16[384,256]{1,0:T(8,128)(2,1)} %constant.32.clone.zblock_ref, f32[2,8,128]{2,1,0:T(8,128)} %constant.33.clone.turn_ref, bf16[512,512]{1,0:T(8,128)(2,1)} %constant.34.clone.wide_ref, ...), custom_call_target="tpu_custom_call" | custom-call | flops 536870912 | bytes 8388608 | tf_op jit(solution)/shard_map/transform_planes/pallas_call | solution.py:447
  291.9 7.6 %all-to-all-done.3.refs_1_ = bf16[8,4,2,32,256]{4,3,2,1,0:T(8,128)(2,1)S(1)} async-done(((bf16[8,4,2,32,256]{4,3,2,1,0:T(8,128)(2,1)}), bf16[8,4,2,32,256]{4,3,2,1,0:T(8,128)(2,1)S(1)}, u32[]{:S(2)}, u32[]{:S(2)}) %all-to-all-start.3) | async-done | bytes 1048608 | tf_op jit(solution)/shard_map/all_to_all | solution.py:468
  299.4 3.6 all-to-all-start.4
  303.1 18.4 %transform_planes.7 = bf16[8,4,2,32,256]{4,3,2,1,0:T(8,128)(2,1)} custom-call(f32[16,32,32,128]{3,2,1,0:T(8,128)} %bitcast.35, f32[4,32,32,128]{3,2,1,0:T(8,128)} %bitcast.19.theirs_ref, bf16[384,256]{1,0:T(8,128)(2,1)} %constant.32.clone.zblock_ref, f32[2,8,128]{2,1,0:T(8,128)} %constant.33.clone.turn_ref, bf16[512,512]{1,0:T(8,128)(2,1)} %constant.34.clone.wide_ref, ...), custom_call_target="tpu_custom_call" | custom-call | flops 536870912 | bytes 8388608 | tf_op jit(solution)/shard_map/transform_planes/pallas_call | solution.py:447
  321.5 7.5 %all-to-all-done.4.refs_2_ = bf16[8,4,2,32,256]{4,3,2,1,0:T(8,128)(2,1)S(1)} async-done(((bf16[8,4,2,32,256]{4,3,2,1,0:T(8,128)(2,1)}), bf16[8,4,2,32,256]{4,3,2,1,0:T(8,128)(2,1)S(1)}, u32[]{:S(2)}, u32[]{:S(2)}) %all-to-all-start.4) | async-done | bytes 1048608 | tf_op jit(solution)/shard_map/all_to_all | solution.py:468
  329.0 4.2 %all-to-all-start.5 = ((bf16[8,4,2,32,256]{4,3,2,1,0:T(8,128)(2,1)}), bf16[8,4,2,32,256]{4,3,2,1,0:T(8,128)(2,1)}, u32[]{:S(2)}, u32[]{:S(2)}) async-start(bf16[8,4,2,32,256]{4,3,2,1,0:T(8,128)(2,1)} %transform_planes.7), calls=%async_computation.5 | async-start | bytes 2097152 | tf_op jit(solution)/shard_map/all_to_all | solution.py:468
  334.0 24.9 %all-to-all-done.5.refs_3_ = bf16[8,4,2,32,256]{4,3,2,1,0:T(8,128)(2,1)} async-done(((bf16[8,4,2,32,256]{4,3,2,1,0:T(8,128)(2,1)}), bf16[8,4,2,32,256]{4,3,2,1,0:T(8,128)(2,1)}, u32[]{:S(2)}, u32[]{:S(2)}) %all-to-all-start.5) | async-done | bytes 1048608 | tf_op jit(solution)/shard_map/all_to_all | solution.py:468
  359.0 9.7 %all_to_all.47 = f32[8,1,8]{2,1,0:T(1,128)S(1)} all-to-all(f32[8,1,8]{2,1,0:T(1,128)S(1)} %bitcast.54), channel_id=1, replica_groups=mesh['groups'=2,'slab'=8,'dom'=2] {'slab'}, dimensions={0} | all-to-all | bytes 512 | tf_op jit(solution)/shard_map/all_to_all | solution.py:610
  369.2 13.1 %transform_first.1 = f32[2,128,32,256]{3,2,1,0:T(8,128)} custom-call(s32[1]{0:T(128)} %bitcast.core_ref, bf16[8,4,2,32,256]{4,3,2,1,0:T(8,128)(2,1)} %copy-done, bf16[8,4,2,32,256]{4,3,2,1,0:T(8,128)(2,1)} %copy-done.1, bf16[8,4,2,32,256]{4,3,2,1,0:T(8,128)(2,1)} %copy-done.2, bf16[8,4,2,32,256]{4,3,2,1,0:T(8,128)(2,1)} %all-to-all-done.5.refs_3_, ...), custom_call_target="tpu_custom_call" | custom-call | tf_op jit(solution)/shard_map/transform_first/pallas_call | solution.py:473
  (73 shorter events, 14.1 us)
Async XLA Ops:
  0.6 26.8 %copy-start.12 = (bf16[8]{0:T(256)(128)(2,1)S(1)}, bf16[8]{0:T(256)(128)(2,1)}, u32[]{:S(2)}) copy-start(bf16[8]{0:T(256)(128)(2,1)} %param.23) | copy-start | bytes 52
  0.6 26.8 %copy-start.11 = (s32[8]{0:T(128)S(1)}, s32[8]{0:T(128)}, u32[]{:S(2)}) copy-start(s32[8]{0:T(128)} %param.21) | copy-start | bytes 100
  7.1 20.4 %copy-start.8 = (s32[8,128]{1,0:T(8,128)S(1)}, s32[8,128]{1,0:T(8,128)}, u32[]{:S(2)}) copy-start(s32[8,128]{1,0:T(8,128)} %get-tuple-element.16) | copy-start | bytes 12292
  41.6 4.7 %copy-start.9 = (f32[64,2]{0,1:T(2,128)S(1)}, f32[64,2]{0,1:T(2,128)}, u32[]{:S(2)}) copy-start(f32[64,2]{0,1:T(2,128)} %param.22) | copy-start | bytes 1540
  41.6 4.8 %copy-start.5 = (bf16[4,128,128]{2,1,0:T(8,128)(2,1)S(1)}, bf16[4,128,128]{2,1,0:T(8,128)(2,1)}, u32[]{:S(2)}) copy-start(bf16[4,128,128]{2,1,0:T(8,128)(2,1)} %param.15) | copy-start | bytes 393220
  41.6 96.7 %all-to-all-start.1 = ((bf16[8,2048,128]{2,1,0:T(8,128)(2,1)}), bf16[8,2048,128]{2,1,0:T(8,128)(2,1)}, u32[]{:S(2)}, u32[]{:S(2)}) async-start(bf16[8,2048,128]{2,1,0:T(8,128)(2,1)} %bitcast.37), calls=%async_computation.1 | async-start | bytes 8388608 | tf_op jit(solution)/shard_map/all_to_all | solution.py:545
  50.0 4.4 %copy-start.7 = (s32[8]{0:T(128)}, s32[8]{0:T(128)S(1)}, u32[]{:S(2)}) copy-start(s32[8]{0:T(128)S(1)} %slice_reduce_fusion.2.totals_ref) | copy-start | bytes 100
  173.6 4.8 %collective-permute-start = (f32[4096,128]{1,0:T(8,128)}, f32[4096,128]{1,0:T(8,128)S(1)}, u32[]{:S(2)}, u32[]{:S(2)}) collective-permute-start(f32[4096,128]{1,0:T(8,128)} %get-tuple-element.19), channel_id=1, source_target_pairs={{0,1},{1,0},{2,3},{3,2},{4,5},{5,4},{6,7},{7,6},{8,9},{9,8},{10,11... | collective-permute-start | bytes 6291464 | tf_op jit(solution)/shard_map/ppermute | solution.py:433
  174.4 69.3 %collective-permute-start.1 = (f32[4096,128]{1,0:T(8,128)}, f32[4096,128]{1,0:T(8,128)S(1)}, u32[]{:S(2)}, u32[]{:S(2)}) collective-permute-start(f32[4096,128]{1,0:T(8,128)} %get-tuple-element.20), channel_id=1, source_target_pairs={{0,1},{1,0},{2,3},{3,2},{4,5},{5,4},{6,7},{7,6},{8,9},{9,8},{10,11... | collective-permute-start | bytes 6291464 | tf_op jit(solution)/shard_map/ppermute | solution.py:433
  198.1 71.8 %all-to-all-start.2 = ((bf16[8,4,2,32,256]{4,3,2,1,0:T(8,128)(2,1)}), bf16[8,4,2,32,256]{4,3,2,1,0:T(8,128)(2,1)S(1)}, u32[]{:S(2)}, u32[]{:S(2)}) async-start(bf16[8,4,2,32,256]{4,3,2,1,0:T(8,128)(2,1)} %transform_planes.4), calls=%async_computation.2 | async-start | bytes 2097152 | tf_op jit(solution)/shard_map/all_to_all | solution.py:468
  243.8 29.8 %collective-permute-start.2 = (f32[4096,128]{1,0:T(8,128)}, f32[4096,128]{1,0:T(8,128)}, u32[]{:S(2)}, u32[]{:S(2)}) collective-permute-start(f32[4096,128]{1,0:T(8,128)} %get-tuple-element.21), channel_id=1, source_target_pairs={{0,1},{1,0},{2,3},{3,2},{4,5},{5,4},{6,7},{7,6},{8,9},{9,8},{10,11... | collective-permute-start | bytes 6291464 | tf_op jit(solution)/shard_map/ppermute | solution.py:433
  269.8 63.4 %copy-start = (bf16[8,4,2,32,256]{4,3,2,1,0:T(8,128)(2,1)}, bf16[8,4,2,32,256]{4,3,2,1,0:T(8,128)(2,1)S(1)}, u32[]{:S(2)}) copy-start(bf16[8,4,2,32,256]{4,3,2,1,0:T(8,128)(2,1)S(1)} %all-to-all-done.2.refs_0_) | copy-start | bytes 3145732
  269.8 29.6 %all-to-all-start.3 = ((bf16[8,4,2,32,256]{4,3,2,1,0:T(8,128)(2,1)}), bf16[8,4,2,32,256]{4,3,2,1,0:T(8,128)(2,1)S(1)}, u32[]{:S(2)}, u32[]{:S(2)}) async-start(bf16[8,4,2,32,256]{4,3,2,1,0:T(8,128)(2,1)} %transform_planes.5), calls=%async_computation.3 | async-start | bytes 2097152 | tf_op jit(solution)/shard_map/all_to_all | solution.py:468
  273.5 29.6 %collective-permute-start.3 = (f32[4096,128]{1,0:T(8,128)}, f32[4096,128]{1,0:T(8,128)}, u32[]{:S(2)}, u32[]{:S(2)}) collective-permute-start(f32[4096,128]{1,0:T(8,128)} %get-tuple-element.22), channel_id=1, source_target_pairs={{0,1},{1,0},{2,3},{3,2},{4,5},{5,4},{6,7},{7,6},{8,9},{9,8},{10,11... | collective-permute-start | bytes 6291464 | tf_op jit(solution)/shard_map/ppermute | solution.py:433
  299.4 33.9 %copy-start.1 = (bf16[8,4,2,32,256]{4,3,2,1,0:T(8,128)(2,1)}, bf16[8,4,2,32,256]{4,3,2,1,0:T(8,128)(2,1)S(1)}, u32[]{:S(2)}) copy-start(bf16[8,4,2,32,256]{4,3,2,1,0:T(8,128)(2,1)S(1)} %all-to-all-done.3.refs_1_) | copy-start | bytes 3145732
  299.4 29.6 %all-to-all-start.4 = ((bf16[8,4,2,32,256]{4,3,2,1,0:T(8,128)(2,1)}), bf16[8,4,2,32,256]{4,3,2,1,0:T(8,128)(2,1)S(1)}, u32[]{:S(2)}, u32[]{:S(2)}) async-start(bf16[8,4,2,32,256]{4,3,2,1,0:T(8,128)(2,1)} %transform_planes.6), calls=%async_computation.4 | async-start | bytes 2097152 | tf_op jit(solution)/shard_map/all_to_all | solution.py:468
  321.5 37.4 %copy-start.6 = (f32[8,8,128]{2,1,0:T(8,128)S(1)}, f32[8,8,128]{2,1,0:T(8,128)}, u32[]{:S(2)}) copy-start(f32[8,8,128]{2,1,0:T(8,128)} %get-tuple-element.23) | copy-start | bytes 98308
  321.5 47.2 %copy-start.10 = (s32[8]{0:T(128)S(1)}, s32[8]{0:T(128)}, u32[]{:S(2)}) copy-start(s32[8]{0:T(128)} %counts_ref.1) | copy-start | bytes 100
  329.0 40.2 %copy-start.2 = (bf16[8,4,2,32,256]{4,3,2,1,0:T(8,128)(2,1)}, bf16[8,4,2,32,256]{4,3,2,1,0:T(8,128)(2,1)S(1)}, u32[]{:S(2)}) copy-start(bf16[8,4,2,32,256]{4,3,2,1,0:T(8,128)(2,1)S(1)} %all-to-all-done.4.refs_2_) | copy-start | bytes 3145732
  329.0 29.9 %all-to-all-start.5 = ((bf16[8,4,2,32,256]{4,3,2,1,0:T(8,128)(2,1)}), bf16[8,4,2,32,256]{4,3,2,1,0:T(8,128)(2,1)}, u32[]{:S(2)}, u32[]{:S(2)}) async-start(bf16[8,4,2,32,256]{4,3,2,1,0:T(8,128)(2,1)} %transform_planes.7), calls=%async_computation.5 | async-start | bytes 2097152 | tf_op jit(solution)/shard_map/all_to_all | solution.py:468
  333.3 35.9 %collective-permute-start.4 = (bf16[8,4,2,32,256]{4,3,2,1,0:T(8,128)(2,1)S(1)}, bf16[8,4,2,32,256]{4,3,2,1,0:T(8,128)(2,1)}, u32[]{:S(2)}, u32[]{:S(2)}) collective-permute-start(bf16[8,4,2,32,256]{4,3,2,1,0:T(8,128)(2,1)S(1)} %all-to-all-done.2.refs_0_), channel_id=1, source_target_pairs={{0,1},{1,0},{2,3},{3,2},{4,5},{5,4},{6,7},{7,6},{8,9},{9,8},{10,11... | collective-permute-start | bytes 3145736 | tf_op jit(solution)/shard_map/ppermute | solution.py:470
  333.4 35.8 %collective-permute-start.5 = (bf16[8,4,2,32,256]{4,3,2,1,0:T(8,128)(2,1)S(1)}, bf16[8,4,2,32,256]{4,3,2,1,0:T(8,128)(2,1)}, u32[]{:S(2)}, u32[]{:S(2)}) collective-permute-start(bf16[8,4,2,32,256]{4,3,2,1,0:T(8,128)(2,1)S(1)} %all-to-all-done.3.refs_1_), channel_id=1, source_target_pairs={{0,1},{1,0},{2,3},{3,2},{4,5},{5,4},{6,7},{7,6},{8,9},{9,8},{10,11... | collective-permute-start | bytes 3145736 | tf_op jit(solution)/shard_map/ppermute | solution.py:470
  333.9 35.4 %collective-permute-start.6 = (bf16[8,4,2,32,256]{4,3,2,1,0:T(8,128)(2,1)S(1)}, bf16[8,4,2,32,256]{4,3,2,1,0:T(8,128)(2,1)}, u32[]{:S(2)}, u32[]{:S(2)}) collective-permute-start(bf16[8,4,2,32,256]{4,3,2,1,0:T(8,128)(2,1)S(1)} %all-to-all-done.4.refs_2_), channel_id=1, source_target_pairs={{0,1},{1,0},{2,3},{3,2},{4,5},{5,4},{6,7},{7,6},{8,9},{9,8},{10,11... | collective-permute-start | bytes 3145736 | tf_op jit(solution)/shard_map/ppermute | solution.py:470
  358.9 10.3 %collective-permute-start.7 = (bf16[8,4,2,32,256]{4,3,2,1,0:T(8,128)(2,1)}, bf16[8,4,2,32,256]{4,3,2,1,0:T(8,128)(2,1)}, u32[]{:S(2)}, u32[]{:S(2)}) collective-permute-start(bf16[8,4,2,32,256]{4,3,2,1,0:T(8,128)(2,1)} %all-to-all-done.5.refs_3_), channel_id=1, source_target_pairs={{0,1},{1,0},{2,3},{3,2},{4,5},{5,4},{6,7},{7,6},{8,9},{9,8},{10,11... | collective-permute-start | bytes 3145736 | tf_op jit(solution)/shard_map/ppermute | solution.py:470
  (2 other events, 2.6 us)

commit v3 on v2

--- a/solution.py
+++ b/solution.py
@@ -10,8 +10,8 @@
 from jax.sharding import PartitionSpec as P
 
 LANES = 128
-QUADS = 1
-GROUP = 8
+TILE = 512
+GROUP = 16
 VMEM_LIMIT = 56 * 1024 * 1024
 
 SMEM_SPEC = pl.BlockSpec(memory_space=pltpu.SMEM)
@@ -67,29 +67,44 @@
     word_ref[...] = word | (particle << (kind_bits + 2 + bits_of(list_length)))
 
 
-def pack_kernel(slots, target_ref, word_ref, image_ref, out_ref, meta_ref, wide_ref, staged_ref):
-    entries = image_ref.shape[0]
+def pack_words_kernel(list_length, target_ref, word_ref, counts_ref, meta_ref):
+    @pl.loop(0, counts_ref.shape[0])
+    def _(particle):
+        @pl.loop(0, (counts_ref[particle] + 15) // 16)
+        def _(i):
+            first = particle * list_length + i * 16
+            targets = [target_ref[first + j] for j in range(16)]
+            words = [word_ref[first + j] for j in range(16)]
+            for j in range(16):
+                meta_ref[targets[j]] = words[j]
+
+
+def pack_images_kernel(slabs, cap, list_length, target_ref, counts_ref, image_ref, *refs):
+    out_refs, (wide_ref, staged_ref) = refs[:-2], refs[-2:]
     step = 256
 
-    @pl.loop(0, entries // step)
+    @pl.loop(0, image_ref.shape[0] // step)
     def _(i):
         at = pl.multiple_of(i * step, step)
         wide_ref[pl.ds(at, step), :] = image_ref[pl.ds(at, step), :].astype(jnp.float32)
 
-    @pl.loop(0, entries // 16)
-    def _(i):
-        first = i * 16
-        targets = [target_ref[first + j] for j in range(16)]
-        rows = [wide_ref[pl.ds(first + j, 1), :] for j in range(16)]
-        for j in range(16):
-            staged_ref[pl.ds(targets[j], 1), :] = rows[j]
-        for j in range(16):
-            meta_ref[targets[j]] = word_ref[first + j]
-
-    @pl.loop(0, slots // step)
-    def _(i):
-        at = pl.multiple_of(i * step, step)
-        out_ref[pl.ds(at, step), :] = staged_ref[pl.ds(at, step), :].astype(jnp.bfloat16)
+    @pl.loop(0, counts_ref.shape[0])
+    def _(particle):
+        @pl.loop(0, (counts_ref[particle] + 15) // 16)
+        def _(i):
+            first = particle * list_length + i * 16
+            targets = [target_ref[first + j] for j in range(16)]
+            rows = [wide_ref[pl.ds(first + j, 1), :] for j in range(16)]
+            for j in range(16):
+                staged_ref[pl.ds(targets[j], 1), :] = rows[j]
+
+    for chunk, out_ref in enumerate(out_refs):
+        width = out_ref.shape[1]
+
+        @pl.loop(0, slabs)
+        def _(slab):
+            at = pl.multiple_of(slab * cap + chunk * width, width)
+            out_ref[slab] = staged_ref[pl.ds(at, width), :].astype(jnp.bfloat16)
 
 
 def decode_kernel(local_bits, dummy, word_ref, live_ref, index_ref):
@@ -155,38 +170,43 @@
 
 
 def slab_kernel(
-    side, local_bits, list_length, particles, tile,
-    totals_ref, defocus_ref, phase_ref, scale_ref, index_ref,
-    core_ref, word_ref, voxel_ref, image_ref, forward_ref, backward_ref, unit_ref,
-    square_ref, mine_ref, *rest,
+    side, local_bits, list_length, particles, cap, offset, first, last,
+    totals_ref, defocus_ref, phase_ref, scale_ref, index_ref, core_ref,
+    word_ref, voxel_ref, image_ref, forward_ref, backward_ref, unit_ref, *rest,
 ):
-    theirs_refs, (sum_ref, staged_ref, sems) = rest[:-3], rest[-3:]
+    if not first:
+        before_ref, rest = rest[0], rest[1:]
+    square_ref, sum_refs, (sum_ref, staged_ref, sems) = rest[0], rest[1:-3], rest[-3:]
     source = pl.program_id(0)
-    cap = word_ref.shape[2]
+    tile = word_ref.shape[2]
     blocks = sum_ref.shape[0] - 8
     features = image_ref.shape[2]
     kinds = forward_ref.shape[0] // features
     position_bits = bits_of(list_length)
     per_row = side // 8
-    live = totals_ref[source]
+    live = jnp.clip(totals_ref[source] - offset, 0, tile)
 
     @pl.when(source == 0)
     def _():
-        @pl.loop(0, blocks // 256)
-        def _(i):
-            at = pl.multiple_of(i * 256, 256)
-            sum_ref[pl.ds(at, 256), :] = jnp.zeros((256, features), jnp.float32)
-
-    square_ref[...] = jnp.zeros_like(square_ref)
-
-    @pl.loop(0, (live + tile - 1) // tile)
-    def _(t):
-        at = pl.multiple_of(t * tile, tile)
-        word = word_ref[0, :, pl.ds(at, tile)]
+        if first:
+            @pl.loop(0, blocks // 256)
+            def _(i):
+                at = pl.multiple_of(i * 256, 256)
+                sum_ref[pl.ds(at, 256), :] = jnp.zeros((256, features), jnp.float32)
+        else:
+            pltpu.make_async_copy(before_ref, sum_ref.at[pl.ds(0, blocks)], sems.at[0]).start()
+
+    @pl.when(live == 0)
+    def _():
+        square_ref[...] = jnp.zeros_like(square_ref)
+
+    @pl.when(live > 0)
+    def _():
+        word = word_ref[0]
         kind = (word >> local_bits) & 3
         position = (word >> (local_bits + 2)) & (list_length - 1)
         particle = (word >> (local_bits + 2 + position_bits)) & (particles - 1)
-        valid = lax.broadcasted_iota(jnp.int32, (1, tile), 1) + at < live
+        valid = lax.broadcasted_iota(jnp.int32, (1, tile), 1) < live
         defocus = jnp.zeros((1, tile), jnp.float32)
         phase = jnp.zeros((1, tile), jnp.float32)
         scale = jnp.zeros((1, tile), jnp.float32)
@@ -197,22 +217,20 @@
             scale = jnp.where(chosen, scale_ref[source * particles + j], scale)
         half = features // 2
         cell = lax.broadcasted_iota(jnp.int32, (half, tile), 0)
-        vert = ((position // per_row) * 8 + cell // 8 - side // 2).astype(jnp.float32)
-        horiz = ((position % per_row) * 8 + cell % 8 - side // 2).astype(jnp.float32)
+        vert = ((position // per_row) * 8 - side // 2 + cell // 8).astype(jnp.float32)
+        horiz = ((position % per_row) * 8 - side // 2 + cell % 8).astype(jnp.float32)
         radius = (vert * vert + horiz * horiz) * (1.0 / float((side // 2) ** 2))
         factor = scale * sine(defocus * radius + phase)
         factor = jnp.concatenate([factor, factor], axis=0)
         contract_last = (((1,), (1,)), ((), ()))
         each_kind = lax.dot_general(
-            forward_ref[...], voxel_ref[0, pl.ds(at, tile), :], contract_last,
-            preferred_element_type=jnp.float32,
+            forward_ref[...], voxel_ref[0], contract_last, preferred_element_type=jnp.float32
         )
         extracted = each_kind[0:features, :]
         for k in range(1, kinds):
             extracted = jnp.where(kind == k, each_kind[k * features:(k + 1) * features, :], extracted)
         picture = lax.dot_general(
-            unit_ref[...], image_ref[0, pl.ds(at, tile), :], contract_last,
-            preferred_element_type=jnp.float32,
+            unit_ref[...], image_ref[0], contract_last, preferred_element_type=jnp.float32
         )
         misfit = jnp.where(valid, factor * extracted - picture, 0.0)
         squares = jnp.sum(misfit * misfit, axis=0, keepdims=True)
@@ -221,7 +239,7 @@
         folded = spread[:, 0:LANES]
         for i in range(1, tile // LANES):
             folded = folded + spread[:, i * LANES:(i + 1) * LANES]
-        square_ref[0] = square_ref[0] + folded
+        square_ref[0] = folded
         weighted = (factor * misfit).astype(jnp.bfloat16)
         none = jnp.zeros_like(weighted)
         spread_back = jnp.concatenate(
@@ -230,40 +248,57 @@
         terms = jnp.dot(backward_ref[...], spread_back, preferred_element_type=jnp.float32)
         staged_ref[...] = terms.T
 
-        @pl.loop(0, (jnp.minimum(live - at, tile) + GROUP - 1) // GROUP)
-        def _(g):
-            base = source * cap + at + g * GROUP
-            marked = index_ref[base]
-            places = [index_ref[base + j] & 0xFFFFFF for j in range(GROUP)]
-
-            @pl.when(marked < (1 << 24))
-            def _():
-                held = [sum_ref[pl.ds(places[j], 1), :] for j in range(GROUP)]
-                new = [staged_ref[pl.ds(g * GROUP + j, 1), :] for j in range(GROUP)]
-                for j in range(GROUP):
-                    sum_ref[pl.ds(places[j], 1), :] = held[j] + new[j]
-
-            @pl.when(marked >= (1 << 24))
-            def _():
-                for j in range(GROUP):
-                    sum_ref[pl.ds(places[j], 1), :] = (
-                        sum_ref[pl.ds(places[j], 1), :] + staged_ref[pl.ds(g * GROUP + j, 1), :]
-                    )
+    if not first:
+        @pl.when(source == 0)
+        def _():
+            pltpu.make_async_copy(before_ref, sum_ref.at[pl.ds(0, blocks)], sems.at[0]).wait()
+
+    @pl.loop(0, (live + GROUP - 1) // GROUP)
+    def _(g):
+        base = source * cap + offset + g * GROUP
+        marked = index_ref[base]
+        places = [index_ref[base + j] & 0xFFFFFF for j in range(GROUP)]
+
+        @pl.when(marked < (1 << 24))
+        def _():
+            held = [sum_ref[pl.ds(places[j], 1), :] for j in range(GROUP)]
+            new = [staged_ref[pl.ds(g * GROUP + j, 1), :] for j in range(GROUP)]
+            for j in range(GROUP):
+                sum_ref[pl.ds(places[j], 1), :] = held[j] + new[j]
+
+        @pl.when(marked >= (1 << 24))
+        def _():
+            for j in range(GROUP):
+                sum_ref[pl.ds(places[j], 1), :] = (
+                    sum_ref[pl.ds(places[j], 1), :] + staged_ref[pl.ds(g * GROUP + j, 1), :]
+                )
 
     @pl.when(source == pl.num_programs(0) - 1)
     def _():
-        half = blocks // 2
-        length = half // len(theirs_refs)
         copies = []
-        for i, theirs_ref in enumerate(theirs_refs):
-            at = pl.multiple_of((1 - core_ref[0]) * half + i * length, length)
-            copies.append(pltpu.make_async_copy(sum_ref.at[pl.ds(at, length)], theirs_ref, sems.at[i + 1]))
-        at = pl.multiple_of(core_ref[0] * half, half)
-        copies.append(pltpu.make_async_copy(sum_ref.at[pl.ds(at, half)], mine_ref, sems.at[0]))
+        if last:
+            half = blocks // 2
+            start = (1 - core_ref[0]) * half
+            places = [core_ref[0] * half]
+            for out_ref in sum_refs[1:]:
+                places.append(start)
+                start = start + out_ref.shape[0]
+        else:
+            places = [0]
+        for i, (place, out_ref) in enumerate(zip(places, sum_refs)):
+            length = out_ref.shape[0]
+            at = pl.multiple_of(place, 8)
+            copies.append(pltpu.make_async_copy(sum_ref.at[pl.ds(at, length)], out_ref, sems.at[i]))
         for copy in copies:
             copy.start()
         for copy in copies:
             copy.wait()
+
+
+def pieces_of(planes):
+    if planes < 16:
+        return [planes]
+    return [4, 4, planes - 8]
 
 
 def rotated(value, turn, length):
@@ -316,7 +351,7 @@
     groups, side = out_ref.shape[0], out_ref.shape[4]
     height = side // groups
 
-    @pl.loop(0, count)
+    @pl.loop(0, count, unroll=4)
     def _(i):
         block = (mine_ref[:, i] + theirs_ref[:, i]).reshape(LANES, LANES)
         high, low = in_halves(block.T)
@@ -362,7 +397,7 @@
     arrays, (out_ref, mid_ref) = refs[:-2], refs[-2:]
     chunks = len(arrays) // 2
     own, other = arrays[:chunks], arrays[chunks:]
-    held = own[0].shape[1]
+    spots = [(i, at) for i, ref in enumerate(own) for at in range(ref.shape[1])]
     core = core_ref[0]
     is_first = core == 0
     sign = (1 - 2 * core).astype(jnp.float32)
@@ -372,8 +407,9 @@
         half, inner = rest // each, rest % each
         loaded = []
         for part in range(2):
-            here = own[inner // held][slab, inner % held, part].astype(jnp.float32)
-            there = other[inner // held][slab, inner % held, part].astype(jnp.float32)
+            chunk, at = spots[inner]
+            here = own[chunk][slab, at, part].astype(jnp.float32)
+            there = other[chunk][slab, at, part].astype(jnp.float32)
             loaded.append(jnp.where(is_first, here, there) if half == 0 else jnp.where(is_first, there, here))
         return tuple(loaded)
 
@@ -423,9 +459,6 @@
     slabs = lax.axis_size("slab")
     per_row = side // 8
     each = side // slabs // 2
-    chunks = len(theirs_sent)
-    real_planes = each // chunks
-    held = max(4, real_planes)
     height = side // slabs
     groups = slabs if height % 16 == 0 else 1
     tables = [jnp.asarray(table) for table in transform_tables(side)]
@@ -433,15 +466,17 @@
     theirs = [lax.ppermute(chunk, "dom", swap) for chunk in theirs_sent]
     grid_shape = (-1, per_row, per_row, LANES)
     mine = mine.reshape(grid_shape)
-    short = held - real_planes
+    short = max(0, 4 - each)
     if short:
         mine = jnp.pad(mine, ((0, short), (0, 0), (0, 0), (0, 0)))
     yblocks = 8
     own, other = [], []
-    for chunk in range(chunks):
-        added = theirs[chunk].reshape(grid_shape)
+    first_quad = 0
+    for real_planes, added in zip(pieces_of(each), theirs):
+        added = added.reshape(grid_shape)
         if short:
             added = jnp.pad(added, ((0, short), (0, 0), (0, 0), (0, 0)))
+        held = real_planes + short
         quads = held // 4
         whole = lambda table: pl.BlockSpec(table.shape, lambda q, y: (0,) * table.ndim)
         sent = pl.pallas_call(
@@ -449,7 +484,7 @@
             grid=(quads, per_row // yblocks),
             out_shape=jax.ShapeDtypeStruct((groups, held, 2, side // groups, side), jnp.bfloat16),
             in_specs=[
-                pl.BlockSpec((4, yblocks, per_row, LANES), lambda q, y, at=chunk * quads: (at + q, y, 0, 0)),
+                pl.BlockSpec((4, yblocks, per_row, LANES), lambda q, y, at=first_quad: (at + q, y, 0, 0)),
                 pl.BlockSpec((4, yblocks, per_row, LANES), lambda q, y: (q, y, 0, 0)),
             ] + [whole(table) for table in tables],
             out_specs=pl.BlockSpec((groups, 4, 2, side // groups, side), lambda q, y: (0, q, 0, 0, 0)),
@@ -464,7 +499,8 @@
             name="transform_planes",
         )(mine, added, *tables)
         if groups != slabs:
-            sent = sent.reshape(held, 2, slabs, height, side).transpose(2, 0, 1, 3, 4)[:, :real_planes]
+            sent = sent.reshape(-1, 2, slabs, height, side).transpose(2, 0, 1, 3, 4)[:, :real_planes]
+        first_quad += quads
         got = lax.all_to_all(sent, "slab", split_axis=0, concat_axis=0, tiled=True)
         own.append(got)
         other.append(lax.ppermute(got, "dom", swap))
@@ -475,8 +511,8 @@
         grid=(height // rows, side // LANES),
         out_shape=jax.ShapeDtypeStruct((2, side // 2, height, side), jnp.float32),
         in_specs=[SMEM_SPEC] + [
-            pl.BlockSpec((slabs, real_planes, 2, rows, LANES), lambda y, z: (0, 0, 0, y, z))
-            for _ in arrays
+            pl.BlockSpec(array.shape[:3] + (rows, LANES), lambda y, z: (0, 0, 0, y, z))
+            for array in arrays
         ],
         out_specs=pl.BlockSpec((2, side // 2, rows, LANES), lambda y, z: (0, 0, y, z)),
         scratch_shapes=[pltpu.VMEM((16, 16, 2, rows, LANES), jnp.float32)],
@@ -508,21 +544,30 @@
     )(
         owners.reshape(rows, LANES), local_block.reshape(rows, LANES), kinds.reshape(rows, LANES), counts
     )
-    packed, meta = pl.pallas_call(
-        functools.partial(pack_kernel, slots),
-        out_shape=(
-            jax.ShapeDtypeStruct((slots, features), jnp.bfloat16),
-            jax.ShapeDtypeStruct((slots + 1024,), jnp.int32),
-        ),
+    target, word = target.reshape(entries), word.reshape(entries)
+    meta = pl.pallas_call(
+        functools.partial(pack_words_kernel, list_length),
+        out_shape=jax.ShapeDtypeStruct((slots + 1024,), jnp.int32),
+        in_specs=[SMEM_SPEC, SMEM_SPEC, SMEM_SPEC],
+        out_specs=SMEM_SPEC,
+        compiler_params=params(),
+        name="pack_words",
+    )(target, word, counts)
+    parts = max(1, cap // TILE)
+    tile = cap // parts
+    packed = pl.pallas_call(
+        functools.partial(pack_images_kernel, slabs, cap, list_length),
+        out_shape=(jax.ShapeDtypeStruct((slabs, tile, features), jnp.bfloat16),) * parts,
         in_specs=[SMEM_SPEC, SMEM_SPEC, VMEM_SPEC],
-        out_specs=(VMEM_SPEC, SMEM_SPEC),
+        out_specs=(VMEM_SPEC,) * parts,
         scratch_shapes=[
             pltpu.VMEM((entries, features), jnp.float32),
             pltpu.VMEM((slots + 8, features), jnp.float32),
         ],
         compiler_params=params(),
-        name="pack",
-    )(target.reshape(entries), word.reshape(entries), images.reshape(entries, features))
+        cost_estimate=pl.CostEstimate(flops=0, bytes_accessed=50 * 1024 * 1024, transcendentals=0),
+        name="pack_images",
+    )(target, counts, images.reshape(entries, features))
 
     code = ctf_code | ((scales.astype(jnp.float32) * 256.0).astype(jnp.int32) << 8)
     header = jnp.concatenate(
@@ -541,10 +586,6 @@
     live = (jnp.arange(cap, dtype=jnp.int32)[None, :] < totals_in[:, None]).astype(jnp.int32)
     table_rows = ctf_table[(codes_in & 255).reshape(-1)]
     scale_in = (codes_in >> 8).astype(jnp.float32).reshape(-1) * (1.0 / 256.0)
-
-    pictures = lax.all_to_all(
-        packed.reshape(slabs, cap, features), "slab", split_axis=0, concat_axis=0, tiled=True
-    )
 
     index = pl.pallas_call(
         functools.partial(decode_kernel, local_bits, blocks),
@@ -573,43 +614,52 @@
     backward = kernels.reshape(kind_count, 2, 8, 8, features).transpose(3, 1, 2, 0, 4)
     backward = backward.reshape(features, kind_count * features)
     unit = jnp.eye(features, dtype=jnp.bfloat16)
-    tile = min(512, cap)
-    per_source = lambda length, width: pl.BlockSpec((1, length, width), lambda s: (s, 0, 0))
-    whole = lambda shape: pl.BlockSpec(shape, lambda s: (0,) * len(shape))
-    planes_each = side // slabs // 2
-    chunks = max(1, planes_each // (4 * QUADS))
-    squares, mine, *theirs = pl.pallas_call(
-        functools.partial(slab_kernel, side, local_bits, list_length, particles, tile),
-        grid=(slabs,),
-        out_shape=(
-            jax.ShapeDtypeStruct((slabs, particles, LANES), jnp.float32),
-            jax.ShapeDtypeStruct((blocks // 2, features), jnp.float32),
-        ) + (jax.ShapeDtypeStruct((blocks // 2 // chunks, features), jnp.float32),) * chunks,
-        in_specs=[SMEM_SPEC] * 6 + [
-            per_source(1, cap),
-            per_source(cap, features),
-            per_source(cap, features),
-            whole(forward.shape),
-            whole(backward.shape),
-            whole(unit.shape),
-        ],
-        out_specs=(per_source(particles, LANES),) + (ANY_SPEC,) * (1 + chunks),
-        scratch_shapes=[
-            pltpu.VMEM((blocks + 8, features), jnp.float32),
-            pltpu.VMEM((tile, features), jnp.float32),
-            pltpu.SemaphoreType.DMA((1 + chunks,)),
-        ],
-        compiler_params=params(),
-        name="compare_and_add",
-    )(
-        totals_in, table_rows[:, 0], table_rows[:, 1], scale_in, index,
-        lax.axis_index("dom").astype(jnp.int32).reshape(1),
-        words.reshape(slabs, 1, cap), voxels.reshape(slabs, cap, features), pictures,
-        forward, backward, unit,
-    )
-    returned = lax.all_to_all(
-        jnp.sum(squares, axis=2), "slab", split_axis=0, concat_axis=0, tiled=True
-    )
+    per_source = lambda length, width, at=0: pl.BlockSpec((1, length, width), lambda s: (s, at, 0))
+    whole = lambda table: pl.BlockSpec(table.shape, lambda s: (0,) * table.ndim)
+    voxels = voxels.reshape(slabs, cap, features)
+    core = lax.axis_index("dom").astype(jnp.int32).reshape(1)
+    plane_blocks = (side // 8) ** 2
+    pieces = [planes * plane_blocks for planes in pieces_of(side // slabs // 2)]
+    squares, sums = 0.0, ()
+    for part in range(parts):
+        first, last = part == 0, part == parts - 1
+        picture = lax.all_to_all(packed[part], "slab", split_axis=0, concat_axis=0, tiled=True)
+        lengths = [blocks // 2] + pieces if last else [blocks]
+        more, *sums = pl.pallas_call(
+            functools.partial(
+                slab_kernel, side, local_bits, list_length, particles, cap, part * tile, first, last
+            ),
+            grid=(slabs,),
+            out_shape=(jax.ShapeDtypeStruct((slabs, particles, LANES), jnp.float32),)
+            + tuple(jax.ShapeDtypeStruct((length, features), jnp.float32) for length in lengths),
+            in_specs=[SMEM_SPEC] * 6 + [
+                per_source(1, tile),
+                per_source(tile, features, part),
+                per_source(tile, features),
+                whole(forward),
+                whole(backward),
+                whole(unit),
+            ] + [ANY_SPEC] * len(sums),
+            out_specs=(per_source(particles, LANES),) + (ANY_SPEC,) * len(lengths),
+            scratch_shapes=[
+                pltpu.VMEM((blocks + 8, features), jnp.float32),
+                pltpu.VMEM((tile, features), jnp.float32),
+                pltpu.SemaphoreType.DMA((len(lengths),)),
+            ],
+            compiler_params=params(),
+            cost_estimate=pl.CostEstimate(
+                flops=slabs * tile * features * features * 9, bytes_accessed=80 * 1024 * 1024, transcendentals=0
+            ),
+            name="compare_and_add",
+        )(
+            totals_in, table_rows[:, 0], table_rows[:, 1], scale_in, index, core,
+            words[:, part * tile:(part + 1) * tile].reshape(slabs, 1, tile), voxels, picture,
+            forward, backward, unit, *sums,
+        )
+        squares = squares + more
+    mine, *theirs = sums
+    shared = lax.all_gather(jnp.sum(squares, axis=2), "slab")
+    returned = lax.dynamic_index_in_dim(shared, lax.axis_index("slab"), axis=1, keepdims=False)
     losses = jnp.sum(returned, axis=0) / (counts.astype(jnp.float32) * 128.0)
     return mine, theirs, losses, side
 

time: 385 us -> 476 us (1.24)
  blocking collectives: 23.7 us -> 123 us
  Pallas kernels: 160 us -> 226 us
  starting transfers between devices: 63.5 us -> 23 us
  waiting for transfers between devices: 121 us -> 81.5 us
    pallas_call x1 -> x4, Pallas kernels: 35.2 us -> 112 us  [gradient_of_slab(): pl.pallas_call(functools.partial(slab_kernel, side, local_bits, list_leng...]
    all_to_all x1 -> x2, waiting for transfers between devices: 70.3 us -> 0.01 us  [the longest x1 0.01 us: gradient_of_slab(): lax.all_to_all(packed[part], 'slab', split_axis=0, concat_axis=0, tiled=T...]
    all_to_all x2 -> x3, blocking collectives: 23.7 us -> 92.5 us  [gradient_of_slab(): lax.all_to_all(packed[part], 'slab', split_axis=0, concat_axis=0, tiled=T...]
    all_to_all x4 -> x3, starting transfers between devices: 57.2 us -> 11.4 us  [to_field(): got = lax.all_to_all(sent, 'slab', split_axis=0, concat_axis=0, tiled=True)]
    pallas_call x4 -> x3, Pallas kernels: 73.3 us -> 36.1 us  [to_field(): pl.pallas_call(planes_kernel, grid=(quads, per_row // yblocks), out_shape...]
    all_gather x0 -> x1, blocking collectives: none -> 30.4 us  [gradient_of_slab(): shared = lax.all_gather(jnp.sum(squares, axis=2), 'slab')]
    all_to_all x4 -> x3, waiting for transfers between devices: 46.5 us -> 67.4 us  [to_field(): got = lax.all_to_all(sent, 'slab', split_axis=0, concat_axis=0, tiled=True)]
    pallas_call x1 -> x2, Pallas kernels: 19.4 us -> 34.2 us  [the longest x1 22.7 us: gradient_of_slab(): pl.pallas_call(functools.partial(pack_words_kernel, list_length), out_sha...]
  transfers between devices with their start and end apart: 13 -> 11, of which waited for: 6 -> 5; matrix products, arithmetic and copies ran while one was open for 2% -> 2% of each run, Pallas kernels for 23% -> 35%
where the time goes in v3:
time: 476 us; the launch traced here: 473 us
  Pallas kernels  226 us (47%)
  blocking collectives  123 us (26%)
  waiting for transfers between devices  81.5 us (17%)
  starting transfers between devices  23 us (5%)
  local copies, waits for them, and re-layouts  15.7 us (3%)
    pallas_call x4, Pallas kernels, gradient_of_slab(): pl.pallas_call(functools.partial(slab_kernel, side, local_bits, list_leng...  112 us
    all_to_all x3, blocking collectives, gradient_of_slab(): lax.all_to_all(packed[part], 'slab', split_axis=0, concat_axis=0, tiled=T...  92.5 us
    all_to_all x3, waiting for transfers between devices, to_field(): got = lax.all_to_all(sent, 'slab', split_axis=0, concat_axis=0, tiled=True)  67.4 us
    pallas_call x3, Pallas kernels, to_field(): pl.pallas_call(planes_kernel, grid=(quads, per_row // yblocks), out_shape...  36.1 us
    all_gather x1, blocking collectives, gradient_of_slab(): shared = lax.all_gather(jnp.sum(squares, axis=2), 'slab')  30.4 us
    pallas_call x1, Pallas kernels, gradient_of_slab(): pl.pallas_call(functools.partial(gather_kernel, slabs, cap), out_shape=ja...  24.6 us
    pallas_call x1, Pallas kernels, gradient_of_slab(): pl.pallas_call(functools.partial(pack_words_kernel, list_length), out_sha...  22.7 us
    ppermute x3, waiting for transfers between devices, to_field(): theirs = [lax.ppermute(chunk, 'dom', swap) for chunk in theirs_sent]  14.1 us
  transfers between devices with their start and end apart: 11, of which 5 were waited for; matrix products, arithmetic and copies ran while one was open for 2% of the time, Pallas kernels for 35%

profile of v3, /device:TPU:0, one launch (start us, length us, event | category | flops | bytes accessed | tf_op | source)
XLA Modules:
  0.0 473.0 jit_solution(678221897156204290)
XLA Ops:
  3.4 3.7 route.1
  7.1 22.7 %pack_words.1 = s32[17408]{0:T(1024)} custom-call(s32[8192]{0:T(1024)} %bitcast.65, s32[8192]{0:T(1024)} %bitcast.69, s32[8]{0:T(128)} %counts_ref.5), custom_call_target="tpu_custom_call" | custom-call | tf_op jit(solution)/shard_map/pack_words/pallas_call | solution.py:548
  32.8 6.6 %all-to-all-start = ((s32[8,1,2176]{2,1,0:T(1,128)}), s32[8,1,2176]{2,1,0:T(1,128)S(1)}, u32[]{:S(2)}, u32[]{:S(2)}) async-start(s32[8,1,2176]{2,1,0:T(1,128)} %all_to_all.29), calls=%async_computation | async-start | bytes 139264 | tf_op jit(solution)/shard_map/all_to_all | solution.py:582
  39.5 11.4 %pack_images.1 = (bf16[8,512,128]{2,1,0:T(8,128)(2,1)}, bf16[8,512,128]{2,1,0:T(8,128)(2,1)}, bf16[8,512,128]{2,1,0:T(8,128)(2,1)}, bf16[8,512,128]{2,1,0:T(8,128)(2,1)}) custom-call(s32[8192]{0:T(1024)} %bitcast.66, s32[8]{0:T(128)} %counts_ref.5, bf16[8192,128]{1,0:T(8,128)(2,1)} %bitcast.55), custom_call_target="tpu_custom_call" | custom-call | bytes 52428800 | tf_op jit(solution)/shard_map/pack_images/pallas_call | solution.py:558
  50.9 32.5 %all_to_all.47.image_ref = bf16[8,512,128]{2,1,0:T(8,128)(2,1)} all-to-all(bf16[8,512,128]{2,1,0:T(8,128)(2,1)} %get-tuple-element.24), channel_id=1, replica_groups=mesh['groups'=2,'slab'=8,'dom'=2] {'slab'}, dimensions={0} | all-to-all | bytes 2097152 | tf_op jit(solution)/shard_map/all_to_all | solution.py:626
  83.4 30.6 %all_to_all.48.image_ref = bf16[8,512,128]{2,1,0:T(8,128)(2,1)} all-to-all(bf16[8,512,128]{2,1,0:T(8,128)(2,1)} %get-tuple-element.25), channel_id=1, replica_groups=mesh['groups'=2,'slab'=8,'dom'=2] {'slab'}, dimensions={0} | all-to-all | bytes 2097152 | tf_op jit(solution)/shard_map/all_to_all | solution.py:626
  113.9 29.4 %all_to_all.49.image_ref = bf16[8,512,128]{2,1,0:T(8,128)(2,1)} all-to-all(bf16[8,512,128]{2,1,0:T(8,128)(2,1)S(1)} %copy-done.5), channel_id=1, replica_groups=mesh['groups'=2,'slab'=8,'dom'=2] {'slab'}, dimensions={0} | all-to-all | bytes 2097152 | tf_op jit(solution)/shard_map/all_to_all | solution.py:626
  143.4 3.6 all-to-all-start.1
  157.2 24.6 %read_voxels.1 = bf16[16384,128]{1,0:T(8,128)(2,1)} custom-call(s32[16384]{0:T(1024)} %bitcast.50, s32[8]{0:T(128)} %copy-done.11, bf16[32768,128]{1,0:T(8,128)(2,1)} %volume_ref.1), custom_call_target="tpu_custom_call" | custom-call | bytes 104857600 | tf_op jit(solution)/shard_map/read_voxels/pallas_call | solution.py:599
  182.6 28.5 %compare_and_add.4 = (f32[8,8,128]{2,1,0:T(8,128)}, f32[32768,128]{1,0:T(8,128)}) custom-call(s32[8]{0:T(128)} %copy-done.11, f32[64]{0:T(128)} %get-tuple-element.39.defocus_ref, f32[64]{0:T(128)} %get-tuple-element.38.phase_ref, f32[64]{0:T(128)} %mul.17.scale_ref, s32[16384]{0:T(1024)} %bitcast.51, s32[1]{0:T(128)} %bitcast.core_ref, ...), custom_call_target="tpu_custom_call" | custom-call | flops 603979776 | bytes 83886080 | tf_op jit(solution)/shard_map/compare_and_add/pallas_call | solution.py:628
  211.0 32.4 %compare_and_add.5 = (f32[8,8,128]{2,1,0:T(8,128)}, f32[32768,128]{1,0:T(8,128)}) custom-call(s32[8]{0:T(128)} %copy-done.11, f32[64]{0:T(128)} %get-tuple-element.39.defocus_ref, f32[64]{0:T(128)} %get-tuple-element.38.phase_ref, f32[64]{0:T(128)} %mul.17.scale_ref, s32[16384]{0:T(1024)} %bitcast.52, s32[1]{0:T(128)} %bitcast.core_ref, ...), custom_call_target="tpu_custom_call" | custom-call | flops 603979776 | bytes 83886080 | tf_op jit(solution)/shard_map/compare_and_add/pallas_call | solution.py:628
  243.5 31.2 %compare_and_add.6 = (f32[8,8,128]{2,1,0:T(8,128)}, f32[32768,128]{1,0:T(8,128)}) custom-call(s32[8]{0:T(128)} %copy-done.11, f32[64]{0:T(128)} %get-tuple-element.39.defocus_ref, f32[64]{0:T(128)} %get-tuple-element.38.phase_ref, f32[64]{0:T(128)} %mul.17.scale_ref, s32[16384]{0:T(1024)} %bitcast.53, s32[1]{0:T(128)} %bitcast.core_ref, ...), custom_call_target="tpu_custom_call" | custom-call | flops 603979776 | bytes 83886080 | tf_op jit(solution)/shard_map/compare_and_add/pallas_call | solution.py:628
  275.8 20.0 %compare_and_add.7 = (f32[8,8,128]{2,1,0:T(8,128)}, f32[16384,128]{1,0:T(8,128)}, f32[4096,128]{1,0:T(8,128)}, f32[4096,128]{1,0:T(8,128)}, f32[8192,128]{1,0:T(8,128)}) custom-call(s32[8]{0:T(128)} %copy-done.11, f32[64]{0:T(128)} %get-tuple-element.39.defocus_ref, f32[64]{0:T(128)} %get-tuple-element.38.phase_ref, f32[64]{0:T(128)} %mul.17.scale_ref, ...), custom_call_target="tpu_custom_call" | custom-call | flops 603979776 | bytes 83886080 | tf_op jit(solution)/shard_map/compare_and_add/pallas_call | solution.py:628
  296.4 9.8 %collective-permute-done = f32[4096,128]{1,0:T(8,128)S(1)} collective-permute-done((f32[4096,128]{1,0:T(8,128)}, f32[4096,128]{1,0:T(8,128)S(1)}, u32[]{:S(2)}, u32[]{:S(2)}) %collective-permute-start) | collective-permute-done | bytes 2097184 | tf_op jit(solution)/shard_map/ppermute | solution.py:466
  307.6 9.5 %transform_planes.3 = bf16[8,4,2,32,256]{4,3,2,1,0:T(8,128)(2,1)} custom-call(f32[16,32,32,128]{3,2,1,0:T(8,128)} %bitcast.39, f32[4,32,32,128]{3,2,1,0:T(8,128)} %bitcast.57, bf16[384,256]{1,0:T(8,128)(2,1)} %constant.40.clone.zblock_ref, f32[2,8,128]{2,1,0:T(8,128)} %constant.41.clone.turn_ref, bf16[512,512]{1,0:T(8,128)(2,1)} %constant.42.clone.wide_ref, ...), custom_call_target="tpu_custom_call" | custom-call | flops 536870912 | bytes 8388608 | tf_op jit(solution)/shard_map/transform_planes/pallas_call | solution.py:482
  320.6 17.0 %transform_planes.5 = bf16[8,8,2,32,256]{4,3,2,1,0:T(8,128)(2,1)} custom-call(f32[16,32,32,128]{3,2,1,0:T(8,128)} %bitcast.40, f32[8,32,32,128]{3,2,1,0:T(8,128)} %bitcast.21.theirs_ref, bf16[384,256]{1,0:T(8,128)(2,1)} %constant.40.clone.zblock_ref, f32[2,8,128]{2,1,0:T(8,128)} %constant.41.clone.turn_ref, bf16[512,512]{1,0:T(8,128)(2,1)} %constant.42.clone.wide_ref, ...), custom_call_target="tpu_custom_call" | custom-call | flops 1073741824 | bytes 16777216 | tf_op jit(solution)/shard_map/transform_planes/pallas_call | solution.py:482
  337.6 9.3 %all-to-all-done.5.refs_0_ = bf16[8,4,2,32,256]{4,3,2,1,0:T(8,128)(2,1)S(1)} async-done(((bf16[8,4,2,32,256]{4,3,2,1,0:T(8,128)(2,1)}), bf16[8,4,2,32,256]{4,3,2,1,0:T(8,128)(2,1)S(1)}, u32[]{:S(2)}, u32[]{:S(2)}) %all-to-all-start.5) | async-done | bytes 1048608 | tf_op jit(solution)/shard_map/all_to_all | solution.py:504
  350.6 4.4 collective-permute-done.1
  356.3 9.6 %transform_planes.4 = bf16[8,4,2,32,256]{4,3,2,1,0:T(8,128)(2,1)} custom-call(f32[16,32,32,128]{3,2,1,0:T(8,128)} %bitcast.41, f32[4,32,32,128]{3,2,1,0:T(8,128)} %bitcast.56, bf16[384,256]{1,0:T(8,128)(2,1)} %constant.40.clone.zblock_ref, f32[2,8,128]{2,1,0:T(8,128)} %constant.41.clone.turn_ref, bf16[512,512]{1,0:T(8,128)(2,1)} %constant.42.clone.wide_ref, ...), custom_call_target="tpu_custom_call" | custom-call | flops 536870912 | bytes 8388608 | tf_op jit(solution)/shard_map/transform_planes/pallas_call | solution.py:482
  365.9 33.0 %all-to-all-done.7.refs_2_ = bf16[8,8,2,32,256]{4,3,2,1,0:T(8,128)(2,1)S(1)} async-done(((bf16[8,8,2,32,256]{4,3,2,1,0:T(8,128)(2,1)}), bf16[8,8,2,32,256]{4,3,2,1,0:T(8,128)(2,1)S(1)}, u32[]{:S(2)}, u32[]{:S(2)}) %all-to-all-start.7) | async-done | bytes 2097184 | tf_op jit(solution)/shard_map/all_to_all | solution.py:504
  398.9 4.2 all-to-all-start.6
  403.8 25.0 %all-to-all-done.6.refs_1_ = bf16[8,4,2,32,256]{4,3,2,1,0:T(8,128)(2,1)} async-done(((bf16[8,4,2,32,256]{4,3,2,1,0:T(8,128)(2,1)}), bf16[8,4,2,32,256]{4,3,2,1,0:T(8,128)(2,1)}, u32[]{:S(2)}, u32[]{:S(2)}) %all-to-all-start.6) | async-done | bytes 1048608 | tf_op jit(solution)/shard_map/all_to_all | solution.py:504
  428.9 30.4 %all-gather = f32[64,8]{1,0:T(8,128)S(1)} all-gather(f32[8,8]{1,0:T(8,128)S(1)} %add_reduce_fusion), channel_id=2, replica_groups=mesh['groups'=2,'slab'=8,'dom'=2] {'slab'}, dimensions={0}, use_global_device_ids=true | all-gather | bytes 2304 | tf_op jit(solution)/shard_map/all_gather | solution.py:661
  459.9 13.0 %transform_first.1 = f32[2,128,32,256]{3,2,1,0:T(8,128)} custom-call(s32[1]{0:T(128)} %bitcast.core_ref, bf16[8,4,2,32,256]{4,3,2,1,0:T(8,128)(2,1)} %copy-done.1, bf16[8,4,2,32,256]{4,3,2,1,0:T(8,128)(2,1)} %all-to-all-done.6.refs_1_, bf16[8,8,2,32,256]{4,3,2,1,0:T(8,128)(2,1)} %copy-done, bf16[8,4,2,32,256]{4,3,2,1,0:T(8,128)(2,1)} %collective-permute-done.3.refs_3_, ...), custom_call_target="tpu_custom_call" | custom-call | tf_op jit(solution)/shard_map/transform_first/pallas_call | solution.py:509
  (80 shorter events, 29.5 us)
Async XLA Ops:
  32.8 18.1 %all-to-all-start = ((s32[8,1,2176]{2,1,0:T(1,128)}), s32[8,1,2176]{2,1,0:T(1,128)S(1)}, u32[]{:S(2)}, u32[]{:S(2)}) async-start(s32[8,1,2176]{2,1,0:T(1,128)} %all_to_all.29), calls=%async_computation | async-start | bytes 139264 | tf_op jit(solution)/shard_map/all_to_all | solution.py:582
  50.9 63.1 %copy-start.5 = (bf16[8,512,128]{2,1,0:T(8,128)(2,1)S(1)}, bf16[8,512,128]{2,1,0:T(8,128)(2,1)}, u32[]{:S(2)}) copy-start(bf16[8,512,128]{2,1,0:T(8,128)(2,1)} %get-tuple-element.26) | copy-start | bytes 3145732
  50.9 96.1 %copy-start.13 = (f32[64,2]{0,1:T(2,128)S(1)}, f32[64,2]{0,1:T(2,128)}, u32[]{:S(2)}) copy-start(f32[64,2]{0,1:T(2,128)} %param.22) | copy-start | bytes 1540
  50.9 96.2 %copy-start.6 = (bf16[4,128,128]{2,1,0:T(8,128)(2,1)S(1)}, bf16[4,128,128]{2,1,0:T(8,128)(2,1)}, u32[]{:S(2)}) copy-start(bf16[4,128,128]{2,1,0:T(8,128)(2,1)} %param.15) | copy-start | bytes 393220
  143.4 131.3 %all-to-all-start.1 = ((bf16[8,512,128]{2,1,0:T(8,128)(2,1)}), bf16[8,512,128]{2,1,0:T(8,128)(2,1)S(1)}, u32[]{:S(2)}, u32[]{:S(2)}) async-start(bf16[8,512,128]{2,1,0:T(8,128)(2,1)} %get-tuple-element.23), calls=%async_computation.1 | async-start | bytes 2097152 | tf_op jit(solution)/shard_map/all_to_all | solution.py:626
  149.3 7.9 %copy-start.11 = (s32[8]{0:T(128)}, s32[8]{0:T(128)S(1)}, u32[]{:S(2)}) copy-start(s32[8]{0:T(128)S(1)} %slice_reduce_fusion.2.totals_ref) | copy-start | bytes 100
  295.8 24.8 %collective-permute-start.2 = (f32[8192,128]{1,0:T(8,128)}, f32[8192,128]{1,0:T(8,128)}, u32[]{:S(2)}, u32[]{:S(2)}) collective-permute-start(f32[8192,128]{1,0:T(8,128)} %get-tuple-element.33), channel_id=1, source_target_pairs={{0,1},{1,0},{2,3},{3,2},{4,5},{5,4},{6,7},{7,6},{8,9},{9,8},{10,11... | collective-permute-start | bytes 12582920 | tf_op jit(solution)/shard_map/ppermute | solution.py:466
  296.4 9.9 %collective-permute-start = (f32[4096,128]{1,0:T(8,128)}, f32[4096,128]{1,0:T(8,128)S(1)}, u32[]{:S(2)}, u32[]{:S(2)}) collective-permute-start(f32[4096,128]{1,0:T(8,128)} %get-tuple-element.31), channel_id=1, source_target_pairs={{0,1},{1,0},{2,3},{3,2},{4,5},{5,4},{6,7},{7,6},{8,9},{9,8},{10,11... | collective-permute-start | bytes 6291464 | tf_op jit(solution)/shard_map/ppermute | solution.py:466
  306.2 1.3 copy-start.4
  317.1 29.8 %all-to-all-start.5 = ((bf16[8,4,2,32,256]{4,3,2,1,0:T(8,128)(2,1)}), bf16[8,4,2,32,256]{4,3,2,1,0:T(8,128)(2,1)S(1)}, u32[]{:S(2)}, u32[]{:S(2)}) async-start(bf16[8,4,2,32,256]{4,3,2,1,0:T(8,128)(2,1)} %transform_planes.3), calls=%async_computation.5 | async-start | bytes 2097152 | tf_op jit(solution)/shard_map/all_to_all | solution.py:504
  346.9 56.4 %copy-start.1 = (bf16[8,4,2,32,256]{4,3,2,1,0:T(8,128)(2,1)}, bf16[8,4,2,32,256]{4,3,2,1,0:T(8,128)(2,1)S(1)}, u32[]{:S(2)}) copy-start(bf16[8,4,2,32,256]{4,3,2,1,0:T(8,128)(2,1)S(1)} %all-to-all-done.5.refs_0_) | copy-start | bytes 3145732
  346.9 52.1 %all-to-all-start.7 = ((bf16[8,8,2,32,256]{4,3,2,1,0:T(8,128)(2,1)}), bf16[8,8,2,32,256]{4,3,2,1,0:T(8,128)(2,1)S(1)}, u32[]{:S(2)}, u32[]{:S(2)}) async-start(bf16[8,8,2,32,256]{4,3,2,1,0:T(8,128)(2,1)} %transform_planes.5), calls=%async_computation.7 | async-start | bytes 4194304 | tf_op jit(solution)/shard_map/all_to_all | solution.py:504
  350.5 4.4 collective-permute-start.1
  354.9 1.3 copy-start.3
  356.3 72.6 %copy-start.7 = (f32[8,8,128]{2,1,0:T(8,128)S(1)}, f32[8,8,128]{2,1,0:T(8,128)}, u32[]{:S(2)}) copy-start(f32[8,8,128]{2,1,0:T(8,128)} %get-tuple-element.34) | copy-start | bytes 98308
  356.3 72.6 %copy-start.8 = (f32[8,8,128]{2,1,0:T(8,128)S(1)}, f32[8,8,128]{2,1,0:T(8,128)}, u32[]{:S(2)}) copy-start(f32[8,8,128]{2,1,0:T(8,128)} %get-tuple-element.35) | copy-start | bytes 98308
  356.3 72.6 %copy-start.9 = (f32[8,8,128]{2,1,0:T(8,128)S(1)}, f32[8,8,128]{2,1,0:T(8,128)}, u32[]{:S(2)}) copy-start(f32[8,8,128]{2,1,0:T(8,128)} %get-tuple-element.36) | copy-start | bytes 98308
  356.3 72.6 %copy-start.10 = (f32[8,8,128]{2,1,0:T(8,128)S(1)}, f32[8,8,128]{2,1,0:T(8,128)}, u32[]{:S(2)}) copy-start(f32[8,8,128]{2,1,0:T(8,128)} %get-tuple-element.37) | copy-start | bytes 98308
  356.3 103.1 %copy-start.12 = (s32[8]{0:T(128)S(1)}, s32[8]{0:T(128)}, u32[]{:S(2)}) copy-start(s32[8]{0:T(128)} %counts_ref.5) | copy-start | bytes 100
  398.9 61.0 %copy-start = (bf16[8,8,2,32,256]{4,3,2,1,0:T(8,128)(2,1)}, bf16[8,8,2,32,256]{4,3,2,1,0:T(8,128)(2,1)S(1)}, u32[]{:S(2)}) copy-start(bf16[8,8,2,32,256]{4,3,2,1,0:T(8,128)(2,1)S(1)} %all-to-all-done.7.refs_2_) | copy-start | bytes 6291460
  398.9 29.9 %all-to-all-start.6 = ((bf16[8,4,2,32,256]{4,3,2,1,0:T(8,128)(2,1)}), bf16[8,4,2,32,256]{4,3,2,1,0:T(8,128)(2,1)}, u32[]{:S(2)}, u32[]{:S(2)}) async-start(bf16[8,4,2,32,256]{4,3,2,1,0:T(8,128)(2,1)} %transform_planes.4), calls=%async_computation.6 | async-start | bytes 2097152 | tf_op jit(solution)/shard_map/all_to_all | solution.py:504
  403.2 56.7 %collective-permute-start.5 = (bf16[8,8,2,32,256]{4,3,2,1,0:T(8,128)(2,1)S(1)}, bf16[8,8,2,32,256]{4,3,2,1,0:T(8,128)(2,1)}, u32[]{:S(2)}, u32[]{:S(2)}) collective-permute-start(bf16[8,8,2,32,256]{4,3,2,1,0:T(8,128)(2,1)S(1)} %all-to-all-done.7.refs_2_), channel_id=1, source_target_pairs={{0,1},{1,0},{2,3},{3,2},{4,5},{5,4},{6,7},{7,6},{8,9},{9,8},{10,11... | collective-permute-start | bytes 6291464 | tf_op jit(solution)/shard_map/ppermute | solution.py:506
  403.3 56.6 %collective-permute-start.3 = (bf16[8,4,2,32,256]{4,3,2,1,0:T(8,128)(2,1)S(1)}, bf16[8,4,2,32,256]{4,3,2,1,0:T(8,128)(2,1)}, u32[]{:S(2)}, u32[]{:S(2)}) collective-permute-start(bf16[8,4,2,32,256]{4,3,2,1,0:T(8,128)(2,1)S(1)} %all-to-all-done.5.refs_0_), channel_id=1, source_target_pairs={{0,1},{1,0},{2,3},{3,2},{4,5},{5,4},{6,7},{7,6},{8,9},{9,8},{10,11... | collective-permute-start | bytes 3145736 | tf_op jit(solution)/shard_map/ppermute | solution.py:506
  428.8 31.1 %collective-permute-start.4 = (bf16[8,4,2,32,256]{4,3,2,1,0:T(8,128)(2,1)}, bf16[8,4,2,32,256]{4,3,2,1,0:T(8,128)(2,1)}, u32[]{:S(2)}, u32[]{:S(2)}) collective-permute-start(bf16[8,4,2,32,256]{4,3,2,1,0:T(8,128)(2,1)} %all-to-all-done.6.refs_1_), channel_id=1, source_target_pairs={{0,1},{1,0},{2,3},{3,2},{4,5},{5,4},{6,7},{7,6},{8,9},{9,8},{10,11... | collective-permute-start | bytes 3145736 | tf_op jit(solution)/shard_map/ppermute | solution.py:506
  (1 other events, 1.1 us)

commit v4 on v3

--- a/solution.py
+++ b/solution.py
@@ -11,6 +11,7 @@
 
 LANES = 128
 TILE = 512
+COPIES = 8
 GROUP = 16
 VMEM_LIMIT = 56 * 1024 * 1024
 
@@ -67,19 +68,7 @@
     word_ref[...] = word | (particle << (kind_bits + 2 + bits_of(list_length)))
 
 
-def pack_words_kernel(list_length, target_ref, word_ref, counts_ref, meta_ref):
-    @pl.loop(0, counts_ref.shape[0])
-    def _(particle):
-        @pl.loop(0, (counts_ref[particle] + 15) // 16)
-        def _(i):
-            first = particle * list_length + i * 16
-            targets = [target_ref[first + j] for j in range(16)]
-            words = [word_ref[first + j] for j in range(16)]
-            for j in range(16):
-                meta_ref[targets[j]] = words[j]
-
-
-def pack_images_kernel(slabs, cap, list_length, target_ref, counts_ref, image_ref, *refs):
+def pack_kernel(slabs, cap, list_length, target_ref, word_ref, counts_ref, image_ref, meta_ref, *refs):
     out_refs, (wide_ref, staged_ref) = refs[:-2], refs[-2:]
     step = 256
 
@@ -95,8 +84,10 @@
             first = particle * list_length + i * 16
             targets = [target_ref[first + j] for j in range(16)]
             rows = [wide_ref[pl.ds(first + j, 1), :] for j in range(16)]
+            words = [word_ref[first + j] for j in range(16)]
             for j in range(16):
                 staged_ref[pl.ds(targets[j], 1), :] = rows[j]
+                meta_ref[targets[j]] = words[j]
 
     for chunk, out_ref in enumerate(out_refs):
         width = out_ref.shape[1]
@@ -186,6 +177,15 @@
     per_row = side // 8
     live = jnp.clip(totals_ref[source] - offset, 0, tile)
 
+    def fetches():
+        length = blocks // COPIES
+        return [
+            pltpu.make_async_copy(
+                before_ref.at[pl.ds(i * length, length)], sum_ref.at[pl.ds(i * length, length)], sems.at[i]
+            )
+            for i in range(COPIES)
+        ]
+
     @pl.when(source == 0)
     def _():
         if first:
@@ -194,7 +194,8 @@
                 at = pl.multiple_of(i * 256, 256)
                 sum_ref[pl.ds(at, 256), :] = jnp.zeros((256, features), jnp.float32)
         else:
-            pltpu.make_async_copy(before_ref, sum_ref.at[pl.ds(0, blocks)], sems.at[0]).start()
+            for copy in fetches():
+                copy.start()
 
     @pl.when(live == 0)
     def _():
@@ -251,7 +252,8 @@
     if not first:
         @pl.when(source == 0)
         def _():
-            pltpu.make_async_copy(before_ref, sum_ref.at[pl.ds(0, blocks)], sems.at[0]).wait()
+            for copy in fetches():
+                copy.wait()
 
     @pl.loop(0, (live + GROUP - 1) // GROUP)
     def _(g):
@@ -285,10 +287,18 @@
                 start = start + out_ref.shape[0]
         else:
             places = [0]
-        for i, (place, out_ref) in enumerate(zip(places, sum_refs)):
-            length = out_ref.shape[0]
-            at = pl.multiple_of(place, 8)
-            copies.append(pltpu.make_async_copy(sum_ref.at[pl.ds(at, length)], out_ref, sems.at[i]))
+        cuts = max(1, COPIES // len(places))
+        for place, out_ref in zip(places, sum_refs):
+            length = out_ref.shape[0] // cuts
+            for i in range(cuts):
+                at = pl.multiple_of(place + i * length, 8)
+                copies.append(
+                    pltpu.make_async_copy(
+                        sum_ref.at[pl.ds(at, length)],
+                        out_ref.at[pl.ds(i * length, length)],
+                        sems.at[len(copies)],
+                    )
+                )
         for copy in copies:
             copy.start()
         for copy in copies:
@@ -345,11 +355,21 @@
     return high, (value - high.astype(jnp.float32)).astype(jnp.bfloat16)
 
 
-def planes_kernel(mine_ref, theirs_ref, zblock_ref, turn_ref, wide_ref, fine_ref, out_ref, high_ref, low_ref):
+def planes_kernel(me_ref, mine_ref, theirs_ref, zblock_ref, turn_ref, wide_ref, fine_ref, *refs):
+    out_refs, (high_ref, low_ref, wide_here_ref, fine_here_ref) = refs[:-4], refs[-4:]
     step = pl.program_id(1)
     count = mine_ref.shape[1]
-    groups, side = out_ref.shape[0], out_ref.shape[4]
-    height = side // groups
+    groups = len(out_refs)
+    height, side = out_refs[0].shape[2:]
+
+    @pl.when((step == 0) & (pl.program_id(0) == 0))
+    def _():
+        for part in range(2):
+            for group in range(groups):
+                at = pl.multiple_of(part * side + (group ^ me_ref[0]) * height, height)
+                to = slice(part * side + group * height, part * side + (group + 1) * height)
+                wide_here_ref[to, :] = wide_ref[pl.ds(at, height), :]
+                fine_here_ref[to, :] = fine_ref[pl.ds(at, height), :]
 
     @pl.loop(0, count, unroll=4)
     def _(i):
@@ -384,17 +404,19 @@
             columns = pl.ds(pl.multiple_of(x * side, side), side)
             product = functools.partial(jnp.dot, preferred_element_type=jnp.float32)
             high = high_ref[:, columns]
-            result = product(wide_ref[...], high) + (
-                product(wide_ref[...], low_ref[:, columns]) + product(fine_ref[...], high)
+            wide = wide_here_ref[...]
+            result = product(wide, high) + (
+                product(wide, low_ref[:, columns]) + product(fine_here_ref[...], high)
             )
             for part in range(2):
                 for group in range(groups):
                     start = part * side + group * height
-                    out_ref[group, x, part] = result[start:start + height, :].astype(jnp.bfloat16)
+                    out_refs[group][x, part] = result[start:start + height, :].astype(jnp.bfloat16)
 
 
 def first_dimension_kernel(slabs, each, core_ref, *refs):
     arrays, (out_ref, mid_ref) = refs[:-2], refs[-2:]
+    me = core_ref[1]
     chunks = len(arrays) // 2
     own, other = arrays[:chunks], arrays[chunks:]
     spots = [(i, at) for i, ref in enumerate(own) for at in range(ref.shape[1])]
@@ -408,8 +430,8 @@
         loaded = []
         for part in range(2):
             chunk, at = spots[inner]
-            here = own[chunk][slab, at, part].astype(jnp.float32)
-            there = other[chunk][slab, at, part].astype(jnp.float32)
+            here = own[chunk][slab ^ me, at, part].astype(jnp.float32)
+            there = other[chunk][slab ^ me, at, part].astype(jnp.float32)
             loaded.append(jnp.where(is_first, here, there) if half == 0 else jnp.where(is_first, there, here))
         return tuple(loaded)
 
@@ -461,6 +483,7 @@
     each = side // slabs // 2
     height = side // slabs
     groups = slabs if height % 16 == 0 else 1
+    me = lax.axis_index("slab").astype(jnp.int32) if groups == slabs else jnp.int32(0)
     tables = [jnp.asarray(table) for table in transform_tables(side)]
     swap = [(0, 1), (1, 0)]
     theirs = [lax.ppermute(chunk, "dom", swap) for chunk in theirs_sent]
@@ -482,26 +505,33 @@
         sent = pl.pallas_call(
             planes_kernel,
             grid=(quads, per_row // yblocks),
-            out_shape=jax.ShapeDtypeStruct((groups, held, 2, side // groups, side), jnp.bfloat16),
-            in_specs=[
+            out_shape=(jax.ShapeDtypeStruct((held, 2, side // groups, side), jnp.bfloat16),) * groups,
+            in_specs=[SMEM_SPEC] + [
                 pl.BlockSpec((4, yblocks, per_row, LANES), lambda q, y, at=first_quad: (at + q, y, 0, 0)),
                 pl.BlockSpec((4, yblocks, per_row, LANES), lambda q, y: (q, y, 0, 0)),
             ] + [whole(table) for table in tables],
-            out_specs=pl.BlockSpec((groups, 4, 2, side // groups, side), lambda q, y: (0, q, 0, 0, 0)),
+            out_specs=(pl.BlockSpec((4, 2, side // groups, side), lambda q, y: (q, 0, 0, 0)),) * groups,
             scratch_shapes=[
                 pltpu.VMEM((2 * side, 4 * side), jnp.bfloat16),
                 pltpu.VMEM((2 * side, 4 * side), jnp.bfloat16),
+                pltpu.VMEM((2 * side, 2 * side), jnp.bfloat16),
+                pltpu.VMEM((2 * side, 2 * side), jnp.bfloat16),
             ],
             compiler_params=params(),
             cost_estimate=pl.CostEstimate(
                 flops=held * 8 * side**3, bytes_accessed=held * 4 * side**2 * 8, transcendentals=0
             ),
             name="transform_planes",
-        )(mine, added, *tables)
+        )(me.reshape(1), mine, added, *tables)
         if groups != slabs:
-            sent = sent.reshape(-1, 2, slabs, height, side).transpose(2, 0, 1, 3, 4)[:, :real_planes]
+            sent = sent[0].reshape(-1, 2, slabs, height, side).transpose(2, 0, 1, 3, 4)[:, :real_planes]
+            got = lax.all_to_all(sent, "slab", split_axis=0, concat_axis=0, tiled=True)
+        else:
+            got = jnp.stack([sent[0]] + [
+                lax.ppermute(sent[i], "slab", [(slab, slab ^ i) for slab in range(slabs)])
+                for i in range(1, slabs)
+            ])
         first_quad += quads
-        got = lax.all_to_all(sent, "slab", split_axis=0, concat_axis=0, tiled=True)
         own.append(got)
         other.append(lax.ppermute(got, "dom", swap))
     rows = min(16, height)
@@ -518,7 +548,7 @@
         scratch_shapes=[pltpu.VMEM((16, 16, 2, rows, LANES), jnp.float32)],
         compiler_params=params(),
         name="transform_first",
-    )(lax.axis_index("dom").astype(jnp.int32).reshape(1), *arrays)
+    )(jnp.stack([lax.axis_index("dom").astype(jnp.int32), me]), *arrays)
 
 
 def gradient_of_slab(volume, kernels, images, owners, local_block, kinds, counts, ctf_code, ctf_table, scales):
@@ -545,29 +575,21 @@
         owners.reshape(rows, LANES), local_block.reshape(rows, LANES), kinds.reshape(rows, LANES), counts
     )
     target, word = target.reshape(entries), word.reshape(entries)
-    meta = pl.pallas_call(
-        functools.partial(pack_words_kernel, list_length),
-        out_shape=jax.ShapeDtypeStruct((slots + 1024,), jnp.int32),
-        in_specs=[SMEM_SPEC, SMEM_SPEC, SMEM_SPEC],
-        out_specs=SMEM_SPEC,
-        compiler_params=params(),
-        name="pack_words",
-    )(target, word, counts)
     parts = max(1, cap // TILE)
     tile = cap // parts
-    packed = pl.pallas_call(
-        functools.partial(pack_images_kernel, slabs, cap, list_length),
-        out_shape=(jax.ShapeDtypeStruct((slabs, tile, features), jnp.bfloat16),) * parts,
-        in_specs=[SMEM_SPEC, SMEM_SPEC, VMEM_SPEC],
-        out_specs=(VMEM_SPEC,) * parts,
+    meta, *packed = pl.pallas_call(
+        functools.partial(pack_kernel, slabs, cap, list_length),
+        out_shape=(jax.ShapeDtypeStruct((slots + 1024,), jnp.int32),)
+        + (jax.ShapeDtypeStruct((slabs, tile, features), jnp.bfloat16),) * parts,
+        in_specs=[SMEM_SPEC, SMEM_SPEC, SMEM_SPEC, VMEM_SPEC],
+        out_specs=(SMEM_SPEC,) + (VMEM_SPEC,) * parts,
         scratch_shapes=[
             pltpu.VMEM((entries, features), jnp.float32),
             pltpu.VMEM((slots + 8, features), jnp.float32),
         ],
         compiler_params=params(),
-        cost_estimate=pl.CostEstimate(flops=0, bytes_accessed=50 * 1024 * 1024, transcendentals=0),
-        name="pack_images",
-    )(target, counts, images.reshape(entries, features))
+        name="pack",
+    )(target, word, counts, images.reshape(entries, features))
 
     code = ctf_code | ((scales.astype(jnp.float32) * 256.0).astype(jnp.int32) << 8)
     header = jnp.concatenate(
@@ -620,9 +642,13 @@
     core = lax.axis_index("dom").astype(jnp.int32).reshape(1)
     plane_blocks = (side // 8) ** 2
     pieces = [planes * plane_blocks for planes in pieces_of(side // slabs // 2)]
-    squares, sums = 0.0, ()
+    squares, sums, behind = 0.0, (), [voxels]
     for part in range(parts):
         first, last = part == 0, part == parts - 1
+        if not first:
+            packed[part], earlier = lax.optimization_barrier((packed[part], behind[part - 1]))
+            if part == 1:
+                voxels = earlier
         picture = lax.all_to_all(packed[part], "slab", split_axis=0, concat_axis=0, tiled=True)
         lengths = [blocks // 2] + pieces if last else [blocks]
         more, *sums = pl.pallas_call(
@@ -644,12 +670,10 @@
             scratch_shapes=[
                 pltpu.VMEM((blocks + 8, features), jnp.float32),
                 pltpu.VMEM((tile, features), jnp.float32),
-                pltpu.SemaphoreType.DMA((len(lengths),)),
+                pltpu.SemaphoreType.DMA((COPIES,)),
             ],
             compiler_params=params(),
-            cost_estimate=pl.CostEstimate(
-                flops=slabs * tile * features * features * 9, bytes_accessed=80 * 1024 * 1024, transcendentals=0
-            ),
+            cost_estimate=pl.CostEstimate(flops=0, bytes_accessed=16 * 1024 * 1024, transcendentals=0),
             name="compare_and_add",
         )(
             totals_in, table_rows[:, 0], table_rows[:, 1], scale_in, index, core,
@@ -657,6 +681,7 @@
             forward, backward, unit, *sums,
         )
         squares = squares + more
+        behind.append(more)
     mine, *theirs = sums
     shared = lax.all_gather(jnp.sum(squares, axis=2), "slab")
     returned = lax.dynamic_index_in_dim(shared, lax.axis_index("slab"), axis=1, keepdims=False)

time: 476 us -> 395 us (0.83)
  blocking collectives: 123 us -> 52.9 us
  starting transfers between devices: 23 us -> 72.7 us
  Pallas kernels: 226 us -> 184 us
  waiting for transfers between devices: 81.5 us -> 58.8 us
  local copies, waits for them, and re-layouts: 15.7 us -> 20.5 us
    all_to_all x3 -> x1, blocking collectives: 92.5 us -> 14.6 us  [gradient_of_slab(): lax.all_to_all(sent, 'slab', split_axis=0, concat_axis=0, tiled=True)]
    all_to_all x4 -> x0, waiting for transfers between devices: 67.4 us -> none  [the longest x3 67.4 us: to_field(): got = lax.all_to_all(sent, 'slab', split_axis=0, concat_axis=0, tiled=True)]
    ppermute x0 -> x21, waiting for transfers between devices: none -> 47.5 us  [to_field(): lax.ppermute(sent[i], 'slab', [(slab, slab ^ i) for slab in range(slabs)])]
    ppermute x0 -> x21, starting transfers between devices: none -> 46.1 us  [to_field(): lax.ppermute(sent[i], 'slab', [(slab, slab ^ i) for slab in range(slabs)])]
    all_to_all x1 -> x4, starting transfers between devices: 3.64 us -> 25.3 us  [gradient_of_slab(): lax.all_to_all(packed[part], 'slab', split_axis=0, concat_axis=0, tiled=T...]
    all_to_all x4 -> x0, starting transfers between devices: 18 us -> none  [the longest x3 11.4 us: to_field(): got = lax.all_to_all(sent, 'slab', split_axis=0, concat_axis=0, tiled=True)]
    pallas_call x2 -> x1, Pallas kernels: 34.2 us -> 16.3 us  [gradient_of_slab(): pl.pallas_call(functools.partial(pack_kernel, slabs, cap, list_length), o...]
    pallas_call x4, Pallas kernels: 112 us -> 95.1 us  [gradient_of_slab(): pl.pallas_call(functools.partial(slab_kernel, side, local_bits, list_leng...]
  transfers between devices with their start and end apart: 11 -> 31, of which waited for: 5 -> 10; matrix products, arithmetic and copies ran while one was open for 2% -> 4% of each run, Pallas kernels for 35% -> 34%
where the time goes in v4:
time: 395 us; the launch traced here: 394 us
  Pallas kernels  184 us (47%)
  starting transfers between devices  72.7 us (18%)
  waiting for transfers between devices  58.8 us (15%)
  blocking collectives  52.9 us (13%)
  local copies, waits for them, and re-layouts  20.5 us (5%)
    pallas_call x4, Pallas kernels, gradient_of_slab(): pl.pallas_call(functools.partial(slab_kernel, side, local_bits, list_leng...  95.1 us
    ppermute x21, waiting for transfers between devices, to_field(): lax.ppermute(sent[i], 'slab', [(slab, slab ^ i) for slab in range(slabs)])  47.5 us
    ppermute x21, starting transfers between devices, to_field(): lax.ppermute(sent[i], 'slab', [(slab, slab ^ i) for slab in range(slabs)])  46.1 us
    all_gather x1, blocking collectives, gradient_of_slab(): shared = lax.all_gather(jnp.sum(squares, axis=2), 'slab')  38.3 us
    pallas_call x3, Pallas kernels, to_field(): pl.pallas_call(planes_kernel, grid=(quads, per_row // yblocks), out_shape...  36.5 us
    all_to_all x4, starting transfers between devices, gradient_of_slab(): lax.all_to_all(packed[part], 'slab', split_axis=0, concat_axis=0, tiled=T...  25.3 us
    pallas_call x1, Pallas kernels, gradient_of_slab(): pl.pallas_call(functools.partial(gather_kernel, slabs, cap), out_shape=ja...  17.2 us
    pallas_call x1, Pallas kernels, gradient_of_slab(): pl.pallas_call(functools.partial(pack_kernel, slabs, cap, list_length), o...  16.3 us
  transfers between devices with their start and end apart: 31, of which 10 were waited for; matrix products, arithmetic and copies ran while one was open for 4% of the time, Pallas kernels for 34%

profile of v4, /device:TPU:0, one launch (start us, length us, event | category | flops | bytes accessed | tf_op | source)
XLA Modules:
  0.0 393.5 jit_solution(4884065279896724886)
XLA Ops:
  7.2 16.3 %pack.1 = (s32[17408]{0:T(1024)}, bf16[8,512,128]{2,1,0:T(8,128)(2,1)}, bf16[8,512,128]{2,1,0:T(8,128)(2,1)}, bf16[8,512,128]{2,1,0:T(8,128)(2,1)}, bf16[8,512,128]{2,1,0:T(8,128)(2,1)}) custom-call(s32[8192]{0:T(1024)} %bitcast.114, s32[8192]{0:T(1024)} %bitcast.115, s32[8]{0:T(128)} %counts_ref.3, bf16[8192,128]{1,0:T(8,128)(2,1)} %bitcast.105), custom_call_target="tpu_custom_call" | custom-call | tf_op jit(solution)/shard_map/pack/pallas_call | solution.py:580
  24.6 14.6 %all_to_all.32 = s32[8,1,2176]{2,1,0:T(1,128)S(1)} all-to-all(s32[8,1,2176]{2,1,0:T(1,128)S(1)} %all_to_all.20), channel_id=1, replica_groups=mesh['groups'=2,'slab'=8,'dom'=2] {'slab'}, dimensions={0} | all-to-all | bytes 139264 | tf_op jit(solution)/shard_map/all_to_all | solution.py:604
  46.8 17.2 %read_voxels.1 = bf16[16384,128]{1,0:T(8,128)(2,1)} custom-call(s32[16384]{0:T(1024)} %bitcast.99, s32[8]{0:T(128)} %copy-done.13, bf16[32768,128]{1,0:T(8,128)(2,1)} %volume_ref.1), custom_call_target="tpu_custom_call" | custom-call | bytes 104857600 | tf_op jit(solution)/shard_map/read_voxels/pallas_call | solution.py:621
  66.6 8.2 %all-to-all-start.1 = ((bf16[8,512,128]{2,1,0:T(8,128)(2,1)}), bf16[8,512,128]{2,1,0:T(8,128)(2,1)S(1)}, u32[]{:S(2)}, u32[]{:S(2)}) async-start(bf16[8,512,128]{2,1,0:T(8,128)(2,1)} %get-tuple-element.56), calls=%async_computation.1 | async-start | bytes 2097152 | tf_op jit(solution)/shard_map/all_to_all | solution.py:652
  79.8 28.7 %compare_and_add.4 = (f32[8,8,128]{2,1,0:T(8,128)}, f32[32768,128]{1,0:T(8,128)}) custom-call(s32[8]{0:T(128)} %copy-done.13, f32[64]{0:T(128)} %get-tuple-element.97.defocus_ref, f32[64]{0:T(128)} %get-tuple-element.96.phase_ref, f32[64]{0:T(128)} %mul.17.scale_ref, s32[16384]{0:T(1024)} %bitcast.100, s32[1]{0:T(128)} %bitcast.core_ref, ...), custom_call_target="tpu_custom_call" | custom-call | bytes 16777216 | tf_op jit(solution)/shard_map/compare_and_add/pallas_call | solution.py:654
  108.6 5.1 %all-to-all-start.4 = ((bf16[8,512,128]{2,1,0:T(8,128)(2,1)}), bf16[8,512,128]{2,1,0:T(8,128)(2,1)S(1)}, u32[]{:S(2)}, u32[]{:S(2)}) async-start(bf16[8,512,128]{2,1,0:T(8,128)(2,1)} %get-tuple-element.63), calls=%async_computation.4 | async-start | bytes 2097152 | tf_op jit(solution)/shard_map/all_to_all | solution.py:652
  114.3 28.8 %compare_and_add.5 = (f32[8,8,128]{2,1,0:T(8,128)}, f32[32768,128]{1,0:T(8,128)}) custom-call(s32[8]{0:T(128)} %copy-done.13, f32[64]{0:T(128)} %get-tuple-element.97.defocus_ref, f32[64]{0:T(128)} %get-tuple-element.96.phase_ref, f32[64]{0:T(128)} %mul.17.scale_ref, s32[16384]{0:T(1024)} %bitcast.101, s32[1]{0:T(128)} %bitcast.core_ref, ...), custom_call_target="tpu_custom_call" | custom-call | bytes 16777216 | tf_op jit(solution)/shard_map/compare_and_add/pallas_call | solution.py:654
  143.2 8.4 %all-to-all-start.3 = ((bf16[8,512,128]{2,1,0:T(8,128)(2,1)}), bf16[8,512,128]{2,1,0:T(8,128)(2,1)S(1)}, u32[]{:S(2)}, u32[]{:S(2)}) async-start(bf16[8,512,128]{2,1,0:T(8,128)(2,1)} %get-tuple-element.60), calls=%async_computation.3 | async-start | bytes 2097152 | tf_op jit(solution)/shard_map/all_to_all | solution.py:652
  152.8 19.4 %compare_and_add.6 = (f32[8,8,128]{2,1,0:T(8,128)}, f32[32768,128]{1,0:T(8,128)}) custom-call(s32[8]{0:T(128)} %copy-done.13, f32[64]{0:T(128)} %get-tuple-element.97.defocus_ref, f32[64]{0:T(128)} %get-tuple-element.96.phase_ref, f32[64]{0:T(128)} %mul.17.scale_ref, s32[16384]{0:T(1024)} %bitcast.102, s32[1]{0:T(128)} %bitcast.core_ref, ...), custom_call_target="tpu_custom_call" | custom-call | bytes 16777216 | tf_op jit(solution)/shard_map/compare_and_add/pallas_call | solution.py:654
  175.8 18.1 %compare_and_add.7 = (f32[8,8,128]{2,1,0:T(8,128)}, f32[16384,128]{1,0:T(8,128)}, f32[4096,128]{1,0:T(8,128)}, f32[4096,128]{1,0:T(8,128)}, f32[8192,128]{1,0:T(8,128)}) custom-call(s32[8]{0:T(128)} %copy-done.13, f32[64]{0:T(128)} %get-tuple-element.97.defocus_ref, f32[64]{0:T(128)} %get-tuple-element.96.phase_ref, f32[64]{0:T(128)} %mul.17.scale_ref, ...), custom_call_target="tpu_custom_call" | custom-call | bytes 16777216 | tf_op jit(solution)/shard_map/compare_and_add/pallas_call | solution.py:654
  194.6 6.1 %collective-permute-done.8 = f32[4096,128]{1,0:T(8,128)} collective-permute-done((f32[4096,128]{1,0:T(8,128)}, f32[4096,128]{1,0:T(8,128)}, u32[]{:S(2)}, u32[]{:S(2)}) %collective-permute-start.8) | collective-permute-done | bytes 2097184 | tf_op jit(solution)/shard_map/ppermute | solution.py:489
  200.7 9.6 %transform_planes.4 = (bf16[4,2,32,256]{3,2,1,0:T(8,128)(2,1)}, bf16[4,2,32,256]{3,2,1,0:T(8,128)(2,1)}, bf16[4,2,32,256]{3,2,1,0:T(8,128)(2,1)}, bf16[4,2,32,25...) custom-call(s32[1]{0:T(128)} %bitcast.1.me_ref, ...), custom_call_target="tpu_custom_call" | custom-call | flops 536870912 | bytes 8388608 | tf_op jit(solution)/shard_map/transform_planes/pallas_call | solution.py:505
  210.3 14.9 %collective-permute-start.9 = (bf16[4,2,32,256]{3,2,1,0:T(8,128)(2,1)}, bf16[4,2,32,256]{3,2,1,0:T(8,128)(2,1)S(1)}, u32[]{:S(2)}, u32[]{:S(2)}) collective-permute-start(bf16[4,2,32,256]{3,2,1,0:T(8,128)(2,1)} %get-tuple-element.78), channel_id=1, source_target_pairs={{0,2},{2,0},{4,6},{6,4},{8,10},{10,8},{12,14},{14,12},{1,3},{3,1},... | collective-permute-start | bytes 393224 | tf_op jit(solution)/shard_map/ppermute | solution.py:531
  228.1 9.7 %transform_planes.3 = (bf16[4,2,32,256]{3,2,1,0:T(8,128)(2,1)}, bf16[4,2,32,256]{3,2,1,0:T(8,128)(2,1)}, bf16[4,2,32,256]{3,2,1,0:T(8,128)(2,1)}, bf16[4,2,32,25...) custom-call(s32[1]{0:T(128)} %bitcast.1.me_ref, ...), custom_call_target="tpu_custom_call" | custom-call | flops 536870912 | bytes 8388608 | tf_op jit(solution)/shard_map/transform_planes/pallas_call | solution.py:505
  250.5 4.3 %collective-permute-done.13 = bf16[4,2,32,256]{3,2,1,0:T(8,128)(2,1)S(1)} collective-permute-done((bf16[4,2,32,256]{3,2,1,0:T(8,128)(2,1)S(1)}, bf16[4,2,32,256]{3,2,1,0:T(8,128)(2,1)S(1)}, u32[]{:S(2)}, u32[]{:S(2)}) %collective-permute-start.13) | collective-permute-done | bytes 131104 | tf_op jit(solution)/shard_map/ppermute | solution.py:531
  263.3 17.2 %transform_planes.5 = (bf16[8,2,32,256]{3,2,1,0:T(8,128)(2,1)}, bf16[8,2,32,256]{3,2,1,0:T(8,128)(2,1)}, bf16[8,2,32,256]{3,2,1,0:T(8,128)(2,1)}, bf16[8,2,32,25...) custom-call(s32[1]{0:T(128)} %bitcast.1.me_ref, ...), custom_call_target="tpu_custom_call" | custom-call | flops 1073741824 | bytes 16777216 | tf_op jit(solution)/shard_map/transform_planes/pallas_call | solution.py:505
  291.0 6.8 %collective-permute-done.19 = bf16[8,2,32,256]{3,2,1,0:T(8,128)(2,1)S(1)} collective-permute-done((bf16[8,2,32,256]{3,2,1,0:T(8,128)(2,1)}, bf16[8,2,32,256]{3,2,1,0:T(8,128)(2,1)S(1)}, u32[]{:S(2)}, u32[]{:S(2)}) %collective-permute-start.19) | collective-permute-done | bytes 262176 | tf_op jit(solution)/shard_map/ppermute | solution.py:531
  301.2 12.2 %collective-permute-done.20 = bf16[8,2,32,256]{3,2,1,0:T(8,128)(2,1)S(1)} collective-permute-done((bf16[8,2,32,256]{3,2,1,0:T(8,128)(2,1)}, bf16[8,2,32,256]{3,2,1,0:T(8,128)(2,1)S(1)}, u32[]{:S(2)}, u32[]{:S(2)}) %collective-permute-start.20) | collective-permute-done | bytes 262176 | tf_op jit(solution)/shard_map/ppermute | solution.py:531
  313.4 9.3 %collective-permute-done.21 = bf16[8,2,32,256]{3,2,1,0:T(8,128)(2,1)S(1)} collective-permute-done((bf16[8,2,32,256]{3,2,1,0:T(8,128)(2,1)}, bf16[8,2,32,256]{3,2,1,0:T(8,128)(2,1)S(1)}, u32[]{:S(2)}, u32[]{:S(2)}) %collective-permute-start.21) | collective-permute-done | bytes 262176 | tf_op jit(solution)/shard_map/ppermute | solution.py:531
  322.8 3.8 collective-permute-start.6
  326.7 6.0 %collective-permute-done.23 = bf16[8,2,32,256]{3,2,1,0:T(8,128)(2,1)S(1)} collective-permute-done((bf16[8,2,32,256]{3,2,1,0:T(8,128)(2,1)S(1)}, bf16[8,2,32,256]{3,2,1,0:T(8,128)(2,1)S(1)}, u32[]{:S(2)}, u32[]{:S(2)}) %collective-permute-start.23) | collective-permute-done | bytes 262176 | tf_op jit(solution)/shard_map/ppermute | solution.py:531
  335.5 5.0 %collective-permute-done.7 = bf16[4,2,32,256]{3,2,1,0:T(8,128)(2,1)S(1)} collective-permute-done((bf16[4,2,32,256]{3,2,1,0:T(8,128)(2,1)S(1)}, bf16[4,2,32,256]{3,2,1,0:T(8,128)(2,1)S(1)}, u32[]{:S(2)}, u32[]{:S(2)}) %collective-permute-start.7) | collective-permute-done | bytes 131104 | tf_op jit(solution)/shard_map/ppermute | solution.py:531
  341.5 38.3 %all-gather = f32[64,8]{1,0:T(8,128)S(1)} all-gather(f32[8,8]{1,0:T(8,128)S(1)} %add_reduce_fusion), channel_id=2, replica_groups=mesh['groups'=2,'slab'=8,'dom'=2] {'slab'}, dimensions={0}, use_global_device_ids=true | all-gather | bytes 2304 | tf_op jit(solution)/shard_map/all_gather | solution.py:686
  380.4 13.1 %transform_first.1 = f32[2,128,32,256]{3,2,1,0:T(8,128)} custom-call(s32[2]{0:T(128)} %pad_add_fusion.core_ref, bf16[8,4,2,32,256]{4,3,2,1,0:T(8,128)(2,1)} %copy-done.6, bf16[8,4,2,32,256]{4,3,2,1,0:T(8,128)(2,1)} %bitcast_dynamic-update-slice_fusion.8.refs_1_, bf16[8,8,2,32,256]{4,3,2,1,0:T(8,128)(2,1)} %copy-done.4, ...), custom_call_target="tpu_custom_call" | custom-call | tf_op jit(solution)/shard_map/transform_first/pallas_call | solution.py:539
  (170 shorter events, 70.9 us)
Async XLA Ops:
  39.1 27.5 %all-to-all-start.2 = ((bf16[8,512,128]{2,1,0:T(8,128)(2,1)}), bf16[8,512,128]{2,1,0:T(8,128)(2,1)S(1)}, u32[]{:S(2)}, u32[]{:S(2)}) async-start(bf16[8,512,128]{2,1,0:T(8,128)(2,1)} %get-tuple-element.57), calls=%async_computation.2 | async-start | bytes 2097152 | tf_op jit(solution)/shard_map/all_to_all | solution.py:652
  66.6 41.9 %all-to-all-start.1 = ((bf16[8,512,128]{2,1,0:T(8,128)(2,1)}), bf16[8,512,128]{2,1,0:T(8,128)(2,1)S(1)}, u32[]{:S(2)}, u32[]{:S(2)}) async-start(bf16[8,512,128]{2,1,0:T(8,128)(2,1)} %get-tuple-element.56), calls=%async_computation.1 | async-start | bytes 2097152 | tf_op jit(solution)/shard_map/all_to_all | solution.py:652
  108.6 34.6 %all-to-all-start.4 = ((bf16[8,512,128]{2,1,0:T(8,128)(2,1)}), bf16[8,512,128]{2,1,0:T(8,128)(2,1)S(1)}, u32[]{:S(2)}, u32[]{:S(2)}) async-start(bf16[8,512,128]{2,1,0:T(8,128)(2,1)} %get-tuple-element.63), calls=%async_computation.4 | async-start | bytes 2097152 | tf_op jit(solution)/shard_map/all_to_all | solution.py:652
  143.2 31.7 %all-to-all-start.3 = ((bf16[8,512,128]{2,1,0:T(8,128)(2,1)}), bf16[8,512,128]{2,1,0:T(8,128)(2,1)S(1)}, u32[]{:S(2)}, u32[]{:S(2)}) async-start(bf16[8,512,128]{2,1,0:T(8,128)(2,1)} %get-tuple-element.60), calls=%async_computation.3 | async-start | bytes 2097152 | tf_op jit(solution)/shard_map/all_to_all | solution.py:652
  194.0 32.8 %collective-permute-start = (f32[4096,128]{1,0:T(8,128)}, f32[4096,128]{1,0:T(8,128)S(1)}, u32[]{:S(2)}, u32[]{:S(2)}) collective-permute-start(f32[4096,128]{1,0:T(8,128)} %get-tuple-element.67), channel_id=1, source_target_pairs={{0,1},{1,0},{2,3},{3,2},{4,5},{5,4},{6,7},{7,6},{8,9},{9,8},{10,11... | collective-permute-start | bytes 6291464 | tf_op jit(solution)/shard_map/ppermute | solution.py:489
  194.5 68.8 %collective-permute-start.16 = (f32[8192,128]{1,0:T(8,128)}, f32[8192,128]{1,0:T(8,128)}, u32[]{:S(2)}, u32[]{:S(2)}) collective-permute-start(f32[8192,128]{1,0:T(8,128)} %get-tuple-element.85), channel_id=1, source_target_pairs={{0,1},{1,0},{2,3},{3,2},{4,5},{5,4},{6,7},{7,6},{8,9},{9,8},{10,11... | collective-permute-start | bytes 12582920 | tf_op jit(solution)/shard_map/ppermute | solution.py:489
  210.3 29.2 %collective-permute-start.9 = (bf16[4,2,32,256]{3,2,1,0:T(8,128)(2,1)}, bf16[4,2,32,256]{3,2,1,0:T(8,128)(2,1)S(1)}, u32[]{:S(2)}, u32[]{:S(2)}) collective-permute-start(bf16[4,2,32,256]{3,2,1,0:T(8,128)(2,1)} %get-tuple-element.78), channel_id=1, source_target_pairs={{0,2},{2,0},{4,6},{6,4},{8,10},{10,8},{12,14},{14,12},{1,3},{3,1},... | collective-permute-start | bytes 393224 | tf_op jit(solution)/shard_map/ppermute | solution.py:531
  225.2 18.0 %collective-permute-start.10 = (bf16[4,2,32,256]{3,2,1,0:T(8,128)(2,1)}, bf16[4,2,32,256]{3,2,1,0:T(8,128)(2,1)S(1)}, u32[]{:S(2)}, u32[]{:S(2)}) collective-permute-start(bf16[4,2,32,256]{3,2,1,0:T(8,128)(2,1)} %get-tuple-element.79), channel_id=1, source_target_pairs={{0,4},{2,6},{4,0},{6,2},{8,12},{10,14},{12,8},{14,10},{1,5},{3,7},... | collective-permute-start | bytes 393224 | tf_op jit(solution)/shard_map/ppermute | solution.py:531
  225.2 19.4 %collective-permute-start.11 = (bf16[4,2,32,256]{3,2,1,0:T(8,128)(2,1)}, bf16[4,2,32,256]{3,2,1,0:T(8,128)(2,1)S(1)}, u32[]{:S(2)}, u32[]{:S(2)}) collective-permute-start(bf16[4,2,32,256]{3,2,1,0:T(8,128)(2,1)} %get-tuple-element.80), channel_id=1, source_target_pairs={{0,6},{2,4},{4,2},{6,0},{8,14},{10,12},{12,10},{14,8},{1,7},{3,5},... | collective-permute-start | bytes 393224 | tf_op jit(solution)/shard_map/ppermute | solution.py:531
  226.8 21.1 %collective-permute-start.12 = (bf16[4,2,32,256]{3,2,1,0:T(8,128)(2,1)}, bf16[4,2,32,256]{3,2,1,0:T(8,128)(2,1)S(1)}, u32[]{:S(2)}, u32[]{:S(2)}) collective-permute-start(bf16[4,2,32,256]{3,2,1,0:T(8,128)(2,1)} %get-tuple-element.81), channel_id=1, source_target_pairs={{0,8},{2,10},{4,12},{6,14},{8,0},{10,2},{12,4},{14,6},{1,9},{3,11}... | collective-permute-start | bytes 393224 | tf_op jit(solution)/shard_map/ppermute | solution.py:531
  239.5 15.3 %collective-permute-start.13 = (bf16[4,2,32,256]{3,2,1,0:T(8,128)(2,1)S(1)}, bf16[4,2,32,256]{3,2,1,0:T(8,128)(2,1)S(1)}, u32[]{:S(2)}, u32[]{:S(2)}) collective-permute-start(bf16[4,2,32,256]{3,2,1,0:T(8,128)(2,1)S(1)} %copy-done.25), channel_id=1, source_target_pairs={{0,10},{2,8},{4,14},{6,12},{8,2},{10,0},{12,6},{14,4},{1,11},{3,9}... | collective-permute-start | bytes 393224 | tf_op jit(solution)/shard_map/ppermute | solution.py:531
  243.2 12.2 %collective-permute-start.14 = (bf16[4,2,32,256]{3,2,1,0:T(8,128)(2,1)S(1)}, bf16[4,2,32,256]{3,2,1,0:T(8,128)(2,1)S(1)}, u32[]{:S(2)}, u32[]{:S(2)}) collective-permute-start(bf16[4,2,32,256]{3,2,1,0:T(8,128)(2,1)S(1)} %copy-done.24), channel_id=1, source_target_pairs={{0,12},{2,14},{4,8},{6,10},{8,4},{10,6},{12,0},{14,2},{1,13},{3,15... | collective-permute-start | bytes 393224 | tf_op jit(solution)/shard_map/ppermute | solution.py:531
  244.7 14.4 %collective-permute-start.15 = (bf16[4,2,32,256]{3,2,1,0:T(8,128)(2,1)S(1)}, bf16[4,2,32,256]{3,2,1,0:T(8,128)(2,1)S(1)}, u32[]{:S(2)}, u32[]{:S(2)}) collective-permute-start(bf16[4,2,32,256]{3,2,1,0:T(8,128)(2,1)S(1)} %copy-done.23), channel_id=1, source_target_pairs={{0,14},{2,12},{4,10},{6,8},{8,6},{10,4},{12,2},{14,0},{1,15},{3,13... | collective-permute-start | bytes 393224 | tf_op jit(solution)/shard_map/ppermute | solution.py:531
  247.9 13.6 %collective-permute-start.1 = (bf16[4,2,32,256]{3,2,1,0:T(8,128)(2,1)}, bf16[4,2,32,256]{3,2,1,0:T(8,128)(2,1)S(1)}, u32[]{:S(2)}, u32[]{:S(2)}) collective-permute-start(bf16[4,2,32,256]{3,2,1,0:T(8,128)(2,1)} %get-tuple-element.69), channel_id=1, source_target_pairs={{0,2},{2,0},{4,6},{6,4},{8,10},{10,8},{12,14},{14,12},{1,3},{3,1},... | collective-permute-start | bytes 393224 | tf_op jit(solution)/shard_map/ppermute | solution.py:531
  254.8 26.6 %collective-permute-start.2 = (bf16[4,2,32,256]{3,2,1,0:T(8,128)(2,1)}, bf16[4,2,32,256]{3,2,1,0:T(8,128)(2,1)S(1)}, u32[]{:S(2)}, u32[]{:S(2)}) collective-permute-start(bf16[4,2,32,256]{3,2,1,0:T(8,128)(2,1)} %get-tuple-element.70), channel_id=1, source_target_pairs={{0,4},{2,6},{4,0},{6,2},{8,12},{10,14},{12,8},{14,10},{1,5},{3,7},... | collective-permute-start | bytes 393224 | tf_op jit(solution)/shard_map/ppermute | solution.py:531
  255.5 79.3 %collective-permute-start.3 = (bf16[4,2,32,256]{3,2,1,0:T(8,128)(2,1)}, bf16[4,2,32,256]{3,2,1,0:T(8,128)(2,1)S(1)}, u32[]{:S(2)}, u32[]{:S(2)}) collective-permute-start(bf16[4,2,32,256]{3,2,1,0:T(8,128)(2,1)} %get-tuple-element.71), channel_id=1, source_target_pairs={{0,6},{2,4},{4,2},{6,0},{8,14},{10,12},{12,10},{14,8},{1,7},{3,5},... | collective-permute-start | bytes 393224 | tf_op jit(solution)/shard_map/ppermute | solution.py:531
  259.1 75.8 %collective-permute-start.4 = (bf16[4,2,32,256]{3,2,1,0:T(8,128)(2,1)S(1)}, bf16[4,2,32,256]{3,2,1,0:T(8,128)(2,1)S(1)}, u32[]{:S(2)}, u32[]{:S(2)}) collective-permute-start(bf16[4,2,32,256]{3,2,1,0:T(8,128)(2,1)S(1)} %copy-done.22), channel_id=1, source_target_pairs={{0,8},{2,10},{4,12},{6,14},{8,0},{10,2},{12,4},{14,6},{1,9},{3,11}... | collective-permute-start | bytes 393224 | tf_op jit(solution)/shard_map/ppermute | solution.py:531
  261.5 73.9 %collective-permute-start.5 = (bf16[4,2,32,256]{3,2,1,0:T(8,128)(2,1)S(1)}, bf16[4,2,32,256]{3,2,1,0:T(8,128)(2,1)S(1)}, u32[]{:S(2)}, u32[]{:S(2)}) collective-permute-start(bf16[4,2,32,256]{3,2,1,0:T(8,128)(2,1)S(1)} %copy-done.21), channel_id=1, source_target_pairs={{0,10},{2,8},{4,14},{6,12},{8,2},{10,0},{12,6},{14,4},{1,11},{3,9}... | collective-permute-start | bytes 393224 | tf_op jit(solution)/shard_map/ppermute | solution.py:531
  290.6 22.8 %collective-permute-start.20 = (bf16[8,2,32,256]{3,2,1,0:T(8,128)(2,1)}, bf16[8,2,32,256]{3,2,1,0:T(8,128)(2,1)S(1)}, u32[]{:S(2)}, u32[]{:S(2)}) collective-permute-start(bf16[8,2,32,256]{3,2,1,0:T(8,128)(2,1)} %get-tuple-element.90), channel_id=1, source_target_pairs={{0,8},{2,10},{4,12},{6,14},{8,0},{10,2},{12,4},{14,6},{1,9},{3,11}... | collective-permute-start | bytes 786440 | tf_op jit(solution)/shard_map/ppermute | solution.py:531
  297.8 25.0 %collective-permute-start.21 = (bf16[8,2,32,256]{3,2,1,0:T(8,128)(2,1)}, bf16[8,2,32,256]{3,2,1,0:T(8,128)(2,1)S(1)}, u32[]{:S(2)}, u32[]{:S(2)}) collective-permute-start(bf16[8,2,32,256]{3,2,1,0:T(8,128)(2,1)} %get-tuple-element.91), channel_id=1, source_target_pairs={{0,10},{2,8},{4,14},{6,12},{8,2},{10,0},{12,6},{14,4},{1,11},{3,9}... | collective-permute-start | bytes 786440 | tf_op jit(solution)/shard_map/ppermute | solution.py:531
  322.8 12.6 %collective-permute-start.6 = (bf16[4,2,32,256]{3,2,1,0:T(8,128)(2,1)S(1)}, bf16[4,2,32,256]{3,2,1,0:T(8,128)(2,1)S(1)}, u32[]{:S(2)}, u32[]{:S(2)}) collective-permute-start(bf16[4,2,32,256]{3,2,1,0:T(8,128)(2,1)S(1)} %copy-done.20), channel_id=1, source_target_pairs={{0,12},{2,14},{4,8},{6,10},{8,4},{10,6},{12,0},{14,2},{1,13},{3,15... | collective-permute-start | bytes 393224 | tf_op jit(solution)/shard_map/ppermute | solution.py:531
  334.8 45.6 %collective-permute-start.26 = (bf16[8,8,2,32,256]{4,3,2,1,0:T(8,128)(2,1)S(1)}, bf16[8,8,2,32,256]{4,3,2,1,0:T(8,128)(2,1)}, u32[]{:S(2)}, u32[]{:S(2)}) collective-permute-start(bf16[8,8,2,32,256]{4,3,2,1,0:T(8,128)(2,1)S(1)} %bitcast_dynamic-update-slice_fusion.refs_2_), channel_id=1, source_target_pairs={{0,1},{1,0},{2,3},{3,2},{4,5},{5,4},{6,7},{7,6},{8,9},{9,8},{10,11... | collective-permute-start | bytes 6291464 | tf_op jit(solution)/shard_map/ppermute | solution.py:536
  334.9 45.5 %collective-permute-start.25 = (bf16[8,4,2,32,256]{4,3,2,1,0:T(8,128)(2,1)}, bf16[8,4,2,32,256]{4,3,2,1,0:T(8,128)(2,1)}, u32[]{:S(2)}, u32[]{:S(2)}) collective-permute-start(bf16[8,4,2,32,256]{4,3,2,1,0:T(8,128)(2,1)} %bitcast_dynamic-update-slice_fusion.8.refs_1_), channel_id=1, source_target_pairs={{0,1},{1,0},{2,3},{3,2},{4,5},{5,4},{6,7},{7,6},{8,9},{9,8},{10,11... | collective-permute-start | bytes 3145736 | tf_op jit(solution)/shard_map/ppermute | solution.py:536
  340.5 39.9 %collective-permute-start.24 = (bf16[8,4,2,32,256]{4,3,2,1,0:T(8,128)(2,1)S(1)}, bf16[8,4,2,32,256]{4,3,2,1,0:T(8,128)(2,1)}, u32[]{:S(2)}, u32[]{:S(2)}) collective-permute-start(bf16[8,4,2,32,256]{4,3,2,1,0:T(8,128)(2,1)S(1)} %bitcast_dynamic-update-slice_fusion.16.refs_0_), channel_id=1, source_target_pairs={{0,1},{1,0},{2,3},{3,2},{4,5},{5,4},{6,7},{7,6},{8,9},{9,8},{10,11... | collective-permute-start | bytes 3145736 | tf_op jit(solution)/shard_map/ppermute | solution.py:536
  (35 other events, 824.6 us)

commit v5 on v3

--- a/solution.py
+++ b/solution.py
@@ -67,19 +67,7 @@
     word_ref[...] = word | (particle << (kind_bits + 2 + bits_of(list_length)))
 
 
-def pack_words_kernel(list_length, target_ref, word_ref, counts_ref, meta_ref):
-    @pl.loop(0, counts_ref.shape[0])
-    def _(particle):
-        @pl.loop(0, (counts_ref[particle] + 15) // 16)
-        def _(i):
-            first = particle * list_length + i * 16
-            targets = [target_ref[first + j] for j in range(16)]
-            words = [word_ref[first + j] for j in range(16)]
-            for j in range(16):
-                meta_ref[targets[j]] = words[j]
-
-
-def pack_images_kernel(slabs, cap, list_length, target_ref, counts_ref, image_ref, *refs):
+def pack_kernel(slabs, cap, list_length, target_ref, word_ref, counts_ref, image_ref, meta_ref, *refs):
     out_refs, (wide_ref, staged_ref) = refs[:-2], refs[-2:]
     step = 256
 
@@ -95,8 +83,10 @@
             first = particle * list_length + i * 16
             targets = [target_ref[first + j] for j in range(16)]
             rows = [wide_ref[pl.ds(first + j, 1), :] for j in range(16)]
+            words = [word_ref[first + j] for j in range(16)]
             for j in range(16):
                 staged_ref[pl.ds(targets[j], 1), :] = rows[j]
+                meta_ref[targets[j]] = words[j]
 
     for chunk, out_ref in enumerate(out_refs):
         width = out_ref.shape[1]
@@ -124,7 +114,8 @@
     index_ref[...] = index | (clash << 24)
 
 
-def gather_kernel(slabs, cap, index_ref, totals_ref, volume_ref, out_ref, wide_ref, staged_ref):
+def gather_kernel(slabs, cap, index_ref, totals_ref, volume_ref, *refs):
+    out_refs, (wide_ref, staged_ref) = refs[:-2], refs[-2:]
     blocks = volume_ref.shape[0]
     step = 256
 
@@ -145,13 +136,12 @@
             for j in range(16):
                 staged_ref[pl.ds(i * 16 + j, 1), :] = rows[j]
 
-        width = min(step, cap)
-
-        @pl.loop(0, (live + width - 1) // width)
-        def _(i):
-            at = pl.multiple_of(i * width, width)
-            to = pl.multiple_of(source * cap + i * width, width)
-            out_ref[pl.ds(to, width), :] = staged_ref[pl.ds(at, width), :].astype(jnp.bfloat16)
+        for chunk, out_ref in enumerate(out_refs):
+            width = out_ref.shape[1]
+
+            @pl.when(live > chunk * width)
+            def _():
+                out_ref[source] = staged_ref[chunk * width:(chunk + 1) * width, :].astype(jnp.bfloat16)
 
 
 def sine(angle):
@@ -175,117 +165,106 @@
     word_ref, voxel_ref, image_ref, forward_ref, backward_ref, unit_ref, *rest,
 ):
     if not first:
-        before_ref, rest = rest[0], rest[1:]
-    square_ref, sum_refs, (sum_ref, staged_ref, sems) = rest[0], rest[1:-3], rest[-3:]
-    source = pl.program_id(0)
-    tile = word_ref.shape[2]
+        rest = rest[1:]
+    square_ref, sum_ref, out_refs, (staged_ref, sems) = rest[0], rest[1], rest[2:-2], rest[-2:]
+    slabs, _, tile = word_ref.shape
     blocks = sum_ref.shape[0] - 8
     features = image_ref.shape[2]
     kinds = forward_ref.shape[0] // features
     position_bits = bits_of(list_length)
     per_row = side // 8
-    live = jnp.clip(totals_ref[source] - offset, 0, tile)
-
-    @pl.when(source == 0)
-    def _():
-        if first:
-            @pl.loop(0, blocks // 256)
-            def _(i):
-                at = pl.multiple_of(i * 256, 256)
-                sum_ref[pl.ds(at, 256), :] = jnp.zeros((256, features), jnp.float32)
-        else:
-            pltpu.make_async_copy(before_ref, sum_ref.at[pl.ds(0, blocks)], sems.at[0]).start()
-
-    @pl.when(live == 0)
-    def _():
-        square_ref[...] = jnp.zeros_like(square_ref)
-
-    @pl.when(live > 0)
-    def _():
-        word = word_ref[0]
-        kind = (word >> local_bits) & 3
-        position = (word >> (local_bits + 2)) & (list_length - 1)
-        particle = (word >> (local_bits + 2 + position_bits)) & (particles - 1)
-        valid = lax.broadcasted_iota(jnp.int32, (1, tile), 1) < live
-        defocus = jnp.zeros((1, tile), jnp.float32)
-        phase = jnp.zeros((1, tile), jnp.float32)
-        scale = jnp.zeros((1, tile), jnp.float32)
-        for j in range(particles):
-            chosen = particle == j
-            defocus = jnp.where(chosen, defocus_ref[source * particles + j], defocus)
-            phase = jnp.where(chosen, phase_ref[source * particles + j], phase)
-            scale = jnp.where(chosen, scale_ref[source * particles + j], scale)
-        half = features // 2
-        cell = lax.broadcasted_iota(jnp.int32, (half, tile), 0)
-        vert = ((position // per_row) * 8 - side // 2 + cell // 8).astype(jnp.float32)
-        horiz = ((position % per_row) * 8 - side // 2 + cell % 8).astype(jnp.float32)
-        radius = (vert * vert + horiz * horiz) * (1.0 / float((side // 2) ** 2))
-        factor = scale * sine(defocus * radius + phase)
-        factor = jnp.concatenate([factor, factor], axis=0)
-        contract_last = (((1,), (1,)), ((), ()))
-        each_kind = lax.dot_general(
-            forward_ref[...], voxel_ref[0], contract_last, preferred_element_type=jnp.float32
-        )
-        extracted = each_kind[0:features, :]
-        for k in range(1, kinds):
-            extracted = jnp.where(kind == k, each_kind[k * features:(k + 1) * features, :], extracted)
-        picture = lax.dot_general(
-            unit_ref[...], image_ref[0], contract_last, preferred_element_type=jnp.float32
-        )
-        misfit = jnp.where(valid, factor * extracted - picture, 0.0)
-        squares = jnp.sum(misfit * misfit, axis=0, keepdims=True)
-        which = lax.broadcasted_iota(jnp.int32, (particles, tile), 0)
-        spread = jnp.where(valid & (particle == which), squares, 0.0)
-        folded = spread[:, 0:LANES]
-        for i in range(1, tile // LANES):
-            folded = folded + spread[:, i * LANES:(i + 1) * LANES]
-        square_ref[0] = folded
-        weighted = (factor * misfit).astype(jnp.bfloat16)
-        none = jnp.zeros_like(weighted)
-        spread_back = jnp.concatenate(
-            [jnp.where(kind == k, weighted, none) for k in range(kinds)], axis=0
-        )
-        terms = jnp.dot(backward_ref[...], spread_back, preferred_element_type=jnp.float32)
-        staged_ref[...] = terms.T
-
-    if not first:
-        @pl.when(source == 0)
+
+    if first:
+        @pl.loop(0, blocks // 256)
+        def _(i):
+            at = pl.multiple_of(i * 256, 256)
+            sum_ref[pl.ds(at, 256), :] = jnp.zeros((256, features), jnp.float32)
+
+    @pl.loop(0, slabs)
+    def _(source):
+        live = jnp.clip(totals_ref[source] - offset, 0, tile)
+
+        @pl.when(live == 0)
         def _():
-            pltpu.make_async_copy(before_ref, sum_ref.at[pl.ds(0, blocks)], sems.at[0]).wait()
-
-    @pl.loop(0, (live + GROUP - 1) // GROUP)
-    def _(g):
-        base = source * cap + offset + g * GROUP
-        marked = index_ref[base]
-        places = [index_ref[base + j] & 0xFFFFFF for j in range(GROUP)]
-
-        @pl.when(marked < (1 << 24))
+            square_ref[source] = jnp.zeros((particles, LANES), jnp.float32)
+
+        @pl.when(live > 0)
         def _():
-            held = [sum_ref[pl.ds(places[j], 1), :] for j in range(GROUP)]
-            new = [staged_ref[pl.ds(g * GROUP + j, 1), :] for j in range(GROUP)]
-            for j in range(GROUP):
-                sum_ref[pl.ds(places[j], 1), :] = held[j] + new[j]
-
-        @pl.when(marked >= (1 << 24))
-        def _():
-            for j in range(GROUP):
-                sum_ref[pl.ds(places[j], 1), :] = (
-                    sum_ref[pl.ds(places[j], 1), :] + staged_ref[pl.ds(g * GROUP + j, 1), :]
-                )
-
-    @pl.when(source == pl.num_programs(0) - 1)
-    def _():
+            word = word_ref[source]
+            kind = (word >> local_bits) & 3
+            position = (word >> (local_bits + 2)) & (list_length - 1)
+            particle = (word >> (local_bits + 2 + position_bits)) & (particles - 1)
+            valid = lax.broadcasted_iota(jnp.int32, (1, tile), 1) < live
+            defocus = jnp.zeros((1, tile), jnp.float32)
+            phase = jnp.zeros((1, tile), jnp.float32)
+            scale = jnp.zeros((1, tile), jnp.float32)
+            for j in range(particles):
+                chosen = particle == j
+                defocus = jnp.where(chosen, defocus_ref[source * particles + j], defocus)
+                phase = jnp.where(chosen, phase_ref[source * particles + j], phase)
+                scale = jnp.where(chosen, scale_ref[source * particles + j], scale)
+            half = features // 2
+            cell = lax.broadcasted_iota(jnp.int32, (half, tile), 0)
+            vert = ((position // per_row) * 8 - side // 2 + cell // 8).astype(jnp.float32)
+            horiz = ((position % per_row) * 8 - side // 2 + cell % 8).astype(jnp.float32)
+            radius = (vert * vert + horiz * horiz) * (1.0 / float((side // 2) ** 2))
+            factor = scale * sine(defocus * radius + phase)
+            factor = jnp.concatenate([factor, factor], axis=0)
+            contract_last = (((1,), (1,)), ((), ()))
+            each_kind = lax.dot_general(
+                forward_ref[...], voxel_ref[source], contract_last, preferred_element_type=jnp.float32
+            )
+            extracted = each_kind[0:features, :]
+            for k in range(1, kinds):
+                extracted = jnp.where(kind == k, each_kind[k * features:(k + 1) * features, :], extracted)
+            picture = lax.dot_general(
+                unit_ref[...], image_ref[source], contract_last, preferred_element_type=jnp.float32
+            )
+            misfit = jnp.where(valid, factor * extracted - picture, 0.0)
+            squares = jnp.sum(misfit * misfit, axis=0, keepdims=True)
+            which = lax.broadcasted_iota(jnp.int32, (particles, tile), 0)
+            spread = jnp.where(valid & (particle == which), squares, 0.0)
+            folded = spread[:, 0:LANES]
+            for i in range(1, tile // LANES):
+                folded = folded + spread[:, i * LANES:(i + 1) * LANES]
+            square_ref[source] = folded
+            weighted = (factor * misfit).astype(jnp.bfloat16)
+            none = jnp.zeros_like(weighted)
+            spread_back = jnp.concatenate(
+                [jnp.where(kind == k, weighted, none) for k in range(kinds)], axis=0
+            )
+            terms = jnp.dot(backward_ref[...], spread_back, preferred_element_type=jnp.float32)
+            staged_ref[...] = terms.T
+
+        @pl.loop(0, (live + GROUP - 1) // GROUP)
+        def _(g):
+            base = source * cap + offset + g * GROUP
+            marked = index_ref[base]
+            places = [index_ref[base + j] & 0xFFFFFF for j in range(GROUP)]
+
+            @pl.when(marked < (1 << 24))
+            def _():
+                held = [sum_ref[pl.ds(places[j], 1), :] for j in range(GROUP)]
+                new = [staged_ref[pl.ds(g * GROUP + j, 1), :] for j in range(GROUP)]
+                for j in range(GROUP):
+                    sum_ref[pl.ds(places[j], 1), :] = held[j] + new[j]
+
+            @pl.when(marked >= (1 << 24))
+            def _():
+                for j in range(GROUP):
+                    sum_ref[pl.ds(places[j], 1), :] = (
+                        sum_ref[pl.ds(places[j], 1), :] + staged_ref[pl.ds(g * GROUP + j, 1), :]
+                    )
+
+    if last:
+        half = blocks // 2
+        start = (1 - core_ref[0]) * half
+        places = [core_ref[0] * half]
+        for out_ref in out_refs[1:]:
+            places.append(start)
+            start = start + out_ref.shape[0]
         copies = []
-        if last:
-            half = blocks // 2
-            start = (1 - core_ref[0]) * half
-            places = [core_ref[0] * half]
-            for out_ref in sum_refs[1:]:
-                places.append(start)
-                start = start + out_ref.shape[0]
-        else:
-            places = [0]
-        for i, (place, out_ref) in enumerate(zip(places, sum_refs)):
+        for i, (place, out_ref) in enumerate(zip(places, out_refs)):
             length = out_ref.shape[0]
             at = pl.multiple_of(place, 8)
             copies.append(pltpu.make_async_copy(sum_ref.at[pl.ds(at, length)], out_ref, sems.at[i]))
@@ -298,7 +277,7 @@
 def pieces_of(planes):
     if planes < 16:
         return [planes]
-    return [4, 4, planes - 8]
+    return [4, planes - 4]
 
 
 def rotated(value, turn, length):
@@ -455,7 +434,7 @@
     return (zblock, turns) + host_halves(matrix)
 
 
-def to_field(mine, theirs_sent, side):
+def to_field(mine, theirs_sent, losses, side):
     slabs = lax.axis_size("slab")
     per_row = side // 8
     each = side // slabs // 2
@@ -471,6 +450,7 @@
         mine = jnp.pad(mine, ((0, short), (0, 0), (0, 0), (0, 0)))
     yblocks = 8
     own, other = [], []
+    theirs[-1], losses = lax.optimization_barrier((theirs[-1], losses))
     first_quad = 0
     for real_planes, added in zip(pieces_of(each), theirs):
         added = added.reshape(grid_shape)
@@ -506,7 +486,7 @@
         other.append(lax.ppermute(got, "dom", swap))
     rows = min(16, height)
     arrays = own + other
-    return pl.pallas_call(
+    field = pl.pallas_call(
         functools.partial(first_dimension_kernel, slabs, each),
         grid=(height // rows, side // LANES),
         out_shape=jax.ShapeDtypeStruct((2, side // 2, height, side), jnp.float32),
@@ -519,6 +499,7 @@
         compiler_params=params(),
         name="transform_first",
     )(lax.axis_index("dom").astype(jnp.int32).reshape(1), *arrays)
+    return field, losses
 
 
 def gradient_of_slab(volume, kernels, images, owners, local_block, kinds, counts, ctf_code, ctf_table, scales):
@@ -545,29 +526,21 @@
         owners.reshape(rows, LANES), local_block.reshape(rows, LANES), kinds.reshape(rows, LANES), counts
     )
     target, word = target.reshape(entries), word.reshape(entries)
-    meta = pl.pallas_call(
-        functools.partial(pack_words_kernel, list_length),
-        out_shape=jax.ShapeDtypeStruct((slots + 1024,), jnp.int32),
-        in_specs=[SMEM_SPEC, SMEM_SPEC, SMEM_SPEC],
-        out_specs=SMEM_SPEC,
-        compiler_params=params(),
-        name="pack_words",
-    )(target, word, counts)
     parts = max(1, cap // TILE)
     tile = cap // parts
-    packed = pl.pallas_call(
-        functools.partial(pack_images_kernel, slabs, cap, list_length),
-        out_shape=(jax.ShapeDtypeStruct((slabs, tile, features), jnp.bfloat16),) * parts,
-        in_specs=[SMEM_SPEC, SMEM_SPEC, VMEM_SPEC],
-        out_specs=(VMEM_SPEC,) * parts,
+    meta, *packed = pl.pallas_call(
+        functools.partial(pack_kernel, slabs, cap, list_length),
+        out_shape=(jax.ShapeDtypeStruct((slots + 1024,), jnp.int32),)
+        + (jax.ShapeDtypeStruct((slabs, tile, features), jnp.bfloat16),) * parts,
+        in_specs=[SMEM_SPEC, SMEM_SPEC, SMEM_SPEC, VMEM_SPEC],
+        out_specs=(SMEM_SPEC,) + (VMEM_SPEC,) * parts,
         scratch_shapes=[
             pltpu.VMEM((entries, features), jnp.float32),
             pltpu.VMEM((slots + 8, features), jnp.float32),
         ],
         compiler_params=params(),
-        cost_estimate=pl.CostEstimate(flops=0, bytes_accessed=50 * 1024 * 1024, transcendentals=0),
-        name="pack_images",
-    )(target, counts, images.reshape(entries, features))
+        name="pack",
+    )(target, word, counts, images.reshape(entries, features))
 
     code = ctf_code | ((scales.astype(jnp.float32) * 256.0).astype(jnp.int32) << 8)
     header = jnp.concatenate(
@@ -596,11 +569,11 @@
         name="decode",
     )(words.reshape(slots // LANES, LANES), live.reshape(slots // LANES, LANES))
     index = index.reshape(slots)
-    voxels = pl.pallas_call(
+    voxels = list(pl.pallas_call(
         functools.partial(gather_kernel, slabs, cap),
-        out_shape=jax.ShapeDtypeStruct((slots, features), jnp.bfloat16),
+        out_shape=(jax.ShapeDtypeStruct((slabs, tile, features), jnp.bfloat16),) * parts,
         in_specs=[SMEM_SPEC, SMEM_SPEC, VMEM_SPEC],
-        out_specs=VMEM_SPEC,
+        out_specs=(VMEM_SPEC,) * parts,
         scratch_shapes=[
             pltpu.VMEM((blocks + 8, features), jnp.float32),
             pltpu.VMEM((cap, features), jnp.float32),
@@ -608,56 +581,56 @@
         compiler_params=params(),
         cost_estimate=pl.CostEstimate(flops=0, bytes_accessed=100 * 1024 * 1024, transcendentals=0),
         name="read_voxels",
-    )(index, totals_in, volume)
+    )(index, totals_in, volume))
 
     forward = jnp.transpose(kernels, (0, 2, 1)).reshape(kind_count * features, features)
     backward = kernels.reshape(kind_count, 2, 8, 8, features).transpose(3, 1, 2, 0, 4)
     backward = backward.reshape(features, kind_count * features)
     unit = jnp.eye(features, dtype=jnp.bfloat16)
-    per_source = lambda length, width, at=0: pl.BlockSpec((1, length, width), lambda s: (s, at, 0))
-    whole = lambda table: pl.BlockSpec(table.shape, lambda s: (0,) * table.ndim)
-    voxels = voxels.reshape(slabs, cap, features)
     core = lax.axis_index("dom").astype(jnp.int32).reshape(1)
     plane_blocks = (side // 8) ** 2
     pieces = [planes * plane_blocks for planes in pieces_of(side // slabs // 2)]
-    squares, sums = 0.0, ()
+    squares, sums, behind = 0.0, None, [voxels[0]]
     for part in range(parts):
         first, last = part == 0, part == parts - 1
+        if not first:
+            packed[part], earlier = lax.optimization_barrier((packed[part], behind[part - 1]))
+            if part == 1:
+                voxels[0] = earlier
         picture = lax.all_to_all(packed[part], "slab", split_axis=0, concat_axis=0, tiled=True)
-        lengths = [blocks // 2] + pieces if last else [blocks]
-        more, *sums = pl.pallas_call(
+        lengths = [blocks // 2] + pieces if last else []
+        arguments = [
+            totals_in, table_rows[:, 0], table_rows[:, 1], scale_in, index, core,
+            words[:, part * tile:(part + 1) * tile].reshape(slabs, 1, tile), voxels[part], picture,
+            forward, backward, unit,
+        ]
+        aliases = {}
+        if not first:
+            aliases = {len(arguments): 1}
+            arguments.append(pltpu.with_memory_space_constraint(sums, pltpu.VMEM))
+        more, sums, *halves = pl.pallas_call(
             functools.partial(
                 slab_kernel, side, local_bits, list_length, particles, cap, part * tile, first, last
             ),
-            grid=(slabs,),
-            out_shape=(jax.ShapeDtypeStruct((slabs, particles, LANES), jnp.float32),)
+            out_shape=(
+                jax.ShapeDtypeStruct((slabs, particles, LANES), jnp.float32),
+                pltpu.VMEM((blocks + 8, features), jnp.float32),
+            )
             + tuple(jax.ShapeDtypeStruct((length, features), jnp.float32) for length in lengths),
-            in_specs=[SMEM_SPEC] * 6 + [
-                per_source(1, tile),
-                per_source(tile, features, part),
-                per_source(tile, features),
-                whole(forward),
-                whole(backward),
-                whole(unit),
-            ] + [ANY_SPEC] * len(sums),
-            out_specs=(per_source(particles, LANES),) + (ANY_SPEC,) * len(lengths),
+            in_specs=[SMEM_SPEC] * 6 + [VMEM_SPEC] * (len(arguments) - 6),
+            out_specs=(VMEM_SPEC, VMEM_SPEC) + (ANY_SPEC,) * len(lengths),
             scratch_shapes=[
-                pltpu.VMEM((blocks + 8, features), jnp.float32),
                 pltpu.VMEM((tile, features), jnp.float32),
-                pltpu.SemaphoreType.DMA((len(lengths),)),
+                pltpu.SemaphoreType.DMA((max(1, len(lengths)),)),
             ],
-            compiler_params=params(),
-            cost_estimate=pl.CostEstimate(
-                flops=slabs * tile * features * features * 9, bytes_accessed=80 * 1024 * 1024, transcendentals=0
-            ),
+            input_output_aliases=aliases,
+            compiler_params=pltpu.CompilerParams(vmem_limit_bytes=24 * 1024 * 1024),
+            cost_estimate=pl.CostEstimate(flops=0, bytes_accessed=16 * 1024 * 1024, transcendentals=0),
             name="compare_and_add",
-        )(
-            totals_in, table_rows[:, 0], table_rows[:, 1], scale_in, index, core,
-            words[:, part * tile:(part + 1) * tile].reshape(slabs, 1, tile), voxels, picture,
-            forward, backward, unit, *sums,
-        )
+        )(*arguments)
         squares = squares + more
-    mine, *theirs = sums
+        behind.append(more)
+    mine, *theirs = halves
     shared = lax.all_gather(jnp.sum(squares, axis=2), "slab")
     returned = lax.dynamic_index_in_dim(shared, lax.axis_index("slab"), axis=1, keepdims=False)
     losses = jnp.sum(returned, axis=0) / (counts.astype(jnp.float32) * 128.0)
@@ -666,7 +639,7 @@
 
 def body(*arrays):
     mine, theirs, losses, side = gradient_of_slab(*arrays)
-    return to_field(mine, theirs, side), losses
+    return to_field(mine, theirs, losses, side)
 
 
 def solution(mesh):

time: 476 us -> 409 us (0.86)
  Pallas kernels: 226 us -> 131 us
  local copies, waits for them, and re-layouts: 15.7 us -> 64.3 us
  blocking collectives: 123 us -> 93.4 us
  starting transfers between devices: 23 us -> 31.9 us
  waiting for transfers between devices: 81.5 us -> 75.2 us
    pallas_call x4, Pallas kernels: 112 us -> 45.9 us  [gradient_of_slab(): pl.pallas_call(functools.partial(slab_kernel, side, local_bits, list_leng...]
    all_to_all x3 -> x2, blocking collectives: 92.5 us -> 43.7 us  [the longest x1 30.1 us: to_field(): got = lax.all_to_all(sent, 'slab', split_axis=0, concat_axis=0, tiled=True)]
    unnamed x30 -> x86, local copies, waits for them, and re-layouts: 3.86 us -> 51.4 us
    pallas_call x3 -> x2, Pallas kernels: 58.8 us -> 32.2 us  [the longest x1 16.6 us: gradient_of_slab(): pl.pallas_call(functools.partial(pack_kernel, slabs, cap, list_length), o...]
    all_to_all x1 -> x4, starting transfers between devices: 3.64 us -> 27.3 us  [gradient_of_slab(): lax.all_to_all(packed[part], 'slab', split_axis=0, concat_axis=0, tiled=T...]
    all_gather x1, blocking collectives: 30.4 us -> 49.8 us  [gradient_of_slab(): shared = lax.all_gather(jnp.sum(squares, axis=2), 'slab')]
    ppermute x3 -> x2, waiting for transfers between devices: 14.1 us -> 0.01 us  [to_field(): theirs = [lax.ppermute(chunk, 'dom', swap) for chunk in theirs_sent]]
    all_to_all x1 -> x4, waiting for transfers between devices: 0.01 us -> 7.13 us  [gradient_of_slab(): lax.all_to_all(packed[part], 'slab', split_axis=0, concat_axis=0, tiled=T...]
  transfers between devices with their start and end apart: 11 -> 9, of which waited for: 5 -> 4; matrix products, arithmetic and copies ran while one was open for 2% -> 3% of each run, Pallas kernels for 35% -> 16%
where the time goes in v5:
time: 409 us; the launch traced here: 402 us
  Pallas kernels  131 us (32%)
  blocking collectives  93.4 us (23%)
  waiting for transfers between devices  75.2 us (18%)
  local copies, waits for them, and re-layouts  64.3 us (16%)
  starting transfers between devices  31.9 us (8%)
  other arithmetic  4.81 us (1%)
    all_to_all x1, waiting for transfers between devices, to_field(): got = lax.all_to_all(sent, 'slab', split_axis=0, concat_axis=0, tiled=True)  65.4 us
    unnamed x86, local copies, waits for them, and re-layouts  51.4 us
    all_gather x1, blocking collectives, gradient_of_slab(): shared = lax.all_gather(jnp.sum(squares, axis=2), 'slab')  49.8 us
    pallas_call x4, Pallas kernels, gradient_of_slab(): pl.pallas_call(functools.partial(slab_kernel, side, local_bits, list_leng...  45.9 us
    pallas_call x2, Pallas kernels, to_field(): pl.pallas_call(planes_kernel, grid=(quads, per_row // yblocks), out_shape...  33.9 us
    all_to_all x1, blocking collectives, to_field(): got = lax.all_to_all(sent, 'slab', split_axis=0, concat_axis=0, tiled=True)  30.1 us
    all_to_all x4, starting transfers between devices, gradient_of_slab(): lax.all_to_all(packed[part], 'slab', split_axis=0, concat_axis=0, tiled=T...  27.3 us
    pallas_call x1, Pallas kernels, gradient_of_slab(): pl.pallas_call(functools.partial(pack_kernel, slabs, cap, list_length), o...  16.6 us
  transfers between devices with their start and end apart: 9, of which 4 were waited for; matrix products, arithmetic and copies ran while one was open for 3% of the time, Pallas kernels for 16%

profile of v5, /device:TPU:0, one launch (start us, length us, event | category | flops | bytes accessed | tf_op | source)
XLA Modules:
  0.0 401.8 jit_solution(14119662267703568820)
XLA Ops:
  3.4 3.7 route.1
  7.1 16.6 %pack.1 = (s32[17408]{0:T(1024)}, bf16[8,512,128]{2,1,0:T(8,128)(2,1)}, bf16[8,512,128]{2,1,0:T(8,128)(2,1)}, bf16[8,512,128]{2,1,0:T(8,128)(2,1)}, bf16[8,512,128]{2,1,0:T(8,128)(2,1)}) custom-call(s32[8192]{0:T(1024)} %bitcast.57, s32[8192]{0:T(1024)} %bitcast.58, s32[8]{0:T(128)} %counts_ref.3, bf16[8192,128]{1,0:T(8,128)(2,1)} %bitcast.48), custom_call_target="tpu_custom_call" | custom-call | tf_op jit(solution)/shard_map/pack/pallas_call | solution.py:531
  26.1 13.5 %all_to_all.42 = s32[8,1,2176]{2,1,0:T(1,128)S(1)} all-to-all(s32[8,1,2176]{2,1,0:T(1,128)S(1)} %all_to_all.26), channel_id=1, replica_groups=mesh['groups'=2,'slab'=8,'dom'=2] {'slab'}, dimensions={0} | all-to-all | bytes 139264 | tf_op jit(solution)/shard_map/all_to_all | solution.py:555
  47.5 15.6 %read_voxels.1 = (bf16[8,512,128]{2,1,0:T(8,128)(2,1)}, bf16[8,512,128]{2,1,0:T(8,128)(2,1)}, bf16[8,512,128]{2,1,0:T(8,128)(2,1)}, bf16[8,512,128]{2,1,0:T(8,128)(2,1)}) custom-call(s32[16384]{0:T(1024)} %bitcast.41, s32[8]{0:T(128)} %copy-done.15, bf16[32768,128]{1,0:T(8,128)(2,1)} %volume_ref.1), custom_call_target="tpu_custom_call" | custom-call | bytes 104857600 | tf_op jit(solution)/shard_map/read_voxels/pallas_call | solution.py:572
  63.1 3.9 all-to-all-done.2.image_ref
  67.0 8.5 %all-to-all-start.1 = ((bf16[8,512,128]{2,1,0:T(8,128)(2,1)}), bf16[8,512,128]{2,1,0:T(8,128)(2,1)S(1)}, u32[]{:S(2)}, u32[]{:S(2)}) async-start(bf16[8,512,128]{2,1,0:T(8,128)(2,1)} %get-tuple-element.38), calls=%async_computation.1 | async-start | bytes 2097152 | tf_op jit(solution)/shard_map/all_to_all | solution.py:600
  87.1 22.7 %compare_and_add.4 = (f32[8,8,128]{2,1,0:T(8,128)S(1)}, f32[32776,128]{1,0:T(8,128)S(1)}) custom-call(s32[8]{0:T(128)S(1)} %copy-done.16, f32[64]{0:T(128)S(1)} %get-tuple-element.57.defocus_ref, f32[64]{0:T(128)S(1)} %get-tuple-element.56.phase_ref, f32[64]{0:T(128)S(1)} %copy-done.28, s32[16384]{0:T(1024)S(1)} %bitcast.42, s32[1]{0:T(128)} %bitcast.core_ref, ...), custom_call_target="tpu_custom_call" | custom-call | bytes 16777216 | tf_op jit(solution)/shard_map/compare_and_add/pallas_call | solution.py:611
  109.8 5.8 %copy-done = f32[32776,128]{1,0:T(8,128)} copy-done((f32[32776,128]{1,0:T(8,128)}, f32[32776,128]{1,0:T(8,128)S(1)}, u32[]{:S(2)}) %copy-start) | copy-done | bytes 16781336
  115.5 4.2 %all-to-all-start.4 = ((bf16[8,512,128]{2,1,0:T(8,128)(2,1)}), bf16[8,512,128]{2,1,0:T(8,128)(2,1)S(1)}, u32[]{:S(2)}, u32[]{:S(2)}) async-start(bf16[8,512,128]{2,1,0:T(8,128)(2,1)} %get-tuple-element.46), calls=%async_computation.4 | async-start | bytes 2097152 | tf_op jit(solution)/shard_map/all_to_all | solution.py:600
  120.5 5.8 %copy-done.1 = f32[32776,128]{1,0:T(8,128)S(1)} copy-done((f32[32776,128]{1,0:T(8,128)S(1)}, f32[32776,128]{1,0:T(8,128)}, u32[]{:S(2)}) %copy-start.1) | copy-done | bytes 16781336
  128.8 13.9 %compare_and_add.5 = (f32[8,8,128]{2,1,0:T(8,128)S(1)}, f32[32776,128]{1,0:T(8,128)S(1)}) custom-call(s32[8]{0:T(128)S(1)} %copy-done.17, f32[64]{0:T(128)S(1)} %copy-done.25, f32[64]{0:T(128)S(1)} %copy-done.21, f32[64]{0:T(128)S(1)} %copy-done.29, s32[16384]{0:T(1024)S(1)} %bitcast.43, s32[1]{0:T(128)} %bitcast.core_ref, ...), custom_call_target="tpu_custom_call", output_to_operand_aliasing={{1}: (12, {})} | custom-call | bytes 16777216 | tf_op jit(solution)/shard_map/compare_and_add/pallas_call | solution.py:611
  142.7 5.8 %copy-done.2 = f32[32776,128]{1,0:T(8,128)} copy-done((f32[32776,128]{1,0:T(8,128)}, f32[32776,128]{1,0:T(8,128)S(1)}, u32[]{:S(2)}) %copy-start.2) | copy-done | bytes 16781336
  149.1 10.9 %all-to-all-start.3 = ((bf16[8,512,128]{2,1,0:T(8,128)(2,1)}), bf16[8,512,128]{2,1,0:T(8,128)(2,1)S(1)}, u32[]{:S(2)}, u32[]{:S(2)}) async-start(bf16[8,512,128]{2,1,0:T(8,128)(2,1)} %get-tuple-element.42), calls=%async_computation.3 | async-start | bytes 2097152 | tf_op jit(solution)/shard_map/all_to_all | solution.py:600
  160.8 5.8 %copy-done.3 = f32[32776,128]{1,0:T(8,128)S(1)} copy-done((f32[32776,128]{1,0:T(8,128)S(1)}, f32[32776,128]{1,0:T(8,128)}, u32[]{:S(2)}) %copy-start.3) | copy-done | bytes 16781336
  172.3 5.8 %copy-done.4 = f32[32776,128]{1,0:T(8,128)} copy-done((f32[32776,128]{1,0:T(8,128)}, f32[32776,128]{1,0:T(8,128)S(1)}, u32[]{:S(2)}) %copy-start.4) | copy-done | bytes 16781336
  181.9 5.8 %copy-done.5 = f32[32776,128]{1,0:T(8,128)S(1)} copy-done((f32[32776,128]{1,0:T(8,128)S(1)}, f32[32776,128]{1,0:T(8,128)}, u32[]{:S(2)}) %copy-start.5) | copy-done | bytes 16781336
  190.2 7.4 %compare_and_add.7 = (f32[8,8,128]{2,1,0:T(8,128)S(1)}, f32[32776,128]{1,0:T(8,128)S(1)}, f32[16384,128]{1,0:T(8,128)}, f32[4096,128]{1,0:T(8,128)S(1)}, f32[12288,128]{1,0:T(8,128)}) custom-call(s32[8]{0:T(128)S(1)} %copy-done.19, f32[64]{0:T(128)S(1)} %copy-done.27, f32[64]{0:T(128)S(1)} %copy-done.23, ...), custom_call_target="tpu_custom_call", output_to_operand_aliasing={{1}: (12, {})} | custom-call | bytes 16777216 | tf_op jit(solution)/shard_map/compare_and_add/pallas_call | solution.py:611
  199.0 49.8 %all-gather = f32[64,8]{1,0:T(8,128)S(1)} all-gather(f32[8,8]{1,0:T(8,128)S(1)} %add_reduce_fusion), channel_id=2, replica_groups=mesh['groups'=2,'slab'=8,'dom'=2] {'slab'}, dimensions={0}, use_global_device_ids=true | all-gather | bytes 2304 | tf_op jit(solution)/shard_map/all_gather | solution.py:634
  249.4 24.4 %transform_planes.3 = bf16[8,12,2,32,256]{4,3,2,1,0:T(8,128)(2,1)} custom-call(f32[16,32,32,128]{3,2,1,0:T(8,128)} %bitcast.46, f32[12,32,32,128]{3,2,1,0:T(8,128)} %bitcast.20.theirs_ref, bf16[384,256]{1,0:T(8,128)(2,1)} %constant.40.clone.zblock_ref, f32[2,8,128]{2,1,0:T(8,128)} %constant.41.clone.turn_ref, bf16[512,512]{1,0:T(8,128)(2,1)} %constant.42.clone.wide_ref, ...), custom_call_target="tpu_custom_call" | custom-call | flops 1610612736 | bytes 25165824 | tf_op jit(solution)/shard_map/transform_planes/pallas_call | solution.py:462
  273.7 4.6 %all-to-all-start.6 = ((bf16[8,12,2,32,256]{4,3,2,1,0:T(8,128)(2,1)}), bf16[8,12,2,32,256]{4,3,2,1,0:T(8,128)(2,1)}, u32[]{:S(2)}, u32[]{:S(2)}) async-start(bf16[8,12,2,32,256]{4,3,2,1,0:T(8,128)(2,1)} %transform_planes.3), calls=%async_computation.6 | async-start | bytes 6291456 | tf_op jit(solution)/shard_map/all_to_all | solution.py:484
  278.4 65.4 %all-to-all-done.6.refs_1_ = bf16[8,12,2,32,256]{4,3,2,1,0:T(8,128)(2,1)} async-done(((bf16[8,12,2,32,256]{4,3,2,1,0:T(8,128)(2,1)}), bf16[8,12,2,32,256]{4,3,2,1,0:T(8,128)(2,1)}, u32[]{:S(2)}, u32[]{:S(2)}) %all-to-all-start.6) | async-done | bytes 3145760 | tf_op jit(solution)/shard_map/all_to_all | solution.py:484
  343.8 9.5 %transform_planes.2 = bf16[8,4,2,32,256]{4,3,2,1,0:T(8,128)(2,1)} custom-call(f32[16,32,32,128]{3,2,1,0:T(8,128)} %bitcast.47, f32[4,32,32,128]{3,2,1,0:T(8,128)} %bitcast.18.theirs_ref, bf16[384,256]{1,0:T(8,128)(2,1)} %constant.40.clone.zblock_ref, f32[2,8,128]{2,1,0:T(8,128)} %constant.41.clone.turn_ref, bf16[512,512]{1,0:T(8,128)(2,1)} %constant.42.clone.wide_ref, ...), custom_call_target="tpu_custom_call" | custom-call | flops 536870912 | bytes 8388608 | tf_op jit(solution)/shard_map/transform_planes/pallas_call | solution.py:462
  353.3 30.1 %all_to_all.43.refs_0_ = bf16[8,4,2,32,256]{4,3,2,1,0:T(8,128)(2,1)S(1)} all-to-all(bf16[8,4,2,32,256]{4,3,2,1,0:T(8,128)(2,1)} %transform_planes.2), channel_id=1, replica_groups=mesh['groups'=2,'slab'=8,'dom'=2] {'slab'}, dimensions={0} | all-to-all | bytes 2097152 | tf_op jit(solution)/shard_map/all_to_all | solution.py:484
  388.8 13.0 %transform_first.1 = f32[2,128,32,256]{3,2,1,0:T(8,128)} custom-call(s32[1]{0:T(128)} %bitcast.core_ref, bf16[8,4,2,32,256]{4,3,2,1,0:T(8,128)(2,1)} %copy-done.34, bf16[8,12,2,32,256]{4,3,2,1,0:T(8,128)(2,1)} %all-to-all-done.6.refs_1_, bf16[8,4,2,32,256]{4,3,2,1,0:T(8,128)(2,1)} %copy-done.36, bf16[8,12,2,32,256]{4,3,2,1,0:T(8,128)(2,1)} %copy-done.35), custom_call_target="tpu_custom_call" | custom-call | tf_op jit(solution)/shard_map/transform_first/pallas_call | solution.py:489
  (129 shorter events, 48.6 us)
Async XLA Ops:
  39.6 35.9 %copy-start.41 = (f32[64,2]{0,1:T(2,128)S(1)}, f32[64,2]{0,1:T(2,128)}, u32[]{:S(2)}) copy-start(f32[64,2]{0,1:T(2,128)} %param.22) | copy-start | bytes 1540
  39.6 36.0 %copy-start.38 = (bf16[4,128,128]{2,1,0:T(8,128)(2,1)S(1)}, bf16[4,128,128]{2,1,0:T(8,128)(2,1)}, u32[]{:S(2)}) copy-start(bf16[4,128,128]{2,1,0:T(8,128)(2,1)} %param.15) | copy-start | bytes 393220
  39.6 27.4 %all-to-all-start.2 = ((bf16[8,512,128]{2,1,0:T(8,128)(2,1)}), bf16[8,512,128]{2,1,0:T(8,128)(2,1)S(1)}, u32[]{:S(2)}, u32[]{:S(2)}) async-start(bf16[8,512,128]{2,1,0:T(8,128)(2,1)} %get-tuple-element.39), calls=%async_computation.2 | async-start | bytes 2097152 | tf_op jit(solution)/shard_map/all_to_all | solution.py:600
  43.4 32.2 %copy-start.37 = (s32[8,1,2176]{2,0,1:T(8,128)}, s32[8,1,2176]{2,0,1:T(8,128)S(1)}, u32[]{:S(2)}) copy-start(s32[8,1,2176]{2,0,1:T(8,128)S(1)} %copy.65) | copy-start | bytes 208900
  47.5 37.0 %copy-start.6 = (s32[128,128]{1,0:T(8,128)S(1)}, s32[128,128]{1,0:T(8,128)}, u32[]{:S(2)}) copy-start(s32[128,128]{1,0:T(8,128)} %decode.1) | copy-start | bytes 196612
  63.1 57.4 %copy-start.9 = (bf16[8,512,128]{2,1,0:T(8,128)(2,1)S(1)}, bf16[8,512,128]{2,1,0:T(8,128)(2,1)}, u32[]{:S(2)}) copy-start(bf16[8,512,128]{2,1,0:T(8,128)(2,1)} %get-tuple-element.35.voxel_ref) | copy-start | bytes 3145732
  67.0 48.5 %all-to-all-start.1 = ((bf16[8,512,128]{2,1,0:T(8,128)(2,1)}), bf16[8,512,128]{2,1,0:T(8,128)(2,1)S(1)}, u32[]{:S(2)}, u32[]{:S(2)}) async-start(bf16[8,512,128]{2,1,0:T(8,128)(2,1)} %get-tuple-element.38), calls=%async_computation.1 | async-start | bytes 2097152 | tf_op jit(solution)/shard_map/all_to_all | solution.py:600
  84.5 31.0 %copy-start.20 = (f32[64]{0:T(128)}, f32[64]{0:T(128)S(1)}, u32[]{:S(2)}) copy-start(f32[64]{0:T(128)S(1)} %get-tuple-element.56.phase_ref) | copy-start | bytes 772
  84.5 31.0 %copy-start.24 = (f32[64]{0:T(128)}, f32[64]{0:T(128)S(1)}, u32[]{:S(2)}) copy-start(f32[64]{0:T(128)S(1)} %get-tuple-element.57.defocus_ref) | copy-start | bytes 772
  115.5 33.6 %all-to-all-start.4 = ((bf16[8,512,128]{2,1,0:T(8,128)(2,1)}), bf16[8,512,128]{2,1,0:T(8,128)(2,1)S(1)}, u32[]{:S(2)}, u32[]{:S(2)}) async-start(bf16[8,512,128]{2,1,0:T(8,128)(2,1)} %get-tuple-element.46), calls=%async_computation.4 | async-start | bytes 2097152 | tf_op jit(solution)/shard_map/all_to_all | solution.py:600
  120.5 5.8 %copy-start.1 = (f32[32776,128]{1,0:T(8,128)S(1)}, f32[32776,128]{1,0:T(8,128)}, u32[]{:S(2)}) copy-start(f32[32776,128]{1,0:T(8,128)} %copy-done) | copy-start | bytes 50343940
  128.8 31.9 %copy-start.39 = (s32[8,512]{1,0:T(8,128)S(1)}, s32[8,512]{1,0:T(8,128)}, u32[]{:S(2)}) copy-start(s32[8,512]{1,0:T(8,128)} %get-tuple-element.61) | copy-start | bytes 49156
  149.1 32.8 %all-to-all-start.3 = ((bf16[8,512,128]{2,1,0:T(8,128)(2,1)}), bf16[8,512,128]{2,1,0:T(8,128)(2,1)S(1)}, u32[]{:S(2)}, u32[]{:S(2)}) async-start(bf16[8,512,128]{2,1,0:T(8,128)(2,1)} %get-tuple-element.42), calls=%async_computation.3 | async-start | bytes 2097152 | tf_op jit(solution)/shard_map/all_to_all | solution.py:600
  160.8 5.8 %copy-start.3 = (f32[32776,128]{1,0:T(8,128)S(1)}, f32[32776,128]{1,0:T(8,128)}, u32[]{:S(2)}) copy-start(f32[32776,128]{1,0:T(8,128)} %copy-done.2) | copy-start | bytes 50343940
  170.3 11.6 %copy-start.7 = (bf16[8,512,128]{2,1,0:T(8,128)(2,1)S(1)}, bf16[8,512,128]{2,1,0:T(8,128)(2,1)}, u32[]{:S(2)}) copy-start(bf16[8,512,128]{2,1,0:T(8,128)(2,1)} %get-tuple-element.33.voxel_ref) | copy-start | bytes 3145732
  181.9 5.8 %copy-start.5 = (f32[32776,128]{1,0:T(8,128)S(1)}, f32[32776,128]{1,0:T(8,128)}, u32[]{:S(2)}) copy-start(f32[32776,128]{1,0:T(8,128)} %copy-done.4) | copy-start | bytes 50343940
  190.2 8.7 %copy-start.12 = (f32[8,8,128]{2,1,0:T(8,128)S(1)}, f32[8,8,128]{2,1,0:T(8,128)}, u32[]{:S(2)}) copy-start(f32[8,8,128]{2,1,0:T(8,128)} %copy-done.11) | copy-start | bytes 98308
  190.2 8.7 %copy-start.14 = (f32[8,8,128]{2,1,0:T(8,128)S(1)}, f32[8,8,128]{2,1,0:T(8,128)}, u32[]{:S(2)}) copy-start(f32[8,8,128]{2,1,0:T(8,128)} %copy-done.13) | copy-start | bytes 98308
  190.2 58.6 %copy-start.40 = (s32[8]{0:T(128)S(1)}, s32[8]{0:T(128)}, u32[]{:S(2)}) copy-start(s32[8]{0:T(128)} %counts_ref.3) | copy-start | bytes 100
  198.9 50.4 %collective-permute-start.1 = (f32[12288,128]{1,0:T(8,128)}, f32[12288,128]{1,0:T(8,128)}, u32[]{:S(2)}, u32[]{:S(2)}) collective-permute-start(f32[12288,128]{1,0:T(8,128)} %get-tuple-element.51), channel_id=1, source_target_pairs={{0,1},{1,0},{2,3},{3,2},{4,5},{5,4},{6,7},{7,6},{8,9},{9,8},{10,11... | collective-permute-start | bytes 18874376 | tf_op jit(solution)/shard_map/ppermute | solution.py:445
  273.7 70.1 %all-to-all-start.6 = ((bf16[8,12,2,32,256]{4,3,2,1,0:T(8,128)(2,1)}), bf16[8,12,2,32,256]{4,3,2,1,0:T(8,128)(2,1)}, u32[]{:S(2)}, u32[]{:S(2)}) async-start(bf16[8,12,2,32,256]{4,3,2,1,0:T(8,128)(2,1)} %transform_planes.3), calls=%async_computation.6 | async-start | bytes 6291456 | tf_op jit(solution)/shard_map/all_to_all | solution.py:484
  278.3 65.5 %collective-permute-start = (f32[4096,128]{1,0:T(8,128)S(1)}, f32[4096,128]{1,0:T(8,128)}, u32[]{:S(2)}, u32[]{:S(2)}) collective-permute-start(f32[4096,128]{1,0:T(8,128)S(1)} %copy-done.33), channel_id=1, source_target_pairs={{0,1},{1,0},{2,3},{3,2},{4,5},{5,4},{6,7},{7,6},{8,9},{9,8},{10,11... | collective-permute-start | bytes 6291464 | tf_op jit(solution)/shard_map/ppermute | solution.py:445
  343.8 42.3 %collective-permute-start.3 = (bf16[8,12,2,32,256]{4,3,2,1,0:T(8,128)(2,1)}, bf16[8,12,2,32,256]{4,3,2,1,0:T(8,128)(2,1)S(1)}, u32[]{:S(2)}, u32[]{:S(2)}) collective-permute-start(bf16[8,12,2,32,256]{4,3,2,1,0:T(8,128)(2,1)} %all-to-all-done.6.refs_1_), channel_id=1, source_target_pairs={{0,1},{1,0},{2,3},{3,2},{4,5},{5,4},{6,7},{7,6},{8,9},{9,8},{10,11... | collective-permute-start | bytes 9437192 | tf_op jit(solution)/shard_map/ppermute | solution.py:486
  383.4 2.7 collective-permute-start.2
  (27 other events, 45.2 us)

commit v6 on v5

--- a/solution.py
+++ b/solution.py
@@ -10,7 +10,7 @@
 from jax.sharding import PartitionSpec as P
 
 LANES = 128
-TILE = 512
+TILE = 1024
 GROUP = 16
 VMEM_LIMIT = 56 * 1024 * 1024
 
@@ -434,7 +434,22 @@
     return (zblock, turns) + host_halves(matrix)
 
 
-def to_field(mine, theirs_sent, losses, side):
+def sum_over_slabs(partial_sums):
+    slabs = partial_sums.shape[0]
+    if slabs <= 8:
+        me = lax.axis_index("slab")
+        row = lambda i: lax.dynamic_index_in_dim(partial_sums, me ^ i, axis=0, keepdims=True)
+        returned = [row(0)] + [
+            lax.ppermute(row(i), "slab", [(slab, slab ^ i) for slab in range(slabs)])
+            for i in range(1, slabs)
+        ]
+        returned = jnp.concatenate(returned)
+    else:
+        returned = lax.all_to_all(partial_sums, "slab", split_axis=0, concat_axis=0, tiled=True)
+    return jnp.sum(returned, axis=0)
+
+
+def to_field(mine, theirs_sent, partial_sums, side):
     slabs = lax.axis_size("slab")
     per_row = side // 8
     each = side // slabs // 2
@@ -449,10 +464,12 @@
     if short:
         mine = jnp.pad(mine, ((0, short), (0, 0), (0, 0), (0, 0)))
     yblocks = 8
-    own, other = [], []
-    theirs[-1], losses = lax.optimization_barrier((theirs[-1], losses))
+    own = []
     first_quad = 0
+    before = []
     for real_planes, added in zip(pieces_of(each), theirs):
+        if before:
+            added, before[0] = lax.optimization_barrier((added, before[0]))
         added = added.reshape(grid_shape)
         if short:
             added = jnp.pad(added, ((0, short), (0, 0), (0, 0), (0, 0)))
@@ -481,9 +498,15 @@
         if groups != slabs:
             sent = sent.reshape(-1, 2, slabs, height, side).transpose(2, 0, 1, 3, 4)[:, :real_planes]
         first_quad += quads
+        if before:
+            sent, own[-1] = lax.optimization_barrier((sent, own[-1]))
+        if first_quad * 4 >= each:
+            sent, partial_sums = lax.optimization_barrier((sent, partial_sums))
+        before = [sent]
         got = lax.all_to_all(sent, "slab", split_axis=0, concat_axis=0, tiled=True)
         own.append(got)
-        other.append(lax.ppermute(got, "dom", swap))
+    own[-1], losses = lax.optimization_barrier((own[-1], sum_over_slabs(partial_sums)))
+    other = [lax.ppermute(got, "dom", swap) for got in own]
     rows = min(16, height)
     arrays = own + other
     field = pl.pallas_call(
@@ -631,15 +654,15 @@
         squares = squares + more
         behind.append(more)
     mine, *theirs = halves
-    shared = lax.all_gather(jnp.sum(squares, axis=2), "slab")
-    returned = lax.dynamic_index_in_dim(shared, lax.axis_index("slab"), axis=1, keepdims=False)
-    losses = jnp.sum(returned, axis=0) / (counts.astype(jnp.float32) * 128.0)
-    return mine, theirs, losses, side
+    partial_sums = jnp.sum(squares, axis=2)
+    return mine, theirs, partial_sums, side
 
 
 def body(*arrays):
-    mine, theirs, losses, side = gradient_of_slab(*arrays)
-    return to_field(mine, theirs, losses, side)
+    mine, theirs, partial_sums, side = gradient_of_slab(*arrays)
+    field, squares = to_field(mine, theirs, partial_sums, side)
+    counts = arrays[6]
+    return field, squares / (counts.astype(jnp.float32) * 128.0)
 
 
 def solution(mesh):

time: 409 us -> 335 us (0.82)
  blocking collectives: 93.4 us -> 14.1 us
  waiting for transfers between devices: 75.2 us -> 115 us
  local copies, waits for them, and re-layouts: 64.3 us -> 26.2 us
  starting transfers between devices: 31.9 us -> 51.5 us
  Pallas kernels: 131 us -> 119 us
    all_to_all x1 -> x2, waiting for transfers between devices: 65.4 us -> 1.83 us  [to_field(): got = lax.all_to_all(sent, 'slab', split_axis=0, concat_axis=0, tiled=True)]
    ppermute x2 -> x9, waiting for transfers between devices: 2.66 us -> 62.6 us  [the longest x7 56.9 us: sum_over_slabs(): lax.ppermute(row(i), 'slab', [(slab, slab ^ i) for slab in range(slabs)])]
    all_gather x1 -> x0, blocking collectives: 49.8 us -> none  [gradient_of_slab(): shared = lax.all_gather(jnp.sum(squares, axis=2), 'slab')]
    all_to_all x4 -> x2, waiting for transfers between devices: 7.13 us -> 39.6 us  [gradient_of_slab(): lax.all_to_all(packed[part], 'slab', split_axis=0, concat_axis=0, tiled=T...]
    unnamed x86 -> x32, local copies, waits for them, and re-layouts: 51.4 us -> 19.6 us
    all_to_all x1 -> x0, blocking collectives: 30.1 us -> none  [to_field(): got = lax.all_to_all(sent, 'slab', split_axis=0, concat_axis=0, tiled=True)]
    all_to_all x1 -> x2, starting transfers between devices: 4.57 us -> 27.7 us  [to_field(): got = lax.all_to_all(sent, 'slab', split_axis=0, concat_axis=0, tiled=True)]
    all_to_all x4 -> x2, starting transfers between devices: 27.3 us -> 7.96 us  [gradient_of_slab(): lax.all_to_all(packed[part], 'slab', split_axis=0, concat_axis=0, tiled=T...]
  transfers between devices with their start and end apart: 9 -> 15, of which waited for: 4 -> 10; matrix products, arithmetic and copies ran while one was open for 3% -> 1% of each run, Pallas kernels for 16% -> 24%
where the time goes in v6:
time: 335 us; the launch traced here: 330 us
  Pallas kernels  119 us (36%)
  waiting for transfers between devices  115 us (34%)
  starting transfers between devices  51.5 us (15%)
  local copies, waits for them, and re-layouts  26.2 us (8%)
  blocking collectives  14.1 us (4%)
    ppermute x7, waiting for transfers between devices, sum_over_slabs(): lax.ppermute(row(i), 'slab', [(slab, slab ^ i) for slab in range(slabs)])  56.9 us
    all_to_all x2, waiting for transfers between devices, gradient_of_slab(): lax.all_to_all(packed[part], 'slab', split_axis=0, concat_axis=0, tiled=T...  39.6 us
    pallas_call x2, Pallas kernels, gradient_of_slab(): pl.pallas_call(functools.partial(slab_kernel, side, local_bits, list_leng...  36 us
    pallas_call x2, Pallas kernels, to_field(): pl.pallas_call(planes_kernel, grid=(quads, per_row // yblocks), out_shape...  33.9 us
    all_to_all x2, starting transfers between devices, to_field(): got = lax.all_to_all(sent, 'slab', split_axis=0, concat_axis=0, tiled=True)  27.7 us
    unnamed x32, local copies, waits for them, and re-layouts  19.6 us
    pallas_call x1, Pallas kernels, gradient_of_slab(): pl.pallas_call(functools.partial(pack_kernel, slabs, cap, list_length), o...  16 us
    ppermute x7, starting transfers between devices, sum_over_slabs(): lax.ppermute(row(i), 'slab', [(slab, slab ^ i) for slab in range(slabs)])  14.7 us
  transfers between devices with their start and end apart: 15, of which 10 were waited for; matrix products, arithmetic and copies ran while one was open for 1% of the time, Pallas kernels for 24%

profile of v6, /device:TPU:0, one launch (start us, length us, event | category | flops | bytes accessed | tf_op | source)
XLA Modules:
  0.0 330.1 jit_solution(16150628660264666191)
XLA Ops:
  3.4 3.7 %route.1 = (s32[64,128]{1,0:T(8,128)}, s32[64,128]{1,0:T(8,128)}, s32[8,128]{1,0:T(8,128)}) custom-call(s32[64,128]{1,0:T(8,128)} %bitcast.49, s32[64,128]{1,0:T(8,128)} %reshape.114.local_ref, s32[64,128]{1,0:T(8,128)} %reshape.115.kind_ref, s32[8]{0:T(128)} %counts_ref.3), custom_call_target="tpu_custom_call" | custom-call | tf_op jit(solution)/shard_map/route/pallas_call | solution.py:541
  7.1 16.0 %pack.1 = (s32[17408]{0:T(1024)}, bf16[8,1024,128]{2,1,0:T(8,128)(2,1)}, bf16[8,1024,128]{2,1,0:T(8,128)(2,1)}) custom-call(s32[8192]{0:T(1024)} %bitcast.47, s32[8192]{0:T(1024)} %bitcast.48, s32[8]{0:T(128)} %counts_ref.3, bf16[8192,128]{1,0:T(8,128)(2,1)} %bitcast.38), custom_call_target="tpu_custom_call" | custom-call | tf_op jit(solution)/shard_map/pack/pallas_call | solution.py:554
  25.5 14.1 %all_to_all.32 = s32[8,1,2176]{2,1,0:T(1,128)S(1)} all-to-all(s32[8,1,2176]{2,1,0:T(1,128)S(1)} %all_to_all.20), channel_id=1, replica_groups=mesh['groups'=2,'slab'=8,'dom'=2] {'slab'}, dimensions={0} | all-to-all | bytes 139264 | tf_op jit(solution)/shard_map/all_to_all | solution.py:578
  39.6 3.6 %all-to-all-start.2 = ((bf16[8,1024,128]{2,1,0:T(8,128)(2,1)}), bf16[8,1024,128]{2,1,0:T(8,128)(2,1)S(1)}, u32[]{:S(2)}, u32[]{:S(2)}) async-start(bf16[8,1024,128]{2,1,0:T(8,128)(2,1)} %get-tuple-element.32), calls=%async_computation.2 | async-start | bytes 4194304 | tf_op jit(solution)/shard_map/all_to_all | solution.py:623
  47.3 14.4 %read_voxels.1 = (bf16[8,1024,128]{2,1,0:T(8,128)(2,1)}, bf16[8,1024,128]{2,1,0:T(8,128)(2,1)}) custom-call(s32[16384]{0:T(1024)} %bitcast.33, s32[8]{0:T(128)} %copy-done.5, bf16[32768,128]{1,0:T(8,128)(2,1)} %volume_ref.1), custom_call_target="tpu_custom_call" | custom-call | bytes 104857600 | tf_op jit(solution)/shard_map/read_voxels/pallas_call | solution.py:595
  61.7 29.4 %all-to-all-done.2.image_ref = bf16[8,1024,128]{2,1,0:T(8,128)(2,1)S(1)} async-done(((bf16[8,1024,128]{2,1,0:T(8,128)(2,1)}), bf16[8,1024,128]{2,1,0:T(8,128)(2,1)S(1)}, u32[]{:S(2)}, u32[]{:S(2)}) %all-to-all-start.2) | async-done | bytes 2097184 | tf_op jit(solution)/shard_map/all_to_all | solution.py:623
  91.1 4.4 %all-to-all-start.1 = ((bf16[8,1024,128]{2,1,0:T(8,128)(2,1)}), bf16[8,1024,128]{2,1,0:T(8,128)(2,1)}, u32[]{:S(2)}, u32[]{:S(2)}) async-start(bf16[8,1024,128]{2,1,0:T(8,128)(2,1)} %get-tuple-element.31), calls=%async_computation.1 | async-start | bytes 4194304 | tf_op jit(solution)/shard_map/all_to_all | solution.py:623
  98.6 28.7 %compare_and_add.2 = (f32[8,8,128]{2,1,0:T(8,128)S(1)}, f32[32776,128]{1,0:T(8,128)S(1)}) custom-call(s32[8]{0:T(128)S(1)} %copy-done.6, f32[64]{0:T(128)S(1)} %get-tuple-element.47.defocus_ref, f32[64]{0:T(128)S(1)} %get-tuple-element.46.phase_ref, f32[64]{0:T(128)S(1)} %mul.17.scale_ref, s32[16384]{0:T(1024)S(1)} %bitcast.34, s32[1]{0:T(128)} %bitcast.core_ref, ...), custom_call_target="tpu_custom_call" | custom-call | bytes 16777216 | tf_op jit(solution)/shard_map/compare_and_add/pallas_call | solution.py:634
  127.3 5.7 %copy-done = f32[32776,128]{1,0:T(8,128)} copy-done((f32[32776,128]{1,0:T(8,128)}, f32[32776,128]{1,0:T(8,128)S(1)}, u32[]{:S(2)}) %copy-start) | copy-done | bytes 16781336
  133.0 10.3 %all-to-all-done.1.image_ref = bf16[8,1024,128]{2,1,0:T(8,128)(2,1)} async-done(((bf16[8,1024,128]{2,1,0:T(8,128)(2,1)}), bf16[8,1024,128]{2,1,0:T(8,128)(2,1)}, u32[]{:S(2)}, u32[]{:S(2)}) %all-to-all-start.1) | async-done | bytes 2097184 | tf_op jit(solution)/shard_map/all_to_all | solution.py:623
  143.2 5.8 %copy-done.1 = f32[32776,128]{1,0:T(8,128)S(1)} copy-done((f32[32776,128]{1,0:T(8,128)S(1)}, f32[32776,128]{1,0:T(8,128)}, u32[]{:S(2)}) %copy-start.1) | copy-done | bytes 16781336
  150.6 7.3 %compare_and_add.3 = (f32[8,8,128]{2,1,0:T(8,128)S(1)}, f32[32776,128]{1,0:T(8,128)S(1)}, f32[16384,128]{1,0:T(8,128)}, f32[4096,128]{1,0:T(8,128)S(1)}, f32[12288,128]{1,0:T(8,128)}) custom-call(s32[8]{0:T(128)S(1)} %copy-done.6, f32[64]{0:T(128)S(1)} %get-tuple-element.47.defocus_ref, ...), custom_call_target="tpu_custom_call", output_to_operand_aliasing={{1}: (12, {})} | custom-call | bytes 16777216 | tf_op jit(solution)/shard_map/compare_and_add/pallas_call | solution.py:634
  158.5 11.3 %collective-permute-done.1 = f32[4096,128]{1,0:T(8,128)S(1)} collective-permute-done((f32[4096,128]{1,0:T(8,128)S(1)}, f32[4096,128]{1,0:T(8,128)S(1)}, u32[]{:S(2)}, u32[]{:S(2)}) %collective-permute-start.1) | collective-permute-done | bytes 2097184 | tf_op jit(solution)/shard_map/ppermute | solution.py:460
  171.2 9.5 %transform_planes.2 = bf16[8,4,2,32,256]{4,3,2,1,0:T(8,128)(2,1)} custom-call(f32[16,32,32,128]{3,2,1,0:T(8,128)} %bitcast.36, f32[4,32,32,128]{3,2,1,0:T(8,128)} %bitcast.39, bf16[384,256]{1,0:T(8,128)(2,1)} %constant.68.clone.zblock_ref, f32[2,8,128]{2,1,0:T(8,128)} %constant.69.clone.turn_ref, bf16[512,512]{1,0:T(8,128)(2,1)} %constant.70.clone.wide_ref, ...), custom_call_target="tpu_custom_call" | custom-call | flops 536870912 | bytes 8388608 | tf_op jit(solution)/shard_map/transform_planes/pallas_call | solution.py:479
  180.7 23.5 %all-to-all-start.3 = ((bf16[8,4,2,32,256]{4,3,2,1,0:T(8,128)(2,1)}), bf16[8,4,2,32,256]{4,3,2,1,0:T(8,128)(2,1)S(1)}, u32[]{:S(2)}, u32[]{:S(2)}) async-start(bf16[8,4,2,32,256]{4,3,2,1,0:T(8,128)(2,1)} %transform_planes.2), calls=%async_computation.3 | async-start | bytes 2097152 | tf_op jit(solution)/shard_map/all_to_all | solution.py:506
  204.3 24.4 %transform_planes.3 = bf16[8,12,2,32,256]{4,3,2,1,0:T(8,128)(2,1)} custom-call(f32[16,32,32,128]{3,2,1,0:T(8,128)} %bitcast.37, f32[12,32,32,128]{3,2,1,0:T(8,128)} %bitcast.17.theirs_ref, bf16[384,256]{1,0:T(8,128)(2,1)} %constant.68.clone.zblock_ref, f32[2,8,128]{2,1,0:T(8,128)} %constant.69.clone.turn_ref, bf16[512,512]{1,0:T(8,128)(2,1)} %constant.70.clone.wide_ref, ...), custom_call_target="tpu_custom_call" | custom-call | flops 1610612736 | bytes 25165824 | tf_op jit(solution)/shard_map/transform_planes/pallas_call | solution.py:479
  231.5 4.2 %all-to-all-start.4 = ((bf16[8,12,2,32,256]{4,3,2,1,0:T(8,128)(2,1)}), bf16[8,12,2,32,256]{4,3,2,1,0:T(8,128)(2,1)S(1)}, u32[]{:S(2)}, u32[]{:S(2)}) async-start(bf16[8,12,2,32,256]{4,3,2,1,0:T(8,128)(2,1)} %transform_planes.3), calls=%async_computation.4 | async-start | bytes 6291456 | tf_op jit(solution)/shard_map/all_to_all | solution.py:506
  243.6 17.6 %collective-permute-done.2 = f32[1,8]{1,0:T(1,128)S(1)} collective-permute-done((f32[1,8]{1,0:T(1,128)S(1)}, f32[1,8]{1,0:T(1,128)S(1)}, u32[]{:S(2)}, u32[]{:S(2)}) %collective-permute-start.2) | collective-permute-done | bytes 64 | tf_op jit(solution)/shard_map/ppermute | solution.py:443
  261.2 3.2 collective-permute-start.7
  264.4 23.1 %collective-permute-done.3 = f32[1,8]{1,0:T(1,128)S(1)} collective-permute-done((f32[1,8]{1,0:T(1,128)S(1)}, f32[1,8]{1,0:T(1,128)S(1)}, u32[]{:S(2)}, u32[]{:S(2)}) %collective-permute-start.3) | collective-permute-done | bytes 64 | tf_op jit(solution)/shard_map/ppermute | solution.py:443
  287.5 3.5 %collective-permute-start.8 = (f32[1,8]{1,0:T(1,128)S(1)}, f32[1,8]{1,0:T(1,128)S(1)}, u32[]{:S(2)}, u32[]{:S(2)}) collective-permute-start(f32[1,8]{1,0:T(1,128)S(1)} %get-tuple-element.51), channel_id=1, source_target_pairs={{0,14},{2,12},{4,10},{6,8},{8,6},{10,4},{12,2},{14,0},{1,15},{3,13... | collective-permute-start | bytes 104 | tf_op jit(solution)/shard_map/ppermute | solution.py:443
  291.0 15.4 %collective-permute-done.5 = f32[1,8]{1,0:T(1,128)S(1)} collective-permute-done((f32[1,8]{1,0:T(1,128)S(1)}, f32[1,8]{1,0:T(1,128)S(1)}, u32[]{:S(2)}, u32[]{:S(2)}) %collective-permute-start.5) | collective-permute-done | bytes 64 | tf_op jit(solution)/shard_map/ppermute | solution.py:443
  308.8 5.5 %collective-permute-done.9.refs_2_ = bf16[8,4,2,32,256]{4,3,2,1,0:T(8,128)(2,1)S(1)} collective-permute-done((bf16[8,4,2,32,256]{4,3,2,1,0:T(8,128)(2,1)}, bf16[8,4,2,32,256]{4,3,2,1,0:T(8,128)(2,1)S(1)}, u32[]{:S(2)}, u32[]{:S(2)}) %collective-permute-start.9) | collective-permute-done | bytes 1048608 | tf_op jit(solution)/shard_map/ppermute | solution.py:509
  317.1 13.0 %transform_first.1 = f32[2,128,32,256]{3,2,1,0:T(8,128)} custom-call(s32[1]{0:T(128)} %bitcast.core_ref, bf16[8,4,2,32,256]{4,3,2,1,0:T(8,128)(2,1)} %copy-done.8, bf16[8,12,2,32,256]{4,3,2,1,0:T(8,128)(2,1)} %copy-done.7, bf16[8,4,2,32,256]{4,3,2,1,0:T(8,128)(2,1)} %copy-done.11, bf16[8,12,2,32,256]{4,3,2,1,0:T(8,128)(2,1)} %copy-done.9), custom_call_target="tpu_custom_call" | custom-call | tf_op jit(solution)/shard_map/transform_first/pallas_call | solution.py:512
  (82 shorter events, 31.6 us)
Async XLA Ops:
  39.6 51.5 %all-to-all-start.2 = ((bf16[8,1024,128]{2,1,0:T(8,128)(2,1)}), bf16[8,1024,128]{2,1,0:T(8,128)(2,1)S(1)}, u32[]{:S(2)}, u32[]{:S(2)}) async-start(bf16[8,1024,128]{2,1,0:T(8,128)(2,1)} %get-tuple-element.32), calls=%async_computation.2 | async-start | bytes 4194304 | tf_op jit(solution)/shard_map/all_to_all | solution.py:623
  43.4 4.0 %copy-start.5 = (s32[8]{0:T(128)}, s32[8]{0:T(128)S(1)}, u32[]{:S(2)}) copy-start(s32[8]{0:T(128)S(1)} %slice_reduce_fusion.2.totals_ref) | copy-start | bytes 100
  61.7 33.7 %copy-start.14 = (f32[64,2]{0,1:T(2,128)S(1)}, f32[64,2]{0,1:T(2,128)}, u32[]{:S(2)}) copy-start(f32[64,2]{0,1:T(2,128)} %param.22) | copy-start | bytes 1540
  61.7 33.9 %copy-start.12 = (bf16[4,128,128]{2,1,0:T(8,128)(2,1)S(1)}, bf16[4,128,128]{2,1,0:T(8,128)(2,1)}, u32[]{:S(2)}) copy-start(bf16[4,128,128]{2,1,0:T(8,128)(2,1)} %param.15) | copy-start | bytes 393220
  61.7 35.2 %copy-start.4 = (s32[128,128]{1,0:T(8,128)S(1)}, s32[128,128]{1,0:T(8,128)}, u32[]{:S(2)}) copy-start(s32[128,128]{1,0:T(8,128)} %decode.1) | copy-start | bytes 196612
  61.7 35.2 %copy-start.6 = (s32[8]{0:T(128)S(1)}, s32[8]{0:T(128)}, u32[]{:S(2)}) copy-start(s32[8]{0:T(128)} %copy-done.5) | copy-start | bytes 100
  91.1 52.2 %all-to-all-start.1 = ((bf16[8,1024,128]{2,1,0:T(8,128)(2,1)}), bf16[8,1024,128]{2,1,0:T(8,128)(2,1)}, u32[]{:S(2)}, u32[]{:S(2)}) async-start(bf16[8,1024,128]{2,1,0:T(8,128)(2,1)} %get-tuple-element.31), calls=%async_computation.1 | async-start | bytes 4194304 | tf_op jit(solution)/shard_map/all_to_all | solution.py:623
  127.2 5.7 %copy-start = (f32[32776,128]{1,0:T(8,128)}, f32[32776,128]{1,0:T(8,128)S(1)}, u32[]{:S(2)}) copy-start(f32[32776,128]{1,0:T(8,128)S(1)} %get-tuple-element.33.rest_0_) | copy-start | bytes 50343940
  143.2 5.8 %copy-start.1 = (f32[32776,128]{1,0:T(8,128)S(1)}, f32[32776,128]{1,0:T(8,128)}, u32[]{:S(2)}) copy-start(f32[32776,128]{1,0:T(8,128)} %copy-done) | copy-start | bytes 50343940
  158.0 46.4 %collective-permute-start = (f32[12288,128]{1,0:T(8,128)}, f32[12288,128]{1,0:T(8,128)}, u32[]{:S(2)}, u32[]{:S(2)}) collective-permute-start(f32[12288,128]{1,0:T(8,128)} %get-tuple-element.35), channel_id=1, source_target_pairs={{0,1},{1,0},{2,3},{3,2},{4,5},{5,4},{6,7},{7,6},{8,9},{9,8},{10,11... | collective-permute-start | bytes 18874376 | tf_op jit(solution)/shard_map/ppermute | solution.py:460
  158.0 11.8 %collective-permute-start.1 = (f32[4096,128]{1,0:T(8,128)S(1)}, f32[4096,128]{1,0:T(8,128)S(1)}, u32[]{:S(2)}, u32[]{:S(2)}) collective-permute-start(f32[4096,128]{1,0:T(8,128)S(1)} %get-tuple-element.36), channel_id=1, source_target_pairs={{0,1},{1,0},{2,3},{3,2},{4,5},{5,4},{6,7},{7,6},{8,9},{9,8},{10,11... | collective-permute-start | bytes 6291464 | tf_op jit(solution)/shard_map/ppermute | solution.py:460
  180.7 49.8 %all-to-all-start.3 = ((bf16[8,4,2,32,256]{4,3,2,1,0:T(8,128)(2,1)}), bf16[8,4,2,32,256]{4,3,2,1,0:T(8,128)(2,1)S(1)}, u32[]{:S(2)}, u32[]{:S(2)}) async-start(bf16[8,4,2,32,256]{4,3,2,1,0:T(8,128)(2,1)} %transform_planes.2), calls=%async_computation.3 | async-start | bytes 2097152 | tf_op jit(solution)/shard_map/all_to_all | solution.py:506
  228.7 79.2 %copy-start.13 = (s32[8]{0:T(128)S(1)}, s32[8]{0:T(128)}, u32[]{:S(2)}) copy-start(s32[8]{0:T(128)} %counts_ref.3) | copy-start | bytes 100
  231.5 75.8 %all-to-all-start.4 = ((bf16[8,12,2,32,256]{4,3,2,1,0:T(8,128)(2,1)}), bf16[8,12,2,32,256]{4,3,2,1,0:T(8,128)(2,1)S(1)}, u32[]{:S(2)}, u32[]{:S(2)}) async-start(bf16[8,12,2,32,256]{4,3,2,1,0:T(8,128)(2,1)} %transform_planes.3), calls=%async_computation.4 | async-start | bytes 6291456 | tf_op jit(solution)/shard_map/all_to_all | solution.py:506
  235.7 25.5 %collective-permute-start.2 = (f32[1,8]{1,0:T(1,128)S(1)}, f32[1,8]{1,0:T(1,128)S(1)}, u32[]{:S(2)}, u32[]{:S(2)}) collective-permute-start(f32[1,8]{1,0:T(1,128)S(1)} %get-tuple-element.50), channel_id=1, source_target_pairs={{0,2},{2,0},{4,6},{6,4},{8,10},{10,8},{12,14},{14,12},{1,3},{3,1},... | collective-permute-start | bytes 104 | tf_op jit(solution)/shard_map/ppermute | solution.py:443
  237.8 49.8 %collective-permute-start.3 = (f32[1,8]{1,0:T(1,128)S(1)}, f32[1,8]{1,0:T(1,128)S(1)}, u32[]{:S(2)}, u32[]{:S(2)}) collective-permute-start(f32[1,8]{1,0:T(1,128)S(1)} %get-tuple-element.56), channel_id=1, source_target_pairs={{0,4},{2,6},{4,0},{6,2},{8,12},{10,14},{12,8},{14,10},{1,5},{3,7},... | collective-permute-start | bytes 104 | tf_op jit(solution)/shard_map/ppermute | solution.py:443
  239.2 51.8 %collective-permute-start.4 = (f32[1,8]{1,0:T(1,128)S(1)}, f32[1,8]{1,0:T(1,128)S(1)}, u32[]{:S(2)}, u32[]{:S(2)}) collective-permute-start(f32[1,8]{1,0:T(1,128)S(1)} %get-tuple-element.55), channel_id=1, source_target_pairs={{0,6},{2,4},{4,2},{6,0},{8,14},{10,12},{12,10},{14,8},{1,7},{3,5},... | collective-permute-start | bytes 104 | tf_op jit(solution)/shard_map/ppermute | solution.py:443
  239.3 67.1 %collective-permute-start.5 = (f32[1,8]{1,0:T(1,128)S(1)}, f32[1,8]{1,0:T(1,128)S(1)}, u32[]{:S(2)}, u32[]{:S(2)}) collective-permute-start(f32[1,8]{1,0:T(1,128)S(1)} %get-tuple-element.54), channel_id=1, source_target_pairs={{0,8},{2,10},{4,12},{6,14},{8,0},{10,2},{12,4},{14,6},{1,9},{3,11}... | collective-permute-start | bytes 104 | tf_op jit(solution)/shard_map/ppermute | solution.py:443
  242.2 65.1 %collective-permute-start.6 = (f32[1,8]{1,0:T(1,128)S(1)}, f32[1,8]{1,0:T(1,128)S(1)}, u32[]{:S(2)}, u32[]{:S(2)}) collective-permute-start(f32[1,8]{1,0:T(1,128)S(1)} %get-tuple-element.53), channel_id=1, source_target_pairs={{0,10},{2,8},{4,14},{6,12},{8,2},{10,0},{12,6},{14,4},{1,11},{3,9}... | collective-permute-start | bytes 104 | tf_op jit(solution)/shard_map/ppermute | solution.py:443
  261.2 46.1 %collective-permute-start.7 = (f32[1,8]{1,0:T(1,128)S(1)}, f32[1,8]{1,0:T(1,128)S(1)}, u32[]{:S(2)}, u32[]{:S(2)}) collective-permute-start(f32[1,8]{1,0:T(1,128)S(1)} %get-tuple-element.52), channel_id=1, source_target_pairs={{0,12},{2,14},{4,8},{6,10},{8,4},{10,6},{12,0},{14,2},{1,13},{3,15... | collective-permute-start | bytes 104 | tf_op jit(solution)/shard_map/ppermute | solution.py:443
  287.5 19.7 %collective-permute-start.8 = (f32[1,8]{1,0:T(1,128)S(1)}, f32[1,8]{1,0:T(1,128)S(1)}, u32[]{:S(2)}, u32[]{:S(2)}) collective-permute-start(f32[1,8]{1,0:T(1,128)S(1)} %get-tuple-element.51), channel_id=1, source_target_pairs={{0,14},{2,12},{4,10},{6,8},{8,6},{10,4},{12,2},{14,0},{1,15},{3,13... | collective-permute-start | bytes 104 | tf_op jit(solution)/shard_map/ppermute | solution.py:443
  307.3 7.2 %copy-start.7 = (bf16[8,12,2,32,256]{4,3,2,1,0:T(8,128)(2,1)}, bf16[8,12,2,32,256]{4,3,2,1,0:T(8,128)(2,1)S(1)}, u32[]{:S(2)}) copy-start(bf16[8,12,2,32,256]{4,3,2,1,0:T(8,128)(2,1)S(1)} %all-to-all-done.4.refs_1_) | copy-start | bytes 9437188
  307.3 7.2 %collective-permute-start.10 = (bf16[8,12,2,32,256]{4,3,2,1,0:T(8,128)(2,1)S(1)}, bf16[8,12,2,32,256]{4,3,2,1,0:T(8,128)(2,1)S(1)}, u32[]{:S(2)}, u32[]{:S(2)}) collective-permute-start(bf16[8,12,2,32,256]{4,3,2,1,0:T(8,128)(2,1)S(1)} %all-to-all-done.4.refs_1_), channel_id=1, source_target_pairs={{0,1},{1,0},{2,3},{3,2},{4,5},{5,4},{6,7},{7,6},{8,9},{9,8},{10,11... | collective-permute-start | bytes 9437192 | tf_op jit(solution)/shard_map/ppermute | solution.py:509
  307.4 7.0 %collective-permute-start.9 = (bf16[8,4,2,32,256]{4,3,2,1,0:T(8,128)(2,1)}, bf16[8,4,2,32,256]{4,3,2,1,0:T(8,128)(2,1)S(1)}, u32[]{:S(2)}, u32[]{:S(2)}) collective-permute-start(bf16[8,4,2,32,256]{4,3,2,1,0:T(8,128)(2,1)} %copy-done.8), channel_id=1, source_target_pairs={{0,1},{1,0},{2,3},{3,2},{4,5},{5,4},{6,7},{7,6},{8,9},{9,8},{10,11... | collective-permute-start | bytes 3145736 | tf_op jit(solution)/shard_map/ppermute | solution.py:509
  (6 other events, 8.2 us)

commit v7 on v6

--- a/solution.py
+++ b/solution.py
@@ -10,35 +10,41 @@
 from jax.sharding import PartitionSpec as P
 
 LANES = 128
-TILE = 1024
-GROUP = 16
-VMEM_LIMIT = 56 * 1024 * 1024
+GROUP = 32
+UNUSED = 100
+MIB = 1024 * 1024
 
 SMEM_SPEC = pl.BlockSpec(memory_space=pltpu.SMEM)
 VMEM_SPEC = pl.BlockSpec(memory_space=pltpu.VMEM)
 ANY_SPEC = pl.BlockSpec(memory_space=pl.ANY)
 
 
-def params(**extra):
-    return pltpu.CompilerParams(vmem_limit_bytes=VMEM_LIMIT, **extra)
+def params(mib):
+    return pltpu.CompilerParams(vmem_limit_bytes=mib * MIB)
 
 
 def bits_of(count):
     return (count - 1).bit_length()
 
 
-def route_kernel(slabs, cap, local_bits, list_length, owner_ref, local_ref, kind_ref, counts_ref, target_ref, word_ref, totals_ref):
-    rows = owner_ref.shape[0]
+def route_kernel(slabs, cap, local_bits, owner_ref, local_ref, kind_ref, counts_ref, target_ref, word_ref, totals_ref):
+    particles, list_length = local_ref.shape
     rows_each = list_length // LANES
-    particles = rows // rows_each
+    rows = particles * rows_each
+    gathered = lambda ref: jnp.concatenate(
+        [ref[:, j * LANES:(j + 1) * LANES] for j in range(rows_each)], axis=0
+    )
     row_id = lax.broadcasted_iota(jnp.int32, (rows, LANES), 0)
     lane_id = lax.broadcasted_iota(jnp.int32, (rows, LANES), 1)
-    particle = row_id // rows_each
-    position = (row_id % rows_each) * LANES + lane_id
+    particle = row_id % particles
+    position = (row_id // particles) * LANES + lane_id
     limit = jnp.zeros((rows, LANES), jnp.int32)
     for i in range(particles):
         limit = jnp.where(particle == i, counts_ref[i], limit)
-    owner = jnp.where(position < limit, owner_ref[...], -1)
+    owner = jnp.concatenate(
+        [owner_ref[pl.ds(j, particles, stride=rows_each), :] for j in range(rows_each)], axis=0
+    )
+    owner = jnp.where(position < limit, owner, -1)
     up_to = (
         lax.broadcasted_iota(jnp.int32, (LANES, LANES), 0)
         <= lax.broadcasted_iota(jnp.int32, (LANES, LANES), 1)
@@ -58,17 +64,19 @@
         rank = (inside + above).astype(jnp.int32) - 1
         total = (above[rows - 1:rows, :] + row_sum[rows - 1:rows, :]).astype(jnp.int32)
         totals_ref[pl.ds(slab, 1), :] = total
-        return jnp.where(mine, slab * cap + rank, target)
-
-    target = lax.fori_loop(0, slabs, one_slab, jnp.full((rows, LANES), slabs * cap, jnp.int32))
+        return jnp.where(mine, slab * (cap + LANES) + rank, target)
+
+    target = lax.fori_loop(0, slabs, one_slab, jnp.full((rows, LANES), cap + UNUSED, jnp.int32))
     target_ref[...] = target
     kind_bits = local_bits
-    word = local_ref[...] | (kind_ref[...] << kind_bits) | (position << (kind_bits + 2))
+    word = gathered(local_ref) | (gathered(kind_ref) << kind_bits) | (position << (kind_bits + 2))
     word_ref[...] = word | (particle << (kind_bits + 2 + bits_of(list_length)))
 
 
-def pack_kernel(slabs, cap, list_length, target_ref, word_ref, counts_ref, image_ref, meta_ref, *refs):
+def pack_kernel(slabs, cap, list_length, target_ref, word_ref, counts_ref, totals_ref, code_ref, image_ref, meta_ref, *refs):
     out_refs, (wide_ref, staged_ref) = refs[:-2], refs[-2:]
+    particles = counts_ref.shape[0]
+    stride = cap + LANES
     step = 256
 
     @pl.loop(0, image_ref.shape[0] // step)
@@ -76,25 +84,36 @@
         at = pl.multiple_of(i * step, step)
         wide_ref[pl.ds(at, step), :] = image_ref[pl.ds(at, step), :].astype(jnp.float32)
 
-    @pl.loop(0, counts_ref.shape[0])
+    @pl.loop(0, particles)
     def _(particle):
         @pl.loop(0, (counts_ref[particle] + 15) // 16)
         def _(i):
-            first = particle * list_length + i * 16
+            first = (i // 8) * (particles * LANES) + particle * LANES + (i % 8) * 16
+            row = particle * list_length + i * 16
             targets = [target_ref[first + j] for j in range(16)]
-            rows = [wide_ref[pl.ds(first + j, 1), :] for j in range(16)]
             words = [word_ref[first + j] for j in range(16)]
+            rows = [wide_ref[pl.ds(row + j, 1), :] for j in range(16)]
             for j in range(16):
                 staged_ref[pl.ds(targets[j], 1), :] = rows[j]
                 meta_ref[targets[j]] = words[j]
 
-    for chunk, out_ref in enumerate(out_refs):
+    @pl.loop(0, slabs)
+    def _(slab):
+        header = slab * stride + cap
+        meta_ref[header] = totals_ref[slab, 0]
+        for j in range(particles):
+            meta_ref[header + 1 + j] = code_ref[j]
+
+    offset = 0
+    for out_ref in out_refs:
         width = out_ref.shape[1]
 
         @pl.loop(0, slabs)
-        def _(slab):
-            at = pl.multiple_of(slab * cap + chunk * width, width)
+        def _(slab, offset=offset):
+            at = pl.multiple_of(slab * stride + offset, LANES)
             out_ref[slab] = staged_ref[pl.ds(at, width), :].astype(jnp.bfloat16)
+
+        offset += width
 
 
 def decode_kernel(local_bits, dummy, word_ref, live_ref, index_ref):
@@ -111,7 +130,7 @@
     while shift < GROUP:
         clash = clash | pltpu.roll(clash, LANES - shift, 1)
         shift *= 2
-    index_ref[...] = index | (clash << 24)
+    index_ref[...] = index | jnp.where(lane % GROUP == 0, clash << 24, 0)
 
 
 def gather_kernel(slabs, cap, index_ref, totals_ref, volume_ref, *refs):
@@ -131,17 +150,20 @@
         @pl.loop(0, (live + 15) // 16)
         def _(i):
             first = source * cap + i * 16
-            places = [index_ref[first + j] & 0xFFFFFF for j in range(16)]
+            places = [index_ref[first] & 0xFFFFFF] + [index_ref[first + j] for j in range(1, 16)]
             rows = [wide_ref[pl.ds(places[j], 1), :] for j in range(16)]
             for j in range(16):
                 staged_ref[pl.ds(i * 16 + j, 1), :] = rows[j]
 
-        for chunk, out_ref in enumerate(out_refs):
+        offset = 0
+        for out_ref in out_refs:
             width = out_ref.shape[1]
 
-            @pl.when(live > chunk * width)
-            def _():
-                out_ref[source] = staged_ref[chunk * width:(chunk + 1) * width, :].astype(jnp.bfloat16)
+            @pl.when(live > offset)
+            def _(offset=offset):
+                out_ref[source] = staged_ref[offset:offset + width, :].astype(jnp.bfloat16)
+
+            offset += width
 
 
 def sine(angle):
@@ -240,7 +262,7 @@
         def _(g):
             base = source * cap + offset + g * GROUP
             marked = index_ref[base]
-            places = [index_ref[base + j] & 0xFFFFFF for j in range(GROUP)]
+            places = [marked & 0xFFFFFF] + [index_ref[base + j] for j in range(1, GROUP)]
 
             @pl.when(marked < (1 << 24))
             def _():
@@ -257,27 +279,35 @@
                     )
 
     if last:
-        half = blocks // 2
-        start = (1 - core_ref[0]) * half
-        places = [core_ref[0] * half]
-        for out_ref in out_refs[1:]:
-            places.append(start)
-            start = start + out_ref.shape[0]
-        copies = []
-        for i, (place, out_ref) in enumerate(zip(places, out_refs)):
-            length = out_ref.shape[0]
-            at = pl.multiple_of(place, 8)
-            copies.append(pltpu.make_async_copy(sum_ref.at[pl.ds(at, length)], out_ref, sems.at[i]))
-        for copy in copies:
-            copy.start()
-        for copy in copies:
-            copy.wait()
+        out_ref = out_refs[0]
+        at = pl.multiple_of((1 - core_ref[0]) * (blocks // 2), 8)
+        copy = pltpu.make_async_copy(sum_ref.at[pl.ds(at, out_ref.shape[0])], out_ref, sems.at[0])
+        copy.start()
+        copy.wait()
+
+
+def split_kernel(core_ref, sum_ref, *refs):
+    out_refs, sems = refs[:-1], refs[-1]
+    half = out_refs[0].shape[0]
+    places = [core_ref[0] * half]
+    start = (2 - core_ref[0]) * half
+    for out_ref in reversed(out_refs[1:]):
+        start = start - out_ref.shape[0]
+        places.insert(1, start)
+    copies = []
+    for i, (place, out_ref) in enumerate(zip(places, out_refs)):
+        at = pl.multiple_of(place, 8)
+        copies.append(pltpu.make_async_copy(sum_ref.at[pl.ds(at, out_ref.shape[0])], out_ref, sems.at[i]))
+    for copy in copies:
+        copy.start()
+    for copy in copies:
+        copy.wait()
 
 
 def pieces_of(planes):
     if planes < 16:
         return [planes]
-    return [4, planes - 4]
+    return [4, 4, planes - 8]
 
 
 def rotated(value, turn, length):
@@ -489,7 +519,7 @@
                 pltpu.VMEM((2 * side, 4 * side), jnp.bfloat16),
                 pltpu.VMEM((2 * side, 4 * side), jnp.bfloat16),
             ],
-            compiler_params=params(),
+            compiler_params=params(24),
             cost_estimate=pl.CostEstimate(
                 flops=held * 8 * side**3, bytes_accessed=held * 4 * side**2 * 8, transcendentals=0
             ),
@@ -519,7 +549,7 @@
         ],
         out_specs=pl.BlockSpec((2, side // 2, rows, LANES), lambda y, z: (0, 0, y, z)),
         scratch_shapes=[pltpu.VMEM((16, 16, 2, rows, LANES), jnp.float32)],
-        compiler_params=params(),
+        compiler_params=params(28),
         name="transform_first",
     )(lax.axis_index("dom").astype(jnp.int32).reshape(1), *arrays)
     return field, losses
@@ -539,43 +569,34 @@
     int_rows = jax.ShapeDtypeStruct((rows, LANES), jnp.int32)
 
     target, word, totals = pl.pallas_call(
-        functools.partial(route_kernel, slabs, cap, local_bits, list_length),
+        functools.partial(route_kernel, slabs, cap, local_bits),
         out_shape=(int_rows, int_rows, jax.ShapeDtypeStruct((slabs, LANES), jnp.int32)),
         in_specs=[VMEM_SPEC, VMEM_SPEC, VMEM_SPEC, SMEM_SPEC],
         out_specs=(VMEM_SPEC, VMEM_SPEC, VMEM_SPEC),
-        compiler_params=params(),
+        compiler_params=params(16),
         name="route",
-    )(
-        owners.reshape(rows, LANES), local_block.reshape(rows, LANES), kinds.reshape(rows, LANES), counts
-    )
+    )(owners.reshape(rows, LANES), local_block, kinds, counts)
     target, word = target.reshape(entries), word.reshape(entries)
-    parts = max(1, cap // TILE)
-    tile = cap // parts
+    tiles = [cap // 2, cap // 2] if cap >= 2048 else [cap]
+    parts = len(tiles)
+    code = ctf_code | ((scales.astype(jnp.float32) * 256.0).astype(jnp.int32) << 8)
+    stride = cap + LANES
     meta, *packed = pl.pallas_call(
         functools.partial(pack_kernel, slabs, cap, list_length),
-        out_shape=(jax.ShapeDtypeStruct((slots + 1024,), jnp.int32),)
-        + (jax.ShapeDtypeStruct((slabs, tile, features), jnp.bfloat16),) * parts,
-        in_specs=[SMEM_SPEC, SMEM_SPEC, SMEM_SPEC, VMEM_SPEC],
+        out_shape=(jax.ShapeDtypeStruct((slabs * stride,), jnp.int32),)
+        + tuple(jax.ShapeDtypeStruct((slabs, tile, features), jnp.bfloat16) for tile in tiles),
+        in_specs=[SMEM_SPEC] * 5 + [VMEM_SPEC],
         out_specs=(SMEM_SPEC,) + (VMEM_SPEC,) * parts,
         scratch_shapes=[
             pltpu.VMEM((entries, features), jnp.float32),
-            pltpu.VMEM((slots + 8, features), jnp.float32),
+            pltpu.VMEM((slabs * stride, features), jnp.float32),
         ],
-        compiler_params=params(),
+        compiler_params=params(32),
         name="pack",
-    )(target, word, counts, images.reshape(entries, features))
-
-    code = ctf_code | ((scales.astype(jnp.float32) * 256.0).astype(jnp.int32) << 8)
-    header = jnp.concatenate(
-        [
-            totals[:, 0:1],
-            jnp.broadcast_to(code[None, :], (slabs, particles)),
-            jnp.zeros((slabs, LANES - 1 - particles), jnp.int32),
-        ],
-        axis=1,
+    )(target, word, counts, totals, code, images.reshape(entries, features))
+    arrived = lax.all_to_all(
+        meta.reshape(slabs, stride), "slab", split_axis=0, concat_axis=0, tiled=True
     )
-    sent = jnp.concatenate([meta[:slots].reshape(slabs, cap), header], axis=1)
-    arrived = lax.all_to_all(sent, "slab", split_axis=0, concat_axis=0, tiled=True)
     words = arrived[:, :cap]
     totals_in = arrived[:, cap]
     codes_in = arrived[:, cap + 1:cap + 1 + particles]
@@ -588,21 +609,23 @@
         out_shape=jax.ShapeDtypeStruct((slots // LANES, LANES), jnp.int32),
         in_specs=[VMEM_SPEC, VMEM_SPEC],
         out_specs=VMEM_SPEC,
-        compiler_params=params(),
+        compiler_params=params(16),
         name="decode",
     )(words.reshape(slots // LANES, LANES), live.reshape(slots // LANES, LANES))
     index = index.reshape(slots)
     voxels = list(pl.pallas_call(
         functools.partial(gather_kernel, slabs, cap),
-        out_shape=(jax.ShapeDtypeStruct((slabs, tile, features), jnp.bfloat16),) * parts,
+        out_shape=tuple(
+            jax.ShapeDtypeStruct((slabs, tile, features), jnp.bfloat16) for tile in tiles
+        ),
         in_specs=[SMEM_SPEC, SMEM_SPEC, VMEM_SPEC],
         out_specs=(VMEM_SPEC,) * parts,
         scratch_shapes=[
             pltpu.VMEM((blocks + 8, features), jnp.float32),
             pltpu.VMEM((cap, features), jnp.float32),
         ],
-        compiler_params=params(),
-        cost_estimate=pl.CostEstimate(flops=0, bytes_accessed=100 * 1024 * 1024, transcendentals=0),
+        compiler_params=params(40),
+        cost_estimate=pl.CostEstimate(flops=0, bytes_accessed=100 * MIB, transcendentals=0),
         name="read_voxels",
     )(index, totals_in, volume))
 
@@ -613,27 +636,27 @@
     core = lax.axis_index("dom").astype(jnp.int32).reshape(1)
     plane_blocks = (side // 8) ** 2
     pieces = [planes * plane_blocks for planes in pieces_of(side // slabs // 2)]
-    squares, sums, behind = 0.0, None, [voxels[0]]
-    for part in range(parts):
+    squares, sums, behind, offset = 0.0, None, [voxels[0]], 0
+    for part, tile in enumerate(tiles):
         first, last = part == 0, part == parts - 1
         if not first:
             packed[part], earlier = lax.optimization_barrier((packed[part], behind[part - 1]))
             if part == 1:
                 voxels[0] = earlier
         picture = lax.all_to_all(packed[part], "slab", split_axis=0, concat_axis=0, tiled=True)
-        lengths = [blocks // 2] + pieces if last else []
+        lengths = pieces[:1] if last else []
         arguments = [
             totals_in, table_rows[:, 0], table_rows[:, 1], scale_in, index, core,
-            words[:, part * tile:(part + 1) * tile].reshape(slabs, 1, tile), voxels[part], picture,
+            words[:, offset:offset + tile].reshape(slabs, 1, tile), voxels[part], picture,
             forward, backward, unit,
         ]
         aliases = {}
         if not first:
             aliases = {len(arguments): 1}
             arguments.append(pltpu.with_memory_space_constraint(sums, pltpu.VMEM))
-        more, sums, *halves = pl.pallas_call(
+        more, sums, *first_piece = pl.pallas_call(
             functools.partial(
-                slab_kernel, side, local_bits, list_length, particles, cap, part * tile, first, last
+                slab_kernel, side, local_bits, list_length, particles, cap, offset, first, last
             ),
             out_shape=(
                 jax.ShapeDtypeStruct((slabs, particles, LANES), jnp.float32),
@@ -647,13 +670,25 @@
                 pltpu.SemaphoreType.DMA((max(1, len(lengths)),)),
             ],
             input_output_aliases=aliases,
-            compiler_params=pltpu.CompilerParams(vmem_limit_bytes=24 * 1024 * 1024),
-            cost_estimate=pl.CostEstimate(flops=0, bytes_accessed=16 * 1024 * 1024, transcendentals=0),
+            compiler_params=params(24),
+            cost_estimate=pl.CostEstimate(flops=0, bytes_accessed=16 * MIB, transcendentals=0),
             name="compare_and_add",
         )(*arguments)
         squares = squares + more
         behind.append(more)
-    mine, *theirs = halves
+        offset += tile
+    lengths = [blocks // 2] + pieces[1:]
+    mine, *theirs = pl.pallas_call(
+        split_kernel,
+        out_shape=tuple(jax.ShapeDtypeStruct((length, features), jnp.float32) for length in lengths),
+        in_specs=[SMEM_SPEC, VMEM_SPEC],
+        out_specs=(ANY_SPEC,) * len(lengths),
+        scratch_shapes=[pltpu.SemaphoreType.DMA((len(lengths),))],
+        compiler_params=params(16),
+        cost_estimate=pl.CostEstimate(flops=0, bytes_accessed=16 * MIB, transcendentals=0),
+        name="split_sums",
+    )(core, pltpu.with_memory_space_constraint(sums, pltpu.VMEM))
+    theirs = first_piece + theirs
     partial_sums = jnp.sum(squares, axis=2)
     return mine, theirs, partial_sums, side
 

time: 335 us -> 347 us (1.036)
  Pallas kernels: 119 us -> 153 us
  waiting for transfers between devices: 115 us -> 82.2 us
  local copies, waits for them, and re-layouts: 26.2 us -> 56.3 us
  starting transfers between devices: 51.5 us -> 34.6 us
    unnamed x32 -> x64, local copies, waits for them, and re-layouts: 19.6 us -> 54.9 us
    pallas_call x2, Pallas kernels: 36 us -> 65.6 us  [gradient_of_slab(): pl.pallas_call(functools.partial(slab_kernel, side, local_bits, list_leng...]
    ppermute x7, waiting for transfers between devices: 56.9 us -> 34.8 us  [sum_over_slabs(): lax.ppermute(row(i), 'slab', [(slab, slab ^ i) for slab in range(slabs)])]
    all_to_all x2, waiting for transfers between devices: 39.6 us -> 20.9 us  [gradient_of_slab(): lax.all_to_all(packed[part], 'slab', split_axis=0, concat_axis=0, tiled=T...]
    all_to_all x2 -> x3, waiting for transfers between devices: 1.83 us -> 20.2 us  [to_field(): got = lax.all_to_all(sent, 'slab', split_axis=0, concat_axis=0, tiled=True)]
    all_to_all x2 -> x3, starting transfers between devices: 27.7 us -> 11 us  [to_field(): got = lax.all_to_all(sent, 'slab', split_axis=0, concat_axis=0, tiled=True)]
    ppermute x2 -> x3, waiting for transfers between devices: 11.3 us -> 0.01 us  [to_field(): theirs = [lax.ppermute(chunk, 'dom', swap) for chunk in theirs_sent]]
    pallas_call x2 -> x3, Pallas kernels: 18.1 us -> 23.6 us  [the longest x1 17.5 us: gradient_of_slab(): pl.pallas_call(functools.partial(gather_kernel, slabs, cap), out_shape=tu...]
  transfers between devices with their start and end apart: 15 -> 18, of which waited for: 10 -> 9; matrix products, arithmetic and copies ran while one was open for 1% -> 1% of each run, Pallas kernels for 24% -> 27%
where the time goes in v7:
time: 347 us; the launch traced here: 343 us
  Pallas kernels  153 us (44%)
  waiting for transfers between devices  82.2 us (24%)
  local copies, waits for them, and re-layouts  56.3 us (16%)
  starting transfers between devices  34.6 us (10%)
  blocking collectives  14.4 us (4%)
    pallas_call x2, Pallas kernels, gradient_of_slab(): pl.pallas_call(functools.partial(slab_kernel, side, local_bits, list_leng...  65.6 us
    unnamed x64, local copies, waits for them, and re-layouts  54.9 us
    ppermute x7, waiting for transfers between devices, sum_over_slabs(): lax.ppermute(row(i), 'slab', [(slab, slab ^ i) for slab in range(slabs)])  34.8 us
    pallas_call x3, Pallas kernels, to_field(): pl.pallas_call(planes_kernel, grid=(quads, per_row // yblocks), out_shape...  31.2 us
    all_to_all x2, waiting for transfers between devices, gradient_of_slab(): lax.all_to_all(packed[part], 'slab', split_axis=0, concat_axis=0, tiled=T...  20.9 us
    all_to_all x3, waiting for transfers between devices, to_field(): got = lax.all_to_all(sent, 'slab', split_axis=0, concat_axis=0, tiled=True)  20.2 us
    pallas_call x1, Pallas kernels, gradient_of_slab(): pl.pallas_call(functools.partial(pack_kernel, slabs, cap, list_length), o...  18.1 us
    pallas_call x1, Pallas kernels, gradient_of_slab(): pl.pallas_call(functools.partial(gather_kernel, slabs, cap), out_shape=tu...  17.5 us
  transfers between devices with their start and end apart: 18, of which 9 were waited for; matrix products, arithmetic and copies ran while one was open for 1% of the time, Pallas kernels for 27%

profile of v7, /device:TPU:0, one launch (start us, length us, event | category | flops | bytes accessed | tf_op | source)
XLA Modules:
  0.0 343.2 jit_solution(5734559424566238678)
XLA Ops:
  9.3 18.1 %pack.1 = (s32[17408]{0:T(1024)S(1)}, bf16[8,1024,128]{2,1,0:T(8,128)(2,1)S(1)}, bf16[8,1024,128]{2,1,0:T(8,128)(2,1)S(1)}) custom-call(s32[8192]{0:T(1024)S(1)} %bitcast.43, s32[8192]{0:T(1024)S(1)} %bitcast.44, s32[8]{0:T(128)S(1)} %copy-done.27, s32[8,128]{1,0:T(8,128)S(1)} %get-tuple-element.31.totals_ref, s32[8]{0:T(128)S(1)} %shift-left_or_fusion.code_ref, ...), custom_call_target="tpu_custom_call" | custom-call | tf_op jit(solution)/shard_map/pack/pallas_call | solution.py:584
  30.1 14.4 %all_to_all.37 = s32[8,1,2176]{2,1,0:T(1,128)S(1)} all-to-all(s32[8,1,2176]{2,1,0:T(1,128)S(1)} %bitcast.42), channel_id=1, replica_groups=mesh['groups'=2,'slab'=8,'dom'=2] {'slab'}, dimensions={0} | all-to-all | bytes 139264 | tf_op jit(solution)/shard_map/all_to_all | solution.py:597
  44.6 3.6 %all-to-all-start.2 = ((bf16[8,1024,128]{2,1,0:T(8,128)(2,1)}), bf16[8,1024,128]{2,1,0:T(8,128)(2,1)S(1)}, u32[]{:S(2)}, u32[]{:S(2)}) async-start(bf16[8,1024,128]{2,1,0:T(8,128)(2,1)} %copy-done.18), calls=%async_computation.2 | async-start | bytes 4194304 | tf_op jit(solution)/shard_map/all_to_all | solution.py:646
  53.6 17.5 %read_voxels.1 = (bf16[8,1024,128]{2,1,0:T(8,128)(2,1)S(1)}, bf16[8,1024,128]{2,1,0:T(8,128)(2,1)S(1)}) custom-call(s32[16384]{0:T(1024)S(1)} %bitcast.39, s32[8]{0:T(128)S(1)} %slice_reduce_fusion.2.totals_ref, bf16[32768,128]{1,0:T(8,128)(2,1)S(1)} %copy-done.8), custom_call_target="tpu_custom_call" | custom-call | bytes 104857600 | tf_op jit(solution)/shard_map/read_voxels/pallas_call | solution.py:616
  73.8 20.9 %all-to-all-done.2.image_ref = bf16[8,1024,128]{2,1,0:T(8,128)(2,1)S(1)} async-done(((bf16[8,1024,128]{2,1,0:T(8,128)(2,1)}), bf16[8,1024,128]{2,1,0:T(8,128)(2,1)S(1)}, u32[]{:S(2)}, u32[]{:S(2)}) %all-to-all-start.2) | async-done | bytes 2097184 | tf_op jit(solution)/shard_map/all_to_all | solution.py:646
  94.7 4.4 %all-to-all-start.1 = ((bf16[8,1024,128]{2,1,0:T(8,128)(2,1)}), bf16[8,1024,128]{2,1,0:T(8,128)(2,1)}, u32[]{:S(2)}, u32[]{:S(2)}) async-start(bf16[8,1024,128]{2,1,0:T(8,128)(2,1)} %copy-done.15), calls=%async_computation.1 | async-start | bytes 4194304 | tf_op jit(solution)/shard_map/all_to_all | solution.py:646
  102.2 40.3 %compare_and_add.2 = (f32[8,8,128]{2,1,0:T(8,128)S(1)}, f32[32776,128]{1,0:T(8,128)S(1)}) custom-call(s32[8]{0:T(128)S(1)} %slice_reduce_fusion.2.totals_ref, f32[64]{0:T(128)S(1)} %get-tuple-element.57.defocus_ref, f32[64]{0:T(128)S(1)} %get-tuple-element.56.phase_ref, f32[64]{0:T(128)S(1)} %mul.17.scale_ref, s32[16384]{0:T(1024)S(1)} %bitcast.40, ...), custom_call_target="tpu_custom_call" | custom-call | bytes 16777216 | tf_op jit(solution)/shard_map/compare_and_add/pallas_call | solution.py:657
  142.4 5.8 %copy-done.3 = f32[32776,128]{1,0:T(8,128)} copy-done((f32[32776,128]{1,0:T(8,128)}, f32[32776,128]{1,0:T(8,128)S(1)}, u32[]{:S(2)}) %copy-start.3) | copy-done | bytes 16781336
  148.2 5.8 %copy-done.4 = f32[32776,128]{1,0:T(8,128)S(1)} copy-done((f32[32776,128]{1,0:T(8,128)S(1)}, f32[32776,128]{1,0:T(8,128)}, u32[]{:S(2)}) %copy-start.4) | copy-done | bytes 16781336
  155.6 25.4 %compare_and_add.3 = (f32[8,8,128]{2,1,0:T(8,128)S(1)}, f32[32776,128]{1,0:T(8,128)S(1)}, f32[4096,128]{1,0:T(8,128)S(1)}) custom-call(s32[8]{0:T(128)S(1)} %slice_reduce_fusion.2.totals_ref, f32[64]{0:T(128)S(1)} %get-tuple-element.57.defocus_ref, f32[64]{0:T(128)S(1)} %get-tuple-element.56.phase_ref, ...), custom_call_target="tpu_custom_call", output_to_operand_aliasing={{1}: (12, {})} | custom-call | bytes 16777216 | tf_op jit(solution)/shard_map/compare_and_add/pallas_call | solution.py:657
  181.0 5.8 %copy-done.5 = f32[32776,128]{1,0:T(8,128)} copy-done((f32[32776,128]{1,0:T(8,128)}, f32[32776,128]{1,0:T(8,128)S(1)}, u32[]{:S(2)}) %copy-start.5) | copy-done | bytes 16781336
  186.7 5.8 %copy-done.6 = f32[32776,128]{1,0:T(8,128)S(1)} copy-done((f32[32776,128]{1,0:T(8,128)S(1)}, f32[32776,128]{1,0:T(8,128)}, u32[]{:S(2)}) %copy-start.6) | copy-done | bytes 16781336
  196.4 8.1 %transform_planes.3 = bf16[8,4,2,32,256]{4,3,2,1,0:T(8,128)(2,1)} custom-call(f32[16,32,32,128]{3,2,1,0:T(8,128)S(1)} %bitcast.30, f32[4,32,32,128]{3,2,1,0:T(8,128)S(1)} %bitcast.34, bf16[384,256]{1,0:T(8,128)(2,1)S(1)} %copy-done.21, f32[2,8,128]{2,1,0:T(8,128)S(1)} %copy-done.22, bf16[512,512]{1,0:T(8,128)(2,1)S(1)} %copy-done.9, ...), custom_call_target="tpu_custom_call" | custom-call | flops 536870912 | bytes 8388608 | tf_op jit(solution)/shard_map/transform_planes/pallas_call | solution.py:509
  214.8 8.0 %transform_planes.4 = bf16[8,4,2,32,256]{4,3,2,1,0:T(8,128)(2,1)S(1)} custom-call(f32[16,32,32,128]{3,2,1,0:T(8,128)S(1)} %bitcast.31, f32[4,32,32,128]{3,2,1,0:T(8,128)} %bitcast.18.theirs_ref, bf16[384,256]{1,0:T(8,128)(2,1)S(1)} %copy-done.21, f32[2,8,128]{2,1,0:T(8,128)S(1)} %copy-done.22, bf16[512,512]{1,0:T(8,128)(2,1)S(1)} %copy-done.9, ...), custom_call_target="tpu_custom_call" | custom-call | flops 536870912 | bytes 8388608 | tf_op jit(solution)/shard_map/transform_planes/pallas_call | solution.py:509
  223.8 14.2 %all-to-all-done.3.refs_0_ = bf16[8,4,2,32,256]{4,3,2,1,0:T(8,128)(2,1)S(1)} async-done(((bf16[8,4,2,32,256]{4,3,2,1,0:T(8,128)(2,1)}), bf16[8,4,2,32,256]{4,3,2,1,0:T(8,128)(2,1)S(1)}, u32[]{:S(2)}, u32[]{:S(2)}) %all-to-all-start.3) | async-done | bytes 1048608 | tf_op jit(solution)/shard_map/all_to_all | solution.py:536
  238.0 3.6 %all-to-all-start.4 = ((bf16[8,4,2,32,256]{4,3,2,1,0:T(8,128)(2,1)}), bf16[8,4,2,32,256]{4,3,2,1,0:T(8,128)(2,1)S(1)}, u32[]{:S(2)}, u32[]{:S(2)}) async-start(bf16[8,4,2,32,256]{4,3,2,1,0:T(8,128)(2,1)} %copy-done.13), calls=%async_computation.4 | async-start | bytes 2097152 | tf_op jit(solution)/shard_map/all_to_all | solution.py:536
  245.1 15.2 %transform_planes.5 = bf16[8,8,2,32,256]{4,3,2,1,0:T(8,128)(2,1)S(1)} custom-call(f32[16,32,32,128]{3,2,1,0:T(8,128)S(1)} %bitcast.32, f32[8,32,32,128]{3,2,1,0:T(8,128)} %bitcast.19.theirs_ref, bf16[384,256]{1,0:T(8,128)(2,1)S(1)} %copy-done.21, f32[2,8,128]{2,1,0:T(8,128)S(1)} %copy-done.22, bf16[512,512]{1,0:T(8,128)(2,1)S(1)} %copy-done.9, ...), custom_call_target="tpu_custom_call" | custom-call | flops 1073741824 | bytes 16777216 | tf_op jit(solution)/shard_map/transform_planes/pallas_call | solution.py:509
  261.6 6.0 %all-to-all-done.4.refs_1_ = bf16[8,4,2,32,256]{4,3,2,1,0:T(8,128)(2,1)S(1)} async-done(((bf16[8,4,2,32,256]{4,3,2,1,0:T(8,128)(2,1)}), bf16[8,4,2,32,256]{4,3,2,1,0:T(8,128)(2,1)S(1)}, u32[]{:S(2)}, u32[]{:S(2)}) %all-to-all-start.4) | async-done | bytes 1048608 | tf_op jit(solution)/shard_map/all_to_all | solution.py:536
  268.6 3.8 %all-to-all-start.5 = ((bf16[8,8,2,32,256]{4,3,2,1,0:T(8,128)(2,1)}), bf16[8,8,2,32,256]{4,3,2,1,0:T(8,128)(2,1)S(1)}, u32[]{:S(2)}, u32[]{:S(2)}) async-start(bf16[8,8,2,32,256]{4,3,2,1,0:T(8,128)(2,1)} %copy-done.7), calls=%async_computation.5 | async-start | bytes 4194304 | tf_op jit(solution)/shard_map/all_to_all | solution.py:536
  280.2 9.3 %collective-permute-done.3 = f32[1,8]{1,0:T(1,128)S(1)} collective-permute-done((f32[1,8]{1,0:T(1,128)S(1)}, f32[1,8]{1,0:T(1,128)S(1)}, u32[]{:S(2)}, u32[]{:S(2)}) %collective-permute-start.3) | collective-permute-done | bytes 64 | tf_op jit(solution)/shard_map/ppermute | solution.py:473
  292.8 14.8 %collective-permute-done.4 = f32[1,8]{1,0:T(1,128)S(1)} collective-permute-done((f32[1,8]{1,0:T(1,128)S(1)}, f32[1,8]{1,0:T(1,128)S(1)}, u32[]{:S(2)}, u32[]{:S(2)}) %collective-permute-start.4) | collective-permute-done | bytes 64 | tf_op jit(solution)/shard_map/ppermute | solution.py:473
  311.0 9.8 %collective-permute-done.6 = f32[1,8]{1,0:T(1,128)S(1)} collective-permute-done((f32[1,8]{1,0:T(1,128)S(1)}, f32[1,8]{1,0:T(1,128)S(1)}, u32[]{:S(2)}, u32[]{:S(2)}) %collective-permute-start.6) | collective-permute-done | bytes 64 | tf_op jit(solution)/shard_map/ppermute | solution.py:473
  322.8 6.0 %collective-permute-done.10.refs_3_ = bf16[8,4,2,32,256]{4,3,2,1,0:T(8,128)(2,1)S(1)} collective-permute-done((bf16[8,4,2,32,256]{4,3,2,1,0:T(8,128)(2,1)S(1)}, bf16[8,4,2,32,256]{4,3,2,1,0:T(8,128)(2,1)S(1)}, u32[]{:S(2)}, u32[]{:S(2)}) %collective-permute-start.10) | collective-permute-done | bytes 1048608 | tf_op jit(solution)/shard_map/ppermute | solution.py:539
  330.3 12.9 %transform_first.1 = f32[2,128,32,256]{3,2,1,0:T(8,128)} custom-call(s32[1]{0:T(128)} %bitcast.core_ref, bf16[8,4,2,32,256]{4,3,2,1,0:T(8,128)(2,1)S(1)} %all-to-all-done.3.refs_0_, bf16[8,4,2,32,256]{4,3,2,1,0:T(8,128)(2,1)S(1)} %copy-done.12, bf16[8,8,2,32,256]{4,3,2,1,0:T(8,128)(2,1)S(1)} %all-to-all-done.5.refs_2_, ...), custom_call_target="tpu_custom_call" | custom-call | tf_op jit(solution)/shard_map/transform_first/pallas_call | solution.py:542
  (114 shorter events, 62.8 us)
Async XLA Ops:
  44.6 50.1 %all-to-all-start.2 = ((bf16[8,1024,128]{2,1,0:T(8,128)(2,1)}), bf16[8,1024,128]{2,1,0:T(8,128)(2,1)S(1)}, u32[]{:S(2)}, u32[]{:S(2)}) async-start(bf16[8,1024,128]{2,1,0:T(8,128)(2,1)} %copy-done.18), calls=%async_computation.2 | async-start | bytes 4194304 | tf_op jit(solution)/shard_map/all_to_all | solution.py:646
  73.8 25.3 %copy-start.30 = (f32[64,2]{0,1:T(2,128)S(1)}, f32[64,2]{0,1:T(2,128)}, u32[]{:S(2)}) copy-start(f32[64,2]{0,1:T(2,128)} %param.22) | copy-start | bytes 1540
  73.8 25.4 %copy-start.29 = (bf16[4,128,128]{2,1,0:T(8,128)(2,1)S(1)}, bf16[4,128,128]{2,1,0:T(8,128)(2,1)}, u32[]{:S(2)}) copy-start(bf16[4,128,128]{2,1,0:T(8,128)(2,1)} %param.15) | copy-start | bytes 393220
  94.7 53.5 %all-to-all-start.1 = ((bf16[8,1024,128]{2,1,0:T(8,128)(2,1)}), bf16[8,1024,128]{2,1,0:T(8,128)(2,1)}, u32[]{:S(2)}, u32[]{:S(2)}) async-start(bf16[8,1024,128]{2,1,0:T(8,128)(2,1)} %copy-done.15), calls=%async_computation.1 | async-start | bytes 4194304 | tf_op jit(solution)/shard_map/all_to_all | solution.py:646
  142.4 5.8 %copy-start.3 = (f32[32776,128]{1,0:T(8,128)}, f32[32776,128]{1,0:T(8,128)S(1)}, u32[]{:S(2)}) copy-start(f32[32776,128]{1,0:T(8,128)S(1)} %get-tuple-element.38.rest_0_) | copy-start | bytes 50343940
  148.2 5.8 %copy-start.4 = (f32[32776,128]{1,0:T(8,128)S(1)}, f32[32776,128]{1,0:T(8,128)}, u32[]{:S(2)}) copy-start(f32[32776,128]{1,0:T(8,128)} %copy-done.3) | copy-start | bytes 50343940
  186.7 9.7 %collective-permute-start.1 = (f32[4096,128]{1,0:T(8,128)S(1)}, f32[4096,128]{1,0:T(8,128)S(1)}, u32[]{:S(2)}, u32[]{:S(2)}) collective-permute-start(f32[4096,128]{1,0:T(8,128)S(1)} %get-tuple-element.42), channel_id=1, source_target_pairs={{0,1},{1,0},{2,3},{3,2},{4,5},{5,4},{6,7},{7,6},{8,9},{9,8},{10,11... | collective-permute-start | bytes 6291464 | tf_op jit(solution)/shard_map/ppermute | solution.py:490
  186.7 5.8 %copy-start.6 = (f32[32776,128]{1,0:T(8,128)S(1)}, f32[32776,128]{1,0:T(8,128)}, u32[]{:S(2)}) copy-start(f32[32776,128]{1,0:T(8,128)} %copy-done.5) | copy-start | bytes 50343940
  195.7 46.0 %collective-permute-start.2 = (f32[8192,128]{1,0:T(8,128)}, f32[8192,128]{1,0:T(8,128)}, u32[]{:S(2)}, u32[]{:S(2)}) collective-permute-start(f32[8192,128]{1,0:T(8,128)} %get-tuple-element.45), channel_id=1, source_target_pairs={{0,1},{1,0},{2,3},{3,2},{4,5},{5,4},{6,7},{7,6},{8,9},{9,8},{10,11... | collective-permute-start | bytes 12582920 | tf_op jit(solution)/shard_map/ppermute | solution.py:490
  196.3 15.1 %collective-permute-start = (f32[4096,128]{1,0:T(8,128)}, f32[4096,128]{1,0:T(8,128)}, u32[]{:S(2)}, u32[]{:S(2)}) collective-permute-start(f32[4096,128]{1,0:T(8,128)} %get-tuple-element.41), channel_id=1, source_target_pairs={{0,1},{1,0},{2,3},{3,2},{4,5},{5,4},{6,7},{7,6},{8,9},{9,8},{10,11... | collective-permute-start | bytes 6291464 | tf_op jit(solution)/shard_map/ppermute | solution.py:490
  207.9 30.1 %all-to-all-start.3 = ((bf16[8,4,2,32,256]{4,3,2,1,0:T(8,128)(2,1)}), bf16[8,4,2,32,256]{4,3,2,1,0:T(8,128)(2,1)S(1)}, u32[]{:S(2)}, u32[]{:S(2)}) async-start(bf16[8,4,2,32,256]{4,3,2,1,0:T(8,128)(2,1)} %transform_planes.3), calls=%async_computation.3 | async-start | bytes 2097152 | tf_op jit(solution)/shard_map/all_to_all | solution.py:536
  238.0 29.6 %all-to-all-start.4 = ((bf16[8,4,2,32,256]{4,3,2,1,0:T(8,128)(2,1)}), bf16[8,4,2,32,256]{4,3,2,1,0:T(8,128)(2,1)S(1)}, u32[]{:S(2)}, u32[]{:S(2)}) async-start(bf16[8,4,2,32,256]{4,3,2,1,0:T(8,128)(2,1)} %copy-done.13), calls=%async_computation.4 | async-start | bytes 2097152 | tf_op jit(solution)/shard_map/all_to_all | solution.py:536
  261.6 60.7 %copy-start.28 = (s32[8]{0:T(128)S(1)}, s32[8]{0:T(128)}, u32[]{:S(2)}) copy-start(s32[8]{0:T(128)} %counts_ref.3) | copy-start | bytes 100
  268.6 53.0 %all-to-all-start.5 = ((bf16[8,8,2,32,256]{4,3,2,1,0:T(8,128)(2,1)}), bf16[8,8,2,32,256]{4,3,2,1,0:T(8,128)(2,1)S(1)}, u32[]{:S(2)}, u32[]{:S(2)}) async-start(bf16[8,8,2,32,256]{4,3,2,1,0:T(8,128)(2,1)} %copy-done.7), calls=%async_computation.5 | async-start | bytes 4194304 | tf_op jit(solution)/shard_map/all_to_all | solution.py:536
  272.4 17.1 %collective-permute-start.3 = (f32[1,8]{1,0:T(1,128)S(1)}, f32[1,8]{1,0:T(1,128)S(1)}, u32[]{:S(2)}, u32[]{:S(2)}) collective-permute-start(f32[1,8]{1,0:T(1,128)S(1)} %get-tuple-element.60), channel_id=1, source_target_pairs={{0,2},{2,0},{4,6},{6,4},{8,10},{10,8},{12,14},{14,12},{1,3},{3,1},... | collective-permute-start | bytes 104 | tf_op jit(solution)/shard_map/ppermute | solution.py:473
  274.3 33.3 %collective-permute-start.4 = (f32[1,8]{1,0:T(1,128)S(1)}, f32[1,8]{1,0:T(1,128)S(1)}, u32[]{:S(2)}, u32[]{:S(2)}) collective-permute-start(f32[1,8]{1,0:T(1,128)S(1)} %get-tuple-element.66), channel_id=1, source_target_pairs={{0,4},{2,6},{4,0},{6,2},{8,12},{10,14},{12,8},{14,10},{1,5},{3,7},... | collective-permute-start | bytes 104 | tf_op jit(solution)/shard_map/ppermute | solution.py:473
  275.8 35.2 %collective-permute-start.5 = (f32[1,8]{1,0:T(1,128)S(1)}, f32[1,8]{1,0:T(1,128)S(1)}, u32[]{:S(2)}, u32[]{:S(2)}) collective-permute-start(f32[1,8]{1,0:T(1,128)S(1)} %get-tuple-element.65), channel_id=1, source_target_pairs={{0,6},{2,4},{4,2},{6,0},{8,14},{10,12},{12,10},{14,8},{1,7},{3,5},... | collective-permute-start | bytes 104 | tf_op jit(solution)/shard_map/ppermute | solution.py:473
  276.0 44.8 %collective-permute-start.6 = (f32[1,8]{1,0:T(1,128)S(1)}, f32[1,8]{1,0:T(1,128)S(1)}, u32[]{:S(2)}, u32[]{:S(2)}) collective-permute-start(f32[1,8]{1,0:T(1,128)S(1)} %get-tuple-element.64), channel_id=1, source_target_pairs={{0,8},{2,10},{4,12},{6,14},{8,0},{10,2},{12,4},{14,6},{1,9},{3,11}... | collective-permute-start | bytes 104 | tf_op jit(solution)/shard_map/ppermute | solution.py:473
  278.7 42.9 %collective-permute-start.7 = (f32[1,8]{1,0:T(1,128)S(1)}, f32[1,8]{1,0:T(1,128)S(1)}, u32[]{:S(2)}, u32[]{:S(2)}) collective-permute-start(f32[1,8]{1,0:T(1,128)S(1)} %get-tuple-element.63), channel_id=1, source_target_pairs={{0,10},{2,8},{4,14},{6,12},{8,2},{10,0},{12,6},{14,4},{1,11},{3,9}... | collective-permute-start | bytes 104 | tf_op jit(solution)/shard_map/ppermute | solution.py:473
  289.5 32.1 %collective-permute-start.8 = (f32[1,8]{1,0:T(1,128)S(1)}, f32[1,8]{1,0:T(1,128)S(1)}, u32[]{:S(2)}, u32[]{:S(2)}) collective-permute-start(f32[1,8]{1,0:T(1,128)S(1)} %get-tuple-element.62), channel_id=1, source_target_pairs={{0,12},{2,14},{4,8},{6,10},{8,4},{10,6},{12,0},{14,2},{1,13},{3,15... | collective-permute-start | bytes 104 | tf_op jit(solution)/shard_map/ppermute | solution.py:473
  307.6 14.0 %collective-permute-start.9 = (f32[1,8]{1,0:T(1,128)S(1)}, f32[1,8]{1,0:T(1,128)S(1)}, u32[]{:S(2)}, u32[]{:S(2)}) collective-permute-start(f32[1,8]{1,0:T(1,128)S(1)} %get-tuple-element.61), channel_id=1, source_target_pairs={{0,14},{2,12},{4,10},{6,8},{8,6},{10,4},{12,2},{14,0},{1,15},{3,13... | collective-permute-start | bytes 104 | tf_op jit(solution)/shard_map/ppermute | solution.py:473
  321.6 7.4 %collective-permute-start.12 = (bf16[8,8,2,32,256]{4,3,2,1,0:T(8,128)(2,1)S(1)}, bf16[8,8,2,32,256]{4,3,2,1,0:T(8,128)(2,1)S(1)}, u32[]{:S(2)}, u32[]{:S(2)}) collective-permute-start(bf16[8,8,2,32,256]{4,3,2,1,0:T(8,128)(2,1)S(1)} %all-to-all-done.5.refs_2_), channel_id=1, source_target_pairs={{0,1},{1,0},{2,3},{3,2},{4,5},{5,4},{6,7},{7,6},{8,9},{9,8},{10,11... | collective-permute-start | bytes 6291464 | tf_op jit(solution)/shard_map/ppermute | solution.py:539
  321.7 7.1 %collective-permute-start.10 = (bf16[8,4,2,32,256]{4,3,2,1,0:T(8,128)(2,1)S(1)}, bf16[8,4,2,32,256]{4,3,2,1,0:T(8,128)(2,1)S(1)}, u32[]{:S(2)}, u32[]{:S(2)}) collective-permute-start(bf16[8,4,2,32,256]{4,3,2,1,0:T(8,128)(2,1)S(1)} %all-to-all-done.3.refs_0_), channel_id=1, source_target_pairs={{0,1},{1,0},{2,3},{3,2},{4,5},{5,4},{6,7},{7,6},{8,9},{9,8},{10,11... | collective-permute-start | bytes 3145736 | tf_op jit(solution)/shard_map/ppermute | solution.py:539
  322.2 6.9 %collective-permute-start.11 = (bf16[8,4,2,32,256]{4,3,2,1,0:T(8,128)(2,1)}, bf16[8,4,2,32,256]{4,3,2,1,0:T(8,128)(2,1)S(1)}, u32[]{:S(2)}, u32[]{:S(2)}) collective-permute-start(bf16[8,4,2,32,256]{4,3,2,1,0:T(8,128)(2,1)} %copy-done.11), channel_id=1, source_target_pairs={{0,1},{1,0},{2,3},{3,2},{4,5},{5,4},{6,7},{7,6},{8,9},{9,8},{10,11... | collective-permute-start | bytes 3145736 | tf_op jit(solution)/shard_map/ppermute | solution.py:539
  (25 other events, 53.1 us)

commit v8 on v7

--- a/solution.py
+++ b/solution.py
@@ -10,7 +10,7 @@
 from jax.sharding import PartitionSpec as P
 
 LANES = 128
-GROUP = 32
+GROUP = 16
 UNUSED = 100
 MIB = 1024 * 1024
 
@@ -279,35 +279,27 @@
                     )
 
     if last:
-        out_ref = out_refs[0]
-        at = pl.multiple_of((1 - core_ref[0]) * (blocks // 2), 8)
-        copy = pltpu.make_async_copy(sum_ref.at[pl.ds(at, out_ref.shape[0])], out_ref, sems.at[0])
-        copy.start()
-        copy.wait()
-
-
-def split_kernel(core_ref, sum_ref, *refs):
-    out_refs, sems = refs[:-1], refs[-1]
-    half = out_refs[0].shape[0]
-    places = [core_ref[0] * half]
-    start = (2 - core_ref[0]) * half
-    for out_ref in reversed(out_refs[1:]):
-        start = start - out_ref.shape[0]
-        places.insert(1, start)
-    copies = []
-    for i, (place, out_ref) in enumerate(zip(places, out_refs)):
-        at = pl.multiple_of(place, 8)
-        copies.append(pltpu.make_async_copy(sum_ref.at[pl.ds(at, out_ref.shape[0])], out_ref, sems.at[i]))
-    for copy in copies:
-        copy.start()
-    for copy in copies:
-        copy.wait()
+        half = blocks // 2
+        start = (1 - core_ref[0]) * half
+        places = [core_ref[0] * half]
+        for out_ref in out_refs[1:]:
+            places.append(start)
+            start = start + out_ref.shape[0]
+        copies = []
+        for i, (place, out_ref) in enumerate(zip(places, out_refs)):
+            length = out_ref.shape[0]
+            at = pl.multiple_of(place, 8)
+            copies.append(pltpu.make_async_copy(sum_ref.at[pl.ds(at, length)], out_ref, sems.at[i]))
+        for copy in copies:
+            copy.start()
+        for copy in copies:
+            copy.wait()
 
 
 def pieces_of(planes):
     if planes < 16:
         return [planes]
-    return [4, 4, planes - 8]
+    return [4, planes - 4]
 
 
 def rotated(value, turn, length):
@@ -360,7 +352,7 @@
     groups, side = out_ref.shape[0], out_ref.shape[4]
     height = side // groups
 
-    @pl.loop(0, count, unroll=4)
+    @pl.loop(0, count, unroll=8)
     def _(i):
         block = (mine_ref[:, i] + theirs_ref[:, i]).reshape(LANES, LANES)
         high, low = in_halves(block.T)
@@ -411,34 +403,39 @@
     is_first = core == 0
     sign = (1 - 2 * core).astype(jnp.float32)
 
-    def plane(x):
+    rows = out_ref.shape[2]
+    strips = [slice(at, min(at + 8, rows)) for at in range(0, rows, 8)]
+
+    def plane(x, strip):
         slab, rest = x // (2 * each), x % (2 * each)
         half, inner = rest // each, rest % each
+        chunk, at = spots[inner]
         loaded = []
         for part in range(2):
-            chunk, at = spots[inner]
-            here = own[chunk][slab, at, part].astype(jnp.float32)
-            there = other[chunk][slab, at, part].astype(jnp.float32)
-            loaded.append(jnp.where(is_first, here, there) if half == 0 else jnp.where(is_first, there, here))
+            here, there = own[chunk][slab, at, part], other[chunk][slab, at, part]
+            value = jnp.where(is_first, here, there) if half == 0 else jnp.where(is_first, there, here)
+            loaded.append(value.astype(jnp.float32)[strip])
         return tuple(loaded)
 
     for low in range(16):
-        values = small_dft([plane(low + 16 * high) for high in range(16)])
-        for k in range(16):
-            real, imag = rotated(values[k], low * k, 256)
-            if low % 2:
-                real, imag = real * sign, imag * sign
-            mid_ref[k, low, 0] = real
-            mid_ref[k, low, 1] = imag
+        for strip in strips:
+            values = small_dft([plane(low + 16 * high, strip) for high in range(16)])
+            for k in range(16):
+                real, imag = rotated(values[k], low * k, 256)
+                if low % 2:
+                    real, imag = real * sign, imag * sign
+                mid_ref[k, low, 0, strip] = real
+                mid_ref[k, low, 1, strip] = imag
 
     @pl.loop(0, 16)
     def _(k):
-        values = [(mid_ref[k, low, 0], mid_ref[k, low, 1]) for low in range(16)]
-        even, odd = small_dft(values[0::2]), small_dft(values[1::2])
-        for m in range(8):
-            turned = rotated(odd[m], m, 16)
-            out_ref[0, k + 16 * m] = even[m][0] + turned[0]
-            out_ref[1, k + 16 * m] = even[m][1] + turned[1]
+        for strip in strips:
+            values = [(mid_ref[k, low, 0, strip], mid_ref[k, low, 1, strip]) for low in range(16)]
+            even, odd = small_dft(values[0::2]), small_dft(values[1::2])
+            for m in range(8):
+                turned = rotated(odd[m], m, 16)
+                out_ref[0, k + 16 * m, strip] = even[m][0] + turned[0]
+                out_ref[1, k + 16 * m, strip] = even[m][1] + turned[1]
 
 
 def host_halves(table):
@@ -519,7 +516,7 @@
                 pltpu.VMEM((2 * side, 4 * side), jnp.bfloat16),
                 pltpu.VMEM((2 * side, 4 * side), jnp.bfloat16),
             ],
-            compiler_params=params(24),
+            compiler_params=params(56),
             cost_estimate=pl.CostEstimate(
                 flops=held * 8 * side**3, bytes_accessed=held * 4 * side**2 * 8, transcendentals=0
             ),
@@ -549,7 +546,7 @@
         ],
         out_specs=pl.BlockSpec((2, side // 2, rows, LANES), lambda y, z: (0, 0, y, z)),
         scratch_shapes=[pltpu.VMEM((16, 16, 2, rows, LANES), jnp.float32)],
-        compiler_params=params(28),
+        compiler_params=params(56),
         name="transform_first",
     )(lax.axis_index("dom").astype(jnp.int32).reshape(1), *arrays)
     return field, losses
@@ -573,7 +570,7 @@
         out_shape=(int_rows, int_rows, jax.ShapeDtypeStruct((slabs, LANES), jnp.int32)),
         in_specs=[VMEM_SPEC, VMEM_SPEC, VMEM_SPEC, SMEM_SPEC],
         out_specs=(VMEM_SPEC, VMEM_SPEC, VMEM_SPEC),
-        compiler_params=params(16),
+        compiler_params=params(56),
         name="route",
     )(owners.reshape(rows, LANES), local_block, kinds, counts)
     target, word = target.reshape(entries), word.reshape(entries)
@@ -591,7 +588,7 @@
             pltpu.VMEM((entries, features), jnp.float32),
             pltpu.VMEM((slabs * stride, features), jnp.float32),
         ],
-        compiler_params=params(32),
+        compiler_params=params(56),
         name="pack",
     )(target, word, counts, totals, code, images.reshape(entries, features))
     arrived = lax.all_to_all(
@@ -609,7 +606,7 @@
         out_shape=jax.ShapeDtypeStruct((slots // LANES, LANES), jnp.int32),
         in_specs=[VMEM_SPEC, VMEM_SPEC],
         out_specs=VMEM_SPEC,
-        compiler_params=params(16),
+        compiler_params=params(56),
         name="decode",
     )(words.reshape(slots // LANES, LANES), live.reshape(slots // LANES, LANES))
     index = index.reshape(slots)
@@ -624,7 +621,7 @@
             pltpu.VMEM((blocks + 8, features), jnp.float32),
             pltpu.VMEM((cap, features), jnp.float32),
         ],
-        compiler_params=params(40),
+        compiler_params=params(56),
         cost_estimate=pl.CostEstimate(flops=0, bytes_accessed=100 * MIB, transcendentals=0),
         name="read_voxels",
     )(index, totals_in, volume))
@@ -644,7 +641,7 @@
             if part == 1:
                 voxels[0] = earlier
         picture = lax.all_to_all(packed[part], "slab", split_axis=0, concat_axis=0, tiled=True)
-        lengths = pieces[:1] if last else []
+        lengths = [blocks // 2] + pieces if last else []
         arguments = [
             totals_in, table_rows[:, 0], table_rows[:, 1], scale_in, index, core,
             words[:, offset:offset + tile].reshape(slabs, 1, tile), voxels[part], picture,
@@ -654,7 +651,7 @@
         if not first:
             aliases = {len(arguments): 1}
             arguments.append(pltpu.with_memory_space_constraint(sums, pltpu.VMEM))
-        more, sums, *first_piece = pl.pallas_call(
+        more, sums, *halves = pl.pallas_call(
             functools.partial(
                 slab_kernel, side, local_bits, list_length, particles, cap, offset, first, last
             ),
@@ -677,18 +674,7 @@
         squares = squares + more
         behind.append(more)
         offset += tile
-    lengths = [blocks // 2] + pieces[1:]
-    mine, *theirs = pl.pallas_call(
-        split_kernel,
-        out_shape=tuple(jax.ShapeDtypeStruct((length, features), jnp.float32) for length in lengths),
-        in_specs=[SMEM_SPEC, VMEM_SPEC],
-        out_specs=(ANY_SPEC,) * len(lengths),
-        scratch_shapes=[pltpu.SemaphoreType.DMA((len(lengths),))],
-        compiler_params=params(16),
-        cost_estimate=pl.CostEstimate(flops=0, bytes_accessed=16 * MIB, transcendentals=0),
-        name="split_sums",
-    )(core, pltpu.with_memory_space_constraint(sums, pltpu.VMEM))
-    theirs = first_piece + theirs
+    mine, *theirs = halves
     partial_sums = jnp.sum(squares, axis=2)
     return mine, theirs, partial_sums, side
 

time: 347 us -> 329 us (0.948)
  local copies, waits for them, and re-layouts: 56.3 us -> 21.7 us
  waiting for transfers between devices: 82.2 us -> 113 us
  Pallas kernels: 153 us -> 124 us
  starting transfers between devices: 34.6 us -> 49 us
    unnamed x64 -> x32, local copies, waits for them, and re-layouts: 54.9 us -> 19.6 us
    pallas_call x2, Pallas kernels: 65.6 us -> 39.3 us  [gradient_of_slab(): pl.pallas_call(functools.partial(slab_kernel, side, local_bits, list_leng...]
    ppermute x7, waiting for transfers between devices: 34.8 us -> 57.3 us  [sum_over_slabs(): lax.ppermute(row(i), 'slab', [(slab, slab ^ i) for slab in range(slabs)])]
    all_to_all x3 -> x2, waiting for transfers between devices: 20.2 us -> 3.63 us  [to_field(): got = lax.all_to_all(sent, 'slab', split_axis=0, concat_axis=0, tiled=True)]
    all_to_all x3 -> x2, starting transfers between devices: 11 us -> 25.4 us  [to_field(): got = lax.all_to_all(sent, 'slab', split_axis=0, concat_axis=0, tiled=True)]
    all_to_all x2, waiting for transfers between devices: 20.9 us -> 35.3 us  [gradient_of_slab(): lax.all_to_all(packed[part], 'slab', split_axis=0, concat_axis=0, tiled=T...]
    ppermute x3 -> x2, waiting for transfers between devices: 0.01 us -> 11.3 us  [to_field(): theirs = [lax.ppermute(chunk, 'dom', swap) for chunk in theirs_sent]]
    pallas_call x3 -> x2, Pallas kernels: 31.2 us -> 31.4 us  [to_field(): pl.pallas_call(planes_kernel, grid=(quads, per_row // yblocks), out_shape...]
  transfers between devices with their start and end apart: 18 -> 15, of which waited for: 9 -> 10; matrix products, arithmetic and copies ran while one was open for 1% -> 1% of each run, Pallas kernels for 27% -> 24%
where the time goes in v8:
time: 329 us; the launch traced here: 326 us
  Pallas kernels  124 us (38%)
  waiting for transfers between devices  113 us (34%)
  starting transfers between devices  49 us (15%)
  local copies, waits for them, and re-layouts  21.7 us (7%)
  blocking collectives  13.6 us (4%)
    ppermute x7, waiting for transfers between devices, sum_over_slabs(): lax.ppermute(row(i), 'slab', [(slab, slab ^ i) for slab in range(slabs)])  57.3 us
    pallas_call x2, Pallas kernels, gradient_of_slab(): pl.pallas_call(functools.partial(slab_kernel, side, local_bits, list_leng...  39.3 us
    all_to_all x2, waiting for transfers between devices, gradient_of_slab(): lax.all_to_all(packed[part], 'slab', split_axis=0, concat_axis=0, tiled=T...  35.3 us
    pallas_call x2, Pallas kernels, to_field(): pl.pallas_call(planes_kernel, grid=(quads, per_row // yblocks), out_shape...  31.4 us
    all_to_all x2, starting transfers between devices, to_field(): got = lax.all_to_all(sent, 'slab', split_axis=0, concat_axis=0, tiled=True)  25.4 us
    pallas_call x1, Pallas kernels, gradient_of_slab(): pl.pallas_call(functools.partial(pack_kernel, slabs, cap, list_length), o...  20.1 us
    unnamed x32, local copies, waits for them, and re-layouts  19.6 us
    pallas_call x1, Pallas kernels, gradient_of_slab(): pl.pallas_call(functools.partial(gather_kernel, slabs, cap), out_shape=tu...  14.5 us
  transfers between devices with their start and end apart: 15, of which 10 were waited for; matrix products, arithmetic and copies ran while one was open for 1% of the time, Pallas kernels for 24%

profile of v8, /device:TPU:0, one launch (start us, length us, event | category | flops | bytes accessed | tf_op | source)
XLA Modules:
  0.0 325.6 jit_solution(7968067189015394652)
XLA Ops:
  1.8 3.7 %route.1 = (s32[64,128]{1,0:T(8,128)}, s32[64,128]{1,0:T(8,128)}, s32[8,128]{1,0:T(8,128)}) custom-call(s32[64,128]{1,0:T(8,128)} %bitcast.50, s32[8,1024]{1,0:T(8,128)} %local_ref.1, s32[8,1024]{1,0:T(8,128)} %kind_ref.1, s32[8]{0:T(128)} %counts_ref.3), custom_call_target="tpu_custom_call" | custom-call | tf_op jit(solution)/shard_map/route/pallas_call | solution.py:568
  5.5 20.1 %pack.1 = (s32[17408]{0:T(1024)}, bf16[8,1024,128]{2,1,0:T(8,128)(2,1)}, bf16[8,1024,128]{2,1,0:T(8,128)(2,1)}) custom-call(s32[8192]{0:T(1024)} %bitcast.48, s32[8192]{0:T(1024)} %bitcast.49, s32[8]{0:T(128)} %counts_ref.3, s32[8,128]{1,0:T(8,128)} %get-tuple-element.26.totals_ref, s32[8]{0:T(128)} %shift-left_or_fusion.code_ref, bf16[8192,128]{1,0:T(8,128)(2,1)} %bitcast.38), custom_call_target="tpu_custom_call" | custom-call | tf_op jit(solution)/shard_map/pack/pallas_call | solution.py:581
  25.6 13.6 %all_to_all.32 = s32[8,1,2176]{2,1,0:T(1,128)S(1)} all-to-all(s32[8,1,2176]{2,1,0:T(1,128)} %bitcast.47), channel_id=1, replica_groups=mesh['groups'=2,'slab'=8,'dom'=2] {'slab'}, dimensions={0} | all-to-all | bytes 139264 | tf_op jit(solution)/shard_map/all_to_all | solution.py:594
  39.3 3.6 %all-to-all-start.2 = ((bf16[8,1024,128]{2,1,0:T(8,128)(2,1)}), bf16[8,1024,128]{2,1,0:T(8,128)(2,1)S(1)}, u32[]{:S(2)}, u32[]{:S(2)}) async-start(bf16[8,1024,128]{2,1,0:T(8,128)(2,1)} %get-tuple-element.32), calls=%async_computation.2 | async-start | bytes 4194304 | tf_op jit(solution)/shard_map/all_to_all | solution.py:643
  47.0 14.5 %read_voxels.1 = (bf16[8,1024,128]{2,1,0:T(8,128)(2,1)}, bf16[8,1024,128]{2,1,0:T(8,128)(2,1)}) custom-call(s32[16384]{0:T(1024)} %bitcast.33, s32[8]{0:T(128)} %copy-done.5, bf16[32768,128]{1,0:T(8,128)(2,1)} %volume_ref.1), custom_call_target="tpu_custom_call" | custom-call | bytes 104857600 | tf_op jit(solution)/shard_map/read_voxels/pallas_call | solution.py:613
  61.5 27.2 %all-to-all-done.2.image_ref = bf16[8,1024,128]{2,1,0:T(8,128)(2,1)S(1)} async-done(((bf16[8,1024,128]{2,1,0:T(8,128)(2,1)}), bf16[8,1024,128]{2,1,0:T(8,128)(2,1)S(1)}, u32[]{:S(2)}, u32[]{:S(2)}) %all-to-all-start.2) | async-done | bytes 2097184 | tf_op jit(solution)/shard_map/all_to_all | solution.py:643
  88.7 4.4 %all-to-all-start.1 = ((bf16[8,1024,128]{2,1,0:T(8,128)(2,1)}), bf16[8,1024,128]{2,1,0:T(8,128)(2,1)}, u32[]{:S(2)}, u32[]{:S(2)}) async-start(bf16[8,1024,128]{2,1,0:T(8,128)(2,1)} %get-tuple-element.31), calls=%async_computation.1 | async-start | bytes 4194304 | tf_op jit(solution)/shard_map/all_to_all | solution.py:643
  96.2 30.7 %compare_and_add.2 = (f32[8,8,128]{2,1,0:T(8,128)S(1)}, f32[32776,128]{1,0:T(8,128)S(1)}) custom-call(s32[8]{0:T(128)S(1)} %copy-done.6, f32[64]{0:T(128)S(1)} %get-tuple-element.47.defocus_ref, f32[64]{0:T(128)S(1)} %get-tuple-element.46.phase_ref, f32[64]{0:T(128)S(1)} %mul.17.scale_ref, s32[16384]{0:T(1024)S(1)} %bitcast.34, s32[1]{0:T(128)} %bitcast.core_ref, ...), custom_call_target="tpu_custom_call" | custom-call | bytes 16777216 | tf_op jit(solution)/shard_map/compare_and_add/pallas_call | solution.py:654
  126.9 5.7 %copy-done = f32[32776,128]{1,0:T(8,128)} copy-done((f32[32776,128]{1,0:T(8,128)}, f32[32776,128]{1,0:T(8,128)S(1)}, u32[]{:S(2)}) %copy-start) | copy-done | bytes 16781336
  132.7 8.1 %all-to-all-done.1.image_ref = bf16[8,1024,128]{2,1,0:T(8,128)(2,1)} async-done(((bf16[8,1024,128]{2,1,0:T(8,128)(2,1)}), bf16[8,1024,128]{2,1,0:T(8,128)(2,1)}, u32[]{:S(2)}, u32[]{:S(2)}) %all-to-all-start.1) | async-done | bytes 2097184 | tf_op jit(solution)/shard_map/all_to_all | solution.py:643
  140.7 5.8 %copy-done.1 = f32[32776,128]{1,0:T(8,128)S(1)} copy-done((f32[32776,128]{1,0:T(8,128)S(1)}, f32[32776,128]{1,0:T(8,128)}, u32[]{:S(2)}) %copy-start.1) | copy-done | bytes 16781336
  148.1 8.6 %compare_and_add.3 = (f32[8,8,128]{2,1,0:T(8,128)S(1)}, f32[32776,128]{1,0:T(8,128)S(1)}, f32[16384,128]{1,0:T(8,128)}, f32[4096,128]{1,0:T(8,128)S(1)}, f32[12288,128]{1,0:T(8,128)}) custom-call(s32[8]{0:T(128)S(1)} %copy-done.6, f32[64]{0:T(128)S(1)} %get-tuple-element.47.defocus_ref, ...), custom_call_target="tpu_custom_call", output_to_operand_aliasing={{1}: (12, {})} | custom-call | bytes 16777216 | tf_op jit(solution)/shard_map/compare_and_add/pallas_call | solution.py:654
  157.2 11.3 %collective-permute-done.1 = f32[4096,128]{1,0:T(8,128)S(1)} collective-permute-done((f32[4096,128]{1,0:T(8,128)S(1)}, f32[4096,128]{1,0:T(8,128)S(1)}, u32[]{:S(2)}, u32[]{:S(2)}) %collective-permute-start.1) | collective-permute-done | bytes 2097184 | tf_op jit(solution)/shard_map/ppermute | solution.py:487
  169.9 8.8 %transform_planes.2 = bf16[8,4,2,32,256]{4,3,2,1,0:T(8,128)(2,1)} custom-call(f32[16,32,32,128]{3,2,1,0:T(8,128)} %bitcast.36, f32[4,32,32,128]{3,2,1,0:T(8,128)} %bitcast.39, bf16[384,256]{1,0:T(8,128)(2,1)} %constant.67.clone.zblock_ref, f32[2,8,128]{2,1,0:T(8,128)} %constant.68.clone.turn_ref, bf16[512,512]{1,0:T(8,128)(2,1)} %constant.69.clone.wide_ref, ...), custom_call_target="tpu_custom_call" | custom-call | flops 536870912 | bytes 8388608 | tf_op jit(solution)/shard_map/transform_planes/pallas_call | solution.py:506
  178.7 21.7 %all-to-all-start.3 = ((bf16[8,4,2,32,256]{4,3,2,1,0:T(8,128)(2,1)}), bf16[8,4,2,32,256]{4,3,2,1,0:T(8,128)(2,1)S(1)}, u32[]{:S(2)}, u32[]{:S(2)}) async-start(bf16[8,4,2,32,256]{4,3,2,1,0:T(8,128)(2,1)} %transform_planes.2), calls=%async_computation.3 | async-start | bytes 2097152 | tf_op jit(solution)/shard_map/all_to_all | solution.py:533
  200.5 22.6 %transform_planes.3 = bf16[8,12,2,32,256]{4,3,2,1,0:T(8,128)(2,1)} custom-call(f32[16,32,32,128]{3,2,1,0:T(8,128)} %bitcast.37, f32[12,32,32,128]{3,2,1,0:T(8,128)} %bitcast.18.theirs_ref, bf16[384,256]{1,0:T(8,128)(2,1)} %constant.67.clone.zblock_ref, f32[2,8,128]{2,1,0:T(8,128)} %constant.68.clone.turn_ref, bf16[512,512]{1,0:T(8,128)(2,1)} %constant.69.clone.wide_ref, ...), custom_call_target="tpu_custom_call" | custom-call | flops 1610612736 | bytes 25165824 | tf_op jit(solution)/shard_map/transform_planes/pallas_call | solution.py:506
  223.1 3.6 %all-to-all-done.3.refs_0_ = bf16[8,4,2,32,256]{4,3,2,1,0:T(8,128)(2,1)S(1)} async-done(((bf16[8,4,2,32,256]{4,3,2,1,0:T(8,128)(2,1)}), bf16[8,4,2,32,256]{4,3,2,1,0:T(8,128)(2,1)S(1)}, u32[]{:S(2)}, u32[]{:S(2)}) %all-to-all-start.3) | async-done | bytes 1048608 | tf_op jit(solution)/shard_map/all_to_all | solution.py:533
  227.7 3.6 %all-to-all-start.4 = ((bf16[8,12,2,32,256]{4,3,2,1,0:T(8,128)(2,1)}), bf16[8,12,2,32,256]{4,3,2,1,0:T(8,128)(2,1)S(1)}, u32[]{:S(2)}, u32[]{:S(2)}) async-start(bf16[8,12,2,32,256]{4,3,2,1,0:T(8,128)(2,1)} %transform_planes.3), calls=%async_computation.4 | async-start | bytes 6291456 | tf_op jit(solution)/shard_map/all_to_all | solution.py:533
  239.3 17.8 %collective-permute-done.2 = f32[1,8]{1,0:T(1,128)S(1)} collective-permute-done((f32[1,8]{1,0:T(1,128)S(1)}, f32[1,8]{1,0:T(1,128)S(1)}, u32[]{:S(2)}, u32[]{:S(2)}) %collective-permute-start.2) | collective-permute-done | bytes 64 | tf_op jit(solution)/shard_map/ppermute | solution.py:470
  260.3 23.3 %collective-permute-done.3 = f32[1,8]{1,0:T(1,128)S(1)} collective-permute-done((f32[1,8]{1,0:T(1,128)S(1)}, f32[1,8]{1,0:T(1,128)S(1)}, u32[]{:S(2)}, u32[]{:S(2)}) %collective-permute-start.3) | collective-permute-done | bytes 64 | tf_op jit(solution)/shard_map/ppermute | solution.py:470
  283.6 3.4 %collective-permute-start.8 = (f32[1,8]{1,0:T(1,128)S(1)}, f32[1,8]{1,0:T(1,128)S(1)}, u32[]{:S(2)}, u32[]{:S(2)}) collective-permute-start(f32[1,8]{1,0:T(1,128)S(1)} %get-tuple-element.51), channel_id=1, source_target_pairs={{0,14},{2,12},{4,10},{6,8},{8,6},{10,4},{12,2},{14,0},{1,15},{3,13... | collective-permute-start | bytes 104 | tf_op jit(solution)/shard_map/ppermute | solution.py:470
  286.9 15.4 %collective-permute-done.5 = f32[1,8]{1,0:T(1,128)S(1)} collective-permute-done((f32[1,8]{1,0:T(1,128)S(1)}, f32[1,8]{1,0:T(1,128)S(1)}, u32[]{:S(2)}, u32[]{:S(2)}) %collective-permute-start.5) | collective-permute-done | bytes 64 | tf_op jit(solution)/shard_map/ppermute | solution.py:470
  304.7 5.5 %collective-permute-done.9.refs_2_ = bf16[8,4,2,32,256]{4,3,2,1,0:T(8,128)(2,1)S(1)} collective-permute-done((bf16[8,4,2,32,256]{4,3,2,1,0:T(8,128)(2,1)}, bf16[8,4,2,32,256]{4,3,2,1,0:T(8,128)(2,1)S(1)}, u32[]{:S(2)}, u32[]{:S(2)}) %collective-permute-start.9) | collective-permute-done | bytes 1048608 | tf_op jit(solution)/shard_map/ppermute | solution.py:536
  313.0 12.6 %transform_first.1 = f32[2,128,32,256]{3,2,1,0:T(8,128)} custom-call(s32[1]{0:T(128)} %bitcast.core_ref, bf16[8,4,2,32,256]{4,3,2,1,0:T(8,128)(2,1)} %copy-done.8, bf16[8,12,2,32,256]{4,3,2,1,0:T(8,128)(2,1)} %copy-done.7, bf16[8,4,2,32,256]{4,3,2,1,0:T(8,128)(2,1)} %copy-done.11, bf16[8,12,2,32,256]{4,3,2,1,0:T(8,128)(2,1)} %copy-done.9), custom_call_target="tpu_custom_call" | custom-call | tf_op jit(solution)/shard_map/transform_first/pallas_call | solution.py:539
  (74 shorter events, 29.1 us)
Async XLA Ops:
  39.3 49.5 %all-to-all-start.2 = ((bf16[8,1024,128]{2,1,0:T(8,128)(2,1)}), bf16[8,1024,128]{2,1,0:T(8,128)(2,1)S(1)}, u32[]{:S(2)}, u32[]{:S(2)}) async-start(bf16[8,1024,128]{2,1,0:T(8,128)(2,1)} %get-tuple-element.32), calls=%async_computation.2 | async-start | bytes 4194304 | tf_op jit(solution)/shard_map/all_to_all | solution.py:643
  43.0 4.0 %copy-start.5 = (s32[8]{0:T(128)}, s32[8]{0:T(128)S(1)}, u32[]{:S(2)}) copy-start(s32[8]{0:T(128)S(1)} %slice_reduce_fusion.2.totals_ref) | copy-start | bytes 100
  61.5 31.6 %copy-start.14 = (f32[64,2]{0,1:T(2,128)S(1)}, f32[64,2]{0,1:T(2,128)}, u32[]{:S(2)}) copy-start(f32[64,2]{0,1:T(2,128)} %param.22) | copy-start | bytes 1540
  61.5 31.7 %copy-start.12 = (bf16[4,128,128]{2,1,0:T(8,128)(2,1)S(1)}, bf16[4,128,128]{2,1,0:T(8,128)(2,1)}, u32[]{:S(2)}) copy-start(bf16[4,128,128]{2,1,0:T(8,128)(2,1)} %param.15) | copy-start | bytes 393220
  61.5 33.1 %copy-start.4 = (s32[128,128]{1,0:T(8,128)S(1)}, s32[128,128]{1,0:T(8,128)}, u32[]{:S(2)}) copy-start(s32[128,128]{1,0:T(8,128)} %decode.1) | copy-start | bytes 196612
  61.5 33.1 %copy-start.6 = (s32[8]{0:T(128)S(1)}, s32[8]{0:T(128)}, u32[]{:S(2)}) copy-start(s32[8]{0:T(128)} %copy-done.5) | copy-start | bytes 100
  88.7 52.0 %all-to-all-start.1 = ((bf16[8,1024,128]{2,1,0:T(8,128)(2,1)}), bf16[8,1024,128]{2,1,0:T(8,128)(2,1)}, u32[]{:S(2)}, u32[]{:S(2)}) async-start(bf16[8,1024,128]{2,1,0:T(8,128)(2,1)} %get-tuple-element.31), calls=%async_computation.1 | async-start | bytes 4194304 | tf_op jit(solution)/shard_map/all_to_all | solution.py:643
  126.9 5.7 %copy-start = (f32[32776,128]{1,0:T(8,128)}, f32[32776,128]{1,0:T(8,128)S(1)}, u32[]{:S(2)}) copy-start(f32[32776,128]{1,0:T(8,128)S(1)} %get-tuple-element.33.rest_0_) | copy-start | bytes 50343940
  140.7 5.8 %copy-start.1 = (f32[32776,128]{1,0:T(8,128)S(1)}, f32[32776,128]{1,0:T(8,128)}, u32[]{:S(2)}) copy-start(f32[32776,128]{1,0:T(8,128)} %copy-done) | copy-start | bytes 50343940
  156.7 43.8 %collective-permute-start = (f32[12288,128]{1,0:T(8,128)}, f32[12288,128]{1,0:T(8,128)}, u32[]{:S(2)}, u32[]{:S(2)}) collective-permute-start(f32[12288,128]{1,0:T(8,128)} %get-tuple-element.35), channel_id=1, source_target_pairs={{0,1},{1,0},{2,3},{3,2},{4,5},{5,4},{6,7},{7,6},{8,9},{9,8},{10,11... | collective-permute-start | bytes 18874376 | tf_op jit(solution)/shard_map/ppermute | solution.py:487
  156.7 11.8 %collective-permute-start.1 = (f32[4096,128]{1,0:T(8,128)S(1)}, f32[4096,128]{1,0:T(8,128)S(1)}, u32[]{:S(2)}, u32[]{:S(2)}) collective-permute-start(f32[4096,128]{1,0:T(8,128)S(1)} %get-tuple-element.36), channel_id=1, source_target_pairs={{0,1},{1,0},{2,3},{3,2},{4,5},{5,4},{6,7},{7,6},{8,9},{9,8},{10,11... | collective-permute-start | bytes 6291464 | tf_op jit(solution)/shard_map/ppermute | solution.py:487
  178.7 48.0 %all-to-all-start.3 = ((bf16[8,4,2,32,256]{4,3,2,1,0:T(8,128)(2,1)}), bf16[8,4,2,32,256]{4,3,2,1,0:T(8,128)(2,1)S(1)}, u32[]{:S(2)}, u32[]{:S(2)}) async-start(bf16[8,4,2,32,256]{4,3,2,1,0:T(8,128)(2,1)} %transform_planes.2), calls=%async_computation.3 | async-start | bytes 2097152 | tf_op jit(solution)/shard_map/all_to_all | solution.py:533
  223.1 80.7 %copy-start.13 = (s32[8]{0:T(128)S(1)}, s32[8]{0:T(128)}, u32[]{:S(2)}) copy-start(s32[8]{0:T(128)} %counts_ref.3) | copy-start | bytes 100
  227.7 75.5 %all-to-all-start.4 = ((bf16[8,12,2,32,256]{4,3,2,1,0:T(8,128)(2,1)}), bf16[8,12,2,32,256]{4,3,2,1,0:T(8,128)(2,1)S(1)}, u32[]{:S(2)}, u32[]{:S(2)}) async-start(bf16[8,12,2,32,256]{4,3,2,1,0:T(8,128)(2,1)} %transform_planes.3), calls=%async_computation.4 | async-start | bytes 6291456 | tf_op jit(solution)/shard_map/all_to_all | solution.py:533
  231.4 25.7 %collective-permute-start.2 = (f32[1,8]{1,0:T(1,128)S(1)}, f32[1,8]{1,0:T(1,128)S(1)}, u32[]{:S(2)}, u32[]{:S(2)}) collective-permute-start(f32[1,8]{1,0:T(1,128)S(1)} %get-tuple-element.50), channel_id=1, source_target_pairs={{0,2},{2,0},{4,6},{6,4},{8,10},{10,8},{12,14},{14,12},{1,3},{3,1},... | collective-permute-start | bytes 104 | tf_op jit(solution)/shard_map/ppermute | solution.py:470
  233.4 50.2 %collective-permute-start.3 = (f32[1,8]{1,0:T(1,128)S(1)}, f32[1,8]{1,0:T(1,128)S(1)}, u32[]{:S(2)}, u32[]{:S(2)}) collective-permute-start(f32[1,8]{1,0:T(1,128)S(1)} %get-tuple-element.56), channel_id=1, source_target_pairs={{0,4},{2,6},{4,0},{6,2},{8,12},{10,14},{12,8},{14,10},{1,5},{3,7},... | collective-permute-start | bytes 104 | tf_op jit(solution)/shard_map/ppermute | solution.py:470
  234.9 52.1 %collective-permute-start.4 = (f32[1,8]{1,0:T(1,128)S(1)}, f32[1,8]{1,0:T(1,128)S(1)}, u32[]{:S(2)}, u32[]{:S(2)}) collective-permute-start(f32[1,8]{1,0:T(1,128)S(1)} %get-tuple-element.55), channel_id=1, source_target_pairs={{0,6},{2,4},{4,2},{6,0},{8,14},{10,12},{12,10},{14,8},{1,7},{3,5},... | collective-permute-start | bytes 104 | tf_op jit(solution)/shard_map/ppermute | solution.py:470
  234.9 67.4 %collective-permute-start.5 = (f32[1,8]{1,0:T(1,128)S(1)}, f32[1,8]{1,0:T(1,128)S(1)}, u32[]{:S(2)}, u32[]{:S(2)}) collective-permute-start(f32[1,8]{1,0:T(1,128)S(1)} %get-tuple-element.54), channel_id=1, source_target_pairs={{0,8},{2,10},{4,12},{6,14},{8,0},{10,2},{12,4},{14,6},{1,9},{3,11}... | collective-permute-start | bytes 104 | tf_op jit(solution)/shard_map/ppermute | solution.py:470
  237.8 65.4 %collective-permute-start.6 = (f32[1,8]{1,0:T(1,128)S(1)}, f32[1,8]{1,0:T(1,128)S(1)}, u32[]{:S(2)}, u32[]{:S(2)}) collective-permute-start(f32[1,8]{1,0:T(1,128)S(1)} %get-tuple-element.53), channel_id=1, source_target_pairs={{0,10},{2,8},{4,14},{6,12},{8,2},{10,0},{12,6},{14,4},{1,11},{3,9}... | collective-permute-start | bytes 104 | tf_op jit(solution)/shard_map/ppermute | solution.py:470
  257.0 46.1 %collective-permute-start.7 = (f32[1,8]{1,0:T(1,128)S(1)}, f32[1,8]{1,0:T(1,128)S(1)}, u32[]{:S(2)}, u32[]{:S(2)}) collective-permute-start(f32[1,8]{1,0:T(1,128)S(1)} %get-tuple-element.52), channel_id=1, source_target_pairs={{0,12},{2,14},{4,8},{6,10},{8,4},{10,6},{12,0},{14,2},{1,13},{3,15... | collective-permute-start | bytes 104 | tf_op jit(solution)/shard_map/ppermute | solution.py:470
  283.6 19.6 %collective-permute-start.8 = (f32[1,8]{1,0:T(1,128)S(1)}, f32[1,8]{1,0:T(1,128)S(1)}, u32[]{:S(2)}, u32[]{:S(2)}) collective-permute-start(f32[1,8]{1,0:T(1,128)S(1)} %get-tuple-element.51), channel_id=1, source_target_pairs={{0,14},{2,12},{4,10},{6,8},{8,6},{10,4},{12,2},{14,0},{1,15},{3,13... | collective-permute-start | bytes 104 | tf_op jit(solution)/shard_map/ppermute | solution.py:470
  303.2 7.2 %copy-start.7 = (bf16[8,12,2,32,256]{4,3,2,1,0:T(8,128)(2,1)}, bf16[8,12,2,32,256]{4,3,2,1,0:T(8,128)(2,1)S(1)}, u32[]{:S(2)}) copy-start(bf16[8,12,2,32,256]{4,3,2,1,0:T(8,128)(2,1)S(1)} %all-to-all-done.4.refs_1_) | copy-start | bytes 9437188
  303.2 7.2 %collective-permute-start.10 = (bf16[8,12,2,32,256]{4,3,2,1,0:T(8,128)(2,1)S(1)}, bf16[8,12,2,32,256]{4,3,2,1,0:T(8,128)(2,1)S(1)}, u32[]{:S(2)}, u32[]{:S(2)}) collective-permute-start(bf16[8,12,2,32,256]{4,3,2,1,0:T(8,128)(2,1)S(1)} %all-to-all-done.4.refs_1_), channel_id=1, source_target_pairs={{0,1},{1,0},{2,3},{3,2},{4,5},{5,4},{6,7},{7,6},{8,9},{9,8},{10,11... | collective-permute-start | bytes 9437192 | tf_op jit(solution)/shard_map/ppermute | solution.py:536
  303.3 7.0 %collective-permute-start.9 = (bf16[8,4,2,32,256]{4,3,2,1,0:T(8,128)(2,1)}, bf16[8,4,2,32,256]{4,3,2,1,0:T(8,128)(2,1)S(1)}, u32[]{:S(2)}, u32[]{:S(2)}) collective-permute-start(bf16[8,4,2,32,256]{4,3,2,1,0:T(8,128)(2,1)} %copy-done.8), channel_id=1, source_target_pairs={{0,1},{1,0},{2,3},{3,2},{4,5},{5,4},{6,7},{7,6},{8,9},{9,8},{10,11... | collective-permute-start | bytes 3145736 | tf_op jit(solution)/shard_map/ppermute | solution.py:536
  (6 other events, 8.2 us)

commit v9 on v8

--- a/solution.py
+++ b/solution.py
@@ -12,6 +12,7 @@
 LANES = 128
 GROUP = 16
 UNUSED = 100
+STEP = 256
 MIB = 1024 * 1024
 
 SMEM_SPEC = pl.BlockSpec(memory_space=pltpu.SMEM)
@@ -127,10 +128,13 @@
         same = (earlier == index) & (lane % GROUP >= shift) & live
         clash = clash | same.astype(jnp.int32)
     shift = 1
-    while shift < GROUP:
+    while shift < LANES:
+        if shift == GROUP:
+            index = index | jnp.where(lane % GROUP == 0, clash << 24, 0)
         clash = clash | pltpu.roll(clash, LANES - shift, 1)
         shift *= 2
-    index_ref[...] = index | jnp.where(lane % GROUP == 0, clash << 24, 0)
+    index_ref[0:rows, :] = index | jnp.where(lane == 0, clash << 25, 0)
+    index_ref[rows:, :] = jnp.full((index_ref.shape[0] - rows, LANES), dummy, jnp.int32)
 
 
 def gather_kernel(slabs, cap, index_ref, totals_ref, volume_ref, *refs):
@@ -169,8 +173,7 @@
 def sine(angle):
     turns = jnp.floor(angle * (1.0 / math.pi) + 0.5)
     rest = angle - turns * 3.140625
-    rest = rest - turns * 9.67502593994140625e-4
-    rest = rest - turns * 1.509957990978376e-7
+    rest = rest - turns * (math.pi - 3.140625)
     odd = turns - 2.0 * jnp.floor(turns * 0.5)
     square = rest * rest
     poly = 2.718121e-6
@@ -188,13 +191,16 @@
 ):
     if not first:
         rest = rest[1:]
-    square_ref, sum_ref, out_refs, (staged_ref, sems) = rest[0], rest[1], rest[2:-2], rest[-2:]
+    square_ref, sum_ref, out_refs, (staged_ref, steps_ref, sems) = rest[0], rest[1], rest[2:-3], rest[-3:]
     slabs, _, tile = word_ref.shape
+    step = staged_ref.shape[0]
+    steps_each = tile // step
     blocks = sum_ref.shape[0] - 8
     features = image_ref.shape[2]
     kinds = forward_ref.shape[0] // features
     position_bits = bits_of(list_length)
     per_row = side // 8
+    half = features // 2
 
     if first:
         @pl.loop(0, blocks // 256)
@@ -202,81 +208,118 @@
             at = pl.multiple_of(i * 256, 256)
             sum_ref[pl.ds(at, 256), :] = jnp.zeros((256, features), jnp.float32)
 
-    @pl.loop(0, slabs)
-    def _(source):
-        live = jnp.clip(totals_ref[source] - offset, 0, tile)
-
-        @pl.when(live == 0)
+    square_ref[...] = jnp.zeros_like(square_ref)
+    live_of = lambda source: jnp.clip(totals_ref[source] - offset, 0, tile)
+
+    def list_source(source, count):
+        def list_step(i, count):
+            steps_ref[count] = source * steps_each + i
+            return count + 1
+
+        return lax.fori_loop(0, (live_of(source) + step - 1) // step, list_step, count)
+
+    steps_ref[0] = 0
+    count = lax.fori_loop(0, slabs, list_source, 0)
+
+    def compare(number):
+        which_step = steps_ref[jnp.minimum(number, jnp.maximum(count - 1, 0))]
+        source, at = which_step // steps_each, (which_step % steps_each) * step
+        at = pl.multiple_of(at, step)
+        live = jnp.where(number < count, live_of(source) - at, 0)
+        word = word_ref[source, :, pl.ds(at, step)]
+        kind = (word >> local_bits) & 3
+        position = (word >> (local_bits + 2)) & (list_length - 1)
+        particle = (word >> (local_bits + 2 + position_bits)) & (particles - 1)
+        valid = lax.broadcasted_iota(jnp.int32, (1, step), 1) < live
+        defocus = jnp.zeros((1, step), jnp.float32)
+        phase = jnp.zeros((1, step), jnp.float32)
+        scale = jnp.zeros((1, step), jnp.float32)
+        for j in range(particles):
+            chosen = particle == j
+            defocus = jnp.where(chosen, defocus_ref[source * particles + j], defocus)
+            phase = jnp.where(chosen, phase_ref[source * particles + j], phase)
+            scale = jnp.where(chosen, scale_ref[source * particles + j], scale)
+        defocus = defocus * (1.0 / float((side // 2) ** 2))
+        cell = lax.broadcasted_iota(jnp.int32, (half, LANES), 0)
+        cell_vert, cell_horiz = (cell // 8).astype(jnp.float32), (cell % 8).astype(jnp.float32)
+        repeat = lambda table: jnp.concatenate([table] * (step // LANES), axis=1)
+        vert = ((position // per_row) * 8 - side // 2).astype(jnp.float32) + repeat(cell_vert)
+        horiz = ((position % per_row) * 8 - side // 2).astype(jnp.float32) + repeat(cell_horiz)
+        factor = scale * sine(defocus * (vert * vert + horiz * horiz) + phase)
+        factor = jnp.concatenate([factor, factor], axis=0)
+        contract_last = (((1,), (1,)), ((), ()))
+        each_kind = lax.dot_general(
+            forward_ref[...], voxel_ref[source, pl.ds(at, step), :], contract_last,
+            preferred_element_type=jnp.float32,
+        )
+        extracted = each_kind[0:features, :]
+        for k in range(1, kinds):
+            extracted = jnp.where(kind == k, each_kind[k * features:(k + 1) * features, :], extracted)
+        picture = lax.dot_general(
+            unit_ref[...], image_ref[source, pl.ds(at, step), :], contract_last,
+            preferred_element_type=jnp.float32,
+        )
+        misfit = jnp.where(valid, factor * extracted - picture, 0.0)
+        squares = jnp.sum(misfit * misfit, axis=0, keepdims=True)
+        which = lax.broadcasted_iota(jnp.int32, (particles, step), 0)
+        spread = jnp.where(valid & (particle == which), squares, 0.0)
+        folded = spread[:, 0:LANES]
+        for i in range(1, step // LANES):
+            folded = folded + spread[:, i * LANES:(i + 1) * LANES]
+        square_ref[source] = square_ref[source] + folded
+        weighted = (factor * misfit).astype(jnp.bfloat16)
+        none = jnp.zeros_like(weighted)
+        spread_back = jnp.concatenate(
+            [jnp.where(kind == k, weighted, none) for k in range(kinds)], axis=0
+        )
+        terms = jnp.dot(backward_ref[...], spread_back, preferred_element_type=jnp.float32)
+        staged_ref[...] = terms.T
+
+    def places_of(base):
+        return [index_ref[base] & 0xFFFFFF] + [index_ref[base + j] for j in range(1, GROUP)]
+
+    def add_group(base, at):
+        places = places_of(base)
+        held = [sum_ref[pl.ds(place, 1), :] for place in places]
+        new = [staged_ref[pl.ds(at + j, 1), :] for j in range(GROUP)]
+        for j in range(GROUP):
+            sum_ref[pl.ds(places[j], 1), :] = held[j] + new[j]
+
+    @pl.loop(0, count + 1)
+    def _(number):
+        earlier = steps_ref[jnp.maximum(number - 1, 0)]
+        base = (earlier // steps_each) * cap + offset + (earlier % steps_each) * step
+        base = jnp.where(number > 0, base, slabs * cap)
+        marks = index_ref[base]
+        for i in range(1, step // LANES):
+            marks = marks | index_ref[base + i * LANES]
+
+        @pl.when(marks < (1 << 25))
         def _():
-            square_ref[source] = jnp.zeros((particles, LANES), jnp.float32)
-
-        @pl.when(live > 0)
+            for g in range(step // GROUP):
+                add_group(base + g * GROUP, g * GROUP)
+            compare(number)
+
+        @pl.when(marks >= (1 << 25))
         def _():
-            word = word_ref[source]
-            kind = (word >> local_bits) & 3
-            position = (word >> (local_bits + 2)) & (list_length - 1)
-            particle = (word >> (local_bits + 2 + position_bits)) & (particles - 1)
-            valid = lax.broadcasted_iota(jnp.int32, (1, tile), 1) < live
-            defocus = jnp.zeros((1, tile), jnp.float32)
-            phase = jnp.zeros((1, tile), jnp.float32)
-            scale = jnp.zeros((1, tile), jnp.float32)
-            for j in range(particles):
-                chosen = particle == j
-                defocus = jnp.where(chosen, defocus_ref[source * particles + j], defocus)
-                phase = jnp.where(chosen, phase_ref[source * particles + j], phase)
-                scale = jnp.where(chosen, scale_ref[source * particles + j], scale)
-            half = features // 2
-            cell = lax.broadcasted_iota(jnp.int32, (half, tile), 0)
-            vert = ((position // per_row) * 8 - side // 2 + cell // 8).astype(jnp.float32)
-            horiz = ((position % per_row) * 8 - side // 2 + cell % 8).astype(jnp.float32)
-            radius = (vert * vert + horiz * horiz) * (1.0 / float((side // 2) ** 2))
-            factor = scale * sine(defocus * radius + phase)
-            factor = jnp.concatenate([factor, factor], axis=0)
-            contract_last = (((1,), (1,)), ((), ()))
-            each_kind = lax.dot_general(
-                forward_ref[...], voxel_ref[source], contract_last, preferred_element_type=jnp.float32
-            )
-            extracted = each_kind[0:features, :]
-            for k in range(1, kinds):
-                extracted = jnp.where(kind == k, each_kind[k * features:(k + 1) * features, :], extracted)
-            picture = lax.dot_general(
-                unit_ref[...], image_ref[source], contract_last, preferred_element_type=jnp.float32
-            )
-            misfit = jnp.where(valid, factor * extracted - picture, 0.0)
-            squares = jnp.sum(misfit * misfit, axis=0, keepdims=True)
-            which = lax.broadcasted_iota(jnp.int32, (particles, tile), 0)
-            spread = jnp.where(valid & (particle == which), squares, 0.0)
-            folded = spread[:, 0:LANES]
-            for i in range(1, tile // LANES):
-                folded = folded + spread[:, i * LANES:(i + 1) * LANES]
-            square_ref[source] = folded
-            weighted = (factor * misfit).astype(jnp.bfloat16)
-            none = jnp.zeros_like(weighted)
-            spread_back = jnp.concatenate(
-                [jnp.where(kind == k, weighted, none) for k in range(kinds)], axis=0
-            )
-            terms = jnp.dot(backward_ref[...], spread_back, preferred_element_type=jnp.float32)
-            staged_ref[...] = terms.T
-
-        @pl.loop(0, (live + GROUP - 1) // GROUP)
-        def _(g):
-            base = source * cap + offset + g * GROUP
-            marked = index_ref[base]
-            places = [marked & 0xFFFFFF] + [index_ref[base + j] for j in range(1, GROUP)]
-
-            @pl.when(marked < (1 << 24))
-            def _():
-                held = [sum_ref[pl.ds(places[j], 1), :] for j in range(GROUP)]
-                new = [staged_ref[pl.ds(g * GROUP + j, 1), :] for j in range(GROUP)]
-                for j in range(GROUP):
-                    sum_ref[pl.ds(places[j], 1), :] = held[j] + new[j]
-
-            @pl.when(marked >= (1 << 24))
-            def _():
-                for j in range(GROUP):
-                    sum_ref[pl.ds(places[j], 1), :] = (
-                        sum_ref[pl.ds(places[j], 1), :] + staged_ref[pl.ds(g * GROUP + j, 1), :]
-                    )
+            @pl.loop(0, step // GROUP)
+            def _(g):
+                start = base + g * GROUP
+                clashes = (index_ref[start] >> 24) & 1
+
+                @pl.when(clashes == 0)
+                def _():
+                    add_group(start, g * GROUP)
+
+                @pl.when(clashes == 1)
+                def _():
+                    places = places_of(start)
+                    for j in range(GROUP):
+                        sum_ref[pl.ds(places[j], 1), :] = (
+                            sum_ref[pl.ds(places[j], 1), :] + staged_ref[pl.ds(g * GROUP + j, 1), :]
+                        )
+
+            compare(number)
 
     if last:
         half = blocks // 2
@@ -302,18 +345,20 @@
     return [4, planes - 4]
 
 
-def rotated(value, turn, length):
+def rotated(value, turn, length, sign=None):
     real, imag = value
-    if turn == 0:
-        return value
-    if 4 * turn == length:
-        return (-imag, real)
-    root = math.sqrt(0.5)
-    if 8 * turn == length:
-        return ((real - imag) * root, (real + imag) * root)
-    if 8 * turn == 3 * length:
+    if turn == 0 or 4 * turn == length:
+        if turn:
+            real, imag = -imag, real
+        return (real, imag) if sign is None else (real * sign, imag * sign)
+    if sign is None and 8 * turn in (length, 3 * length):
+        root = math.sqrt(0.5)
+        if 8 * turn == length:
+            return ((real - imag) * root, (real + imag) * root)
         return ((real + imag) * -root, (real - imag) * root)
     cos, sin = math.cos(2 * math.pi * turn / length), math.sin(2 * math.pi * turn / length)
+    if sign is not None:
+        cos, sin = cos * sign, sin * sign
     return (real * cos - imag * sin, real * sin + imag * cos)
 
 
@@ -421,9 +466,7 @@
         for strip in strips:
             values = small_dft([plane(low + 16 * high, strip) for high in range(16)])
             for k in range(16):
-                real, imag = rotated(values[k], low * k, 256)
-                if low % 2:
-                    real, imag = real * sign, imag * sign
+                real, imag = rotated(values[k], low * k, 256, sign if low % 2 else None)
                 mid_ref[k, low, 0, strip] = real
                 mid_ref[k, low, 1, strip] = imag
 
@@ -603,13 +646,13 @@
 
     index = pl.pallas_call(
         functools.partial(decode_kernel, local_bits, blocks),
-        out_shape=jax.ShapeDtypeStruct((slots // LANES, LANES), jnp.int32),
+        out_shape=jax.ShapeDtypeStruct((slots // LANES + 8, LANES), jnp.int32),
         in_specs=[VMEM_SPEC, VMEM_SPEC],
         out_specs=VMEM_SPEC,
         compiler_params=params(56),
         name="decode",
     )(words.reshape(slots // LANES, LANES), live.reshape(slots // LANES, LANES))
-    index = index.reshape(slots)
+    index = index.reshape(slots + 8 * LANES)
     voxels = list(pl.pallas_call(
         functools.partial(gather_kernel, slabs, cap),
         out_shape=tuple(
@@ -663,7 +706,8 @@
             in_specs=[SMEM_SPEC] * 6 + [VMEM_SPEC] * (len(arguments) - 6),
             out_specs=(VMEM_SPEC, VMEM_SPEC) + (ANY_SPEC,) * len(lengths),
             scratch_shapes=[
-                pltpu.VMEM((tile, features), jnp.float32),
+                pltpu.VMEM((min(tile, STEP), features), jnp.float32),
+                pltpu.SMEM((slabs * tile // min(tile, STEP) + 1,), jnp.int32),
                 pltpu.SemaphoreType.DMA((max(1, len(lengths)),)),
             ],
             input_output_aliases=aliases,

time: 329 us -> 324 us (0.985)
  Pallas kernels: 124 us -> 114 us
  waiting for transfers between devices: 113 us -> 123 us
  starting transfers between devices: 49 us -> 43.5 us
    all_to_all x2, waiting for transfers between devices: 35.3 us -> 45.6 us  [gradient_of_slab(): lax.all_to_all(packed[part], 'slab', split_axis=0, concat_axis=0, tiled=T...]
    pallas_call x2, Pallas kernels: 39.3 us -> 30.2 us  [gradient_of_slab(): pl.pallas_call(functools.partial(slab_kernel, side, local_bits, list_leng...]
    all_to_all x2, starting transfers between devices: 25.4 us -> 20.5 us  [to_field(): got = lax.all_to_all(sent, 'slab', split_axis=0, concat_axis=0, tiled=True)]
    unnamed x32 -> x36, local copies, waits for them, and re-layouts: 19.6 us -> 22.5 us
  transfers between devices with their start and end apart: 15 -> 15, of which waited for: 10 -> 10; matrix products, arithmetic and copies ran while one was open for 1% -> 1% of each run, Pallas kernels for 24% -> 22%
where the time goes in v9:
time: 324 us; the launch traced here: 322 us
  waiting for transfers between devices  123 us (38%)
  Pallas kernels  114 us (35%)
  starting transfers between devices  43.5 us (13%)
  local copies, waits for them, and re-layouts  24.6 us (8%)
  blocking collectives  12.8 us (4%)
    ppermute x7, waiting for transfers between devices, sum_over_slabs(): lax.ppermute(row(i), 'slab', [(slab, slab ^ i) for slab in range(slabs)])  56.7 us
    all_to_all x2, waiting for transfers between devices, gradient_of_slab(): lax.all_to_all(packed[part], 'slab', split_axis=0, concat_axis=0, tiled=T...  45.6 us
    pallas_call x2, Pallas kernels, to_field(): pl.pallas_call(planes_kernel, grid=(quads, per_row // yblocks), out_shape...  31.3 us
    pallas_call x2, Pallas kernels, gradient_of_slab(): pl.pallas_call(functools.partial(slab_kernel, side, local_bits, list_leng...  30.2 us
    unnamed x36, local copies, waits for them, and re-layouts  22.5 us
    all_to_all x2, starting transfers between devices, to_field(): got = lax.all_to_all(sent, 'slab', split_axis=0, concat_axis=0, tiled=True)  20.5 us
    pallas_call x1, Pallas kernels, gradient_of_slab(): pl.pallas_call(functools.partial(pack_kernel, slabs, cap, list_length), o...  19.9 us
    ppermute x7, starting transfers between devices, sum_over_slabs(): lax.ppermute(row(i), 'slab', [(slab, slab ^ i) for slab in range(slabs)])  14.7 us
  transfers between devices with their start and end apart: 15, of which 10 were waited for; matrix products, arithmetic and copies ran while one was open for 1% of the time, Pallas kernels for 22%

profile of v9, /device:TPU:0, one launch (start us, length us, event | category | flops | bytes accessed | tf_op | source)
XLA Modules:
  0.0 321.8 jit_solution(1248599586668086667)
XLA Ops:
  1.8 3.7 %route.1 = (s32[64,128]{1,0:T(8,128)}, s32[64,128]{1,0:T(8,128)}, s32[8,128]{1,0:T(8,128)}) custom-call(s32[64,128]{1,0:T(8,128)} %bitcast.50, s32[8,1024]{1,0:T(8,128)} %local_ref.1, s32[8,1024]{1,0:T(8,128)} %kind_ref.1, s32[8]{0:T(128)} %counts_ref.3), custom_call_target="tpu_custom_call" | custom-call | tf_op jit(solution)/shard_map/route/pallas_call | solution.py:611
  5.5 19.9 %pack.1 = (s32[17408]{0:T(1024)}, bf16[8,1024,128]{2,1,0:T(8,128)(2,1)}, bf16[8,1024,128]{2,1,0:T(8,128)(2,1)}) custom-call(s32[8192]{0:T(1024)} %bitcast.48, s32[8192]{0:T(1024)} %bitcast.49, s32[8]{0:T(128)} %counts_ref.3, s32[8,128]{1,0:T(8,128)} %get-tuple-element.26.totals_ref, s32[8]{0:T(128)} %shift-left_or_fusion.code_ref, bf16[8192,128]{1,0:T(8,128)(2,1)} %bitcast.38), custom_call_target="tpu_custom_call" | custom-call | tf_op jit(solution)/shard_map/pack/pallas_call | solution.py:624
  25.5 12.8 %all_to_all.32 = s32[8,1,2176]{2,1,0:T(1,128)S(1)} all-to-all(s32[8,1,2176]{2,1,0:T(1,128)} %bitcast.47), channel_id=1, replica_groups=mesh['groups'=2,'slab'=8,'dom'=2] {'slab'}, dimensions={0} | all-to-all | bytes 139264 | tf_op jit(solution)/shard_map/all_to_all | solution.py:637
  38.3 3.6 %all-to-all-start.2 = ((bf16[8,1024,128]{2,1,0:T(8,128)(2,1)}), bf16[8,1024,128]{2,1,0:T(8,128)(2,1)S(1)}, u32[]{:S(2)}, u32[]{:S(2)}) async-start(bf16[8,1024,128]{2,1,0:T(8,128)(2,1)} %get-tuple-element.32), calls=%async_computation.2 | async-start | bytes 4194304 | tf_op jit(solution)/shard_map/all_to_all | solution.py:686
  46.3 13.4 %read_voxels.1 = (bf16[8,1024,128]{2,1,0:T(8,128)(2,1)}, bf16[8,1024,128]{2,1,0:T(8,128)(2,1)}) custom-call(s32[17408]{0:T(1024)} %bitcast.33, s32[8]{0:T(128)} %copy-done.7, bf16[32768,128]{1,0:T(8,128)(2,1)} %volume_ref.1), custom_call_target="tpu_custom_call" | custom-call | bytes 104857600 | tf_op jit(solution)/shard_map/read_voxels/pallas_call | solution.py:656
  59.7 29.8 %all-to-all-done.2.image_ref = bf16[8,1024,128]{2,1,0:T(8,128)(2,1)S(1)} async-done(((bf16[8,1024,128]{2,1,0:T(8,128)(2,1)}), bf16[8,1024,128]{2,1,0:T(8,128)(2,1)S(1)}, u32[]{:S(2)}, u32[]{:S(2)}) %all-to-all-start.2) | async-done | bytes 2097184 | tf_op jit(solution)/shard_map/all_to_all | solution.py:686
  90.9 3.6 %all-to-all-start.1 = ((bf16[8,1024,128]{2,1,0:T(8,128)(2,1)}), bf16[8,1024,128]{2,1,0:T(8,128)(2,1)S(1)}, u32[]{:S(2)}, u32[]{:S(2)}) async-start(bf16[8,1024,128]{2,1,0:T(8,128)(2,1)} %get-tuple-element.31), calls=%async_computation.1 | async-start | bytes 4194304 | tf_op jit(solution)/shard_map/all_to_all | solution.py:686
  99.2 22.2 %compare_and_add.2 = (f32[8,8,128]{2,1,0:T(8,128)S(1)}, f32[32776,128]{1,0:T(8,128)S(1)}) custom-call(s32[8]{0:T(128)S(1)} %copy-done.8, f32[64]{0:T(128)S(1)} %get-tuple-element.47.defocus_ref, f32[64]{0:T(128)S(1)} %get-tuple-element.46.phase_ref, f32[64]{0:T(128)S(1)} %mul.17.scale_ref, s32[17408]{0:T(1024)S(1)} %bitcast.34, s32[1]{0:T(128)} %bitcast.core_ref, ...), custom_call_target="tpu_custom_call" | custom-call | bytes 16777216 | tf_op jit(solution)/shard_map/compare_and_add/pallas_call | solution.py:697
  121.4 5.7 %copy-done = f32[32776,128]{1,0:T(8,128)} copy-done((f32[32776,128]{1,0:T(8,128)}, f32[32776,128]{1,0:T(8,128)S(1)}, u32[]{:S(2)}) %copy-start) | copy-done | bytes 16781336
  127.1 15.8 %all-to-all-done.1.image_ref = bf16[8,1024,128]{2,1,0:T(8,128)(2,1)S(1)} async-done(((bf16[8,1024,128]{2,1,0:T(8,128)(2,1)}), bf16[8,1024,128]{2,1,0:T(8,128)(2,1)S(1)}, u32[]{:S(2)}, u32[]{:S(2)}) %all-to-all-start.1) | async-done | bytes 2097184 | tf_op jit(solution)/shard_map/all_to_all | solution.py:686
  142.9 5.8 %copy-done.1 = f32[32776,128]{1,0:T(8,128)S(1)} copy-done((f32[32776,128]{1,0:T(8,128)S(1)}, f32[32776,128]{1,0:T(8,128)}, u32[]{:S(2)}) %copy-start.1) | copy-done | bytes 16781336
  150.3 8.0 %compare_and_add.3 = (f32[8,8,128]{2,1,0:T(8,128)S(1)}, f32[32776,128]{1,0:T(8,128)S(1)}, f32[16384,128]{1,0:T(8,128)}, f32[4096,128]{1,0:T(8,128)S(1)}, f32[12288,128]{1,0:T(8,128)}) custom-call(s32[8]{0:T(128)S(1)} %copy-done.8, f32[64]{0:T(128)S(1)} %get-tuple-element.47.defocus_ref, ...), custom_call_target="tpu_custom_call", output_to_operand_aliasing={{1}: (12, {})} | custom-call | bytes 16777216 | tf_op jit(solution)/shard_map/compare_and_add/pallas_call | solution.py:697
  158.9 11.3 %collective-permute-done.1 = f32[4096,128]{1,0:T(8,128)S(1)} collective-permute-done((f32[4096,128]{1,0:T(8,128)S(1)}, f32[4096,128]{1,0:T(8,128)S(1)}, u32[]{:S(2)}, u32[]{:S(2)}) %collective-permute-start.1) | collective-permute-done | bytes 2097184 | tf_op jit(solution)/shard_map/ppermute | solution.py:530
  171.5 8.8 %transform_planes.2 = bf16[8,4,2,32,256]{4,3,2,1,0:T(8,128)(2,1)} custom-call(f32[16,32,32,128]{3,2,1,0:T(8,128)} %bitcast.36, f32[4,32,32,128]{3,2,1,0:T(8,128)} %bitcast.39, bf16[384,256]{1,0:T(8,128)(2,1)} %constant.67.clone.zblock_ref, f32[2,8,128]{2,1,0:T(8,128)} %constant.68.clone.turn_ref, bf16[512,512]{1,0:T(8,128)(2,1)} %constant.69.clone.wide_ref, ...), custom_call_target="tpu_custom_call" | custom-call | flops 536870912 | bytes 8388608 | tf_op jit(solution)/shard_map/transform_planes/pallas_call | solution.py:549
  180.3 16.9 %all-to-all-start.3 = ((bf16[8,4,2,32,256]{4,3,2,1,0:T(8,128)(2,1)}), bf16[8,4,2,32,256]{4,3,2,1,0:T(8,128)(2,1)S(1)}, u32[]{:S(2)}, u32[]{:S(2)}) async-start(bf16[8,4,2,32,256]{4,3,2,1,0:T(8,128)(2,1)} %transform_planes.2), calls=%async_computation.3 | async-start | bytes 2097152 | tf_op jit(solution)/shard_map/all_to_all | solution.py:576
  197.3 22.6 %transform_planes.3 = bf16[8,12,2,32,256]{4,3,2,1,0:T(8,128)(2,1)} custom-call(f32[16,32,32,128]{3,2,1,0:T(8,128)} %bitcast.37, f32[12,32,32,128]{3,2,1,0:T(8,128)} %bitcast.18.theirs_ref, bf16[384,256]{1,0:T(8,128)(2,1)} %constant.67.clone.zblock_ref, f32[2,8,128]{2,1,0:T(8,128)} %constant.68.clone.turn_ref, bf16[512,512]{1,0:T(8,128)(2,1)} %constant.69.clone.wide_ref, ...), custom_call_target="tpu_custom_call" | custom-call | flops 1610612736 | bytes 25165824 | tf_op jit(solution)/shard_map/transform_planes/pallas_call | solution.py:549
  219.8 3.7 %all-to-all-done.3.refs_0_ = bf16[8,4,2,32,256]{4,3,2,1,0:T(8,128)(2,1)S(1)} async-done(((bf16[8,4,2,32,256]{4,3,2,1,0:T(8,128)(2,1)}), bf16[8,4,2,32,256]{4,3,2,1,0:T(8,128)(2,1)S(1)}, u32[]{:S(2)}, u32[]{:S(2)}) %all-to-all-start.3) | async-done | bytes 1048608 | tf_op jit(solution)/shard_map/all_to_all | solution.py:576
  224.5 3.6 %all-to-all-start.4 = ((bf16[8,12,2,32,256]{4,3,2,1,0:T(8,128)(2,1)}), bf16[8,12,2,32,256]{4,3,2,1,0:T(8,128)(2,1)S(1)}, u32[]{:S(2)}, u32[]{:S(2)}) async-start(bf16[8,12,2,32,256]{4,3,2,1,0:T(8,128)(2,1)} %transform_planes.3), calls=%async_computation.4 | async-start | bytes 6291456 | tf_op jit(solution)/shard_map/all_to_all | solution.py:576
  236.1 17.4 %collective-permute-done.2 = f32[1,8]{1,0:T(1,128)S(1)} collective-permute-done((f32[1,8]{1,0:T(1,128)S(1)}, f32[1,8]{1,0:T(1,128)S(1)}, u32[]{:S(2)}, u32[]{:S(2)}) %collective-permute-start.2) | collective-permute-done | bytes 64 | tf_op jit(solution)/shard_map/ppermute | solution.py:513
  256.7 23.0 %collective-permute-done.3 = f32[1,8]{1,0:T(1,128)S(1)} collective-permute-done((f32[1,8]{1,0:T(1,128)S(1)}, f32[1,8]{1,0:T(1,128)S(1)}, u32[]{:S(2)}, u32[]{:S(2)}) %collective-permute-start.3) | collective-permute-done | bytes 64 | tf_op jit(solution)/shard_map/ppermute | solution.py:513
  279.8 3.6 %collective-permute-start.8 = (f32[1,8]{1,0:T(1,128)S(1)}, f32[1,8]{1,0:T(1,128)S(1)}, u32[]{:S(2)}, u32[]{:S(2)}) collective-permute-start(f32[1,8]{1,0:T(1,128)S(1)} %get-tuple-element.51), channel_id=1, source_target_pairs={{0,14},{2,12},{4,10},{6,8},{8,6},{10,4},{12,2},{14,0},{1,15},{3,13... | collective-permute-start | bytes 104 | tf_op jit(solution)/shard_map/ppermute | solution.py:513
  283.3 15.4 %collective-permute-done.5 = f32[1,8]{1,0:T(1,128)S(1)} collective-permute-done((f32[1,8]{1,0:T(1,128)S(1)}, f32[1,8]{1,0:T(1,128)S(1)}, u32[]{:S(2)}, u32[]{:S(2)}) %collective-permute-start.5) | collective-permute-done | bytes 64 | tf_op jit(solution)/shard_map/ppermute | solution.py:513
  301.1 5.5 %collective-permute-done.9.refs_2_ = bf16[8,4,2,32,256]{4,3,2,1,0:T(8,128)(2,1)S(1)} collective-permute-done((bf16[8,4,2,32,256]{4,3,2,1,0:T(8,128)(2,1)}, bf16[8,4,2,32,256]{4,3,2,1,0:T(8,128)(2,1)S(1)}, u32[]{:S(2)}, u32[]{:S(2)}) %collective-permute-start.9) | collective-permute-done | bytes 1048608 | tf_op jit(solution)/shard_map/ppermute | solution.py:579
  309.3 12.5 %transform_first.1 = f32[2,128,32,256]{3,2,1,0:T(8,128)} custom-call(s32[1]{0:T(128)} %bitcast.core_ref, bf16[8,4,2,32,256]{4,3,2,1,0:T(8,128)(2,1)} %copy-done.10, bf16[8,12,2,32,256]{4,3,2,1,0:T(8,128)(2,1)} %copy-done.9, bf16[8,4,2,32,256]{4,3,2,1,0:T(8,128)(2,1)} %copy-done.13, bf16[8,12,2,32,256]{4,3,2,1,0:T(8,128)(2,1)} %copy-done.11), custom_call_target="tpu_custom_call" | custom-call | tf_op jit(solution)/shard_map/transform_first/pallas_call | solution.py:582
  (78 shorter events, 32.1 us)
Async XLA Ops:
  38.3 51.2 %all-to-all-start.2 = ((bf16[8,1024,128]{2,1,0:T(8,128)(2,1)}), bf16[8,1024,128]{2,1,0:T(8,128)(2,1)S(1)}, u32[]{:S(2)}, u32[]{:S(2)}) async-start(bf16[8,1024,128]{2,1,0:T(8,128)(2,1)} %get-tuple-element.32), calls=%async_computation.2 | async-start | bytes 4194304 | tf_op jit(solution)/shard_map/all_to_all | solution.py:686
  42.1 4.2 %copy-start.7 = (s32[8]{0:T(128)}, s32[8]{0:T(128)S(1)}, u32[]{:S(2)}) copy-start(s32[8]{0:T(128)S(1)} %slice_reduce_fusion.2.totals_ref) | copy-start | bytes 100
  59.7 34.8 %copy-start.16 = (f32[64,2]{0,1:T(2,128)S(1)}, f32[64,2]{0,1:T(2,128)}, u32[]{:S(2)}) copy-start(f32[64,2]{0,1:T(2,128)} %param.22) | copy-start | bytes 1540
  59.7 34.9 %copy-start.14 = (bf16[4,128,128]{2,1,0:T(8,128)(2,1)S(1)}, bf16[4,128,128]{2,1,0:T(8,128)(2,1)}, u32[]{:S(2)}) copy-start(bf16[4,128,128]{2,1,0:T(8,128)(2,1)} %param.15) | copy-start | bytes 393220
  59.7 36.3 %copy-start.6 = (s32[136,128]{1,0:T(8,128)S(1)}, s32[136,128]{1,0:T(8,128)}, u32[]{:S(2)}) copy-start(s32[136,128]{1,0:T(8,128)} %decode.1) | copy-start | bytes 208900
  59.7 36.3 %copy-start.8 = (s32[8]{0:T(128)S(1)}, s32[8]{0:T(128)}, u32[]{:S(2)}) copy-start(s32[8]{0:T(128)} %copy-done.7) | copy-start | bytes 100
  90.9 52.0 %all-to-all-start.1 = ((bf16[8,1024,128]{2,1,0:T(8,128)(2,1)}), bf16[8,1024,128]{2,1,0:T(8,128)(2,1)S(1)}, u32[]{:S(2)}, u32[]{:S(2)}) async-start(bf16[8,1024,128]{2,1,0:T(8,128)(2,1)} %get-tuple-element.31), calls=%async_computation.1 | async-start | bytes 4194304 | tf_op jit(solution)/shard_map/all_to_all | solution.py:686
  121.4 5.7 %copy-start = (f32[32776,128]{1,0:T(8,128)}, f32[32776,128]{1,0:T(8,128)S(1)}, u32[]{:S(2)}) copy-start(f32[32776,128]{1,0:T(8,128)S(1)} %get-tuple-element.33.rest_0_) | copy-start | bytes 50343940
  142.9 5.8 %copy-start.1 = (f32[32776,128]{1,0:T(8,128)S(1)}, f32[32776,128]{1,0:T(8,128)}, u32[]{:S(2)}) copy-start(f32[32776,128]{1,0:T(8,128)} %copy-done) | copy-start | bytes 50343940
  158.3 38.9 %collective-permute-start = (f32[12288,128]{1,0:T(8,128)}, f32[12288,128]{1,0:T(8,128)}, u32[]{:S(2)}, u32[]{:S(2)}) collective-permute-start(f32[12288,128]{1,0:T(8,128)} %get-tuple-element.35), channel_id=1, source_target_pairs={{0,1},{1,0},{2,3},{3,2},{4,5},{5,4},{6,7},{7,6},{8,9},{9,8},{10,11... | collective-permute-start | bytes 18874376 | tf_op jit(solution)/shard_map/ppermute | solution.py:530
  158.4 11.8 %collective-permute-start.1 = (f32[4096,128]{1,0:T(8,128)S(1)}, f32[4096,128]{1,0:T(8,128)S(1)}, u32[]{:S(2)}, u32[]{:S(2)}) collective-permute-start(f32[4096,128]{1,0:T(8,128)S(1)} %get-tuple-element.36), channel_id=1, source_target_pairs={{0,1},{1,0},{2,3},{3,2},{4,5},{5,4},{6,7},{7,6},{8,9},{9,8},{10,11... | collective-permute-start | bytes 6291464 | tf_op jit(solution)/shard_map/ppermute | solution.py:530
  180.3 43.2 %all-to-all-start.3 = ((bf16[8,4,2,32,256]{4,3,2,1,0:T(8,128)(2,1)}), bf16[8,4,2,32,256]{4,3,2,1,0:T(8,128)(2,1)S(1)}, u32[]{:S(2)}, u32[]{:S(2)}) async-start(bf16[8,4,2,32,256]{4,3,2,1,0:T(8,128)(2,1)} %transform_planes.2), calls=%async_computation.3 | async-start | bytes 2097152 | tf_op jit(solution)/shard_map/all_to_all | solution.py:576
  219.8 80.4 %copy-start.15 = (s32[8]{0:T(128)S(1)}, s32[8]{0:T(128)}, u32[]{:S(2)}) copy-start(s32[8]{0:T(128)} %counts_ref.3) | copy-start | bytes 100
  224.5 75.1 %all-to-all-start.4 = ((bf16[8,12,2,32,256]{4,3,2,1,0:T(8,128)(2,1)}), bf16[8,12,2,32,256]{4,3,2,1,0:T(8,128)(2,1)S(1)}, u32[]{:S(2)}, u32[]{:S(2)}) async-start(bf16[8,12,2,32,256]{4,3,2,1,0:T(8,128)(2,1)} %transform_planes.3), calls=%async_computation.4 | async-start | bytes 6291456 | tf_op jit(solution)/shard_map/all_to_all | solution.py:576
  228.2 25.3 %collective-permute-start.2 = (f32[1,8]{1,0:T(1,128)S(1)}, f32[1,8]{1,0:T(1,128)S(1)}, u32[]{:S(2)}, u32[]{:S(2)}) collective-permute-start(f32[1,8]{1,0:T(1,128)S(1)} %get-tuple-element.50), channel_id=1, source_target_pairs={{0,2},{2,0},{4,6},{6,4},{8,10},{10,8},{12,14},{14,12},{1,3},{3,1},... | collective-permute-start | bytes 104 | tf_op jit(solution)/shard_map/ppermute | solution.py:513
  230.2 49.6 %collective-permute-start.3 = (f32[1,8]{1,0:T(1,128)S(1)}, f32[1,8]{1,0:T(1,128)S(1)}, u32[]{:S(2)}, u32[]{:S(2)}) collective-permute-start(f32[1,8]{1,0:T(1,128)S(1)} %get-tuple-element.56), channel_id=1, source_target_pairs={{0,4},{2,6},{4,0},{6,2},{8,12},{10,14},{12,8},{14,10},{1,5},{3,7},... | collective-permute-start | bytes 104 | tf_op jit(solution)/shard_map/ppermute | solution.py:513
  231.7 51.7 %collective-permute-start.4 = (f32[1,8]{1,0:T(1,128)S(1)}, f32[1,8]{1,0:T(1,128)S(1)}, u32[]{:S(2)}, u32[]{:S(2)}) collective-permute-start(f32[1,8]{1,0:T(1,128)S(1)} %get-tuple-element.55), channel_id=1, source_target_pairs={{0,6},{2,4},{4,2},{6,0},{8,14},{10,12},{12,10},{14,8},{1,7},{3,5},... | collective-permute-start | bytes 104 | tf_op jit(solution)/shard_map/ppermute | solution.py:513
  231.7 67.0 %collective-permute-start.5 = (f32[1,8]{1,0:T(1,128)S(1)}, f32[1,8]{1,0:T(1,128)S(1)}, u32[]{:S(2)}, u32[]{:S(2)}) collective-permute-start(f32[1,8]{1,0:T(1,128)S(1)} %get-tuple-element.54), channel_id=1, source_target_pairs={{0,8},{2,10},{4,12},{6,14},{8,0},{10,2},{12,4},{14,6},{1,9},{3,11}... | collective-permute-start | bytes 104 | tf_op jit(solution)/shard_map/ppermute | solution.py:513
  234.6 65.0 %collective-permute-start.6 = (f32[1,8]{1,0:T(1,128)S(1)}, f32[1,8]{1,0:T(1,128)S(1)}, u32[]{:S(2)}, u32[]{:S(2)}) collective-permute-start(f32[1,8]{1,0:T(1,128)S(1)} %get-tuple-element.53), channel_id=1, source_target_pairs={{0,10},{2,8},{4,14},{6,12},{8,2},{10,0},{12,6},{14,4},{1,11},{3,9}... | collective-permute-start | bytes 104 | tf_op jit(solution)/shard_map/ppermute | solution.py:513
  253.5 46.1 %collective-permute-start.7 = (f32[1,8]{1,0:T(1,128)S(1)}, f32[1,8]{1,0:T(1,128)S(1)}, u32[]{:S(2)}, u32[]{:S(2)}) collective-permute-start(f32[1,8]{1,0:T(1,128)S(1)} %get-tuple-element.52), channel_id=1, source_target_pairs={{0,12},{2,14},{4,8},{6,10},{8,4},{10,6},{12,0},{14,2},{1,13},{3,15... | collective-permute-start | bytes 104 | tf_op jit(solution)/shard_map/ppermute | solution.py:513
  279.8 19.8 %collective-permute-start.8 = (f32[1,8]{1,0:T(1,128)S(1)}, f32[1,8]{1,0:T(1,128)S(1)}, u32[]{:S(2)}, u32[]{:S(2)}) collective-permute-start(f32[1,8]{1,0:T(1,128)S(1)} %get-tuple-element.51), channel_id=1, source_target_pairs={{0,14},{2,12},{4,10},{6,8},{8,6},{10,4},{12,2},{14,0},{1,15},{3,13... | collective-permute-start | bytes 104 | tf_op jit(solution)/shard_map/ppermute | solution.py:513
  299.6 7.2 %copy-start.9 = (bf16[8,12,2,32,256]{4,3,2,1,0:T(8,128)(2,1)}, bf16[8,12,2,32,256]{4,3,2,1,0:T(8,128)(2,1)S(1)}, u32[]{:S(2)}) copy-start(bf16[8,12,2,32,256]{4,3,2,1,0:T(8,128)(2,1)S(1)} %all-to-all-done.4.refs_1_) | copy-start | bytes 9437188
  299.6 7.2 %collective-permute-start.10 = (bf16[8,12,2,32,256]{4,3,2,1,0:T(8,128)(2,1)S(1)}, bf16[8,12,2,32,256]{4,3,2,1,0:T(8,128)(2,1)S(1)}, u32[]{:S(2)}, u32[]{:S(2)}) collective-permute-start(bf16[8,12,2,32,256]{4,3,2,1,0:T(8,128)(2,1)S(1)} %all-to-all-done.4.refs_1_), channel_id=1, source_target_pairs={{0,1},{1,0},{2,3},{3,2},{4,5},{5,4},{6,7},{7,6},{8,9},{9,8},{10,11... | collective-permute-start | bytes 9437192 | tf_op jit(solution)/shard_map/ppermute | solution.py:579
  299.7 7.0 %collective-permute-start.9 = (bf16[8,4,2,32,256]{4,3,2,1,0:T(8,128)(2,1)}, bf16[8,4,2,32,256]{4,3,2,1,0:T(8,128)(2,1)S(1)}, u32[]{:S(2)}, u32[]{:S(2)}) collective-permute-start(bf16[8,4,2,32,256]{4,3,2,1,0:T(8,128)(2,1)} %copy-done.10), channel_id=1, source_target_pairs={{0,1},{1,0},{2,3},{3,2},{4,5},{5,4},{6,7},{7,6},{8,9},{9,8},{10,11... | collective-permute-start | bytes 3145736 | tf_op jit(solution)/shard_map/ppermute | solution.py:579
  (8 other events, 11.0 us)

commit v10 on v9

--- a/solution.py
+++ b/solution.py
@@ -185,13 +185,11 @@
 
 
 def slab_kernel(
-    side, local_bits, list_length, particles, cap, offset, first, last,
+    side, local_bits, list_length, particles, cap, offset,
     totals_ref, defocus_ref, phase_ref, scale_ref, index_ref, core_ref,
     word_ref, voxel_ref, image_ref, forward_ref, backward_ref, unit_ref, *rest,
 ):
-    if not first:
-        rest = rest[1:]
-    square_ref, sum_ref, out_refs, (staged_ref, steps_ref, sems) = rest[0], rest[1], rest[2:-3], rest[-3:]
+    square_ref, out_refs, (sum_ref, staged_ref, steps_ref, sems) = rest[0], rest[1:-4], rest[-4:]
     slabs, _, tile = word_ref.shape
     step = staged_ref.shape[0]
     steps_each = tile // step
@@ -202,11 +200,10 @@
     per_row = side // 8
     half = features // 2
 
-    if first:
-        @pl.loop(0, blocks // 256)
-        def _(i):
-            at = pl.multiple_of(i * 256, 256)
-            sum_ref[pl.ds(at, 256), :] = jnp.zeros((256, features), jnp.float32)
+    @pl.loop(0, blocks // 256)
+    def _(i):
+        at = pl.multiple_of(i * 256, 256)
+        sum_ref[pl.ds(at, 256), :] = jnp.zeros((256, features), jnp.float32)
 
     square_ref[...] = jnp.zeros_like(square_ref)
     live_of = lambda source: jnp.clip(totals_ref[source] - offset, 0, tile)
@@ -321,22 +318,21 @@
 
             compare(number)
 
-    if last:
-        half = blocks // 2
-        start = (1 - core_ref[0]) * half
-        places = [core_ref[0] * half]
-        for out_ref in out_refs[1:]:
-            places.append(start)
-            start = start + out_ref.shape[0]
-        copies = []
-        for i, (place, out_ref) in enumerate(zip(places, out_refs)):
-            length = out_ref.shape[0]
-            at = pl.multiple_of(place, 8)
-            copies.append(pltpu.make_async_copy(sum_ref.at[pl.ds(at, length)], out_ref, sems.at[i]))
-        for copy in copies:
-            copy.start()
-        for copy in copies:
-            copy.wait()
+    half = blocks // 2
+    start = (1 - core_ref[0]) * half
+    places = [core_ref[0] * half]
+    for out_ref in out_refs[1:]:
+        places.append(start)
+        start = start + out_ref.shape[0]
+    copies = []
+    for i, (place, out_ref) in enumerate(zip(places, out_refs)):
+        length = out_ref.shape[0]
+        at = pl.multiple_of(place, 8)
+        copies.append(pltpu.make_async_copy(sum_ref.at[pl.ds(at, length)], out_ref, sems.at[i]))
+    for copy in copies:
+        copy.start()
+    for copy in copies:
+        copy.wait()
 
 
 def pieces_of(planes):
@@ -391,15 +387,17 @@
     return high, (value - high.astype(jnp.float32)).astype(jnp.bfloat16)
 
 
-def planes_kernel(mine_ref, theirs_ref, zblock_ref, turn_ref, wide_ref, fine_ref, out_ref, high_ref, low_ref):
+def planes_kernel(halves, *refs):
+    half_refs, rest = refs[:halves], refs[halves:]
+    zblock_ref, turn_ref, wide_ref, fine_ref, out_ref, high_ref, low_ref = rest
     step = pl.program_id(1)
-    count = mine_ref.shape[1]
+    count = half_refs[0].shape[1]
     groups, side = out_ref.shape[0], out_ref.shape[4]
     height = side // groups
 
     @pl.loop(0, count, unroll=8)
     def _(i):
-        block = (mine_ref[:, i] + theirs_ref[:, i]).reshape(LANES, LANES)
+        block = sum(ref[:, i] for ref in half_refs).reshape(LANES, LANES)
         high, low = in_halves(block.T)
         both = jnp.dot(
             jnp.concatenate([high, low, high], axis=1), zblock_ref[...],
@@ -519,7 +517,7 @@
     return jnp.sum(returned, axis=0)
 
 
-def to_field(mine, theirs_sent, partial_sums, side):
+def to_field(mine, theirs, partial_sums, side):
     slabs = lax.axis_size("slab")
     per_row = side // 8
     each = side // slabs // 2
@@ -527,32 +525,34 @@
     groups = slabs if height % 16 == 0 else 1
     tables = [jnp.asarray(table) for table in transform_tables(side)]
     swap = [(0, 1), (1, 0)]
-    theirs = [lax.ppermute(chunk, "dom", swap) for chunk in theirs_sent]
-    grid_shape = (-1, per_row, per_row, LANES)
-    mine = mine.reshape(grid_shape)
     short = max(0, 4 - each)
-    if short:
-        mine = jnp.pad(mine, ((0, short), (0, 0), (0, 0), (0, 0)))
+
+    def gridded(half):
+        half = half.reshape(-1, per_row, per_row, LANES)
+        return jnp.pad(half, ((0, short), (0, 0), (0, 0), (0, 0))) if short else half
+
+    mine = [gridded(half) for half in mine]
     yblocks = 8
     own = []
     first_quad = 0
     before = []
-    for real_planes, added in zip(pieces_of(each), theirs):
+    for chunk, real_planes in enumerate(pieces_of(each)):
+        added = [part[chunk] for part in theirs]
         if before:
-            added, before[0] = lax.optimization_barrier((added, before[0]))
-        added = added.reshape(grid_shape)
-        if short:
-            added = jnp.pad(added, ((0, short), (0, 0), (0, 0), (0, 0)))
+            added[-1], before[0] = lax.optimization_barrier((added[-1], before[0]))
+        added = [gridded(half) for half in added]
         held = real_planes + short
         quads = held // 4
         whole = lambda table: pl.BlockSpec(table.shape, lambda q, y: (0,) * table.ndim)
         sent = pl.pallas_call(
-            planes_kernel,
+            functools.partial(planes_kernel, len(mine) + len(added)),
             grid=(quads, per_row // yblocks),
             out_shape=jax.ShapeDtypeStruct((groups, held, 2, side // groups, side), jnp.bfloat16),
             in_specs=[
-                pl.BlockSpec((4, yblocks, per_row, LANES), lambda q, y, at=first_quad: (at + q, y, 0, 0)),
-                pl.BlockSpec((4, yblocks, per_row, LANES), lambda q, y: (q, y, 0, 0)),
+                pl.BlockSpec((4, yblocks, per_row, LANES), lambda q, y, at=first_quad: (at + q, y, 0, 0))
+                for _ in mine
+            ] + [
+                pl.BlockSpec((4, yblocks, per_row, LANES), lambda q, y: (q, y, 0, 0)) for _ in added
             ] + [whole(table) for table in tables],
             out_specs=pl.BlockSpec((groups, 4, 2, side // groups, side), lambda q, y: (0, q, 0, 0, 0)),
             scratch_shapes=[
@@ -564,7 +564,7 @@
                 flops=held * 8 * side**3, bytes_accessed=held * 4 * side**2 * 8, transcendentals=0
             ),
             name="transform_planes",
-        )(mine, added, *tables)
+        )(*mine, *added, *tables)
         if groups != slabs:
             sent = sent.reshape(-1, 2, slabs, height, side).transpose(2, 0, 1, 3, 4)[:, :real_planes]
         first_quad += quads
@@ -575,8 +575,9 @@
         before = [sent]
         got = lax.all_to_all(sent, "slab", split_axis=0, concat_axis=0, tiled=True)
         own.append(got)
-    own[-1], losses = lax.optimization_barrier((own[-1], sum_over_slabs(partial_sums)))
-    other = [lax.ppermute(got, "dom", swap) for got in own]
+    other = [lax.ppermute(got, "dom", swap) for got in own[:-1]]
+    own[-1], losses, *other = lax.optimization_barrier((own[-1], sum_over_slabs(partial_sums), *other))
+    other.append(lax.ppermute(own[-1], "dom", swap))
     rows = min(16, height)
     arrays = own + other
     field = pl.pallas_call(
@@ -589,7 +590,7 @@
         ],
         out_specs=pl.BlockSpec((2, side // 2, rows, LANES), lambda y, z: (0, 0, y, z)),
         scratch_shapes=[pltpu.VMEM((16, 16, 2, rows, LANES), jnp.float32)],
-        compiler_params=params(56),
+        compiler_params=params(28),
         name="transform_first",
     )(lax.axis_index("dom").astype(jnp.int32).reshape(1), *arrays)
     return field, losses
@@ -617,7 +618,7 @@
         name="route",
     )(owners.reshape(rows, LANES), local_block, kinds, counts)
     target, word = target.reshape(entries), word.reshape(entries)
-    tiles = [cap // 2, cap // 2] if cap >= 2048 else [cap]
+    tiles = [cap * 5 // 8, cap * 3 // 8] if cap >= 2048 else [cap]
     parts = len(tiles)
     code = ctf_code | ((scales.astype(jnp.float32) * 256.0).astype(jnp.int32) << 8)
     stride = cap + LANES
@@ -676,49 +677,41 @@
     core = lax.axis_index("dom").astype(jnp.int32).reshape(1)
     plane_blocks = (side // 8) ** 2
     pieces = [planes * plane_blocks for planes in pieces_of(side // slabs // 2)]
-    squares, sums, behind, offset = 0.0, None, [voxels[0]], 0
+    squares, offset, mine, theirs = 0.0, 0, [], []
+    lengths = [blocks // 2] + pieces
     for part, tile in enumerate(tiles):
-        first, last = part == 0, part == parts - 1
-        if not first:
-            packed[part], earlier = lax.optimization_barrier((packed[part], behind[part - 1]))
-            if part == 1:
-                voxels[0] = earlier
+        if part == 1:
+            packed[1], voxels[0] = lax.optimization_barrier((packed[1], voxels[0]))
         picture = lax.all_to_all(packed[part], "slab", split_axis=0, concat_axis=0, tiled=True)
-        lengths = [blocks // 2] + pieces if last else []
-        arguments = [
+        more, own_half, *other_half = pl.pallas_call(
+            functools.partial(slab_kernel, side, local_bits, list_length, particles, cap, offset),
+            out_shape=(jax.ShapeDtypeStruct((slabs, particles, LANES), jnp.float32),)
+            + tuple(jax.ShapeDtypeStruct((length, features), jnp.float32) for length in lengths),
+            in_specs=[SMEM_SPEC] * 6 + [VMEM_SPEC] * 6,
+            out_specs=(VMEM_SPEC,) + (ANY_SPEC,) * len(lengths),
+            scratch_shapes=[
+                pltpu.VMEM((blocks + 8, features), jnp.float32),
+                pltpu.VMEM((min(tile, STEP), features), jnp.float32),
+                pltpu.SMEM((slabs * tile // min(tile, STEP) + 1,), jnp.int32),
+                pltpu.SemaphoreType.DMA((len(lengths),)),
+            ],
+            compiler_params=params(56),
+            cost_estimate=pl.CostEstimate(flops=0, bytes_accessed=16 * MIB, transcendentals=0),
+            name="compare_and_add",
+        )(
             totals_in, table_rows[:, 0], table_rows[:, 1], scale_in, index, core,
             words[:, offset:offset + tile].reshape(slabs, 1, tile), voxels[part], picture,
             forward, backward, unit,
-        ]
-        aliases = {}
-        if not first:
-            aliases = {len(arguments): 1}
-            arguments.append(pltpu.with_memory_space_constraint(sums, pltpu.VMEM))
-        more, sums, *halves = pl.pallas_call(
-            functools.partial(
-                slab_kernel, side, local_bits, list_length, particles, cap, offset, first, last
-            ),
-            out_shape=(
-                jax.ShapeDtypeStruct((slabs, particles, LANES), jnp.float32),
-                pltpu.VMEM((blocks + 8, features), jnp.float32),
+        )
+        received = [lax.ppermute(piece, "dom", [(0, 1), (1, 0)]) for piece in other_half]
+        if part + 1 < parts:
+            voxels[part + 1], more, received[0] = lax.optimization_barrier(
+                (voxels[part + 1], more, received[0])
             )
-            + tuple(jax.ShapeDtypeStruct((length, features), jnp.float32) for length in lengths),
-            in_specs=[SMEM_SPEC] * 6 + [VMEM_SPEC] * (len(arguments) - 6),
-            out_specs=(VMEM_SPEC, VMEM_SPEC) + (ANY_SPEC,) * len(lengths),
-            scratch_shapes=[
-                pltpu.VMEM((min(tile, STEP), features), jnp.float32),
-                pltpu.SMEM((slabs * tile // min(tile, STEP) + 1,), jnp.int32),
-                pltpu.SemaphoreType.DMA((max(1, len(lengths)),)),
-            ],
-            input_output_aliases=aliases,
-            compiler_params=params(24),
-            cost_estimate=pl.CostEstimate(flops=0, bytes_accessed=16 * MIB, transcendentals=0),
-            name="compare_and_add",
-        )(*arguments)
         squares = squares + more
-        behind.append(more)
+        mine.append(own_half)
+        theirs.append(received)
         offset += tile
-    mine, *theirs = halves
     partial_sums = jnp.sum(squares, axis=2)
     return mine, theirs, partial_sums, side
 

time: 324 us -> 338 us (1.043)
  Pallas kernels: 114 us -> 159 us
  waiting for transfers between devices: 123 us -> 105 us
  local copies, waits for them, and re-layouts: 24.6 us -> 9.42 us
    pallas_call x2, Pallas kernels: 30.2 us -> 65.4 us  [gradient_of_slab(): pl.pallas_call(functools.partial(slab_kernel, side, local_bits, list_leng...]
    unnamed x36 -> x24, local copies, waits for them, and re-layouts: 22.5 us -> 3.71 us
    all_to_all x2, waiting for transfers between devices: 45.6 us -> 30.7 us  [gradient_of_slab(): lax.all_to_all(packed[part], 'slab', split_axis=0, concat_axis=0, tiled=T...]
    all_to_all x2, starting transfers between devices: 20.5 us -> 7.93 us  [to_field(): got = lax.all_to_all(sent, 'slab', split_axis=0, concat_axis=0, tiled=True)]
    ppermute x7, starting transfers between devices: 14.7 us -> 27 us  [sum_over_slabs(): lax.ppermute(row(i), 'slab', [(slab, slab ^ i) for slab in range(slabs)])]
    pallas_call x1, Pallas kernels: 13.4 us -> 21.5 us  [gradient_of_slab(): pl.pallas_call(functools.partial(gather_kernel, slabs, cap), out_shape=tu...]
    ppermute x7, waiting for transfers between devices: 56.7 us -> 51.2 us  [sum_over_slabs(): lax.ppermute(row(i), 'slab', [(slab, slab ^ i) for slab in range(slabs)])]
    ppermute x4 -> x6, waiting for transfers between devices: 17 us -> 21 us  [the longest x4 15.9 us: gradient_of_slab(): lax.ppermute(piece, 'dom', [(0, 1), (1, 0)])]
  transfers between devices with their start and end apart: 15 -> 17, of which waited for: 10 -> 8; matrix products, arithmetic and copies ran while one was open for 1% -> 2% of each run, Pallas kernels for 22% -> 30%
where the time goes in v10:
time: 338 us
  Pallas kernels  159 us (47%)
  waiting for transfers between devices  105 us (31%)
  starting transfers between devices  45.9 us (14%)
  blocking collectives  15 us (4%)
  local copies, waits for them, and re-layouts  9.42 us (3%)
    pallas_call x2, Pallas kernels, gradient_of_slab(): pl.pallas_call(functools.partial(slab_kernel, side, local_bits, list_leng...  65.4 us
    ppermute x7, waiting for transfers between devices, sum_over_slabs(): lax.ppermute(row(i), 'slab', [(slab, slab ^ i) for slab in range(slabs)])  51.2 us
    pallas_call x2, Pallas kernels, to_field(): pl.pallas_call(functools.partial(planes_kernel, len(mine) + len(added)),...  34.1 us
    all_to_all x2, waiting for transfers between devices, gradient_of_slab(): lax.all_to_all(packed[part], 'slab', split_axis=0, concat_axis=0, tiled=T...  30.7 us
    ppermute x7, starting transfers between devices, sum_over_slabs(): lax.ppermute(row(i), 'slab', [(slab, slab ^ i) for slab in range(slabs)])  27 us
    pallas_call x1, Pallas kernels, gradient_of_slab(): pl.pallas_call(functools.partial(gather_kernel, slabs, cap), out_shape=tu...  21.5 us
    pallas_call x1, Pallas kernels, gradient_of_slab(): pl.pallas_call(functools.partial(pack_kernel, slabs, cap, list_length), o...  19.2 us
    ppermute x4, waiting for transfers between devices, gradient_of_slab(): lax.ppermute(piece, 'dom', [(0, 1), (1, 0)])  15.9 us
  transfers between devices with their start and end apart: 17, of which 8 were waited for; matrix products, arithmetic and copies ran while one was open for 2% of the time, Pallas kernels for 30%

profile of v10, /device:TPU:0, one launch (start us, length us, event | category | flops | bytes accessed | tf_op | source)
XLA Modules:
  0.0 338.4 jit_solution(5097237864157000209)
XLA Ops:
  1.8 3.7 %route.1 = (s32[64,128]{1,0:T(8,128)}, s32[64,128]{1,0:T(8,128)}, s32[8,128]{1,0:T(8,128)}) custom-call(s32[64,128]{1,0:T(8,128)} %bitcast.57, s32[8,1024]{1,0:T(8,128)} %local_ref.1, s32[8,1024]{1,0:T(8,128)} %kind_ref.1, s32[8]{0:T(128)} %counts_ref.3), custom_call_target="tpu_custom_call" | custom-call | tf_op jit(solution)/shard_map/route/pallas_call | solution.py:612
  5.6 19.2 %pack.1 = (s32[17408]{0:T(1024)}, bf16[8,1280,128]{2,1,0:T(8,128)(2,1)}, bf16[8,768,128]{2,1,0:T(8,128)(2,1)}) custom-call(s32[8192]{0:T(1024)} %bitcast.55, s32[8192]{0:T(1024)} %bitcast.56, s32[8]{0:T(128)} %counts_ref.3, s32[8,128]{1,0:T(8,128)} %get-tuple-element.32.totals_ref, s32[8]{0:T(128)} %shift-left_or_fusion.code_ref, bf16[8192,128]{1,0:T(8,128)(2,1)} %bitcast.36), custom_call_target="tpu_custom_call" | custom-call | tf_op jit(solution)/shard_map/pack/pallas_call | solution.py:625
  24.8 15.0 %all_to_all.32 = s32[8,1,2176]{2,1,0:T(1,128)S(1)} all-to-all(s32[8,1,2176]{2,1,0:T(1,128)} %bitcast.54), channel_id=1, replica_groups=mesh['groups'=2,'slab'=8,'dom'=2] {'slab'}, dimensions={0} | all-to-all | bytes 139264 | tf_op jit(solution)/shard_map/all_to_all | solution.py:638
  39.8 3.6 %all-to-all-start.1 = ((bf16[8,1280,128]{2,1,0:T(8,128)(2,1)}), bf16[8,1280,128]{2,1,0:T(8,128)(2,1)S(1)}, u32[]{:S(2)}, u32[]{:S(2)}) async-start(bf16[8,1280,128]{2,1,0:T(8,128)(2,1)} %get-tuple-element.35), calls=%async_computation.1 | async-start | bytes 5242880 | tf_op jit(solution)/shard_map/all_to_all | solution.py:685
  47.4 2.7 decode.1
  50.1 21.5 %read_voxels.1 = (bf16[8,1280,128]{2,1,0:T(8,128)(2,1)}, bf16[8,768,128]{2,1,0:T(8,128)(2,1)}) custom-call(s32[17408]{0:T(1024)} %bitcast.43, s32[8]{0:T(128)} %copy-done.8, bf16[32768,128]{1,0:T(8,128)(2,1)} %volume_ref.1), custom_call_target="tpu_custom_call" | custom-call | bytes 104857600 | tf_op jit(solution)/shard_map/read_voxels/pallas_call | solution.py:657
  71.6 30.7 %all-to-all-done.1.image_ref = bf16[8,1280,128]{2,1,0:T(8,128)(2,1)S(1)} async-done(((bf16[8,1280,128]{2,1,0:T(8,128)(2,1)}), bf16[8,1280,128]{2,1,0:T(8,128)(2,1)S(1)}, u32[]{:S(2)}, u32[]{:S(2)}) %all-to-all-start.1) | async-done | bytes 2621472 | tf_op jit(solution)/shard_map/all_to_all | solution.py:685
  102.4 4.3 %all-to-all-start.2 = ((bf16[8,768,128]{2,1,0:T(8,128)(2,1)}), bf16[8,768,128]{2,1,0:T(8,128)(2,1)}, u32[]{:S(2)}, u32[]{:S(2)}) async-start(bf16[8,768,128]{2,1,0:T(8,128)(2,1)} %get-tuple-element.42), calls=%async_computation.2 | async-start | bytes 3145728 | tf_op jit(solution)/shard_map/all_to_all | solution.py:685
  109.4 44.0 %compare_and_add.2 = (f32[8,8,128]{2,1,0:T(8,128)}, f32[16384,128]{1,0:T(8,128)}, f32[4096,128]{1,0:T(8,128)}, f32[12288,128]{1,0:T(8,128)}) custom-call(s32[8]{0:T(128)} %copy-done.8, f32[64]{0:T(128)} %get-tuple-element.59.defocus_ref, f32[64]{0:T(128)} %get-tuple-element.58.phase_ref, f32[64]{0:T(128)} %mul.17.scale_ref, s32[17408]{0:T(1024)} %bitcast.44, ...), custom_call_target="tpu_custom_call" | custom-call | bytes 16777216 | tf_op jit(solution)/shard_map/compare_and_add/pallas_call | solution.py:686
  154.1 3.7 %collective-permute-done = f32[4096,128]{1,0:T(8,128)S(1)} collective-permute-done((f32[4096,128]{1,0:T(8,128)}, f32[4096,128]{1,0:T(8,128)S(1)}, u32[]{:S(2)}, u32[]{:S(2)}) %collective-permute-start) | collective-permute-done | bytes 2097184 | tf_op jit(solution)/shard_map/ppermute | solution.py:706
  157.8 21.4 %compare_and_add.3 = (f32[8,8,128]{2,1,0:T(8,128)}, f32[16384,128]{1,0:T(8,128)}, f32[4096,128]{1,0:T(8,128)}, f32[12288,128]{1,0:T(8,128)}) custom-call(s32[8]{0:T(128)} %copy-done.8, f32[64]{0:T(128)} %get-tuple-element.59.defocus_ref, f32[64]{0:T(128)} %get-tuple-element.58.phase_ref, f32[64]{0:T(128)} %mul.17.scale_ref, s32[17408]{0:T(1024)} %bitcast.45, ...), custom_call_target="tpu_custom_call" | custom-call | bytes 16777216 | tf_op jit(solution)/shard_map/compare_and_add/pallas_call | solution.py:686
  179.2 2.4 collective-permute-start.2
  182.1 12.2 %collective-permute-done.3 = f32[4096,128]{1,0:T(8,128)S(1)} collective-permute-done((f32[4096,128]{1,0:T(8,128)}, f32[4096,128]{1,0:T(8,128)S(1)}, u32[]{:S(2)}, u32[]{:S(2)}) %collective-permute-start.3) | collective-permute-done | bytes 2097184 | tf_op jit(solution)/shard_map/ppermute | solution.py:706
  195.7 9.5 %transform_planes.2 = bf16[8,4,2,32,256]{4,3,2,1,0:T(8,128)(2,1)} custom-call(f32[16,32,32,128]{3,2,1,0:T(8,128)} %bitcast.32, f32[16,32,32,128]{3,2,1,0:T(8,128)} %bitcast.34, f32[4,32,32,128]{3,2,1,0:T(8,128)} %bitcast.37, f32[4,32,32,128]{3,2,1,0:T(8,128)} %bitcast.38, bf16[384,256]{1,0:T(8,128)(2,1)} %constant.67.clone.refs_4_, ...), custom_call_target="tpu_custom_call" | custom-call | flops 536870912 | bytes 8388608 | tf_op jit(solution)/shard_map/transform_planes/pallas_call | solution.py:547
  205.3 3.6 %all-to-all-start.3 = ((bf16[8,4,2,32,256]{4,3,2,1,0:T(8,128)(2,1)}), bf16[8,4,2,32,256]{4,3,2,1,0:T(8,128)(2,1)S(1)}, u32[]{:S(2)}, u32[]{:S(2)}) async-start(bf16[8,4,2,32,256]{4,3,2,1,0:T(8,128)(2,1)} %transform_planes.2), calls=%async_computation.3 | async-start | bytes 2097152 | tf_op jit(solution)/shard_map/all_to_all | solution.py:576
  208.9 24.6 %transform_planes.3 = bf16[8,12,2,32,256]{4,3,2,1,0:T(8,128)(2,1)} custom-call(f32[16,32,32,128]{3,2,1,0:T(8,128)} %bitcast.33, f32[16,32,32,128]{3,2,1,0:T(8,128)} %bitcast.35, f32[12,32,32,128]{3,2,1,0:T(8,128)} %bitcast.18.refs_2_, f32[12,32,32,128]{3,2,1,0:T(8,128)} %bitcast.21.refs_3_, bf16[384,256]{1,0:T(8,128)(2,1)} %constant.67.clone.refs_4_, ...), custom_call_target="tpu_custom_call" | custom-call | flops 1610612736 | bytes 25165824 | tf_op jit(solution)/shard_map/transform_planes/pallas_call | solution.py:547
  236.1 4.4 %all-to-all-start.4 = ((bf16[8,12,2,32,256]{4,3,2,1,0:T(8,128)(2,1)}), bf16[8,12,2,32,256]{4,3,2,1,0:T(8,128)(2,1)S(1)}, u32[]{:S(2)}, u32[]{:S(2)}) async-start(bf16[8,12,2,32,256]{4,3,2,1,0:T(8,128)(2,1)} %transform_planes.3), calls=%async_computation.4 | async-start | bytes 6291456 | tf_op jit(solution)/shard_map/all_to_all | solution.py:576
  240.5 4.7 %collective-permute-start.10 = (f32[1,8]{1,0:T(1,128)S(1)}, f32[1,8]{1,0:T(1,128)S(1)}, u32[]{:S(2)}, u32[]{:S(2)}) collective-permute-start(f32[1,8]{1,0:T(1,128)S(1)} %get-tuple-element.61), channel_id=1, source_target_pairs={{0,14},{2,12},{4,10},{6,8},{8,6},{10,4},{12,2},{14,0},{1,15},{3,13... | collective-permute-start | bytes 104 | tf_op jit(solution)/shard_map/ppermute | solution.py:511
  245.8 2.9 collective-permute-start.6
  248.7 47.5 %collective-permute-done.10 = f32[1,8]{1,0:T(1,128)S(1)} collective-permute-done((f32[1,8]{1,0:T(1,128)S(1)}, f32[1,8]{1,0:T(1,128)S(1)}, u32[]{:S(2)}, u32[]{:S(2)}) %collective-permute-start.10) | collective-permute-done | bytes 64 | tf_op jit(solution)/shard_map/ppermute | solution.py:511
  296.2 16.4 %collective-permute-start.7 = (f32[1,8]{1,0:T(1,128)S(1)}, f32[1,8]{1,0:T(1,128)S(1)}, u32[]{:S(2)}, u32[]{:S(2)}) collective-permute-start(f32[1,8]{1,0:T(1,128)S(1)} %get-tuple-element.64), channel_id=1, source_target_pairs={{0,8},{2,10},{4,12},{6,14},{8,0},{10,2},{12,4},{14,6},{1,9},{3,11}... | collective-permute-start | bytes 104 | tf_op jit(solution)/shard_map/ppermute | solution.py:511
  315.1 2.9 collective-permute-done.8
  319.4 5.1 %collective-permute-done.12.refs_3_ = bf16[8,12,2,32,256]{4,3,2,1,0:T(8,128)(2,1)S(1)} collective-permute-done((bf16[8,12,2,32,256]{4,3,2,1,0:T(8,128)(2,1)S(1)}, bf16[8,12,2,32,256]{4,3,2,1,0:T(8,128)(2,1)S(1)}, u32[]{:S(2)}, u32[]{:S(2)}) %collective-permute-start.12) | collective-permute-done | bytes 3145760 | tf_op jit(solution)/shard_map/ppermute | solution.py:580
  325.8 12.6 %transform_first.1 = f32[2,128,32,256]{3,2,1,0:T(8,128)} custom-call(s32[1]{0:T(128)} %bitcast.core_ref, bf16[8,4,2,32,256]{4,3,2,1,0:T(8,128)(2,1)S(1)} %copy-done.1, bf16[8,12,2,32,256]{4,3,2,1,0:T(8,128)(2,1)S(1)} %all-to-all-done.4.refs_1_, bf16[8,4,2,32,256]{4,3,2,1,0:T(8,128)(2,1)} %collective-permute-done.11.refs_2_, ...), custom_call_target="tpu_custom_call" | custom-call | tf_op jit(solution)/shard_map/transform_first/pallas_call | solution.py:583
  (71 shorter events, 18.8 us)
Async XLA Ops:
  24.8 18.7 %copy-start.10 = (f32[64,2]{0,1:T(2,128)S(1)}, f32[64,2]{0,1:T(2,128)}, u32[]{:S(2)}) copy-start(f32[64,2]{0,1:T(2,128)} %param.22) | copy-start | bytes 1540
  24.8 18.8 %copy-start.5 = (bf16[4,128,128]{2,1,0:T(8,128)(2,1)S(1)}, bf16[4,128,128]{2,1,0:T(8,128)(2,1)}, u32[]{:S(2)}) copy-start(bf16[4,128,128]{2,1,0:T(8,128)(2,1)} %param.15) | copy-start | bytes 393220
  39.8 62.5 %all-to-all-start.1 = ((bf16[8,1280,128]{2,1,0:T(8,128)(2,1)}), bf16[8,1280,128]{2,1,0:T(8,128)(2,1)S(1)}, u32[]{:S(2)}, u32[]{:S(2)}) async-start(bf16[8,1280,128]{2,1,0:T(8,128)(2,1)} %get-tuple-element.35), calls=%async_computation.1 | async-start | bytes 5242880 | tf_op jit(solution)/shard_map/all_to_all | solution.py:685
  102.4 7.0 %copy-start.2 = (bf16[8,1280,128]{2,1,0:T(8,128)(2,1)}, bf16[8,1280,128]{2,1,0:T(8,128)(2,1)S(1)}, u32[]{:S(2)}) copy-start(bf16[8,1280,128]{2,1,0:T(8,128)(2,1)S(1)} %all-to-all-done.1.image_ref) | copy-start | bytes 7864324
  102.4 55.5 %all-to-all-start.2 = ((bf16[8,768,128]{2,1,0:T(8,128)(2,1)}), bf16[8,768,128]{2,1,0:T(8,128)(2,1)}, u32[]{:S(2)}, u32[]{:S(2)}) async-start(bf16[8,768,128]{2,1,0:T(8,128)(2,1)} %get-tuple-element.42), calls=%async_computation.2 | async-start | bytes 3145728 | tf_op jit(solution)/shard_map/all_to_all | solution.py:685
  153.4 4.4 %collective-permute-start = (f32[4096,128]{1,0:T(8,128)}, f32[4096,128]{1,0:T(8,128)S(1)}, u32[]{:S(2)}, u32[]{:S(2)}) collective-permute-start(f32[4096,128]{1,0:T(8,128)} %get-tuple-element.39), channel_id=1, source_target_pairs={{0,1},{1,0},{2,3},{3,2},{4,5},{5,4},{6,7},{7,6},{8,9},{9,8},{10,11... | collective-permute-start | bytes 6291464 | tf_op jit(solution)/shard_map/ppermute | solution.py:706
  157.8 36.5 %copy-start.3 = (f32[4096,128]{1,0:T(8,128)}, f32[4096,128]{1,0:T(8,128)S(1)}, u32[]{:S(2)}) copy-start(f32[4096,128]{1,0:T(8,128)S(1)} %collective-permute-done) | copy-start | bytes 6291460
  179.2 29.7 %collective-permute-start.2 = (f32[12288,128]{1,0:T(8,128)}, f32[12288,128]{1,0:T(8,128)}, u32[]{:S(2)}, u32[]{:S(2)}) collective-permute-start(f32[12288,128]{1,0:T(8,128)} %get-tuple-element.45), channel_id=1, source_target_pairs={{0,1},{1,0},{2,3},{3,2},{4,5},{5,4},{6,7},{7,6},{8,9},{9,8},{10,11... | collective-permute-start | bytes 18874376 | tf_op jit(solution)/shard_map/ppermute | solution.py:706
  181.6 27.3 %collective-permute-start.1 = (f32[12288,128]{1,0:T(8,128)}, f32[12288,128]{1,0:T(8,128)}, u32[]{:S(2)}, u32[]{:S(2)}) collective-permute-start(f32[12288,128]{1,0:T(8,128)} %get-tuple-element.44), channel_id=1, source_target_pairs={{0,1},{1,0},{2,3},{3,2},{4,5},{5,4},{6,7},{7,6},{8,9},{9,8},{10,11... | collective-permute-start | bytes 18874376 | tf_op jit(solution)/shard_map/ppermute | solution.py:706
  181.7 12.6 %collective-permute-start.3 = (f32[4096,128]{1,0:T(8,128)}, f32[4096,128]{1,0:T(8,128)S(1)}, u32[]{:S(2)}, u32[]{:S(2)}) collective-permute-start(f32[4096,128]{1,0:T(8,128)} %get-tuple-element.47), channel_id=1, source_target_pairs={{0,1},{1,0},{2,3},{3,2},{4,5},{5,4},{6,7},{7,6},{8,9},{9,8},{10,11... | collective-permute-start | bytes 6291464 | tf_op jit(solution)/shard_map/ppermute | solution.py:706
  195.7 13.1 %copy-start.6 = (f32[8,8,128]{2,1,0:T(8,128)S(1)}, f32[8,8,128]{2,1,0:T(8,128)}, u32[]{:S(2)}) copy-start(f32[8,8,128]{2,1,0:T(8,128)} %get-tuple-element.51) | copy-start | bytes 98308
  195.7 13.1 %copy-start.7 = (f32[8,8,128]{2,1,0:T(8,128)S(1)}, f32[8,8,128]{2,1,0:T(8,128)}, u32[]{:S(2)}) copy-start(f32[8,8,128]{2,1,0:T(8,128)} %get-tuple-element.52) | copy-start | bytes 98308
  205.3 29.8 %all-to-all-start.3 = ((bf16[8,4,2,32,256]{4,3,2,1,0:T(8,128)(2,1)}), bf16[8,4,2,32,256]{4,3,2,1,0:T(8,128)(2,1)S(1)}, u32[]{:S(2)}, u32[]{:S(2)}) async-start(bf16[8,4,2,32,256]{4,3,2,1,0:T(8,128)(2,1)} %transform_planes.2), calls=%async_computation.3 | async-start | bytes 2097152 | tf_op jit(solution)/shard_map/all_to_all | solution.py:576
  233.5 85.4 %copy-start.9 = (s32[8]{0:T(128)S(1)}, s32[8]{0:T(128)}, u32[]{:S(2)}) copy-start(s32[8]{0:T(128)} %counts_ref.3) | copy-start | bytes 100
  236.1 82.7 %all-to-all-start.4 = ((bf16[8,12,2,32,256]{4,3,2,1,0:T(8,128)(2,1)}), bf16[8,12,2,32,256]{4,3,2,1,0:T(8,128)(2,1)S(1)}, u32[]{:S(2)}, u32[]{:S(2)}) async-start(bf16[8,12,2,32,256]{4,3,2,1,0:T(8,128)(2,1)} %transform_planes.3), calls=%async_computation.4 | async-start | bytes 6291456 | tf_op jit(solution)/shard_map/all_to_all | solution.py:576
  240.4 78.4 %collective-permute-start.11 = (bf16[8,4,2,32,256]{4,3,2,1,0:T(8,128)(2,1)}, bf16[8,4,2,32,256]{4,3,2,1,0:T(8,128)(2,1)}, u32[]{:S(2)}, u32[]{:S(2)}) collective-permute-start(bf16[8,4,2,32,256]{4,3,2,1,0:T(8,128)(2,1)} %copy-done), channel_id=1, source_target_pairs={{0,1},{1,0},{2,3},{3,2},{4,5},{5,4},{6,7},{7,6},{8,9},{9,8},{10,11... | collective-permute-start | bytes 3145736 | tf_op jit(solution)/shard_map/ppermute | solution.py:578
  240.5 55.7 %collective-permute-start.10 = (f32[1,8]{1,0:T(1,128)S(1)}, f32[1,8]{1,0:T(1,128)S(1)}, u32[]{:S(2)}, u32[]{:S(2)}) collective-permute-start(f32[1,8]{1,0:T(1,128)S(1)} %get-tuple-element.61), channel_id=1, source_target_pairs={{0,14},{2,12},{4,10},{6,8},{8,6},{10,4},{12,2},{14,0},{1,15},{3,13... | collective-permute-start | bytes 104 | tf_op jit(solution)/shard_map/ppermute | solution.py:511
  245.2 67.4 %collective-permute-start.4 = (f32[1,8]{1,0:T(1,128)S(1)}, f32[1,8]{1,0:T(1,128)S(1)}, u32[]{:S(2)}, u32[]{:S(2)}) collective-permute-start(f32[1,8]{1,0:T(1,128)S(1)} %get-tuple-element.60), channel_id=1, source_target_pairs={{0,2},{2,0},{4,6},{6,4},{8,10},{10,8},{12,14},{14,12},{1,3},{3,1},... | collective-permute-start | bytes 104 | tf_op jit(solution)/shard_map/ppermute | solution.py:511
  245.8 67.6 %collective-permute-start.5 = (f32[1,8]{1,0:T(1,128)S(1)}, f32[1,8]{1,0:T(1,128)S(1)}, u32[]{:S(2)}, u32[]{:S(2)}) collective-permute-start(f32[1,8]{1,0:T(1,128)S(1)} %get-tuple-element.66), channel_id=1, source_target_pairs={{0,4},{2,6},{4,0},{6,2},{8,12},{10,14},{12,8},{14,10},{1,5},{3,7},... | collective-permute-start | bytes 104 | tf_op jit(solution)/shard_map/ppermute | solution.py:511
  245.8 69.3 %collective-permute-start.6 = (f32[1,8]{1,0:T(1,128)S(1)}, f32[1,8]{1,0:T(1,128)S(1)}, u32[]{:S(2)}, u32[]{:S(2)}) collective-permute-start(f32[1,8]{1,0:T(1,128)S(1)} %get-tuple-element.65), channel_id=1, source_target_pairs={{0,6},{2,4},{4,2},{6,0},{8,14},{10,12},{12,10},{14,8},{1,7},{3,5},... | collective-permute-start | bytes 104 | tf_op jit(solution)/shard_map/ppermute | solution.py:511
  296.2 18.8 %collective-permute-start.7 = (f32[1,8]{1,0:T(1,128)S(1)}, f32[1,8]{1,0:T(1,128)S(1)}, u32[]{:S(2)}, u32[]{:S(2)}) collective-permute-start(f32[1,8]{1,0:T(1,128)S(1)} %get-tuple-element.64), channel_id=1, source_target_pairs={{0,8},{2,10},{4,12},{6,14},{8,0},{10,2},{12,4},{14,6},{1,9},{3,11}... | collective-permute-start | bytes 104 | tf_op jit(solution)/shard_map/ppermute | solution.py:511
  312.6 5.3 %collective-permute-start.8 = (f32[1,8]{1,0:T(1,128)S(1)}, f32[1,8]{1,0:T(1,128)S(1)}, u32[]{:S(2)}, u32[]{:S(2)}) collective-permute-start(f32[1,8]{1,0:T(1,128)S(1)} %get-tuple-element.63), channel_id=1, source_target_pairs={{0,10},{2,8},{4,14},{6,12},{8,2},{10,0},{12,6},{14,4},{1,11},{3,9}... | collective-permute-start | bytes 104 | tf_op jit(solution)/shard_map/ppermute | solution.py:511
  313.4 5.3 %collective-permute-start.9 = (f32[1,8]{1,0:T(1,128)S(1)}, f32[1,8]{1,0:T(1,128)S(1)}, u32[]{:S(2)}, u32[]{:S(2)}) collective-permute-start(f32[1,8]{1,0:T(1,128)S(1)} %get-tuple-element.62), channel_id=1, source_target_pairs={{0,12},{2,14},{4,8},{6,10},{8,4},{10,6},{12,0},{14,2},{1,13},{3,15... | collective-permute-start | bytes 104 | tf_op jit(solution)/shard_map/ppermute | solution.py:511
  318.8 5.7 %collective-permute-start.12 = (bf16[8,12,2,32,256]{4,3,2,1,0:T(8,128)(2,1)S(1)}, bf16[8,12,2,32,256]{4,3,2,1,0:T(8,128)(2,1)S(1)}, u32[]{:S(2)}, u32[]{:S(2)}) collective-permute-start(bf16[8,12,2,32,256]{4,3,2,1,0:T(8,128)(2,1)S(1)} %all-to-all-done.4.refs_1_), channel_id=1, source_target_pairs={{0,1},{1,0},{2,3},{3,2},{4,5},{5,4},{6,7},{7,6},{8,9},{9,8},{10,11... | collective-permute-start | bytes 9437192 | tf_op jit(solution)/shard_map/ppermute | solution.py:580
  (4 other events, 7.9 us)

commit v11 on v9

--- a/solution.py
+++ b/solution.py
@@ -12,7 +12,7 @@
 LANES = 128
 GROUP = 16
 UNUSED = 100
-STEP = 256
+STEP = 128
 MIB = 1024 * 1024
 
 SMEM_SPEC = pl.BlockSpec(memory_space=pltpu.SMEM)
@@ -75,10 +75,11 @@
 
 
 def pack_kernel(slabs, cap, list_length, target_ref, word_ref, counts_ref, totals_ref, code_ref, image_ref, meta_ref, *refs):
-    out_refs, (wide_ref, staged_ref) = refs[:-2], refs[-2:]
+    out_refs, (wide_ref, staged_ref, narrow_ref, sem) = refs[:-4], refs[-4:]
     particles = counts_ref.shape[0]
     stride = cap + LANES
     step = 256
+    turn = 32
 
     @pl.loop(0, image_ref.shape[0] // step)
     def _(i):
@@ -87,14 +88,15 @@
 
     @pl.loop(0, particles)
     def _(particle):
-        @pl.loop(0, (counts_ref[particle] + 15) // 16)
+        @pl.loop(0, (counts_ref[particle] + turn - 1) // turn)
         def _(i):
-            first = (i // 8) * (particles * LANES) + particle * LANES + (i % 8) * 16
-            row = particle * list_length + i * 16
-            targets = [target_ref[first + j] for j in range(16)]
-            words = [word_ref[first + j] for j in range(16)]
-            rows = [wide_ref[pl.ds(row + j, 1), :] for j in range(16)]
-            for j in range(16):
+            per_row = LANES // turn
+            first = (i // per_row) * (particles * LANES) + particle * LANES + (i % per_row) * turn
+            row = particle * list_length + i * turn
+            targets = [target_ref[first + j] for j in range(turn)]
+            words = [word_ref[first + j] for j in range(turn)]
+            rows = [wide_ref[pl.ds(row + j, 1), :] for j in range(turn)]
+            for j in range(turn):
                 staged_ref[pl.ds(targets[j], 1), :] = rows[j]
                 meta_ref[targets[j]] = words[j]
 
@@ -105,16 +107,32 @@
         for j in range(particles):
             meta_ref[header + 1 + j] = code_ref[j]
 
-    offset = 0
-    for out_ref in out_refs:
-        width = out_ref.shape[1]
-
-        @pl.loop(0, slabs)
-        def _(slab, offset=offset):
-            at = pl.multiple_of(slab * stride + offset, LANES)
-            out_ref[slab] = staged_ref[pl.ds(at, width), :].astype(jnp.bfloat16)
-
-        offset += width
+    def blocks_of(act):
+        offset = 0
+        for out_ref in out_refs:
+            width = out_ref.shape[1]
+
+            @pl.loop(0, slabs)
+            def _(slab, offset=offset, width=width, out_ref=out_ref):
+                live = jnp.clip(totals_ref[slab, 0] - offset, 0, width)
+
+                @pl.loop(0, (live + LANES - 1) // LANES)
+                def _(i):
+                    at = pl.multiple_of(slab * cap + offset + i * LANES, LANES)
+                    to = pl.multiple_of(i * LANES, LANES)
+                    copy = pltpu.make_async_copy(
+                        narrow_ref.at[pl.ds(at, LANES)], out_ref.at[slab, pl.ds(to, LANES)], sem
+                    )
+                    act(copy, at, pl.multiple_of(at + slab * LANES, LANES))
+
+            offset += width
+
+    def convert_and_start(copy, at, staged_at):
+        narrow_ref[pl.ds(at, LANES), :] = staged_ref[pl.ds(staged_at, LANES), :].astype(jnp.bfloat16)
+        copy.start()
+
+    blocks_of(convert_and_start)
+    blocks_of(lambda copy, at, staged_at: copy.wait())
 
 
 def decode_kernel(local_bits, dummy, word_ref, live_ref, index_ref):
@@ -575,8 +593,9 @@
         before = [sent]
         got = lax.all_to_all(sent, "slab", split_axis=0, concat_axis=0, tiled=True)
         own.append(got)
-    own[-1], losses = lax.optimization_barrier((own[-1], sum_over_slabs(partial_sums)))
-    other = [lax.ppermute(got, "dom", swap) for got in own]
+    other = [lax.ppermute(got, "dom", swap) for got in own[:-1]]
+    own[-1], losses, *other = lax.optimization_barrier((own[-1], sum_over_slabs(partial_sums), *other))
+    other.append(lax.ppermute(own[-1], "dom", swap))
     rows = min(16, height)
     arrays = own + other
     field = pl.pallas_call(
@@ -589,7 +608,7 @@
         ],
         out_specs=pl.BlockSpec((2, side // 2, rows, LANES), lambda y, z: (0, 0, y, z)),
         scratch_shapes=[pltpu.VMEM((16, 16, 2, rows, LANES), jnp.float32)],
-        compiler_params=params(56),
+        compiler_params=params(28),
         name="transform_first",
     )(lax.axis_index("dom").astype(jnp.int32).reshape(1), *arrays)
     return field, losses
@@ -617,7 +636,7 @@
         name="route",
     )(owners.reshape(rows, LANES), local_block, kinds, counts)
     target, word = target.reshape(entries), word.reshape(entries)
-    tiles = [cap // 2, cap // 2] if cap >= 2048 else [cap]
+    tiles = [cap * 9 // 16, cap * 7 // 16] if cap >= 2048 else [cap]
     parts = len(tiles)
     code = ctf_code | ((scales.astype(jnp.float32) * 256.0).astype(jnp.int32) << 8)
     stride = cap + LANES
@@ -626,10 +645,12 @@
         out_shape=(jax.ShapeDtypeStruct((slabs * stride,), jnp.int32),)
         + tuple(jax.ShapeDtypeStruct((slabs, tile, features), jnp.bfloat16) for tile in tiles),
         in_specs=[SMEM_SPEC] * 5 + [VMEM_SPEC],
-        out_specs=(SMEM_SPEC,) + (VMEM_SPEC,) * parts,
+        out_specs=(SMEM_SPEC,) + (ANY_SPEC,) * parts,
         scratch_shapes=[
             pltpu.VMEM((entries, features), jnp.float32),
             pltpu.VMEM((slabs * stride, features), jnp.float32),
+            pltpu.VMEM((slots, features), jnp.bfloat16),
+            pltpu.SemaphoreType.DMA(()),
         ],
         compiler_params=params(56),
         name="pack",

time: 324 us -> 336 us (1.037)
  starting transfers between devices: 43.5 us -> 61.4 us
  waiting for transfers between devices: 123 us -> 118 us
  local copies, waits for them, and re-layouts: 24.6 us -> 20.3 us
    all_to_all x2, starting transfers between devices: 20.5 us -> 37.5 us  [to_field(): got = lax.all_to_all(sent, 'slab', split_axis=0, concat_axis=0, tiled=True)]
    pallas_call x2, Pallas kernels: 30.2 us -> 34.5 us  [gradient_of_slab(): pl.pallas_call(functools.partial(slab_kernel, side, local_bits, list_leng...]
    unnamed x36 -> x28, local copies, waits for them, and re-layouts: 22.5 us -> 18.3 us
    all_to_all x2, waiting for transfers between devices: 45.6 us -> 41.4 us  [gradient_of_slab(): lax.all_to_all(packed[part], 'slab', split_axis=0, concat_axis=0, tiled=T...]
  transfers between devices with their start and end apart: 15 -> 15, of which waited for: 10 -> 9; matrix products, arithmetic and copies ran while one was open for 1% -> 1% of each run, Pallas kernels for 22% -> 22%
where the time goes in v11:
time: 336 us; the launch traced here: 333 us
  waiting for transfers between devices  118 us (35%)
  Pallas kernels  114 us (34%)
  starting transfers between devices  61.4 us (18%)
  local copies, waits for them, and re-layouts  20.3 us (6%)
  blocking collectives  15.7 us (5%)
    ppermute x7, waiting for transfers between devices, sum_over_slabs(): lax.ppermute(row(i), 'slab', [(slab, slab ^ i) for slab in range(slabs)])  56.4 us
    all_to_all x2, waiting for transfers between devices, gradient_of_slab(): lax.all_to_all(packed[part], 'slab', split_axis=0, concat_axis=0, tiled=T...  41.4 us
    all_to_all x2, starting transfers between devices, to_field(): got = lax.all_to_all(sent, 'slab', split_axis=0, concat_axis=0, tiled=True)  37.5 us
    pallas_call x2, Pallas kernels, gradient_of_slab(): pl.pallas_call(functools.partial(slab_kernel, side, local_bits, list_leng...  34.5 us
    pallas_call x2, Pallas kernels, to_field(): pl.pallas_call(planes_kernel, grid=(quads, per_row // yblocks), out_shape...  31.3 us
    unnamed x28, local copies, waits for them, and re-layouts  18.3 us
    pallas_call x1, Pallas kernels, gradient_of_slab(): pl.pallas_call(functools.partial(pack_kernel, slabs, cap, list_length), o...  16.8 us
    all_to_all x1, blocking collectives, gradient_of_slab(): lax.all_to_all(meta.reshape(slabs, stride), 'slab', split_axis=0, concat_...  15.7 us
  transfers between devices with their start and end apart: 15, of which 9 were waited for; matrix products, arithmetic and copies ran while one was open for 1% of the time, Pallas kernels for 22%

profile of v11, /device:TPU:0, one launch (start us, length us, event | category | flops | bytes accessed | tf_op | source)
XLA Modules:
  0.0 333.5 jit_solution(3933760325328698643)
XLA Ops:
  1.8 3.7 %route.1 = (s32[64,128]{1,0:T(8,128)}, s32[64,128]{1,0:T(8,128)}, s32[8,128]{1,0:T(8,128)}) custom-call(s32[64,128]{1,0:T(8,128)} %bitcast.51, s32[8,1024]{1,0:T(8,128)} %local_ref.1, s32[8,1024]{1,0:T(8,128)} %kind_ref.1, s32[8]{0:T(128)} %counts_ref.3), custom_call_target="tpu_custom_call" | custom-call | tf_op jit(solution)/shard_map/route/pallas_call | solution.py:630
  5.6 16.8 %pack.1 = (s32[17408]{0:T(1024)}, bf16[8,1152,128]{2,1,0:T(8,128)(2,1)}, bf16[8,896,128]{2,1,0:T(8,128)(2,1)}) custom-call(s32[8192]{0:T(1024)} %bitcast.49, s32[8192]{0:T(1024)} %bitcast.50, s32[8]{0:T(128)} %counts_ref.3, s32[8,128]{1,0:T(8,128)} %get-tuple-element.27.totals_ref, s32[8]{0:T(128)} %shift-left_or_fusion.code_ref, bf16[8192,128]{1,0:T(8,128)(2,1)} %bitcast.38), custom_call_target="tpu_custom_call" | custom-call | tf_op jit(solution)/shard_map/pack/pallas_call | solution.py:643
  22.4 15.7 %all_to_all.32 = s32[8,1,2176]{2,1,0:T(1,128)S(1)} all-to-all(s32[8,1,2176]{2,1,0:T(1,128)} %bitcast.48), channel_id=1, replica_groups=mesh['groups'=2,'slab'=8,'dom'=2] {'slab'}, dimensions={0} | all-to-all | bytes 139264 | tf_op jit(solution)/shard_map/all_to_all | solution.py:658
  38.0 3.6 %all-to-all-start.2 = ((bf16[8,1152,128]{2,1,0:T(8,128)(2,1)}), bf16[8,1152,128]{2,1,0:T(8,128)(2,1)S(1)}, u32[]{:S(2)}, u32[]{:S(2)}) async-start(bf16[8,1152,128]{2,1,0:T(8,128)(2,1)} %get-tuple-element.33), calls=%async_computation.2 | async-start | bytes 4718592 | tf_op jit(solution)/shard_map/all_to_all | solution.py:707
  46.0 12.8 %read_voxels.1 = (bf16[8,1152,128]{2,1,0:T(8,128)(2,1)}, bf16[8,896,128]{2,1,0:T(8,128)(2,1)}) custom-call(s32[17408]{0:T(1024)} %bitcast.33, s32[8]{0:T(128)} %copy-done.7, bf16[32768,128]{1,0:T(8,128)(2,1)} %volume_ref.1), custom_call_target="tpu_custom_call" | custom-call | bytes 104857600 | tf_op jit(solution)/shard_map/read_voxels/pallas_call | solution.py:677
  58.8 34.8 %all-to-all-done.2.image_ref = bf16[8,1152,128]{2,1,0:T(8,128)(2,1)S(1)} async-done(((bf16[8,1152,128]{2,1,0:T(8,128)(2,1)}), bf16[8,1152,128]{2,1,0:T(8,128)(2,1)S(1)}, u32[]{:S(2)}, u32[]{:S(2)}) %all-to-all-start.2) | async-done | bytes 2359328 | tf_op jit(solution)/shard_map/all_to_all | solution.py:707
  93.6 4.3 %all-to-all-start.1 = ((bf16[8,896,128]{2,1,0:T(8,128)(2,1)}), bf16[8,896,128]{2,1,0:T(8,128)(2,1)}, u32[]{:S(2)}, u32[]{:S(2)}) async-start(bf16[8,896,128]{2,1,0:T(8,128)(2,1)} %get-tuple-element.32), calls=%async_computation.1 | async-start | bytes 3670016 | tf_op jit(solution)/shard_map/all_to_all | solution.py:707
  101.1 26.6 %compare_and_add.2 = (f32[8,8,128]{2,1,0:T(8,128)S(1)}, f32[32776,128]{1,0:T(8,128)S(1)}) custom-call(s32[8]{0:T(128)S(1)} %copy-done.8, f32[64]{0:T(128)S(1)} %get-tuple-element.49.defocus_ref, f32[64]{0:T(128)S(1)} %get-tuple-element.48.phase_ref, f32[64]{0:T(128)S(1)} %mul.17.scale_ref, s32[17408]{0:T(1024)S(1)} %bitcast.34, s32[1]{0:T(128)} %bitcast.core_ref, ...), custom_call_target="tpu_custom_call" | custom-call | bytes 16777216 | tf_op jit(solution)/shard_map/compare_and_add/pallas_call | solution.py:718
  127.8 5.7 %copy-done = f32[32776,128]{1,0:T(8,128)} copy-done((f32[32776,128]{1,0:T(8,128)}, f32[32776,128]{1,0:T(8,128)S(1)}, u32[]{:S(2)}) %copy-start) | copy-done | bytes 16781336
  133.5 6.6 %all-to-all-done.1.image_ref = bf16[8,896,128]{2,1,0:T(8,128)(2,1)} async-done(((bf16[8,896,128]{2,1,0:T(8,128)(2,1)}), bf16[8,896,128]{2,1,0:T(8,128)(2,1)}, u32[]{:S(2)}, u32[]{:S(2)}) %all-to-all-start.1) | async-done | bytes 1835040 | tf_op jit(solution)/shard_map/all_to_all | solution.py:707
  140.1 5.8 %copy-done.1 = f32[32776,128]{1,0:T(8,128)S(1)} copy-done((f32[32776,128]{1,0:T(8,128)S(1)}, f32[32776,128]{1,0:T(8,128)}, u32[]{:S(2)}) %copy-start.1) | copy-done | bytes 16781336
  147.4 7.9 %compare_and_add.3 = (f32[8,8,128]{2,1,0:T(8,128)S(1)}, f32[32776,128]{1,0:T(8,128)S(1)}, f32[16384,128]{1,0:T(8,128)}, f32[4096,128]{1,0:T(8,128)S(1)}, f32[12288,128]{1,0:T(8,128)}) custom-call(s32[8]{0:T(128)S(1)} %copy-done.8, f32[64]{0:T(128)S(1)} %get-tuple-element.49.defocus_ref, ...), custom_call_target="tpu_custom_call", output_to_operand_aliasing={{1}: (12, {})} | custom-call | bytes 16777216 | tf_op jit(solution)/shard_map/compare_and_add/pallas_call | solution.py:718
  155.9 11.3 %collective-permute-done.1 = f32[4096,128]{1,0:T(8,128)S(1)} collective-permute-done((f32[4096,128]{1,0:T(8,128)S(1)}, f32[4096,128]{1,0:T(8,128)S(1)}, u32[]{:S(2)}, u32[]{:S(2)}) %collective-permute-start.1) | collective-permute-done | bytes 2097184 | tf_op jit(solution)/shard_map/ppermute | solution.py:548
  168.5 8.8 %transform_planes.2 = bf16[8,4,2,32,256]{4,3,2,1,0:T(8,128)(2,1)} custom-call(f32[16,32,32,128]{3,2,1,0:T(8,128)} %bitcast.36, f32[4,32,32,128]{3,2,1,0:T(8,128)} %bitcast.39, bf16[384,256]{1,0:T(8,128)(2,1)} %constant.67.clone.zblock_ref, f32[2,8,128]{2,1,0:T(8,128)} %constant.68.clone.turn_ref, bf16[512,512]{1,0:T(8,128)(2,1)} %constant.69.clone.wide_ref, ...), custom_call_target="tpu_custom_call" | custom-call | flops 536870912 | bytes 8388608 | tf_op jit(solution)/shard_map/transform_planes/pallas_call | solution.py:567
  177.3 33.8 %all-to-all-start.3 = ((bf16[8,4,2,32,256]{4,3,2,1,0:T(8,128)(2,1)}), bf16[8,4,2,32,256]{4,3,2,1,0:T(8,128)(2,1)S(1)}, u32[]{:S(2)}, u32[]{:S(2)}) async-start(bf16[8,4,2,32,256]{4,3,2,1,0:T(8,128)(2,1)} %transform_planes.2), calls=%async_computation.3 | async-start | bytes 2097152 | tf_op jit(solution)/shard_map/all_to_all | solution.py:594
  211.2 22.5 %transform_planes.3 = bf16[8,12,2,32,256]{4,3,2,1,0:T(8,128)(2,1)} custom-call(f32[16,32,32,128]{3,2,1,0:T(8,128)} %bitcast.37, f32[12,32,32,128]{3,2,1,0:T(8,128)} %bitcast.18.theirs_ref, bf16[384,256]{1,0:T(8,128)(2,1)} %constant.67.clone.zblock_ref, f32[2,8,128]{2,1,0:T(8,128)} %constant.68.clone.turn_ref, bf16[512,512]{1,0:T(8,128)(2,1)} %constant.69.clone.wide_ref, ...), custom_call_target="tpu_custom_call" | custom-call | flops 1610612736 | bytes 25165824 | tf_op jit(solution)/shard_map/transform_planes/pallas_call | solution.py:567
  233.7 3.7 %all-to-all-done.3.refs_0_ = bf16[8,4,2,32,256]{4,3,2,1,0:T(8,128)(2,1)S(1)} async-done(((bf16[8,4,2,32,256]{4,3,2,1,0:T(8,128)(2,1)}), bf16[8,4,2,32,256]{4,3,2,1,0:T(8,128)(2,1)S(1)}, u32[]{:S(2)}, u32[]{:S(2)}) %all-to-all-start.3) | async-done | bytes 1048608 | tf_op jit(solution)/shard_map/all_to_all | solution.py:594
  238.4 3.6 %all-to-all-start.4 = ((bf16[8,12,2,32,256]{4,3,2,1,0:T(8,128)(2,1)}), bf16[8,12,2,32,256]{4,3,2,1,0:T(8,128)(2,1)S(1)}, u32[]{:S(2)}, u32[]{:S(2)}) async-start(bf16[8,12,2,32,256]{4,3,2,1,0:T(8,128)(2,1)} %transform_planes.3), calls=%async_computation.4 | async-start | bytes 6291456 | tf_op jit(solution)/shard_map/all_to_all | solution.py:594
  248.5 19.2 %collective-permute-done.2 = f32[1,8]{1,0:T(1,128)S(1)} collective-permute-done((f32[1,8]{1,0:T(1,128)S(1)}, f32[1,8]{1,0:T(1,128)S(1)}, u32[]{:S(2)}, u32[]{:S(2)}) %collective-permute-start.2) | collective-permute-done | bytes 64 | tf_op jit(solution)/shard_map/ppermute | solution.py:531
  267.7 4.5 %collective-permute-start.6 = (f32[1,8]{1,0:T(1,128)S(1)}, f32[1,8]{1,0:T(1,128)S(1)}, u32[]{:S(2)}, u32[]{:S(2)}) collective-permute-start(f32[1,8]{1,0:T(1,128)S(1)} %get-tuple-element.53), channel_id=1, source_target_pairs={{0,10},{2,8},{4,14},{6,12},{8,2},{10,0},{12,6},{14,4},{1,11},{3,9}... | collective-permute-start | bytes 104 | tf_op jit(solution)/shard_map/ppermute | solution.py:531
  272.3 22.0 %collective-permute-done.3 = f32[1,8]{1,0:T(1,128)S(1)} collective-permute-done((f32[1,8]{1,0:T(1,128)S(1)}, f32[1,8]{1,0:T(1,128)S(1)}, u32[]{:S(2)}, u32[]{:S(2)}) %collective-permute-start.3) | collective-permute-done | bytes 64 | tf_op jit(solution)/shard_map/ppermute | solution.py:531
  298.7 14.4 %collective-permute-done.5 = f32[1,8]{1,0:T(1,128)S(1)} collective-permute-done((f32[1,8]{1,0:T(1,128)S(1)}, f32[1,8]{1,0:T(1,128)S(1)}, u32[]{:S(2)}, u32[]{:S(2)}) %collective-permute-start.5) | collective-permute-done | bytes 64 | tf_op jit(solution)/shard_map/ppermute | solution.py:531
  314.5 5.1 %collective-permute-done.10.refs_3_ = bf16[8,12,2,32,256]{4,3,2,1,0:T(8,128)(2,1)S(1)} collective-permute-done((bf16[8,12,2,32,256]{4,3,2,1,0:T(8,128)(2,1)S(1)}, bf16[8,12,2,32,256]{4,3,2,1,0:T(8,128)(2,1)S(1)}, u32[]{:S(2)}, u32[]{:S(2)}) %collective-permute-start.10) | collective-permute-done | bytes 3145760 | tf_op jit(solution)/shard_map/ppermute | solution.py:598
  320.8 12.6 %transform_first.1 = f32[2,128,32,256]{3,2,1,0:T(8,128)} custom-call(s32[1]{0:T(128)} %bitcast.core_ref, bf16[8,4,2,32,256]{4,3,2,1,0:T(8,128)(2,1)S(1)} %copy-done.3, bf16[8,12,2,32,256]{4,3,2,1,0:T(8,128)(2,1)S(1)} %all-to-all-done.4.refs_1_, bf16[8,4,2,32,256]{4,3,2,1,0:T(8,128)(2,1)} %collective-permute-done.9.refs_2_, ...), custom_call_target="tpu_custom_call" | custom-call | tf_op jit(solution)/shard_map/transform_first/pallas_call | solution.py:601
  (71 shorter events, 26.5 us)
Async XLA Ops:
  38.0 55.6 %all-to-all-start.2 = ((bf16[8,1152,128]{2,1,0:T(8,128)(2,1)}), bf16[8,1152,128]{2,1,0:T(8,128)(2,1)S(1)}, u32[]{:S(2)}, u32[]{:S(2)}) async-start(bf16[8,1152,128]{2,1,0:T(8,128)(2,1)} %get-tuple-element.33), calls=%async_computation.2 | async-start | bytes 4718592 | tf_op jit(solution)/shard_map/all_to_all | solution.py:707
  41.8 4.2 %copy-start.7 = (s32[8]{0:T(128)}, s32[8]{0:T(128)S(1)}, u32[]{:S(2)}) copy-start(s32[8]{0:T(128)S(1)} %slice_reduce_fusion.2.totals_ref) | copy-start | bytes 100
  58.8 39.1 %copy-start.12 = (f32[64,2]{0,1:T(2,128)S(1)}, f32[64,2]{0,1:T(2,128)}, u32[]{:S(2)}) copy-start(f32[64,2]{0,1:T(2,128)} %param.22) | copy-start | bytes 1540
  58.8 39.2 %copy-start.10 = (bf16[4,128,128]{2,1,0:T(8,128)(2,1)S(1)}, bf16[4,128,128]{2,1,0:T(8,128)(2,1)}, u32[]{:S(2)}) copy-start(bf16[4,128,128]{2,1,0:T(8,128)(2,1)} %param.15) | copy-start | bytes 393220
  58.8 40.6 %copy-start.6 = (s32[136,128]{1,0:T(8,128)S(1)}, s32[136,128]{1,0:T(8,128)}, u32[]{:S(2)}) copy-start(s32[136,128]{1,0:T(8,128)} %decode.1) | copy-start | bytes 208900
  58.8 40.6 %copy-start.8 = (s32[8]{0:T(128)S(1)}, s32[8]{0:T(128)}, u32[]{:S(2)}) copy-start(s32[8]{0:T(128)} %copy-done.7) | copy-start | bytes 100
  93.6 46.5 %all-to-all-start.1 = ((bf16[8,896,128]{2,1,0:T(8,128)(2,1)}), bf16[8,896,128]{2,1,0:T(8,128)(2,1)}, u32[]{:S(2)}, u32[]{:S(2)}) async-start(bf16[8,896,128]{2,1,0:T(8,128)(2,1)} %get-tuple-element.32), calls=%async_computation.1 | async-start | bytes 3670016 | tf_op jit(solution)/shard_map/all_to_all | solution.py:707
  99.5 1.7 copy-start.4
  127.8 5.7 %copy-start = (f32[32776,128]{1,0:T(8,128)}, f32[32776,128]{1,0:T(8,128)S(1)}, u32[]{:S(2)}) copy-start(f32[32776,128]{1,0:T(8,128)S(1)} %get-tuple-element.34.rest_0_) | copy-start | bytes 50343940
  140.1 5.8 %copy-start.1 = (f32[32776,128]{1,0:T(8,128)S(1)}, f32[32776,128]{1,0:T(8,128)}, u32[]{:S(2)}) copy-start(f32[32776,128]{1,0:T(8,128)} %copy-done) | copy-start | bytes 50343940
  155.3 55.9 %collective-permute-start = (f32[12288,128]{1,0:T(8,128)}, f32[12288,128]{1,0:T(8,128)}, u32[]{:S(2)}, u32[]{:S(2)}) collective-permute-start(f32[12288,128]{1,0:T(8,128)} %get-tuple-element.36), channel_id=1, source_target_pairs={{0,1},{1,0},{2,3},{3,2},{4,5},{5,4},{6,7},{7,6},{8,9},{9,8},{10,11... | collective-permute-start | bytes 18874376 | tf_op jit(solution)/shard_map/ppermute | solution.py:548
  155.4 11.8 %collective-permute-start.1 = (f32[4096,128]{1,0:T(8,128)S(1)}, f32[4096,128]{1,0:T(8,128)S(1)}, u32[]{:S(2)}, u32[]{:S(2)}) collective-permute-start(f32[4096,128]{1,0:T(8,128)S(1)} %get-tuple-element.37), channel_id=1, source_target_pairs={{0,1},{1,0},{2,3},{3,2},{4,5},{5,4},{6,7},{7,6},{8,9},{9,8},{10,11... | collective-permute-start | bytes 6291464 | tf_op jit(solution)/shard_map/ppermute | solution.py:548
  177.3 60.1 %all-to-all-start.3 = ((bf16[8,4,2,32,256]{4,3,2,1,0:T(8,128)(2,1)}), bf16[8,4,2,32,256]{4,3,2,1,0:T(8,128)(2,1)S(1)}, u32[]{:S(2)}, u32[]{:S(2)}) async-start(bf16[8,4,2,32,256]{4,3,2,1,0:T(8,128)(2,1)} %transform_planes.2), calls=%async_computation.3 | async-start | bytes 2097152 | tf_op jit(solution)/shard_map/all_to_all | solution.py:594
  233.7 80.2 %copy-start.11 = (s32[8]{0:T(128)S(1)}, s32[8]{0:T(128)}, u32[]{:S(2)}) copy-start(s32[8]{0:T(128)} %counts_ref.3) | copy-start | bytes 100
  238.4 75.5 %all-to-all-start.4 = ((bf16[8,12,2,32,256]{4,3,2,1,0:T(8,128)(2,1)}), bf16[8,12,2,32,256]{4,3,2,1,0:T(8,128)(2,1)S(1)}, u32[]{:S(2)}, u32[]{:S(2)}) async-start(bf16[8,12,2,32,256]{4,3,2,1,0:T(8,128)(2,1)} %transform_planes.3), calls=%async_computation.4 | async-start | bytes 6291456 | tf_op jit(solution)/shard_map/all_to_all | solution.py:594
  242.0 71.9 %collective-permute-start.9 = (bf16[8,4,2,32,256]{4,3,2,1,0:T(8,128)(2,1)}, bf16[8,4,2,32,256]{4,3,2,1,0:T(8,128)(2,1)}, u32[]{:S(2)}, u32[]{:S(2)}) collective-permute-start(bf16[8,4,2,32,256]{4,3,2,1,0:T(8,128)(2,1)} %copy-done.2), channel_id=1, source_target_pairs={{0,1},{1,0},{2,3},{3,2},{4,5},{5,4},{6,7},{7,6},{8,9},{9,8},{10,11... | collective-permute-start | bytes 3145736 | tf_op jit(solution)/shard_map/ppermute | solution.py:596
  242.2 25.6 %collective-permute-start.2 = (f32[1,8]{1,0:T(1,128)S(1)}, f32[1,8]{1,0:T(1,128)S(1)}, u32[]{:S(2)}, u32[]{:S(2)}) collective-permute-start(f32[1,8]{1,0:T(1,128)S(1)} %get-tuple-element.50), channel_id=1, source_target_pairs={{0,2},{2,0},{4,6},{6,4},{8,10},{10,8},{12,14},{14,12},{1,3},{3,1},... | collective-permute-start | bytes 104 | tf_op jit(solution)/shard_map/ppermute | solution.py:531
  244.1 50.1 %collective-permute-start.3 = (f32[1,8]{1,0:T(1,128)S(1)}, f32[1,8]{1,0:T(1,128)S(1)}, u32[]{:S(2)}, u32[]{:S(2)}) collective-permute-start(f32[1,8]{1,0:T(1,128)S(1)} %get-tuple-element.56), channel_id=1, source_target_pairs={{0,4},{2,6},{4,0},{6,2},{8,12},{10,14},{12,8},{14,10},{1,5},{3,7},... | collective-permute-start | bytes 104 | tf_op jit(solution)/shard_map/ppermute | solution.py:531
  245.6 51.2 %collective-permute-start.4 = (f32[1,8]{1,0:T(1,128)S(1)}, f32[1,8]{1,0:T(1,128)S(1)}, u32[]{:S(2)}, u32[]{:S(2)}) collective-permute-start(f32[1,8]{1,0:T(1,128)S(1)} %get-tuple-element.55), channel_id=1, source_target_pairs={{0,6},{2,4},{4,2},{6,0},{8,14},{10,12},{12,10},{14,8},{1,7},{3,5},... | collective-permute-start | bytes 104 | tf_op jit(solution)/shard_map/ppermute | solution.py:531
  245.7 67.3 %collective-permute-start.5 = (f32[1,8]{1,0:T(1,128)S(1)}, f32[1,8]{1,0:T(1,128)S(1)}, u32[]{:S(2)}, u32[]{:S(2)}) collective-permute-start(f32[1,8]{1,0:T(1,128)S(1)} %get-tuple-element.54), channel_id=1, source_target_pairs={{0,8},{2,10},{4,12},{6,14},{8,0},{10,2},{12,4},{14,6},{1,9},{3,11}... | collective-permute-start | bytes 104 | tf_op jit(solution)/shard_map/ppermute | solution.py:531
  267.7 46.1 %collective-permute-start.6 = (f32[1,8]{1,0:T(1,128)S(1)}, f32[1,8]{1,0:T(1,128)S(1)}, u32[]{:S(2)}, u32[]{:S(2)}) collective-permute-start(f32[1,8]{1,0:T(1,128)S(1)} %get-tuple-element.53), channel_id=1, source_target_pairs={{0,10},{2,8},{4,14},{6,12},{8,2},{10,0},{12,6},{14,4},{1,11},{3,9}... | collective-permute-start | bytes 104 | tf_op jit(solution)/shard_map/ppermute | solution.py:531
  294.3 19.6 %collective-permute-start.7 = (f32[1,8]{1,0:T(1,128)S(1)}, f32[1,8]{1,0:T(1,128)S(1)}, u32[]{:S(2)}, u32[]{:S(2)}) collective-permute-start(f32[1,8]{1,0:T(1,128)S(1)} %get-tuple-element.52), channel_id=1, source_target_pairs={{0,12},{2,14},{4,8},{6,10},{8,4},{10,6},{12,0},{14,2},{1,13},{3,15... | collective-permute-start | bytes 104 | tf_op jit(solution)/shard_map/ppermute | solution.py:531
  296.7 17.1 %collective-permute-start.8 = (f32[1,8]{1,0:T(1,128)S(1)}, f32[1,8]{1,0:T(1,128)S(1)}, u32[]{:S(2)}, u32[]{:S(2)}) collective-permute-start(f32[1,8]{1,0:T(1,128)S(1)} %get-tuple-element.51), channel_id=1, source_target_pairs={{0,14},{2,12},{4,10},{6,8},{8,6},{10,4},{12,2},{14,0},{1,15},{3,13... | collective-permute-start | bytes 104 | tf_op jit(solution)/shard_map/ppermute | solution.py:531
  313.9 5.7 %collective-permute-start.10 = (bf16[8,12,2,32,256]{4,3,2,1,0:T(8,128)(2,1)S(1)}, bf16[8,12,2,32,256]{4,3,2,1,0:T(8,128)(2,1)S(1)}, u32[]{:S(2)}, u32[]{:S(2)}) collective-permute-start(bf16[8,12,2,32,256]{4,3,2,1,0:T(8,128)(2,1)S(1)} %all-to-all-done.4.refs_1_), channel_id=1, source_target_pairs={{0,1},{1,0},{2,3},{3,2},{4,5},{5,4},{6,7},{7,6},{8,9},{9,8},{10,11... | collective-permute-start | bytes 9437192 | tf_op jit(solution)/shard_map/ppermute | solution.py:598
  (4 other events, 5.0 us)

commit v12 on v11

--- a/solution.py
+++ b/solution.py
@@ -12,7 +12,8 @@
 LANES = 128
 GROUP = 16
 UNUSED = 100
-STEP = 128
+STEP = 256
+PAIR = 2
 MIB = 1024 * 1024
 
 SMEM_SPEC = pl.BlockSpec(memory_space=pltpu.SMEM)
@@ -211,7 +212,7 @@
         rest = rest[1:]
     square_ref, sum_ref, out_refs, (staged_ref, steps_ref, sems) = rest[0], rest[1], rest[2:-3], rest[-3:]
     slabs, _, tile = word_ref.shape
-    step = staged_ref.shape[0]
+    step = staged_ref.shape[0] // PAIR
     steps_each = tile // step
     blocks = sum_ref.shape[0] - 8
     features = image_ref.shape[2]
@@ -239,7 +240,7 @@
     steps_ref[0] = 0
     count = lax.fori_loop(0, slabs, list_source, 0)
 
-    def compare(number):
+    def compare(number, slot):
         which_step = steps_ref[jnp.minimum(number, jnp.maximum(count - 1, 0))]
         source, at = which_step // steps_each, (which_step % steps_each) * step
         at = pl.multiple_of(at, step)
@@ -291,7 +292,7 @@
             [jnp.where(kind == k, weighted, none) for k in range(kinds)], axis=0
         )
         terms = jnp.dot(backward_ref[...], spread_back, preferred_element_type=jnp.float32)
-        staged_ref[...] = terms.T
+        staged_ref[slot * step:(slot + 1) * step, :] = terms.T
 
     def places_of(base):
         return [index_ref[base] & 0xFFFFFF] + [index_ref[base + j] for j in range(1, GROUP)]
@@ -303,41 +304,50 @@
         for j in range(GROUP):
             sum_ref[pl.ds(places[j], 1), :] = held[j] + new[j]
 
-    @pl.loop(0, count + 1)
-    def _(number):
-        earlier = steps_ref[jnp.maximum(number - 1, 0)]
+    def base_of(number):
+        earlier = steps_ref[jnp.clip(number, 0, jnp.maximum(count - 1, 0))]
         base = (earlier // steps_each) * cap + offset + (earlier % steps_each) * step
-        base = jnp.where(number > 0, base, slabs * cap)
-        marks = index_ref[base]
-        for i in range(1, step // LANES):
-            marks = marks | index_ref[base + i * LANES]
+        return jnp.where((number >= 0) & (number < count), base, slabs * cap)
+
+    @pl.loop(0, (count + PAIR - 1) // PAIR + 1)
+    def _(turn):
+        bases = [base_of((turn - 1) * PAIR + slot) for slot in range(PAIR)]
+        marks = 0
+        for base in bases:
+            for i in range(step // LANES):
+                marks = marks | index_ref[base + i * LANES]
 
         @pl.when(marks < (1 << 25))
         def _():
-            for g in range(step // GROUP):
-                add_group(base + g * GROUP, g * GROUP)
-            compare(number)
+            for slot, base in enumerate(bases):
+                for g in range(step // GROUP):
+                    add_group(base + g * GROUP, slot * step + g * GROUP)
+            for slot in range(PAIR):
+                compare(turn * PAIR + slot, slot)
 
         @pl.when(marks >= (1 << 25))
         def _():
-            @pl.loop(0, step // GROUP)
-            def _(g):
-                start = base + g * GROUP
-                clashes = (index_ref[start] >> 24) & 1
-
-                @pl.when(clashes == 0)
-                def _():
-                    add_group(start, g * GROUP)
-
-                @pl.when(clashes == 1)
-                def _():
-                    places = places_of(start)
-                    for j in range(GROUP):
-                        sum_ref[pl.ds(places[j], 1), :] = (
-                            sum_ref[pl.ds(places[j], 1), :] + staged_ref[pl.ds(g * GROUP + j, 1), :]
-                        )
-
-            compare(number)
+            for slot, base in enumerate(bases):
+                @pl.loop(0, step // GROUP)
+                def _(g, slot=slot, base=base):
+                    start = base + g * GROUP
+                    at = slot * step + g * GROUP
+                    clashes = (index_ref[start] >> 24) & 1
+
+                    @pl.when(clashes == 0)
+                    def _():
+                        add_group(start, at)
+
+                    @pl.when(clashes == 1)
+                    def _():
+                        places = places_of(start)
+                        for j in range(GROUP):
+                            sum_ref[pl.ds(places[j], 1), :] = (
+                                sum_ref[pl.ds(places[j], 1), :] + staged_ref[pl.ds(at + j, 1), :]
+                            )
+
+            for slot in range(PAIR):
+                compare(turn * PAIR + slot, slot)
 
     if last:
         half = blocks // 2
@@ -636,7 +646,7 @@
         name="route",
     )(owners.reshape(rows, LANES), local_block, kinds, counts)
     target, word = target.reshape(entries), word.reshape(entries)
-    tiles = [cap * 9 // 16, cap * 7 // 16] if cap >= 2048 else [cap]
+    tiles = [cap * 5 // 8, cap * 3 // 8] if cap >= 2048 else [cap]
     parts = len(tiles)
     code = ctf_code | ((scales.astype(jnp.float32) * 256.0).astype(jnp.int32) << 8)
     stride = cap + LANES
@@ -727,7 +737,7 @@
             in_specs=[SMEM_SPEC] * 6 + [VMEM_SPEC] * (len(arguments) - 6),
             out_specs=(VMEM_SPEC, VMEM_SPEC) + (ANY_SPEC,) * len(lengths),
             scratch_shapes=[
-                pltpu.VMEM((min(tile, STEP), features), jnp.float32),
+                pltpu.VMEM((PAIR * min(tile, STEP), features), jnp.float32),
                 pltpu.SMEM((slabs * tile // min(tile, STEP) + 1,), jnp.int32),
                 pltpu.SemaphoreType.DMA((max(1, len(lengths)),)),
             ],

time: 336 us -> 321 us (0.955)
  starting transfers between devices: 61.4 us -> 42.8 us
  Pallas kernels: 114 us -> 102 us
  waiting for transfers between devices: 118 us -> 130 us
    all_to_all x2, starting transfers between devices: 37.5 us -> 19.1 us  [to_field(): got = lax.all_to_all(sent, 'slab', split_axis=0, concat_axis=0, tiled=True)]
    all_to_all x2, waiting for transfers between devices: 41.4 us -> 53.9 us  [gradient_of_slab(): lax.all_to_all(packed[part], 'slab', split_axis=0, concat_axis=0, tiled=T...]
    pallas_call x2, Pallas kernels: 34.5 us -> 24.8 us  [gradient_of_slab(): pl.pallas_call(functools.partial(slab_kernel, side, local_bits, list_leng...]
  transfers between devices with their start and end apart: 15 -> 15, of which waited for: 9 -> 9; matrix products, arithmetic and copies ran while one was open for 1% -> 1% of each run, Pallas kernels for 22% -> 19%
where the time goes in v12:
time: 321 us; the launch traced here: 316 us
  waiting for transfers between devices  130 us (40%)
  Pallas kernels  102 us (32%)
  starting transfers between devices  42.8 us (13%)
  local copies, waits for them, and re-layouts  20.3 us (6%)
  blocking collectives  16.4 us (5%)
    ppermute x7, waiting for transfers between devices, sum_over_slabs(): lax.ppermute(row(i), 'slab', [(slab, slab ^ i) for slab in range(slabs)])  56.4 us
    all_to_all x2, waiting for transfers between devices, gradient_of_slab(): lax.all_to_all(packed[part], 'slab', split_axis=0, concat_axis=0, tiled=T...  53.9 us
    pallas_call x2, Pallas kernels, to_field(): pl.pallas_call(planes_kernel, grid=(quads, per_row // yblocks), out_shape...  31.3 us
    pallas_call x2, Pallas kernels, gradient_of_slab(): pl.pallas_call(functools.partial(slab_kernel, side, local_bits, list_leng...  24.8 us
    all_to_all x2, starting transfers between devices, to_field(): got = lax.all_to_all(sent, 'slab', split_axis=0, concat_axis=0, tiled=True)  19.1 us
    unnamed x28, local copies, waits for them, and re-layouts  18.2 us
    all_to_all x1, blocking collectives, gradient_of_slab(): lax.all_to_all(meta.reshape(slabs, stride), 'slab', split_axis=0, concat_...  16.4 us
    pallas_call x1, Pallas kernels, gradient_of_slab(): pl.pallas_call(functools.partial(pack_kernel, slabs, cap, list_length), o...  16.2 us
  transfers between devices with their start and end apart: 15, of which 9 were waited for; matrix products, arithmetic and copies ran while one was open for 1% of the time, Pallas kernels for 19%

profile of v12, /device:TPU:0, one launch (start us, length us, event | category | flops | bytes accessed | tf_op | source)
XLA Modules:
  0.0 316.1 jit_solution(10471747531154373162)
XLA Ops:
  1.8 3.7 %route.1 = (s32[64,128]{1,0:T(8,128)}, s32[64,128]{1,0:T(8,128)}, s32[8,128]{1,0:T(8,128)}) custom-call(s32[64,128]{1,0:T(8,128)} %bitcast.51, s32[8,1024]{1,0:T(8,128)} %local_ref.1, s32[8,1024]{1,0:T(8,128)} %kind_ref.1, s32[8]{0:T(128)} %counts_ref.3), custom_call_target="tpu_custom_call" | custom-call | tf_op jit(solution)/shard_map/route/pallas_call | solution.py:640
  5.6 16.2 %pack.1 = (s32[17408]{0:T(1024)}, bf16[8,1280,128]{2,1,0:T(8,128)(2,1)}, bf16[8,768,128]{2,1,0:T(8,128)(2,1)}) custom-call(s32[8192]{0:T(1024)} %bitcast.49, s32[8192]{0:T(1024)} %bitcast.50, s32[8]{0:T(128)} %counts_ref.3, s32[8,128]{1,0:T(8,128)} %get-tuple-element.27.totals_ref, s32[8]{0:T(128)} %shift-left_or_fusion.code_ref, bf16[8192,128]{1,0:T(8,128)(2,1)} %bitcast.38), custom_call_target="tpu_custom_call" | custom-call | tf_op jit(solution)/shard_map/pack/pallas_call | solution.py:653
  21.8 16.4 %all_to_all.32 = s32[8,1,2176]{2,1,0:T(1,128)S(1)} all-to-all(s32[8,1,2176]{2,1,0:T(1,128)} %bitcast.48), channel_id=1, replica_groups=mesh['groups'=2,'slab'=8,'dom'=2] {'slab'}, dimensions={0} | all-to-all | bytes 139264 | tf_op jit(solution)/shard_map/all_to_all | solution.py:668
  38.2 3.6 %all-to-all-start.2 = ((bf16[8,1280,128]{2,1,0:T(8,128)(2,1)}), bf16[8,1280,128]{2,1,0:T(8,128)(2,1)S(1)}, u32[]{:S(2)}, u32[]{:S(2)}) async-start(bf16[8,1280,128]{2,1,0:T(8,128)(2,1)} %get-tuple-element.33), calls=%async_computation.2 | async-start | bytes 5242880 | tf_op jit(solution)/shard_map/all_to_all | solution.py:717
  46.2 11.1 %read_voxels.1 = (bf16[8,1280,128]{2,1,0:T(8,128)(2,1)}, bf16[8,768,128]{2,1,0:T(8,128)(2,1)}) custom-call(s32[17408]{0:T(1024)} %bitcast.33, s32[8]{0:T(128)} %copy-done.7, bf16[32768,128]{1,0:T(8,128)(2,1)} %volume_ref.1), custom_call_target="tpu_custom_call" | custom-call | bytes 104857600 | tf_op jit(solution)/shard_map/read_voxels/pallas_call | solution.py:687
  57.3 42.4 %all-to-all-done.2.image_ref = bf16[8,1280,128]{2,1,0:T(8,128)(2,1)S(1)} async-done(((bf16[8,1280,128]{2,1,0:T(8,128)(2,1)}), bf16[8,1280,128]{2,1,0:T(8,128)(2,1)S(1)}, u32[]{:S(2)}, u32[]{:S(2)}) %all-to-all-start.2) | async-done | bytes 2621472 | tf_op jit(solution)/shard_map/all_to_all | solution.py:717
  99.7 4.3 %all-to-all-start.1 = ((bf16[8,768,128]{2,1,0:T(8,128)(2,1)}), bf16[8,768,128]{2,1,0:T(8,128)(2,1)}, u32[]{:S(2)}, u32[]{:S(2)}) async-start(bf16[8,768,128]{2,1,0:T(8,128)(2,1)} %get-tuple-element.32), calls=%async_computation.1 | async-start | bytes 3145728 | tf_op jit(solution)/shard_map/all_to_all | solution.py:717
  107.3 16.1 %compare_and_add.2 = (f32[8,8,128]{2,1,0:T(8,128)S(1)}, f32[32776,128]{1,0:T(8,128)S(1)}) custom-call(s32[8]{0:T(128)S(1)} %copy-done.8, f32[64]{0:T(128)S(1)} %get-tuple-element.49.defocus_ref, f32[64]{0:T(128)S(1)} %get-tuple-element.48.phase_ref, f32[64]{0:T(128)S(1)} %mul.17.scale_ref, s32[17408]{0:T(1024)S(1)} %bitcast.34, s32[1]{0:T(128)} %bitcast.core_ref, ...), custom_call_target="tpu_custom_call" | custom-call | bytes 16777216 | tf_op jit(solution)/shard_map/compare_and_add/pallas_call | solution.py:728
  123.4 5.7 %copy-done = f32[32776,128]{1,0:T(8,128)} copy-done((f32[32776,128]{1,0:T(8,128)}, f32[32776,128]{1,0:T(8,128)S(1)}, u32[]{:S(2)}) %copy-start) | copy-done | bytes 16781336
  129.1 11.5 %all-to-all-done.1.image_ref = bf16[8,768,128]{2,1,0:T(8,128)(2,1)} async-done(((bf16[8,768,128]{2,1,0:T(8,128)(2,1)}), bf16[8,768,128]{2,1,0:T(8,128)(2,1)}, u32[]{:S(2)}, u32[]{:S(2)}) %all-to-all-start.1) | async-done | bytes 1572896 | tf_op jit(solution)/shard_map/all_to_all | solution.py:717
  140.6 5.8 %copy-done.1 = f32[32776,128]{1,0:T(8,128)S(1)} copy-done((f32[32776,128]{1,0:T(8,128)S(1)}, f32[32776,128]{1,0:T(8,128)}, u32[]{:S(2)}) %copy-start.1) | copy-done | bytes 16781336
  147.8 8.6 %compare_and_add.3 = (f32[8,8,128]{2,1,0:T(8,128)S(1)}, f32[32776,128]{1,0:T(8,128)S(1)}, f32[16384,128]{1,0:T(8,128)}, f32[4096,128]{1,0:T(8,128)S(1)}, f32[12288,128]{1,0:T(8,128)}) custom-call(s32[8]{0:T(128)S(1)} %copy-done.8, f32[64]{0:T(128)S(1)} %get-tuple-element.49.defocus_ref, ...), custom_call_target="tpu_custom_call", output_to_operand_aliasing={{1}: (12, {})} | custom-call | bytes 16777216 | tf_op jit(solution)/shard_map/compare_and_add/pallas_call | solution.py:728
  157.0 11.3 %collective-permute-done.1 = f32[4096,128]{1,0:T(8,128)S(1)} collective-permute-done((f32[4096,128]{1,0:T(8,128)S(1)}, f32[4096,128]{1,0:T(8,128)S(1)}, u32[]{:S(2)}, u32[]{:S(2)}) %collective-permute-start.1) | collective-permute-done | bytes 2097184 | tf_op jit(solution)/shard_map/ppermute | solution.py:558
  169.6 8.8 %transform_planes.2 = bf16[8,4,2,32,256]{4,3,2,1,0:T(8,128)(2,1)} custom-call(f32[16,32,32,128]{3,2,1,0:T(8,128)} %bitcast.36, f32[4,32,32,128]{3,2,1,0:T(8,128)} %bitcast.39, bf16[384,256]{1,0:T(8,128)(2,1)} %constant.67.clone.zblock_ref, f32[2,8,128]{2,1,0:T(8,128)} %constant.68.clone.turn_ref, bf16[512,512]{1,0:T(8,128)(2,1)} %constant.69.clone.wide_ref, ...), custom_call_target="tpu_custom_call" | custom-call | flops 536870912 | bytes 8388608 | tf_op jit(solution)/shard_map/transform_planes/pallas_call | solution.py:577
  178.4 15.3 %all-to-all-start.3 = ((bf16[8,4,2,32,256]{4,3,2,1,0:T(8,128)(2,1)}), bf16[8,4,2,32,256]{4,3,2,1,0:T(8,128)(2,1)S(1)}, u32[]{:S(2)}, u32[]{:S(2)}) async-start(bf16[8,4,2,32,256]{4,3,2,1,0:T(8,128)(2,1)} %transform_planes.2), calls=%async_computation.3 | async-start | bytes 2097152 | tf_op jit(solution)/shard_map/all_to_all | solution.py:604
  193.8 22.5 %transform_planes.3 = bf16[8,12,2,32,256]{4,3,2,1,0:T(8,128)(2,1)} custom-call(f32[16,32,32,128]{3,2,1,0:T(8,128)} %bitcast.37, f32[12,32,32,128]{3,2,1,0:T(8,128)} %bitcast.18.theirs_ref, bf16[384,256]{1,0:T(8,128)(2,1)} %constant.67.clone.zblock_ref, f32[2,8,128]{2,1,0:T(8,128)} %constant.68.clone.turn_ref, bf16[512,512]{1,0:T(8,128)(2,1)} %constant.69.clone.wide_ref, ...), custom_call_target="tpu_custom_call" | custom-call | flops 1610612736 | bytes 25165824 | tf_op jit(solution)/shard_map/transform_planes/pallas_call | solution.py:577
  216.3 3.7 %all-to-all-done.3.refs_0_ = bf16[8,4,2,32,256]{4,3,2,1,0:T(8,128)(2,1)S(1)} async-done(((bf16[8,4,2,32,256]{4,3,2,1,0:T(8,128)(2,1)}), bf16[8,4,2,32,256]{4,3,2,1,0:T(8,128)(2,1)S(1)}, u32[]{:S(2)}, u32[]{:S(2)}) %all-to-all-start.3) | async-done | bytes 1048608 | tf_op jit(solution)/shard_map/all_to_all | solution.py:604
  221.0 3.8 %all-to-all-start.4 = ((bf16[8,12,2,32,256]{4,3,2,1,0:T(8,128)(2,1)}), bf16[8,12,2,32,256]{4,3,2,1,0:T(8,128)(2,1)S(1)}, u32[]{:S(2)}, u32[]{:S(2)}) async-start(bf16[8,12,2,32,256]{4,3,2,1,0:T(8,128)(2,1)} %transform_planes.3), calls=%async_computation.4 | async-start | bytes 6291456 | tf_op jit(solution)/shard_map/all_to_all | solution.py:604
  231.1 19.2 %collective-permute-done.2 = f32[1,8]{1,0:T(1,128)S(1)} collective-permute-done((f32[1,8]{1,0:T(1,128)S(1)}, f32[1,8]{1,0:T(1,128)S(1)}, u32[]{:S(2)}, u32[]{:S(2)}) %collective-permute-start.2) | collective-permute-done | bytes 64 | tf_op jit(solution)/shard_map/ppermute | solution.py:541
  250.3 4.5 %collective-permute-start.6 = (f32[1,8]{1,0:T(1,128)S(1)}, f32[1,8]{1,0:T(1,128)S(1)}, u32[]{:S(2)}, u32[]{:S(2)}) collective-permute-start(f32[1,8]{1,0:T(1,128)S(1)} %get-tuple-element.53), channel_id=1, source_target_pairs={{0,10},{2,8},{4,14},{6,12},{8,2},{10,0},{12,6},{14,4},{1,11},{3,9}... | collective-permute-start | bytes 104 | tf_op jit(solution)/shard_map/ppermute | solution.py:541
  254.9 22.0 %collective-permute-done.3 = f32[1,8]{1,0:T(1,128)S(1)} collective-permute-done((f32[1,8]{1,0:T(1,128)S(1)}, f32[1,8]{1,0:T(1,128)S(1)}, u32[]{:S(2)}, u32[]{:S(2)}) %collective-permute-start.3) | collective-permute-done | bytes 64 | tf_op jit(solution)/shard_map/ppermute | solution.py:541
  281.3 14.4 %collective-permute-done.5 = f32[1,8]{1,0:T(1,128)S(1)} collective-permute-done((f32[1,8]{1,0:T(1,128)S(1)}, f32[1,8]{1,0:T(1,128)S(1)}, u32[]{:S(2)}, u32[]{:S(2)}) %collective-permute-start.5) | collective-permute-done | bytes 64 | tf_op jit(solution)/shard_map/ppermute | solution.py:541
  297.1 5.1 %collective-permute-done.10.refs_3_ = bf16[8,12,2,32,256]{4,3,2,1,0:T(8,128)(2,1)S(1)} collective-permute-done((bf16[8,12,2,32,256]{4,3,2,1,0:T(8,128)(2,1)S(1)}, bf16[8,12,2,32,256]{4,3,2,1,0:T(8,128)(2,1)S(1)}, u32[]{:S(2)}, u32[]{:S(2)}) %collective-permute-start.10) | collective-permute-done | bytes 3145760 | tf_op jit(solution)/shard_map/ppermute | solution.py:608
  303.4 12.6 %transform_first.1 = f32[2,128,32,256]{3,2,1,0:T(8,128)} custom-call(s32[1]{0:T(128)} %bitcast.core_ref, bf16[8,4,2,32,256]{4,3,2,1,0:T(8,128)(2,1)S(1)} %copy-done.3, bf16[8,12,2,32,256]{4,3,2,1,0:T(8,128)(2,1)S(1)} %all-to-all-done.4.refs_1_, bf16[8,4,2,32,256]{4,3,2,1,0:T(8,128)(2,1)} %collective-permute-done.9.refs_2_, ...), custom_call_target="tpu_custom_call" | custom-call | tf_op jit(solution)/shard_map/transform_first/pallas_call | solution.py:611
  (71 shorter events, 26.3 us)
Async XLA Ops:
  38.2 61.5 %all-to-all-start.2 = ((bf16[8,1280,128]{2,1,0:T(8,128)(2,1)}), bf16[8,1280,128]{2,1,0:T(8,128)(2,1)S(1)}, u32[]{:S(2)}, u32[]{:S(2)}) async-start(bf16[8,1280,128]{2,1,0:T(8,128)(2,1)} %get-tuple-element.33), calls=%async_computation.2 | async-start | bytes 5242880 | tf_op jit(solution)/shard_map/all_to_all | solution.py:717
  42.0 4.2 %copy-start.7 = (s32[8]{0:T(128)}, s32[8]{0:T(128)S(1)}, u32[]{:S(2)}) copy-start(s32[8]{0:T(128)S(1)} %slice_reduce_fusion.2.totals_ref) | copy-start | bytes 100
  57.2 46.8 %copy-start.12 = (f32[64,2]{0,1:T(2,128)S(1)}, f32[64,2]{0,1:T(2,128)}, u32[]{:S(2)}) copy-start(f32[64,2]{0,1:T(2,128)} %param.22) | copy-start | bytes 1540
  57.3 46.9 %copy-start.10 = (bf16[4,128,128]{2,1,0:T(8,128)(2,1)S(1)}, bf16[4,128,128]{2,1,0:T(8,128)(2,1)}, u32[]{:S(2)}) copy-start(bf16[4,128,128]{2,1,0:T(8,128)(2,1)} %param.15) | copy-start | bytes 393220
  57.3 48.3 %copy-start.6 = (s32[136,128]{1,0:T(8,128)S(1)}, s32[136,128]{1,0:T(8,128)}, u32[]{:S(2)}) copy-start(s32[136,128]{1,0:T(8,128)} %decode.1) | copy-start | bytes 208900
  57.3 48.3 %copy-start.8 = (s32[8]{0:T(128)S(1)}, s32[8]{0:T(128)}, u32[]{:S(2)}) copy-start(s32[8]{0:T(128)} %copy-done.7) | copy-start | bytes 100
  99.7 40.9 %all-to-all-start.1 = ((bf16[8,768,128]{2,1,0:T(8,128)(2,1)}), bf16[8,768,128]{2,1,0:T(8,128)(2,1)}, u32[]{:S(2)}, u32[]{:S(2)}) async-start(bf16[8,768,128]{2,1,0:T(8,128)(2,1)} %get-tuple-element.32), calls=%async_computation.1 | async-start | bytes 3145728 | tf_op jit(solution)/shard_map/all_to_all | solution.py:717
  105.5 1.7 copy-start.4
  123.4 5.7 %copy-start = (f32[32776,128]{1,0:T(8,128)}, f32[32776,128]{1,0:T(8,128)S(1)}, u32[]{:S(2)}) copy-start(f32[32776,128]{1,0:T(8,128)S(1)} %get-tuple-element.34.rest_0_) | copy-start | bytes 50343940
  140.6 5.8 %copy-start.1 = (f32[32776,128]{1,0:T(8,128)S(1)}, f32[32776,128]{1,0:T(8,128)}, u32[]{:S(2)}) copy-start(f32[32776,128]{1,0:T(8,128)} %copy-done) | copy-start | bytes 50343940
  156.4 37.3 %collective-permute-start = (f32[12288,128]{1,0:T(8,128)}, f32[12288,128]{1,0:T(8,128)}, u32[]{:S(2)}, u32[]{:S(2)}) collective-permute-start(f32[12288,128]{1,0:T(8,128)} %get-tuple-element.36), channel_id=1, source_target_pairs={{0,1},{1,0},{2,3},{3,2},{4,5},{5,4},{6,7},{7,6},{8,9},{9,8},{10,11... | collective-permute-start | bytes 18874376 | tf_op jit(solution)/shard_map/ppermute | solution.py:558
  156.5 11.8 %collective-permute-start.1 = (f32[4096,128]{1,0:T(8,128)S(1)}, f32[4096,128]{1,0:T(8,128)S(1)}, u32[]{:S(2)}, u32[]{:S(2)}) collective-permute-start(f32[4096,128]{1,0:T(8,128)S(1)} %get-tuple-element.37), channel_id=1, source_target_pairs={{0,1},{1,0},{2,3},{3,2},{4,5},{5,4},{6,7},{7,6},{8,9},{9,8},{10,11... | collective-permute-start | bytes 6291464 | tf_op jit(solution)/shard_map/ppermute | solution.py:558
  178.4 41.6 %all-to-all-start.3 = ((bf16[8,4,2,32,256]{4,3,2,1,0:T(8,128)(2,1)}), bf16[8,4,2,32,256]{4,3,2,1,0:T(8,128)(2,1)S(1)}, u32[]{:S(2)}, u32[]{:S(2)}) async-start(bf16[8,4,2,32,256]{4,3,2,1,0:T(8,128)(2,1)} %transform_planes.2), calls=%async_computation.3 | async-start | bytes 2097152 | tf_op jit(solution)/shard_map/all_to_all | solution.py:604
  216.3 80.2 %copy-start.11 = (s32[8]{0:T(128)S(1)}, s32[8]{0:T(128)}, u32[]{:S(2)}) copy-start(s32[8]{0:T(128)} %counts_ref.3) | copy-start | bytes 100
  221.0 75.5 %all-to-all-start.4 = ((bf16[8,12,2,32,256]{4,3,2,1,0:T(8,128)(2,1)}), bf16[8,12,2,32,256]{4,3,2,1,0:T(8,128)(2,1)S(1)}, u32[]{:S(2)}, u32[]{:S(2)}) async-start(bf16[8,12,2,32,256]{4,3,2,1,0:T(8,128)(2,1)} %transform_planes.3), calls=%async_computation.4 | async-start | bytes 6291456 | tf_op jit(solution)/shard_map/all_to_all | solution.py:604
  224.8 71.7 %collective-permute-start.9 = (bf16[8,4,2,32,256]{4,3,2,1,0:T(8,128)(2,1)}, bf16[8,4,2,32,256]{4,3,2,1,0:T(8,128)(2,1)}, u32[]{:S(2)}, u32[]{:S(2)}) collective-permute-start(bf16[8,4,2,32,256]{4,3,2,1,0:T(8,128)(2,1)} %copy-done.2), channel_id=1, source_target_pairs={{0,1},{1,0},{2,3},{3,2},{4,5},{5,4},{6,7},{7,6},{8,9},{9,8},{10,11... | collective-permute-start | bytes 3145736 | tf_op jit(solution)/shard_map/ppermute | solution.py:606
  224.9 25.4 %collective-permute-start.2 = (f32[1,8]{1,0:T(1,128)S(1)}, f32[1,8]{1,0:T(1,128)S(1)}, u32[]{:S(2)}, u32[]{:S(2)}) collective-permute-start(f32[1,8]{1,0:T(1,128)S(1)} %get-tuple-element.50), channel_id=1, source_target_pairs={{0,2},{2,0},{4,6},{6,4},{8,10},{10,8},{12,14},{14,12},{1,3},{3,1},... | collective-permute-start | bytes 104 | tf_op jit(solution)/shard_map/ppermute | solution.py:541
  226.7 50.1 %collective-permute-start.3 = (f32[1,8]{1,0:T(1,128)S(1)}, f32[1,8]{1,0:T(1,128)S(1)}, u32[]{:S(2)}, u32[]{:S(2)}) collective-permute-start(f32[1,8]{1,0:T(1,128)S(1)} %get-tuple-element.56), channel_id=1, source_target_pairs={{0,4},{2,6},{4,0},{6,2},{8,12},{10,14},{12,8},{14,10},{1,5},{3,7},... | collective-permute-start | bytes 104 | tf_op jit(solution)/shard_map/ppermute | solution.py:541
  228.2 51.2 %collective-permute-start.4 = (f32[1,8]{1,0:T(1,128)S(1)}, f32[1,8]{1,0:T(1,128)S(1)}, u32[]{:S(2)}, u32[]{:S(2)}) collective-permute-start(f32[1,8]{1,0:T(1,128)S(1)} %get-tuple-element.55), channel_id=1, source_target_pairs={{0,6},{2,4},{4,2},{6,0},{8,14},{10,12},{12,10},{14,8},{1,7},{3,5},... | collective-permute-start | bytes 104 | tf_op jit(solution)/shard_map/ppermute | solution.py:541
  228.5 67.2 %collective-permute-start.5 = (f32[1,8]{1,0:T(1,128)S(1)}, f32[1,8]{1,0:T(1,128)S(1)}, u32[]{:S(2)}, u32[]{:S(2)}) collective-permute-start(f32[1,8]{1,0:T(1,128)S(1)} %get-tuple-element.54), channel_id=1, source_target_pairs={{0,8},{2,10},{4,12},{6,14},{8,0},{10,2},{12,4},{14,6},{1,9},{3,11}... | collective-permute-start | bytes 104 | tf_op jit(solution)/shard_map/ppermute | solution.py:541
  250.3 46.1 %collective-permute-start.6 = (f32[1,8]{1,0:T(1,128)S(1)}, f32[1,8]{1,0:T(1,128)S(1)}, u32[]{:S(2)}, u32[]{:S(2)}) collective-permute-start(f32[1,8]{1,0:T(1,128)S(1)} %get-tuple-element.53), channel_id=1, source_target_pairs={{0,10},{2,8},{4,14},{6,12},{8,2},{10,0},{12,6},{14,4},{1,11},{3,9}... | collective-permute-start | bytes 104 | tf_op jit(solution)/shard_map/ppermute | solution.py:541
  276.8 19.6 %collective-permute-start.7 = (f32[1,8]{1,0:T(1,128)S(1)}, f32[1,8]{1,0:T(1,128)S(1)}, u32[]{:S(2)}, u32[]{:S(2)}) collective-permute-start(f32[1,8]{1,0:T(1,128)S(1)} %get-tuple-element.52), channel_id=1, source_target_pairs={{0,12},{2,14},{4,8},{6,10},{8,4},{10,6},{12,0},{14,2},{1,13},{3,15... | collective-permute-start | bytes 104 | tf_op jit(solution)/shard_map/ppermute | solution.py:541
  279.3 17.1 %collective-permute-start.8 = (f32[1,8]{1,0:T(1,128)S(1)}, f32[1,8]{1,0:T(1,128)S(1)}, u32[]{:S(2)}, u32[]{:S(2)}) collective-permute-start(f32[1,8]{1,0:T(1,128)S(1)} %get-tuple-element.51), channel_id=1, source_target_pairs={{0,14},{2,12},{4,10},{6,8},{8,6},{10,4},{12,2},{14,0},{1,15},{3,13... | collective-permute-start | bytes 104 | tf_op jit(solution)/shard_map/ppermute | solution.py:541
  296.5 5.7 %collective-permute-start.10 = (bf16[8,12,2,32,256]{4,3,2,1,0:T(8,128)(2,1)S(1)}, bf16[8,12,2,32,256]{4,3,2,1,0:T(8,128)(2,1)S(1)}, u32[]{:S(2)}, u32[]{:S(2)}) collective-permute-start(bf16[8,12,2,32,256]{4,3,2,1,0:T(8,128)(2,1)S(1)} %all-to-all-done.4.refs_1_), channel_id=1, source_target_pairs={{0,1},{1,0},{2,3},{3,2},{4,5},{5,4},{6,7},{7,6},{8,9},{9,8},{10,11... | collective-permute-start | bytes 9437192 | tf_op jit(solution)/shard_map/ppermute | solution.py:608
  (4 other events, 4.9 us)

commit v13 on v12

--- a/solution.py
+++ b/solution.py
@@ -13,7 +13,7 @@
 GROUP = 16
 UNUSED = 100
 STEP = 256
-PAIR = 2
+PAIR = 1
 MIB = 1024 * 1024
 
 SMEM_SPEC = pl.BlockSpec(memory_space=pltpu.SMEM)
@@ -206,7 +206,7 @@
 def slab_kernel(
     side, local_bits, list_length, particles, cap, offset, first, last,
     totals_ref, defocus_ref, phase_ref, scale_ref, index_ref, core_ref,
-    word_ref, voxel_ref, image_ref, forward_ref, backward_ref, unit_ref, *rest,
+    word_ref, voxel_ref, image_ref, forward_ref, backward_ref, *rest,
 ):
     if not first:
         rest = rest[1:]
@@ -216,7 +216,7 @@
     steps_each = tile // step
     blocks = sum_ref.shape[0] - 8
     features = image_ref.shape[2]
-    kinds = forward_ref.shape[0] // features
+    kinds = forward_ref.shape[1] // features
     position_bits = bits_of(list_length)
     per_row = side // 8
     half = features // 2
@@ -266,18 +266,14 @@
         horiz = ((position % per_row) * 8 - side // 2).astype(jnp.float32) + repeat(cell_horiz)
         factor = scale * sine(defocus * (vert * vert + horiz * horiz) + phase)
         factor = jnp.concatenate([factor, factor], axis=0)
-        contract_last = (((1,), (1,)), ((), ()))
-        each_kind = lax.dot_general(
-            forward_ref[...], voxel_ref[source, pl.ds(at, step), :], contract_last,
-            preferred_element_type=jnp.float32,
-        )
-        extracted = each_kind[0:features, :]
-        for k in range(1, kinds):
-            extracted = jnp.where(kind == k, each_kind[k * features:(k + 1) * features, :], extracted)
-        picture = lax.dot_general(
-            unit_ref[...], image_ref[source, pl.ds(at, step), :], contract_last,
-            preferred_element_type=jnp.float32,
-        )
+        voxel = voxel_ref[source, pl.ds(at, step), :].astype(jnp.float32).T.astype(jnp.bfloat16)
+        picture = image_ref[source, pl.ds(at, step), :].astype(jnp.float32).T
+
+        def by_kind(value):
+            none = jnp.zeros_like(value)
+            return jnp.concatenate([jnp.where(kind == k, value, none) for k in range(kinds)], axis=0)
+
+        extracted = jnp.dot(forward_ref[...], by_kind(voxel), preferred_element_type=jnp.float32)
         misfit = jnp.where(valid, factor * extracted - picture, 0.0)
         squares = jnp.sum(misfit * misfit, axis=0, keepdims=True)
         which = lax.broadcasted_iota(jnp.int32, (particles, step), 0)
@@ -287,11 +283,7 @@
             folded = folded + spread[:, i * LANES:(i + 1) * LANES]
         square_ref[source] = square_ref[source] + folded
         weighted = (factor * misfit).astype(jnp.bfloat16)
-        none = jnp.zeros_like(weighted)
-        spread_back = jnp.concatenate(
-            [jnp.where(kind == k, weighted, none) for k in range(kinds)], axis=0
-        )
-        terms = jnp.dot(backward_ref[...], spread_back, preferred_element_type=jnp.float32)
+        terms = jnp.dot(backward_ref[...], by_kind(weighted), preferred_element_type=jnp.float32)
         staged_ref[slot * step:(slot + 1) * step, :] = terms.T
 
     def places_of(base):
@@ -646,7 +638,7 @@
         name="route",
     )(owners.reshape(rows, LANES), local_block, kinds, counts)
     target, word = target.reshape(entries), word.reshape(entries)
-    tiles = [cap * 5 // 8, cap * 3 // 8] if cap >= 2048 else [cap]
+    tiles = [cap // 2, cap // 2] if cap >= 2048 else [cap]
     parts = len(tiles)
     code = ctf_code | ((scales.astype(jnp.float32) * 256.0).astype(jnp.int32) << 8)
     stride = cap + LANES
@@ -700,10 +692,9 @@
         name="read_voxels",
     )(index, totals_in, volume))
 
-    forward = jnp.transpose(kernels, (0, 2, 1)).reshape(kind_count * features, features)
+    forward = jnp.transpose(kernels, (2, 0, 1)).reshape(features, kind_count * features)
     backward = kernels.reshape(kind_count, 2, 8, 8, features).transpose(3, 1, 2, 0, 4)
     backward = backward.reshape(features, kind_count * features)
-    unit = jnp.eye(features, dtype=jnp.bfloat16)
     core = lax.axis_index("dom").astype(jnp.int32).reshape(1)
     plane_blocks = (side // 8) ** 2
     pieces = [planes * plane_blocks for planes in pieces_of(side // slabs // 2)]
@@ -719,7 +710,7 @@
         arguments = [
             totals_in, table_rows[:, 0], table_rows[:, 1], scale_in, index, core,
             words[:, offset:offset + tile].reshape(slabs, 1, tile), voxels[part], picture,
-            forward, backward, unit,
+            forward, backward,
         ]
         aliases = {}
         if not first:

time: 321 us -> 320 us (level)
  Pallas kernels: 102 us -> 128 us
  waiting for transfers between devices: 130 us -> 113 us
  starting transfers between devices: 42.8 us -> 37.6 us
  blocking collectives: 16.4 us -> 12 us
    all_to_all x2, waiting for transfers between devices: 53.9 us -> 36.9 us  [gradient_of_slab(): lax.all_to_all(packed[part], 'slab', split_axis=0, concat_axis=0, tiled=T...]
    pallas_call x2, Pallas kernels: 24.8 us -> 40.2 us  [gradient_of_slab(): pl.pallas_call(functools.partial(slab_kernel, side, local_bits, list_leng...]
    pallas_call x1, Pallas kernels: 11.1 us -> 18.3 us  [gradient_of_slab(): pl.pallas_call(functools.partial(gather_kernel, slabs, cap), out_shape=tu...]
    all_to_all x2, starting transfers between devices: 19.1 us -> 13.1 us  [to_field(): got = lax.all_to_all(sent, 'slab', split_axis=0, concat_axis=0, tiled=True)]
    all_to_all x1, blocking collectives: 16.4 us -> 12 us  [gradient_of_slab(): lax.all_to_all(meta.reshape(slabs, stride), 'slab', split_axis=0, concat_...]
    unnamed x28 -> x32, local copies, waits for them, and re-layouts: 18.2 us -> 21.2 us
  transfers between devices with their start and end apart: 15 -> 15, of which waited for: 9 -> 9; matrix products, arithmetic and copies ran while one was open for 1% -> 1% of each run, Pallas kernels for 19% -> 25%
where the time goes in v13:
time: 320 us; the launch traced here: 318 us
  Pallas kernels  128 us (40%)
  waiting for transfers between devices  113 us (35%)
  starting transfers between devices  37.6 us (12%)
  local copies, waits for them, and re-layouts  23.3 us (7%)
  blocking collectives  12 us (4%)
    ppermute x7, waiting for transfers between devices, sum_over_slabs(): lax.ppermute(row(i), 'slab', [(slab, slab ^ i) for slab in range(slabs)])  56.4 us
    pallas_call x2, Pallas kernels, gradient_of_slab(): pl.pallas_call(functools.partial(slab_kernel, side, local_bits, list_leng...  40.2 us
    all_to_all x2, waiting for transfers between devices, gradient_of_slab(): lax.all_to_all(packed[part], 'slab', split_axis=0, concat_axis=0, tiled=T...  36.9 us
    pallas_call x2, Pallas kernels, to_field(): pl.pallas_call(planes_kernel, grid=(quads, per_row // yblocks), out_shape...  31.4 us
    unnamed x32, local copies, waits for them, and re-layouts  21.2 us
    pallas_call x1, Pallas kernels, gradient_of_slab(): pl.pallas_call(functools.partial(pack_kernel, slabs, cap, list_length), o...  19.4 us
    pallas_call x1, Pallas kernels, gradient_of_slab(): pl.pallas_call(functools.partial(gather_kernel, slabs, cap), out_shape=tu...  18.3 us
    ppermute x7, starting transfers between devices, sum_over_slabs(): lax.ppermute(row(i), 'slab', [(slab, slab ^ i) for slab in range(slabs)])  15.2 us
  transfers between devices with their start and end apart: 15, of which 9 were waited for; matrix products, arithmetic and copies ran while one was open for 1% of the time, Pallas kernels for 25%

profile of v13, /device:TPU:0, one launch (start us, length us, event | category | flops | bytes accessed | tf_op | source)
XLA Modules:
  0.0 318.2 jit_solution(10041060973562235450)
XLA Ops:
  1.8 3.7 %route.1 = (s32[64,128]{1,0:T(8,128)}, s32[64,128]{1,0:T(8,128)}, s32[8,128]{1,0:T(8,128)}) custom-call(s32[64,128]{1,0:T(8,128)} %bitcast.49, s32[8,1024]{1,0:T(8,128)} %local_ref.1, s32[8,1024]{1,0:T(8,128)} %kind_ref.1, s32[8]{0:T(128)} %counts_ref.3), custom_call_target="tpu_custom_call" | custom-call | tf_op jit(solution)/shard_map/route/pallas_call | solution.py:632
  5.5 19.4 %pack.1 = (s32[17408]{0:T(1024)}, bf16[8,1024,128]{2,1,0:T(8,128)(2,1)}, bf16[8,1024,128]{2,1,0:T(8,128)(2,1)}) custom-call(s32[8192]{0:T(1024)} %bitcast.47, s32[8192]{0:T(1024)} %bitcast.48, s32[8]{0:T(128)} %counts_ref.3, s32[8,128]{1,0:T(8,128)} %get-tuple-element.27.totals_ref, s32[8]{0:T(128)} %shift-left_or_fusion.code_ref, bf16[8192,128]{1,0:T(8,128)(2,1)} %bitcast.37), custom_call_target="tpu_custom_call" | custom-call | tf_op jit(solution)/shard_map/pack/pallas_call | solution.py:645
  24.9 12.0 %all_to_all.32 = s32[8,1,2176]{2,1,0:T(1,128)S(1)} all-to-all(s32[8,1,2176]{2,1,0:T(1,128)} %bitcast.46), channel_id=1, replica_groups=mesh['groups'=2,'slab'=8,'dom'=2] {'slab'}, dimensions={0} | all-to-all | bytes 139264 | tf_op jit(solution)/shard_map/all_to_all | solution.py:660
  36.9 3.6 %all-to-all-start.2 = ((bf16[8,1024,128]{2,1,0:T(8,128)(2,1)}), bf16[8,1024,128]{2,1,0:T(8,128)(2,1)S(1)}, u32[]{:S(2)}, u32[]{:S(2)}) async-start(bf16[8,1024,128]{2,1,0:T(8,128)(2,1)} %get-tuple-element.33), calls=%async_computation.2 | async-start | bytes 4194304 | tf_op jit(solution)/shard_map/all_to_all | solution.py:708
  44.9 18.3 %read_voxels.1 = (bf16[8,1024,128]{2,1,0:T(8,128)(2,1)}, bf16[8,1024,128]{2,1,0:T(8,128)(2,1)}) custom-call(s32[17408]{0:T(1024)} %bitcast.32, s32[8]{0:T(128)} %copy-done.9, bf16[32768,128]{1,0:T(8,128)(2,1)} %volume_ref.1), custom_call_target="tpu_custom_call" | custom-call | bytes 104857600 | tf_op jit(solution)/shard_map/read_voxels/pallas_call | solution.py:679
  63.2 25.6 %all-to-all-done.2.image_ref = bf16[8,1024,128]{2,1,0:T(8,128)(2,1)S(1)} async-done(((bf16[8,1024,128]{2,1,0:T(8,128)(2,1)}), bf16[8,1024,128]{2,1,0:T(8,128)(2,1)S(1)}, u32[]{:S(2)}, u32[]{:S(2)}) %all-to-all-start.2) | async-done | bytes 2097184 | tf_op jit(solution)/shard_map/all_to_all | solution.py:708
  90.1 3.6 %all-to-all-start.1 = ((bf16[8,1024,128]{2,1,0:T(8,128)(2,1)}), bf16[8,1024,128]{2,1,0:T(8,128)(2,1)S(1)}, u32[]{:S(2)}, u32[]{:S(2)}) async-start(bf16[8,1024,128]{2,1,0:T(8,128)(2,1)} %get-tuple-element.32), calls=%async_computation.1 | async-start | bytes 4194304 | tf_op jit(solution)/shard_map/all_to_all | solution.py:708
  98.3 26.7 %compare_and_add.2 = (f32[8,8,128]{2,1,0:T(8,128)S(1)}, f32[32776,128]{1,0:T(8,128)S(1)}) custom-call(s32[8]{0:T(128)S(1)} %copy-done.10, f32[64]{0:T(128)S(1)} %get-tuple-element.49.defocus_ref, f32[64]{0:T(128)S(1)} %get-tuple-element.48.phase_ref, f32[64]{0:T(128)S(1)} %mul.17.scale_ref, s32[17408]{0:T(1024)S(1)} %bitcast.33, s32[1]{0:T(128)} %bitcast.core_ref, ...), custom_call_target="tpu_custom_call" | custom-call | bytes 16777216 | tf_op jit(solution)/shard_map/compare_and_add/pallas_call | solution.py:719
  125.0 5.7 %copy-done = f32[32776,128]{1,0:T(8,128)} copy-done((f32[32776,128]{1,0:T(8,128)}, f32[32776,128]{1,0:T(8,128)S(1)}, u32[]{:S(2)}) %copy-start) | copy-done | bytes 16781336
  130.8 11.3 %all-to-all-done.1.image_ref = bf16[8,1024,128]{2,1,0:T(8,128)(2,1)S(1)} async-done(((bf16[8,1024,128]{2,1,0:T(8,128)(2,1)}), bf16[8,1024,128]{2,1,0:T(8,128)(2,1)S(1)}, u32[]{:S(2)}, u32[]{:S(2)}) %all-to-all-start.1) | async-done | bytes 2097184 | tf_op jit(solution)/shard_map/all_to_all | solution.py:708
  142.1 5.8 %copy-done.1 = f32[32776,128]{1,0:T(8,128)S(1)} copy-done((f32[32776,128]{1,0:T(8,128)S(1)}, f32[32776,128]{1,0:T(8,128)}, u32[]{:S(2)}) %copy-start.1) | copy-done | bytes 16781336
  149.5 13.5 %compare_and_add.3 = (f32[8,8,128]{2,1,0:T(8,128)S(1)}, f32[32776,128]{1,0:T(8,128)S(1)}, f32[16384,128]{1,0:T(8,128)}, f32[4096,128]{1,0:T(8,128)S(1)}, f32[12288,128]{1,0:T(8,128)}) custom-call(s32[8]{0:T(128)S(1)} %copy-done.10, f32[64]{0:T(128)S(1)} %get-tuple-element.49.defocus_ref, ...), custom_call_target="tpu_custom_call", output_to_operand_aliasing={{1}: (11, {})} | custom-call | bytes 16777216 | tf_op jit(solution)/shard_map/compare_and_add/pallas_call | solution.py:719
  164.9 11.6 %collective-permute-done.1 = f32[4096,128]{1,0:T(8,128)S(1)} collective-permute-done((f32[4096,128]{1,0:T(8,128)S(1)}, f32[4096,128]{1,0:T(8,128)S(1)}, u32[]{:S(2)}, u32[]{:S(2)}) %collective-permute-start.1) | collective-permute-done | bytes 2097184 | tf_op jit(solution)/shard_map/ppermute | solution.py:550
  177.8 8.8 %transform_planes.2 = bf16[8,4,2,32,256]{4,3,2,1,0:T(8,128)(2,1)} custom-call(f32[16,32,32,128]{3,2,1,0:T(8,128)} %bitcast.35, f32[4,32,32,128]{3,2,1,0:T(8,128)} %bitcast.38, bf16[384,256]{1,0:T(8,128)(2,1)} %constant.67.clone.zblock_ref, f32[2,8,128]{2,1,0:T(8,128)} %constant.68.clone.turn_ref, bf16[512,512]{1,0:T(8,128)(2,1)} %constant.69.clone.wide_ref, ...), custom_call_target="tpu_custom_call" | custom-call | flops 536870912 | bytes 8388608 | tf_op jit(solution)/shard_map/transform_planes/pallas_call | solution.py:569
  186.6 9.4 %all-to-all-start.3 = ((bf16[8,4,2,32,256]{4,3,2,1,0:T(8,128)(2,1)}), bf16[8,4,2,32,256]{4,3,2,1,0:T(8,128)(2,1)S(1)}, u32[]{:S(2)}, u32[]{:S(2)}) async-start(bf16[8,4,2,32,256]{4,3,2,1,0:T(8,128)(2,1)} %transform_planes.2), calls=%async_computation.3 | async-start | bytes 2097152 | tf_op jit(solution)/shard_map/all_to_all | solution.py:596
  196.1 22.6 %transform_planes.3 = bf16[8,12,2,32,256]{4,3,2,1,0:T(8,128)(2,1)} custom-call(f32[16,32,32,128]{3,2,1,0:T(8,128)} %bitcast.36, f32[12,32,32,128]{3,2,1,0:T(8,128)} %bitcast.19.theirs_ref, bf16[384,256]{1,0:T(8,128)(2,1)} %constant.67.clone.zblock_ref, f32[2,8,128]{2,1,0:T(8,128)} %constant.68.clone.turn_ref, bf16[512,512]{1,0:T(8,128)(2,1)} %constant.69.clone.wide_ref, ...), custom_call_target="tpu_custom_call" | custom-call | flops 1610612736 | bytes 25165824 | tf_op jit(solution)/shard_map/transform_planes/pallas_call | solution.py:569
  218.7 3.4 %all-to-all-done.3.refs_0_ = bf16[8,4,2,32,256]{4,3,2,1,0:T(8,128)(2,1)S(1)} async-done(((bf16[8,4,2,32,256]{4,3,2,1,0:T(8,128)(2,1)}), bf16[8,4,2,32,256]{4,3,2,1,0:T(8,128)(2,1)S(1)}, u32[]{:S(2)}, u32[]{:S(2)}) %all-to-all-start.3) | async-done | bytes 1048608 | tf_op jit(solution)/shard_map/all_to_all | solution.py:596
  223.1 3.6 %all-to-all-start.4 = ((bf16[8,12,2,32,256]{4,3,2,1,0:T(8,128)(2,1)}), bf16[8,12,2,32,256]{4,3,2,1,0:T(8,128)(2,1)S(1)}, u32[]{:S(2)}, u32[]{:S(2)}) async-start(bf16[8,12,2,32,256]{4,3,2,1,0:T(8,128)(2,1)} %transform_planes.3), calls=%async_computation.4 | async-start | bytes 6291456 | tf_op jit(solution)/shard_map/all_to_all | solution.py:596
  233.2 19.2 %collective-permute-done.2 = f32[1,8]{1,0:T(1,128)S(1)} collective-permute-done((f32[1,8]{1,0:T(1,128)S(1)}, f32[1,8]{1,0:T(1,128)S(1)}, u32[]{:S(2)}, u32[]{:S(2)}) %collective-permute-start.2) | collective-permute-done | bytes 64 | tf_op jit(solution)/shard_map/ppermute | solution.py:533
  252.4 4.5 %collective-permute-start.6 = (f32[1,8]{1,0:T(1,128)S(1)}, f32[1,8]{1,0:T(1,128)S(1)}, u32[]{:S(2)}, u32[]{:S(2)}) collective-permute-start(f32[1,8]{1,0:T(1,128)S(1)} %get-tuple-element.55), channel_id=1, source_target_pairs={{0,10},{2,8},{4,14},{6,12},{8,2},{10,0},{12,6},{14,4},{1,11},{3,9}... | collective-permute-start | bytes 104 | tf_op jit(solution)/shard_map/ppermute | solution.py:533
  257.0 22.0 %collective-permute-done.3 = f32[1,8]{1,0:T(1,128)S(1)} collective-permute-done((f32[1,8]{1,0:T(1,128)S(1)}, f32[1,8]{1,0:T(1,128)S(1)}, u32[]{:S(2)}, u32[]{:S(2)}) %collective-permute-start.3) | collective-permute-done | bytes 64 | tf_op jit(solution)/shard_map/ppermute | solution.py:533
  283.4 14.4 %collective-permute-done.5 = f32[1,8]{1,0:T(1,128)S(1)} collective-permute-done((f32[1,8]{1,0:T(1,128)S(1)}, f32[1,8]{1,0:T(1,128)S(1)}, u32[]{:S(2)}, u32[]{:S(2)}) %collective-permute-start.5) | collective-permute-done | bytes 64 | tf_op jit(solution)/shard_map/ppermute | solution.py:533
  299.2 5.1 %collective-permute-done.10.refs_3_ = bf16[8,12,2,32,256]{4,3,2,1,0:T(8,128)(2,1)S(1)} collective-permute-done((bf16[8,12,2,32,256]{4,3,2,1,0:T(8,128)(2,1)S(1)}, bf16[8,12,2,32,256]{4,3,2,1,0:T(8,128)(2,1)S(1)}, u32[]{:S(2)}, u32[]{:S(2)}) %collective-permute-start.10) | collective-permute-done | bytes 3145760 | tf_op jit(solution)/shard_map/ppermute | solution.py:600
  305.5 12.6 %transform_first.1 = f32[2,128,32,256]{3,2,1,0:T(8,128)} custom-call(s32[1]{0:T(128)} %bitcast.core_ref, bf16[8,4,2,32,256]{4,3,2,1,0:T(8,128)(2,1)S(1)} %copy-done.5, bf16[8,12,2,32,256]{4,3,2,1,0:T(8,128)(2,1)S(1)} %all-to-all-done.4.refs_1_, bf16[8,4,2,32,256]{4,3,2,1,0:T(8,128)(2,1)} %collective-permute-done.9.refs_2_, ...), custom_call_target="tpu_custom_call" | custom-call | tf_op jit(solution)/shard_map/transform_first/pallas_call | solution.py:603
  (73 shorter events, 30.7 us)
Async XLA Ops:
  36.9 51.8 %all-to-all-start.2 = ((bf16[8,1024,128]{2,1,0:T(8,128)(2,1)}), bf16[8,1024,128]{2,1,0:T(8,128)(2,1)S(1)}, u32[]{:S(2)}, u32[]{:S(2)}) async-start(bf16[8,1024,128]{2,1,0:T(8,128)(2,1)} %get-tuple-element.33), calls=%async_computation.2 | async-start | bytes 4194304 | tf_op jit(solution)/shard_map/all_to_all | solution.py:708
  40.7 4.2 %copy-start.9 = (s32[8]{0:T(128)}, s32[8]{0:T(128)S(1)}, u32[]{:S(2)}) copy-start(s32[8]{0:T(128)S(1)} %slice_reduce_fusion.2.totals_ref) | copy-start | bytes 100
  63.2 30.5 %copy-start.14 = (f32[64,2]{0,1:T(2,128)S(1)}, f32[64,2]{0,1:T(2,128)}, u32[]{:S(2)}) copy-start(f32[64,2]{0,1:T(2,128)} %param.22) | copy-start | bytes 1540
  63.2 30.6 %copy-start.12 = (bf16[4,128,128]{2,1,0:T(8,128)(2,1)S(1)}, bf16[4,128,128]{2,1,0:T(8,128)(2,1)}, u32[]{:S(2)}) copy-start(bf16[4,128,128]{2,1,0:T(8,128)(2,1)} %param.15) | copy-start | bytes 393220
  63.2 32.0 %copy-start.8 = (s32[136,128]{1,0:T(8,128)S(1)}, s32[136,128]{1,0:T(8,128)}, u32[]{:S(2)}) copy-start(s32[136,128]{1,0:T(8,128)} %decode.1) | copy-start | bytes 208900
  63.2 32.0 %copy-start.10 = (s32[8]{0:T(128)S(1)}, s32[8]{0:T(128)}, u32[]{:S(2)}) copy-start(s32[8]{0:T(128)} %copy-done.9) | copy-start | bytes 100
  90.1 52.0 %all-to-all-start.1 = ((bf16[8,1024,128]{2,1,0:T(8,128)(2,1)}), bf16[8,1024,128]{2,1,0:T(8,128)(2,1)S(1)}, u32[]{:S(2)}, u32[]{:S(2)}) async-start(bf16[8,1024,128]{2,1,0:T(8,128)(2,1)} %get-tuple-element.32), calls=%async_computation.1 | async-start | bytes 4194304 | tf_op jit(solution)/shard_map/all_to_all | solution.py:708
  95.1 1.6 copy-start.3
  125.0 5.7 %copy-start = (f32[32776,128]{1,0:T(8,128)}, f32[32776,128]{1,0:T(8,128)S(1)}, u32[]{:S(2)}) copy-start(f32[32776,128]{1,0:T(8,128)S(1)} %get-tuple-element.34.rest_0_) | copy-start | bytes 50343940
  142.1 5.8 %copy-start.1 = (f32[32776,128]{1,0:T(8,128)S(1)}, f32[32776,128]{1,0:T(8,128)}, u32[]{:S(2)}) copy-start(f32[32776,128]{1,0:T(8,128)} %copy-done) | copy-start | bytes 50343940
  163.0 33.1 %collective-permute-start = (f32[12288,128]{1,0:T(8,128)}, f32[12288,128]{1,0:T(8,128)}, u32[]{:S(2)}, u32[]{:S(2)}) collective-permute-start(f32[12288,128]{1,0:T(8,128)} %get-tuple-element.36), channel_id=1, source_target_pairs={{0,1},{1,0},{2,3},{3,2},{4,5},{5,4},{6,7},{7,6},{8,9},{9,8},{10,11... | collective-permute-start | bytes 18874376 | tf_op jit(solution)/shard_map/ppermute | solution.py:550
  164.8 11.7 %collective-permute-start.1 = (f32[4096,128]{1,0:T(8,128)S(1)}, f32[4096,128]{1,0:T(8,128)S(1)}, u32[]{:S(2)}, u32[]{:S(2)}) collective-permute-start(f32[4096,128]{1,0:T(8,128)S(1)} %get-tuple-element.37), channel_id=1, source_target_pairs={{0,1},{1,0},{2,3},{3,2},{4,5},{5,4},{6,7},{7,6},{8,9},{9,8},{10,11... | collective-permute-start | bytes 6291464 | tf_op jit(solution)/shard_map/ppermute | solution.py:550
  186.6 35.5 %all-to-all-start.3 = ((bf16[8,4,2,32,256]{4,3,2,1,0:T(8,128)(2,1)}), bf16[8,4,2,32,256]{4,3,2,1,0:T(8,128)(2,1)S(1)}, u32[]{:S(2)}, u32[]{:S(2)}) async-start(bf16[8,4,2,32,256]{4,3,2,1,0:T(8,128)(2,1)} %transform_planes.2), calls=%async_computation.3 | async-start | bytes 2097152 | tf_op jit(solution)/shard_map/all_to_all | solution.py:596
  218.7 80.0 %copy-start.13 = (s32[8]{0:T(128)S(1)}, s32[8]{0:T(128)}, u32[]{:S(2)}) copy-start(s32[8]{0:T(128)} %counts_ref.3) | copy-start | bytes 100
  223.1 75.5 %all-to-all-start.4 = ((bf16[8,12,2,32,256]{4,3,2,1,0:T(8,128)(2,1)}), bf16[8,12,2,32,256]{4,3,2,1,0:T(8,128)(2,1)S(1)}, u32[]{:S(2)}, u32[]{:S(2)}) async-start(bf16[8,12,2,32,256]{4,3,2,1,0:T(8,128)(2,1)} %transform_planes.3), calls=%async_computation.4 | async-start | bytes 6291456 | tf_op jit(solution)/shard_map/all_to_all | solution.py:596
  226.7 71.8 %collective-permute-start.9 = (bf16[8,4,2,32,256]{4,3,2,1,0:T(8,128)(2,1)}, bf16[8,4,2,32,256]{4,3,2,1,0:T(8,128)(2,1)}, u32[]{:S(2)}, u32[]{:S(2)}) collective-permute-start(bf16[8,4,2,32,256]{4,3,2,1,0:T(8,128)(2,1)} %copy-done.4), channel_id=1, source_target_pairs={{0,1},{1,0},{2,3},{3,2},{4,5},{5,4},{6,7},{7,6},{8,9},{9,8},{10,11... | collective-permute-start | bytes 3145736 | tf_op jit(solution)/shard_map/ppermute | solution.py:598
  226.9 25.6 %collective-permute-start.2 = (f32[1,8]{1,0:T(1,128)S(1)}, f32[1,8]{1,0:T(1,128)S(1)}, u32[]{:S(2)}, u32[]{:S(2)}) collective-permute-start(f32[1,8]{1,0:T(1,128)S(1)} %get-tuple-element.52), channel_id=1, source_target_pairs={{0,2},{2,0},{4,6},{6,4},{8,10},{10,8},{12,14},{14,12},{1,3},{3,1},... | collective-permute-start | bytes 104 | tf_op jit(solution)/shard_map/ppermute | solution.py:533
  228.8 50.1 %collective-permute-start.3 = (f32[1,8]{1,0:T(1,128)S(1)}, f32[1,8]{1,0:T(1,128)S(1)}, u32[]{:S(2)}, u32[]{:S(2)}) collective-permute-start(f32[1,8]{1,0:T(1,128)S(1)} %get-tuple-element.58), channel_id=1, source_target_pairs={{0,4},{2,6},{4,0},{6,2},{8,12},{10,14},{12,8},{14,10},{1,5},{3,7},... | collective-permute-start | bytes 104 | tf_op jit(solution)/shard_map/ppermute | solution.py:533
  230.3 51.1 %collective-permute-start.4 = (f32[1,8]{1,0:T(1,128)S(1)}, f32[1,8]{1,0:T(1,128)S(1)}, u32[]{:S(2)}, u32[]{:S(2)}) collective-permute-start(f32[1,8]{1,0:T(1,128)S(1)} %get-tuple-element.57), channel_id=1, source_target_pairs={{0,6},{2,4},{4,2},{6,0},{8,14},{10,12},{12,10},{14,8},{1,7},{3,5},... | collective-permute-start | bytes 104 | tf_op jit(solution)/shard_map/ppermute | solution.py:533
  230.4 67.3 %collective-permute-start.5 = (f32[1,8]{1,0:T(1,128)S(1)}, f32[1,8]{1,0:T(1,128)S(1)}, u32[]{:S(2)}, u32[]{:S(2)}) collective-permute-start(f32[1,8]{1,0:T(1,128)S(1)} %get-tuple-element.56), channel_id=1, source_target_pairs={{0,8},{2,10},{4,12},{6,14},{8,0},{10,2},{12,4},{14,6},{1,9},{3,11}... | collective-permute-start | bytes 104 | tf_op jit(solution)/shard_map/ppermute | solution.py:533
  252.4 46.1 %collective-permute-start.6 = (f32[1,8]{1,0:T(1,128)S(1)}, f32[1,8]{1,0:T(1,128)S(1)}, u32[]{:S(2)}, u32[]{:S(2)}) collective-permute-start(f32[1,8]{1,0:T(1,128)S(1)} %get-tuple-element.55), channel_id=1, source_target_pairs={{0,10},{2,8},{4,14},{6,12},{8,2},{10,0},{12,6},{14,4},{1,11},{3,9}... | collective-permute-start | bytes 104 | tf_op jit(solution)/shard_map/ppermute | solution.py:533
  278.9 19.6 %collective-permute-start.7 = (f32[1,8]{1,0:T(1,128)S(1)}, f32[1,8]{1,0:T(1,128)S(1)}, u32[]{:S(2)}, u32[]{:S(2)}) collective-permute-start(f32[1,8]{1,0:T(1,128)S(1)} %get-tuple-element.54), channel_id=1, source_target_pairs={{0,12},{2,14},{4,8},{6,10},{8,4},{10,6},{12,0},{14,2},{1,13},{3,15... | collective-permute-start | bytes 104 | tf_op jit(solution)/shard_map/ppermute | solution.py:533
  281.4 17.1 %collective-permute-start.8 = (f32[1,8]{1,0:T(1,128)S(1)}, f32[1,8]{1,0:T(1,128)S(1)}, u32[]{:S(2)}, u32[]{:S(2)}) collective-permute-start(f32[1,8]{1,0:T(1,128)S(1)} %get-tuple-element.53), channel_id=1, source_target_pairs={{0,14},{2,12},{4,10},{6,8},{8,6},{10,4},{12,2},{14,0},{1,15},{3,13... | collective-permute-start | bytes 104 | tf_op jit(solution)/shard_map/ppermute | solution.py:533
  298.6 5.7 %collective-permute-start.10 = (bf16[8,12,2,32,256]{4,3,2,1,0:T(8,128)(2,1)S(1)}, bf16[8,12,2,32,256]{4,3,2,1,0:T(8,128)(2,1)S(1)}, u32[]{:S(2)}, u32[]{:S(2)}) collective-permute-start(bf16[8,12,2,32,256]{4,3,2,1,0:T(8,128)(2,1)S(1)} %all-to-all-done.4.refs_1_), channel_id=1, source_target_pairs={{0,1},{1,0},{2,3},{3,2},{4,5},{5,4},{6,7},{7,6},{8,9},{9,8},{10,11... | collective-permute-start | bytes 9437192 | tf_op jit(solution)/shard_map/ppermute | solution.py:600
  (6 other events, 8.0 us)

commit v14 on v13

--- a/solution.py
+++ b/solution.py
@@ -210,7 +210,7 @@
 ):
     if not first:
         rest = rest[1:]
-    square_ref, sum_ref, out_refs, (staged_ref, steps_ref, sems) = rest[0], rest[1], rest[2:-3], rest[-3:]
+    square_ref, sum_ref, out_refs, (staged_ref, zero_ref, steps_ref, sems) = rest[0], rest[1], rest[2:-4], rest[-4:]
     slabs, _, tile = word_ref.shape
     step = staged_ref.shape[0] // PAIR
     steps_each = tile // step
@@ -222,10 +222,19 @@
     half = features // 2
 
     if first:
-        @pl.loop(0, blocks // 256)
+        zero_ref[...] = jnp.zeros_like(zero_ref)
+        length = zero_ref.shape[0]
+        clear = lambda i: pltpu.make_async_copy(
+            zero_ref, sum_ref.at[pl.ds(pl.multiple_of(i * length, length), length)], sems.at[0]
+        )
+
+        @pl.loop(0, blocks // length)
         def _(i):
-            at = pl.multiple_of(i * 256, 256)
-            sum_ref[pl.ds(at, 256), :] = jnp.zeros((256, features), jnp.float32)
+            clear(i).start()
+
+        @pl.loop(0, blocks // length)
+        def _(i):
+            clear(i).wait()
 
     square_ref[...] = jnp.zeros_like(square_ref)
     live_of = lambda source: jnp.clip(totals_ref[source] - offset, 0, tile)
@@ -291,10 +300,10 @@
 
     def add_group(base, at):
         places = places_of(base)
-        held = [sum_ref[pl.ds(place, 1), :] for place in places]
+        held = [sum_ref[place] for place in places]
         new = [staged_ref[pl.ds(at + j, 1), :] for j in range(GROUP)]
         for j in range(GROUP):
-            sum_ref[pl.ds(places[j], 1), :] = held[j] + new[j]
+            sum_ref[places[j]] = held[j] + new[j]
 
     def base_of(number):
         earlier = steps_ref[jnp.clip(number, 0, jnp.maximum(count - 1, 0))]
@@ -334,9 +343,7 @@
                     def _():
                         places = places_of(start)
                         for j in range(GROUP):
-                            sum_ref[pl.ds(places[j], 1), :] = (
-                                sum_ref[pl.ds(places[j], 1), :] + staged_ref[pl.ds(at + j, 1), :]
-                            )
+                            sum_ref[places[j]] = sum_ref[places[j]] + staged_ref[pl.ds(at + j, 1), :]
 
             for slot in range(PAIR):
                 compare(turn * PAIR + slot, slot)
@@ -722,13 +729,14 @@
             ),
             out_shape=(
                 jax.ShapeDtypeStruct((slabs, particles, LANES), jnp.float32),
-                pltpu.VMEM((blocks + 8, features), jnp.float32),
+                pltpu.VMEM((blocks + 8, 1, features), jnp.float32),
             )
-            + tuple(jax.ShapeDtypeStruct((length, features), jnp.float32) for length in lengths),
+            + tuple(jax.ShapeDtypeStruct((length, 1, features), jnp.float32) for length in lengths),
             in_specs=[SMEM_SPEC] * 6 + [VMEM_SPEC] * (len(arguments) - 6),
             out_specs=(VMEM_SPEC, VMEM_SPEC) + (ANY_SPEC,) * len(lengths),
             scratch_shapes=[
                 pltpu.VMEM((PAIR * min(tile, STEP), features), jnp.float32),
+                pltpu.VMEM((256, 1, features), jnp.float32),
                 pltpu.SMEM((slabs * tile // min(tile, STEP) + 1,), jnp.int32),
                 pltpu.SemaphoreType.DMA((max(1, len(lengths)),)),
             ],
@@ -740,7 +748,7 @@
         squares = squares + more
         behind.append(more)
         offset += tile
-    mine, *theirs = halves
+    mine, *theirs = [half.reshape(-1, features) for half in halves]
     partial_sums = jnp.sum(squares, axis=2)
     return mine, theirs, partial_sums, side
 

time: 320 us -> 333 us (1.041); the launches traced: 318 us -> 328 us
  starting transfers between devices: 37.6 us -> 52.9 us
  waiting for transfers between devices: 113 us -> 109 us
    all_to_all x2, starting transfers between devices: 13.1 us -> 26.7 us  [to_field(): got = lax.all_to_all(sent, 'slab', split_axis=0, concat_axis=0, tiled=True)]
    pallas_call x1, Pallas kernels: 18.3 us -> 11.3 us  [gradient_of_slab(): pl.pallas_call(functools.partial(gather_kernel, slabs, cap), out_shape=tu...]
    pallas_call x2, Pallas kernels: 40.2 us -> 44.8 us  [gradient_of_slab(): pl.pallas_call(functools.partial(slab_kernel, side, local_bits, list_leng...]
    all_to_all x2, waiting for transfers between devices: 36.9 us -> 32.6 us  [gradient_of_slab(): lax.all_to_all(packed[part], 'slab', split_axis=0, concat_axis=0, tiled=T...]
where the time goes in v14:
time: 333 us; the launch traced here: 328 us
  Pallas kernels  126 us (38%)
  waiting for transfers between devices  109 us (33%)
  starting transfers between devices  52.9 us (16%)
  local copies, waits for them, and re-layouts  23.3 us (7%)
  blocking collectives  12.7 us (4%)
    ppermute x7, waiting for transfers between devices, sum_over_slabs(): lax.ppermute(row(i), 'slab', [(slab, slab ^ i) for slab in range(slabs)])  56.4 us
    pallas_call x2, Pallas kernels, gradient_of_slab(): pl.pallas_call(functools.partial(slab_kernel, side, local_bits, list_leng...  44.8 us
    all_to_all x2, waiting for transfers between devices, gradient_of_slab(): lax.all_to_all(packed[part], 'slab', split_axis=0, concat_axis=0, tiled=T...  32.6 us
    pallas_call x2, Pallas kernels, to_field(): pl.pallas_call(planes_kernel, grid=(quads, per_row // yblocks), out_shape...  31.4 us
    all_to_all x2, starting transfers between devices, to_field(): got = lax.all_to_all(sent, 'slab', split_axis=0, concat_axis=0, tiled=True)  26.7 us
    unnamed x32, local copies, waits for them, and re-layouts  21.2 us
    pallas_call x1, Pallas kernels, gradient_of_slab(): pl.pallas_call(functools.partial(pack_kernel, slabs, cap, list_length), o...  19.3 us
    ppermute x7, starting transfers between devices, sum_over_slabs(): lax.ppermute(row(i), 'slab', [(slab, slab ^ i) for slab in range(slabs)])  15.2 us
  transfers between devices with their start and end apart: 15, of which 9 were waited for; matrix products, arithmetic and copies ran while one was open for 1% of the time, Pallas kernels for 25%

profile of v14, /device:TPU:0, one launch (start us, length us, event | category | flops | bytes accessed | tf_op | source)
XLA Modules:
  0.0 327.5 jit_solution(11747323780734218756)
XLA Ops:
  1.8 3.7 %route.1 = (s32[64,128]{1,0:T(8,128)}, s32[64,128]{1,0:T(8,128)}, s32[8,128]{1,0:T(8,128)}) custom-call(s32[64,128]{1,0:T(8,128)} %bitcast.52, s32[8,1024]{1,0:T(8,128)} %local_ref.1, s32[8,1024]{1,0:T(8,128)} %kind_ref.1, s32[8]{0:T(128)} %counts_ref.3), custom_call_target="tpu_custom_call" | custom-call | tf_op jit(solution)/shard_map/route/pallas_call | solution.py:639
  5.5 19.3 %pack.1 = (s32[17408]{0:T(1024)}, bf16[8,1024,128]{2,1,0:T(8,128)(2,1)}, bf16[8,1024,128]{2,1,0:T(8,128)(2,1)}) custom-call(s32[8192]{0:T(1024)} %bitcast.50, s32[8192]{0:T(1024)} %bitcast.51, s32[8]{0:T(128)} %counts_ref.3, s32[8,128]{1,0:T(8,128)} %get-tuple-element.27.totals_ref, s32[8]{0:T(128)} %shift-left_or_fusion.code_ref, bf16[8192,128]{1,0:T(8,128)(2,1)} %bitcast.40), custom_call_target="tpu_custom_call" | custom-call | tf_op jit(solution)/shard_map/pack/pallas_call | solution.py:652
  24.8 12.7 %all_to_all.32 = s32[8,1,2176]{2,1,0:T(1,128)S(1)} all-to-all(s32[8,1,2176]{2,1,0:T(1,128)} %bitcast.49), channel_id=1, replica_groups=mesh['groups'=2,'slab'=8,'dom'=2] {'slab'}, dimensions={0} | all-to-all | bytes 139264 | tf_op jit(solution)/shard_map/all_to_all | solution.py:667
  37.5 3.6 %all-to-all-start.2 = ((bf16[8,1024,128]{2,1,0:T(8,128)(2,1)}), bf16[8,1024,128]{2,1,0:T(8,128)(2,1)S(1)}, u32[]{:S(2)}, u32[]{:S(2)}) async-start(bf16[8,1024,128]{2,1,0:T(8,128)(2,1)} %get-tuple-element.33), calls=%async_computation.2 | async-start | bytes 4194304 | tf_op jit(solution)/shard_map/all_to_all | solution.py:715
  45.4 11.3 %read_voxels.1 = (bf16[8,1024,128]{2,1,0:T(8,128)(2,1)}, bf16[8,1024,128]{2,1,0:T(8,128)(2,1)}) custom-call(s32[17408]{0:T(1024)} %bitcast.34, s32[8]{0:T(128)} %copy-done.9, bf16[32768,128]{1,0:T(8,128)(2,1)} %volume_ref.1), custom_call_target="tpu_custom_call" | custom-call | bytes 104857600 | tf_op jit(solution)/shard_map/read_voxels/pallas_call | solution.py:686
  56.7 31.3 %all-to-all-done.2.image_ref = bf16[8,1024,128]{2,1,0:T(8,128)(2,1)S(1)} async-done(((bf16[8,1024,128]{2,1,0:T(8,128)(2,1)}), bf16[8,1024,128]{2,1,0:T(8,128)(2,1)S(1)}, u32[]{:S(2)}, u32[]{:S(2)}) %all-to-all-start.2) | async-done | bytes 2097184 | tf_op jit(solution)/shard_map/all_to_all | solution.py:715
  89.4 3.6 %all-to-all-start.1 = ((bf16[8,1024,128]{2,1,0:T(8,128)(2,1)}), bf16[8,1024,128]{2,1,0:T(8,128)(2,1)S(1)}, u32[]{:S(2)}, u32[]{:S(2)}) async-start(bf16[8,1024,128]{2,1,0:T(8,128)(2,1)} %get-tuple-element.32), calls=%async_computation.1 | async-start | bytes 4194304 | tf_op jit(solution)/shard_map/all_to_all | solution.py:715
  97.7 36.8 %compare_and_add.2 = (f32[8,8,128]{2,1,0:T(8,128)S(1)}, f32[32776,1,128]{2,1,0:T(1,128)S(1)}) custom-call(s32[8]{0:T(128)S(1)} %copy-done.10, f32[64]{0:T(128)S(1)} %get-tuple-element.49.defocus_ref, f32[64]{0:T(128)S(1)} %get-tuple-element.48.phase_ref, f32[64]{0:T(128)S(1)} %mul.17.scale_ref, s32[17408]{0:T(1024)S(1)} %bitcast.35, s32[1]{0:T(128)} %bitcast.core_ref, ...), custom_call_target="tpu_custom_call" | custom-call | bytes 16777216 | tf_op jit(solution)/shard_map/compare_and_add/pallas_call | solution.py:726
  134.5 5.7 %copy-done = f32[32776,1,128]{2,1,0:T(1,128)} copy-done((f32[32776,1,128]{2,1,0:T(1,128)}, f32[32776,1,128]{2,1,0:T(1,128)S(1)}, u32[]{:S(2)}) %copy-start) | copy-done | bytes 16781336
  141.5 5.8 %copy-done.1 = f32[32776,1,128]{2,1,0:T(1,128)S(1)} copy-done((f32[32776,1,128]{2,1,0:T(1,128)S(1)}, f32[32776,1,128]{2,1,0:T(1,128)}, u32[]{:S(2)}) %copy-start.1) | copy-done | bytes 16781336
  148.8 8.0 %compare_and_add.3 = (f32[8,8,128]{2,1,0:T(8,128)S(1)}, f32[32776,1,128]{2,1,0:T(1,128)S(1)}, f32[16384,1,128]{2,1,0:T(1,128)}, f32[4096,1,128]{2,1,0:T(1,128)S(1)}, f32[12288,1,128]{2,1,0:T(1,128)}) custom-call(s32[8]{0:T(128)S(1)} %copy-done.10, f32[64]{0:T(128)S(1)} %get-tuple-element.49.defocus_ref, ...), custom_call_target="tpu_custom_call", output_to_operand_aliasing={{1}: (11, {})} | custom-call | bytes 16777216 | tf_op jit(solution)/shard_map/compare_and_add/pallas_call | solution.py:726
  156.8 3.4 %collective-permute-start = (f32[12288,128]{1,0:T(8,128)}, f32[12288,128]{1,0:T(8,128)}, u32[]{:S(2)}, u32[]{:S(2)}) collective-permute-start(f32[12288,128]{1,0:T(8,128)} %bitcast.18), channel_id=1, source_target_pairs={{0,1},{1,0},{2,3},{3,2},{4,5},{5,4},{6,7},{7,6},{8,9},{9,8},{10,11... | collective-permute-start | bytes 18874376 | tf_op jit(solution)/shard_map/ppermute | solution.py:557
  160.3 11.6 %collective-permute-done.1 = f32[4096,128]{1,0:T(8,128)S(1)} collective-permute-done((f32[4096,128]{1,0:T(8,128)S(1)}, f32[4096,128]{1,0:T(8,128)S(1)}, u32[]{:S(2)}, u32[]{:S(2)}) %collective-permute-start.1) | collective-permute-done | bytes 2097184 | tf_op jit(solution)/shard_map/ppermute | solution.py:557
  173.3 8.8 %transform_planes.2 = bf16[8,4,2,32,256]{4,3,2,1,0:T(8,128)(2,1)} custom-call(f32[16,32,32,128]{3,2,1,0:T(8,128)} %bitcast.38, f32[4,32,32,128]{3,2,1,0:T(8,128)} %bitcast.41, bf16[384,256]{1,0:T(8,128)(2,1)} %constant.67.clone.zblock_ref, f32[2,8,128]{2,1,0:T(8,128)} %constant.68.clone.turn_ref, bf16[512,512]{1,0:T(8,128)(2,1)} %constant.69.clone.wide_ref, ...), custom_call_target="tpu_custom_call" | custom-call | flops 536870912 | bytes 8388608 | tf_op jit(solution)/shard_map/transform_planes/pallas_call | solution.py:576
  182.1 23.1 %all-to-all-start.3 = ((bf16[8,4,2,32,256]{4,3,2,1,0:T(8,128)(2,1)}), bf16[8,4,2,32,256]{4,3,2,1,0:T(8,128)(2,1)S(1)}, u32[]{:S(2)}, u32[]{:S(2)}) async-start(bf16[8,4,2,32,256]{4,3,2,1,0:T(8,128)(2,1)} %transform_planes.2), calls=%async_computation.3 | async-start | bytes 2097152 | tf_op jit(solution)/shard_map/all_to_all | solution.py:603
  205.2 22.6 %transform_planes.3 = bf16[8,12,2,32,256]{4,3,2,1,0:T(8,128)(2,1)} custom-call(f32[16,32,32,128]{3,2,1,0:T(8,128)} %bitcast.39, f32[12,32,32,128]{3,2,1,0:T(8,128)} %bitcast.21.theirs_ref, bf16[384,256]{1,0:T(8,128)(2,1)} %constant.67.clone.zblock_ref, f32[2,8,128]{2,1,0:T(8,128)} %constant.68.clone.turn_ref, bf16[512,512]{1,0:T(8,128)(2,1)} %constant.69.clone.wide_ref, ...), custom_call_target="tpu_custom_call" | custom-call | flops 1610612736 | bytes 25165824 | tf_op jit(solution)/shard_map/transform_planes/pallas_call | solution.py:576
  227.8 3.6 %all-to-all-done.3.refs_0_ = bf16[8,4,2,32,256]{4,3,2,1,0:T(8,128)(2,1)S(1)} async-done(((bf16[8,4,2,32,256]{4,3,2,1,0:T(8,128)(2,1)}), bf16[8,4,2,32,256]{4,3,2,1,0:T(8,128)(2,1)S(1)}, u32[]{:S(2)}, u32[]{:S(2)}) %all-to-all-start.3) | async-done | bytes 1048608 | tf_op jit(solution)/shard_map/all_to_all | solution.py:603
  232.4 3.6 %all-to-all-start.4 = ((bf16[8,12,2,32,256]{4,3,2,1,0:T(8,128)(2,1)}), bf16[8,12,2,32,256]{4,3,2,1,0:T(8,128)(2,1)S(1)}, u32[]{:S(2)}, u32[]{:S(2)}) async-start(bf16[8,12,2,32,256]{4,3,2,1,0:T(8,128)(2,1)} %transform_planes.3), calls=%async_computation.4 | async-start | bytes 6291456 | tf_op jit(solution)/shard_map/all_to_all | solution.py:603
  242.6 19.2 %collective-permute-done.2 = f32[1,8]{1,0:T(1,128)S(1)} collective-permute-done((f32[1,8]{1,0:T(1,128)S(1)}, f32[1,8]{1,0:T(1,128)S(1)}, u32[]{:S(2)}, u32[]{:S(2)}) %collective-permute-start.2) | collective-permute-done | bytes 64 | tf_op jit(solution)/shard_map/ppermute | solution.py:540
  261.8 4.5 %collective-permute-start.6 = (f32[1,8]{1,0:T(1,128)S(1)}, f32[1,8]{1,0:T(1,128)S(1)}, u32[]{:S(2)}, u32[]{:S(2)}) collective-permute-start(f32[1,8]{1,0:T(1,128)S(1)} %get-tuple-element.55), channel_id=1, source_target_pairs={{0,10},{2,8},{4,14},{6,12},{8,2},{10,0},{12,6},{14,4},{1,11},{3,9}... | collective-permute-start | bytes 104 | tf_op jit(solution)/shard_map/ppermute | solution.py:540
  266.3 22.0 %collective-permute-done.3 = f32[1,8]{1,0:T(1,128)S(1)} collective-permute-done((f32[1,8]{1,0:T(1,128)S(1)}, f32[1,8]{1,0:T(1,128)S(1)}, u32[]{:S(2)}, u32[]{:S(2)}) %collective-permute-start.3) | collective-permute-done | bytes 64 | tf_op jit(solution)/shard_map/ppermute | solution.py:540
  292.7 14.4 %collective-permute-done.5 = f32[1,8]{1,0:T(1,128)S(1)} collective-permute-done((f32[1,8]{1,0:T(1,128)S(1)}, f32[1,8]{1,0:T(1,128)S(1)}, u32[]{:S(2)}, u32[]{:S(2)}) %collective-permute-start.5) | collective-permute-done | bytes 64 | tf_op jit(solution)/shard_map/ppermute | solution.py:540
  308.6 5.1 %collective-permute-done.10.refs_3_ = bf16[8,12,2,32,256]{4,3,2,1,0:T(8,128)(2,1)S(1)} collective-permute-done((bf16[8,12,2,32,256]{4,3,2,1,0:T(8,128)(2,1)S(1)}, bf16[8,12,2,32,256]{4,3,2,1,0:T(8,128)(2,1)S(1)}, u32[]{:S(2)}, u32[]{:S(2)}) %collective-permute-start.10) | collective-permute-done | bytes 3145760 | tf_op jit(solution)/shard_map/ppermute | solution.py:607
  314.9 12.6 %transform_first.1 = f32[2,128,32,256]{3,2,1,0:T(8,128)} custom-call(s32[1]{0:T(128)} %bitcast.core_ref, bf16[8,4,2,32,256]{4,3,2,1,0:T(8,128)(2,1)S(1)} %copy-done.5, bf16[8,12,2,32,256]{4,3,2,1,0:T(8,128)(2,1)S(1)} %all-to-all-done.4.refs_1_, bf16[8,4,2,32,256]{4,3,2,1,0:T(8,128)(2,1)} %collective-permute-done.9.refs_2_, ...), custom_call_target="tpu_custom_call" | custom-call | tf_op jit(solution)/shard_map/transform_first/pallas_call | solution.py:610
  (73 shorter events, 30.1 us)
Async XLA Ops:
  37.5 50.6 %all-to-all-start.2 = ((bf16[8,1024,128]{2,1,0:T(8,128)(2,1)}), bf16[8,1024,128]{2,1,0:T(8,128)(2,1)S(1)}, u32[]{:S(2)}, u32[]{:S(2)}) async-start(bf16[8,1024,128]{2,1,0:T(8,128)(2,1)} %get-tuple-element.33), calls=%async_computation.2 | async-start | bytes 4194304 | tf_op jit(solution)/shard_map/all_to_all | solution.py:715
  41.2 4.2 %copy-start.9 = (s32[8]{0:T(128)}, s32[8]{0:T(128)S(1)}, u32[]{:S(2)}) copy-start(s32[8]{0:T(128)S(1)} %slice_reduce_fusion.2.totals_ref) | copy-start | bytes 100
  56.7 36.3 %copy-start.14 = (f32[64,2]{0,1:T(2,128)S(1)}, f32[64,2]{0,1:T(2,128)}, u32[]{:S(2)}) copy-start(f32[64,2]{0,1:T(2,128)} %param.22) | copy-start | bytes 1540
  56.7 36.4 %copy-start.12 = (bf16[4,128,128]{2,1,0:T(8,128)(2,1)S(1)}, bf16[4,128,128]{2,1,0:T(8,128)(2,1)}, u32[]{:S(2)}) copy-start(bf16[4,128,128]{2,1,0:T(8,128)(2,1)} %param.15) | copy-start | bytes 393220
  56.7 37.7 %copy-start.8 = (s32[136,128]{1,0:T(8,128)S(1)}, s32[136,128]{1,0:T(8,128)}, u32[]{:S(2)}) copy-start(s32[136,128]{1,0:T(8,128)} %decode.1) | copy-start | bytes 208900
  56.7 37.8 %copy-start.10 = (s32[8]{0:T(128)S(1)}, s32[8]{0:T(128)}, u32[]{:S(2)}) copy-start(s32[8]{0:T(128)} %copy-done.9) | copy-start | bytes 100
  89.4 52.0 %all-to-all-start.1 = ((bf16[8,1024,128]{2,1,0:T(8,128)(2,1)}), bf16[8,1024,128]{2,1,0:T(8,128)(2,1)S(1)}, u32[]{:S(2)}, u32[]{:S(2)}) async-start(bf16[8,1024,128]{2,1,0:T(8,128)(2,1)} %get-tuple-element.32), calls=%async_computation.1 | async-start | bytes 4194304 | tf_op jit(solution)/shard_map/all_to_all | solution.py:715
  94.5 1.6 copy-start.3
  134.5 5.7 %copy-start = (f32[32776,1,128]{2,1,0:T(1,128)}, f32[32776,1,128]{2,1,0:T(1,128)S(1)}, u32[]{:S(2)}) copy-start(f32[32776,1,128]{2,1,0:T(1,128)S(1)} %get-tuple-element.34.rest_0_) | copy-start | bytes 50343940
  141.4 5.8 %copy-start.1 = (f32[32776,1,128]{2,1,0:T(1,128)S(1)}, f32[32776,1,128]{2,1,0:T(1,128)}, u32[]{:S(2)}) copy-start(f32[32776,1,128]{2,1,0:T(1,128)} %copy-done) | copy-start | bytes 50343940
  156.8 48.4 %collective-permute-start = (f32[12288,128]{1,0:T(8,128)}, f32[12288,128]{1,0:T(8,128)}, u32[]{:S(2)}, u32[]{:S(2)}) collective-permute-start(f32[12288,128]{1,0:T(8,128)} %bitcast.18), channel_id=1, source_target_pairs={{0,1},{1,0},{2,3},{3,2},{4,5},{5,4},{6,7},{7,6},{8,9},{9,8},{10,11... | collective-permute-start | bytes 18874376 | tf_op jit(solution)/shard_map/ppermute | solution.py:557
  160.3 11.7 %collective-permute-start.1 = (f32[4096,128]{1,0:T(8,128)S(1)}, f32[4096,128]{1,0:T(8,128)S(1)}, u32[]{:S(2)}, u32[]{:S(2)}) collective-permute-start(f32[4096,128]{1,0:T(8,128)S(1)} %bitcast.37), channel_id=1, source_target_pairs={{0,1},{1,0},{2,3},{3,2},{4,5},{5,4},{6,7},{7,6},{8,9},{9,8},{10,11... | collective-permute-start | bytes 6291464 | tf_op jit(solution)/shard_map/ppermute | solution.py:557
  182.1 49.4 %all-to-all-start.3 = ((bf16[8,4,2,32,256]{4,3,2,1,0:T(8,128)(2,1)}), bf16[8,4,2,32,256]{4,3,2,1,0:T(8,128)(2,1)S(1)}, u32[]{:S(2)}, u32[]{:S(2)}) async-start(bf16[8,4,2,32,256]{4,3,2,1,0:T(8,128)(2,1)} %transform_planes.2), calls=%async_computation.3 | async-start | bytes 2097152 | tf_op jit(solution)/shard_map/all_to_all | solution.py:603
  227.8 80.2 %copy-start.13 = (s32[8]{0:T(128)S(1)}, s32[8]{0:T(128)}, u32[]{:S(2)}) copy-start(s32[8]{0:T(128)} %counts_ref.3) | copy-start | bytes 100
  232.4 75.5 %all-to-all-start.4 = ((bf16[8,12,2,32,256]{4,3,2,1,0:T(8,128)(2,1)}), bf16[8,12,2,32,256]{4,3,2,1,0:T(8,128)(2,1)S(1)}, u32[]{:S(2)}, u32[]{:S(2)}) async-start(bf16[8,12,2,32,256]{4,3,2,1,0:T(8,128)(2,1)} %transform_planes.3), calls=%async_computation.4 | async-start | bytes 6291456 | tf_op jit(solution)/shard_map/all_to_all | solution.py:603
  236.1 71.9 %collective-permute-start.9 = (bf16[8,4,2,32,256]{4,3,2,1,0:T(8,128)(2,1)}, bf16[8,4,2,32,256]{4,3,2,1,0:T(8,128)(2,1)}, u32[]{:S(2)}, u32[]{:S(2)}) collective-permute-start(bf16[8,4,2,32,256]{4,3,2,1,0:T(8,128)(2,1)} %copy-done.4), channel_id=1, source_target_pairs={{0,1},{1,0},{2,3},{3,2},{4,5},{5,4},{6,7},{7,6},{8,9},{9,8},{10,11... | collective-permute-start | bytes 3145736 | tf_op jit(solution)/shard_map/ppermute | solution.py:605
  236.2 25.6 %collective-permute-start.2 = (f32[1,8]{1,0:T(1,128)S(1)}, f32[1,8]{1,0:T(1,128)S(1)}, u32[]{:S(2)}, u32[]{:S(2)}) collective-permute-start(f32[1,8]{1,0:T(1,128)S(1)} %get-tuple-element.52), channel_id=1, source_target_pairs={{0,2},{2,0},{4,6},{6,4},{8,10},{10,8},{12,14},{14,12},{1,3},{3,1},... | collective-permute-start | bytes 104 | tf_op jit(solution)/shard_map/ppermute | solution.py:540
  238.2 50.1 %collective-permute-start.3 = (f32[1,8]{1,0:T(1,128)S(1)}, f32[1,8]{1,0:T(1,128)S(1)}, u32[]{:S(2)}, u32[]{:S(2)}) collective-permute-start(f32[1,8]{1,0:T(1,128)S(1)} %get-tuple-element.58), channel_id=1, source_target_pairs={{0,4},{2,6},{4,0},{6,2},{8,12},{10,14},{12,8},{14,10},{1,5},{3,7},... | collective-permute-start | bytes 104 | tf_op jit(solution)/shard_map/ppermute | solution.py:540
  239.6 51.2 %collective-permute-start.4 = (f32[1,8]{1,0:T(1,128)S(1)}, f32[1,8]{1,0:T(1,128)S(1)}, u32[]{:S(2)}, u32[]{:S(2)}) collective-permute-start(f32[1,8]{1,0:T(1,128)S(1)} %get-tuple-element.57), channel_id=1, source_target_pairs={{0,6},{2,4},{4,2},{6,0},{8,14},{10,12},{12,10},{14,8},{1,7},{3,5},... | collective-permute-start | bytes 104 | tf_op jit(solution)/shard_map/ppermute | solution.py:540
  239.8 67.3 %collective-permute-start.5 = (f32[1,8]{1,0:T(1,128)S(1)}, f32[1,8]{1,0:T(1,128)S(1)}, u32[]{:S(2)}, u32[]{:S(2)}) collective-permute-start(f32[1,8]{1,0:T(1,128)S(1)} %get-tuple-element.56), channel_id=1, source_target_pairs={{0,8},{2,10},{4,12},{6,14},{8,0},{10,2},{12,4},{14,6},{1,9},{3,11}... | collective-permute-start | bytes 104 | tf_op jit(solution)/shard_map/ppermute | solution.py:540
  261.8 46.1 %collective-permute-start.6 = (f32[1,8]{1,0:T(1,128)S(1)}, f32[1,8]{1,0:T(1,128)S(1)}, u32[]{:S(2)}, u32[]{:S(2)}) collective-permute-start(f32[1,8]{1,0:T(1,128)S(1)} %get-tuple-element.55), channel_id=1, source_target_pairs={{0,10},{2,8},{4,14},{6,12},{8,2},{10,0},{12,6},{14,4},{1,11},{3,9}... | collective-permute-start | bytes 104 | tf_op jit(solution)/shard_map/ppermute | solution.py:540
  288.3 19.6 %collective-permute-start.7 = (f32[1,8]{1,0:T(1,128)S(1)}, f32[1,8]{1,0:T(1,128)S(1)}, u32[]{:S(2)}, u32[]{:S(2)}) collective-permute-start(f32[1,8]{1,0:T(1,128)S(1)} %get-tuple-element.54), channel_id=1, source_target_pairs={{0,12},{2,14},{4,8},{6,10},{8,4},{10,6},{12,0},{14,2},{1,13},{3,15... | collective-permute-start | bytes 104 | tf_op jit(solution)/shard_map/ppermute | solution.py:540
  290.8 17.1 %collective-permute-start.8 = (f32[1,8]{1,0:T(1,128)S(1)}, f32[1,8]{1,0:T(1,128)S(1)}, u32[]{:S(2)}, u32[]{:S(2)}) collective-permute-start(f32[1,8]{1,0:T(1,128)S(1)} %get-tuple-element.53), channel_id=1, source_target_pairs={{0,14},{2,12},{4,10},{6,8},{8,6},{10,4},{12,2},{14,0},{1,15},{3,13... | collective-permute-start | bytes 104 | tf_op jit(solution)/shard_map/ppermute | solution.py:540
  307.9 5.7 %collective-permute-start.10 = (bf16[8,12,2,32,256]{4,3,2,1,0:T(8,128)(2,1)S(1)}, bf16[8,12,2,32,256]{4,3,2,1,0:T(8,128)(2,1)S(1)}, u32[]{:S(2)}, u32[]{:S(2)}) collective-permute-start(bf16[8,12,2,32,256]{4,3,2,1,0:T(8,128)(2,1)S(1)} %all-to-all-done.4.refs_1_), channel_id=1, source_target_pairs={{0,1},{1,0},{2,3},{3,2},{4,5},{5,4},{6,7},{7,6},{8,9},{9,8},{10,11... | collective-permute-start | bytes 9437192 | tf_op jit(solution)/shard_map/ppermute | solution.py:607
  (6 other events, 8.0 us)

commit v15 on v13

--- a/solution.py
+++ b/solution.py
@@ -638,7 +638,7 @@
         name="route",
     )(owners.reshape(rows, LANES), local_block, kinds, counts)
     target, word = target.reshape(entries), word.reshape(entries)
-    tiles = [cap // 2, cap // 2] if cap >= 2048 else [cap]
+    tiles = [cap * 5 // 8, cap * 3 // 8] if cap >= 2048 else [cap]
     parts = len(tiles)
     code = ctf_code | ((scales.astype(jnp.float32) * 256.0).astype(jnp.int32) << 8)
     stride = cap + LANES

time: 320 us -> 329 us (1.028)
  starting transfers between devices: 37.6 us -> 42.3 us
    pallas_call x2, Pallas kernels: 40.2 us -> 46.7 us  [gradient_of_slab(): pl.pallas_call(functools.partial(slab_kernel, side, local_bits, list_leng...]
    all_to_all x2, starting transfers between devices: 13.1 us -> 18.4 us  [to_field(): got = lax.all_to_all(sent, 'slab', split_axis=0, concat_axis=0, tiled=True)]
    unnamed x32 -> x28, local copies, waits for them, and re-layouts: 21.2 us -> 18.2 us
  transfers between devices with their start and end apart: 15 -> 15, of which waited for: 9 -> 8; matrix products, arithmetic and copies ran while one was open for 1% -> 1% of each run, Pallas kernels for 25% -> 27%
where the time goes in v15:
time: 329 us; the launch traced here: 326 us
  Pallas kernels  131 us (40%)
  waiting for transfers between devices  114 us (35%)
  starting transfers between devices  42.3 us (13%)
  local copies, waits for them, and re-layouts  20.3 us (6%)
  blocking collectives  15.2 us (5%)
    ppermute x7, waiting for transfers between devices, sum_over_slabs(): lax.ppermute(row(i), 'slab', [(slab, slab ^ i) for slab in range(slabs)])  56.4 us
    pallas_call x2, Pallas kernels, gradient_of_slab(): pl.pallas_call(functools.partial(slab_kernel, side, local_bits, list_leng...  46.7 us
    all_to_all x2, waiting for transfers between devices, gradient_of_slab(): lax.all_to_all(packed[part], 'slab', split_axis=0, concat_axis=0, tiled=T...  37 us
    pallas_call x2, Pallas kernels, to_field(): pl.pallas_call(planes_kernel, grid=(quads, per_row // yblocks), out_shape...  31.4 us
    all_to_all x2, starting transfers between devices, to_field(): got = lax.all_to_all(sent, 'slab', split_axis=0, concat_axis=0, tiled=True)  18.4 us
    unnamed x28, local copies, waits for them, and re-layouts  18.2 us
    pallas_call x1, Pallas kernels, gradient_of_slab(): pl.pallas_call(functools.partial(gather_kernel, slabs, cap), out_shape=tu...  17.5 us
    pallas_call x1, Pallas kernels, gradient_of_slab(): pl.pallas_call(functools.partial(pack_kernel, slabs, cap, list_length), o...  16.2 us
  transfers between devices with their start and end apart: 15, of which 8 were waited for; matrix products, arithmetic and copies ran while one was open for 1% of the time, Pallas kernels for 27%

profile of v15, /device:TPU:0, one launch (start us, length us, event | category | flops | bytes accessed | tf_op | source)
XLA Modules:
  0.0 325.8 jit_solution(6452537128843788306)
XLA Ops:
  1.8 3.7 %route.1 = (s32[64,128]{1,0:T(8,128)}, s32[64,128]{1,0:T(8,128)}, s32[8,128]{1,0:T(8,128)}) custom-call(s32[64,128]{1,0:T(8,128)} %bitcast.50, s32[8,1024]{1,0:T(8,128)} %local_ref.1, s32[8,1024]{1,0:T(8,128)} %kind_ref.1, s32[8]{0:T(128)} %counts_ref.3), custom_call_target="tpu_custom_call" | custom-call | tf_op jit(solution)/shard_map/route/pallas_call | solution.py:632
  5.6 16.2 %pack.1 = (s32[17408]{0:T(1024)}, bf16[8,1280,128]{2,1,0:T(8,128)(2,1)}, bf16[8,768,128]{2,1,0:T(8,128)(2,1)}) custom-call(s32[8192]{0:T(1024)} %bitcast.48, s32[8192]{0:T(1024)} %bitcast.49, s32[8]{0:T(128)} %counts_ref.3, s32[8,128]{1,0:T(8,128)} %get-tuple-element.27.totals_ref, s32[8]{0:T(128)} %shift-left_or_fusion.code_ref, bf16[8192,128]{1,0:T(8,128)(2,1)} %bitcast.37), custom_call_target="tpu_custom_call" | custom-call | tf_op jit(solution)/shard_map/pack/pallas_call | solution.py:645
  21.8 15.2 %all_to_all.32 = s32[8,1,2176]{2,1,0:T(1,128)S(1)} all-to-all(s32[8,1,2176]{2,1,0:T(1,128)} %bitcast.47), channel_id=1, replica_groups=mesh['groups'=2,'slab'=8,'dom'=2] {'slab'}, dimensions={0} | all-to-all | bytes 139264 | tf_op jit(solution)/shard_map/all_to_all | solution.py:660
  37.0 3.6 %all-to-all-start.2 = ((bf16[8,1280,128]{2,1,0:T(8,128)(2,1)}), bf16[8,1280,128]{2,1,0:T(8,128)(2,1)S(1)}, u32[]{:S(2)}, u32[]{:S(2)}) async-start(bf16[8,1280,128]{2,1,0:T(8,128)(2,1)} %get-tuple-element.33), calls=%async_computation.2 | async-start | bytes 5242880 | tf_op jit(solution)/shard_map/all_to_all | solution.py:708
  44.9 17.5 %read_voxels.1 = (bf16[8,1280,128]{2,1,0:T(8,128)(2,1)}, bf16[8,768,128]{2,1,0:T(8,128)(2,1)}) custom-call(s32[17408]{0:T(1024)} %bitcast.32, s32[8]{0:T(128)} %copy-done.7, bf16[32768,128]{1,0:T(8,128)(2,1)} %volume_ref.1), custom_call_target="tpu_custom_call" | custom-call | bytes 104857600 | tf_op jit(solution)/shard_map/read_voxels/pallas_call | solution.py:679
  62.5 37.0 %all-to-all-done.2.image_ref = bf16[8,1280,128]{2,1,0:T(8,128)(2,1)S(1)} async-done(((bf16[8,1280,128]{2,1,0:T(8,128)(2,1)}), bf16[8,1280,128]{2,1,0:T(8,128)(2,1)S(1)}, u32[]{:S(2)}, u32[]{:S(2)}) %all-to-all-start.2) | async-done | bytes 2621472 | tf_op jit(solution)/shard_map/all_to_all | solution.py:708
  99.5 4.3 %all-to-all-start.1 = ((bf16[8,768,128]{2,1,0:T(8,128)(2,1)}), bf16[8,768,128]{2,1,0:T(8,128)(2,1)}, u32[]{:S(2)}, u32[]{:S(2)}) async-start(bf16[8,768,128]{2,1,0:T(8,128)(2,1)} %get-tuple-element.32), calls=%async_computation.1 | async-start | bytes 3145728 | tf_op jit(solution)/shard_map/all_to_all | solution.py:708
  107.1 35.9 %compare_and_add.2 = (f32[8,8,128]{2,1,0:T(8,128)S(1)}, f32[32776,128]{1,0:T(8,128)S(1)}) custom-call(s32[8]{0:T(128)S(1)} %copy-done.8, f32[64]{0:T(128)S(1)} %get-tuple-element.49.defocus_ref, f32[64]{0:T(128)S(1)} %get-tuple-element.48.phase_ref, f32[64]{0:T(128)S(1)} %mul.17.scale_ref, s32[17408]{0:T(1024)S(1)} %bitcast.33, s32[1]{0:T(128)} %bitcast.core_ref, ...), custom_call_target="tpu_custom_call" | custom-call | bytes 16777216 | tf_op jit(solution)/shard_map/compare_and_add/pallas_call | solution.py:719
  143.0 5.7 %copy-done = f32[32776,128]{1,0:T(8,128)} copy-done((f32[32776,128]{1,0:T(8,128)}, f32[32776,128]{1,0:T(8,128)S(1)}, u32[]{:S(2)}) %copy-start) | copy-done | bytes 16781336
  148.7 5.8 %copy-done.1 = f32[32776,128]{1,0:T(8,128)S(1)} copy-done((f32[32776,128]{1,0:T(8,128)S(1)}, f32[32776,128]{1,0:T(8,128)}, u32[]{:S(2)}) %copy-start.1) | copy-done | bytes 16781336
  155.9 10.8 %compare_and_add.3 = (f32[8,8,128]{2,1,0:T(8,128)S(1)}, f32[32776,128]{1,0:T(8,128)S(1)}, f32[16384,128]{1,0:T(8,128)}, f32[4096,128]{1,0:T(8,128)S(1)}, f32[12288,128]{1,0:T(8,128)}) custom-call(s32[8]{0:T(128)S(1)} %copy-done.8, f32[64]{0:T(128)S(1)} %get-tuple-element.49.defocus_ref, ...), custom_call_target="tpu_custom_call", output_to_operand_aliasing={{1}: (11, {})} | custom-call | bytes 16777216 | tf_op jit(solution)/shard_map/compare_and_add/pallas_call | solution.py:719
  167.3 11.5 %collective-permute-done.1 = f32[4096,128]{1,0:T(8,128)S(1)} collective-permute-done((f32[4096,128]{1,0:T(8,128)S(1)}, f32[4096,128]{1,0:T(8,128)S(1)}, u32[]{:S(2)}, u32[]{:S(2)}) %collective-permute-start.1) | collective-permute-done | bytes 2097184 | tf_op jit(solution)/shard_map/ppermute | solution.py:550
  180.2 8.8 %transform_planes.2 = bf16[8,4,2,32,256]{4,3,2,1,0:T(8,128)(2,1)} custom-call(f32[16,32,32,128]{3,2,1,0:T(8,128)} %bitcast.35, f32[4,32,32,128]{3,2,1,0:T(8,128)} %bitcast.38, bf16[384,256]{1,0:T(8,128)(2,1)} %constant.67.clone.zblock_ref, f32[2,8,128]{2,1,0:T(8,128)} %constant.68.clone.turn_ref, bf16[512,512]{1,0:T(8,128)(2,1)} %constant.69.clone.wide_ref, ...), custom_call_target="tpu_custom_call" | custom-call | flops 536870912 | bytes 8388608 | tf_op jit(solution)/shard_map/transform_planes/pallas_call | solution.py:569
  189.0 14.7 %all-to-all-start.3 = ((bf16[8,4,2,32,256]{4,3,2,1,0:T(8,128)(2,1)}), bf16[8,4,2,32,256]{4,3,2,1,0:T(8,128)(2,1)S(1)}, u32[]{:S(2)}, u32[]{:S(2)}) async-start(bf16[8,4,2,32,256]{4,3,2,1,0:T(8,128)(2,1)} %transform_planes.2), calls=%async_computation.3 | async-start | bytes 2097152 | tf_op jit(solution)/shard_map/all_to_all | solution.py:596
  203.8 22.5 %transform_planes.3 = bf16[8,12,2,32,256]{4,3,2,1,0:T(8,128)(2,1)} custom-call(f32[16,32,32,128]{3,2,1,0:T(8,128)} %bitcast.36, f32[12,32,32,128]{3,2,1,0:T(8,128)} %bitcast.19.theirs_ref, bf16[384,256]{1,0:T(8,128)(2,1)} %constant.67.clone.zblock_ref, f32[2,8,128]{2,1,0:T(8,128)} %constant.68.clone.turn_ref, bf16[512,512]{1,0:T(8,128)(2,1)} %constant.69.clone.wide_ref, ...), custom_call_target="tpu_custom_call" | custom-call | flops 1610612736 | bytes 25165824 | tf_op jit(solution)/shard_map/transform_planes/pallas_call | solution.py:569
  226.3 3.4 %all-to-all-done.3.refs_0_ = bf16[8,4,2,32,256]{4,3,2,1,0:T(8,128)(2,1)S(1)} async-done(((bf16[8,4,2,32,256]{4,3,2,1,0:T(8,128)(2,1)}), bf16[8,4,2,32,256]{4,3,2,1,0:T(8,128)(2,1)S(1)}, u32[]{:S(2)}, u32[]{:S(2)}) %all-to-all-start.3) | async-done | bytes 1048608 | tf_op jit(solution)/shard_map/all_to_all | solution.py:596
  230.7 3.6 %all-to-all-start.4 = ((bf16[8,12,2,32,256]{4,3,2,1,0:T(8,128)(2,1)}), bf16[8,12,2,32,256]{4,3,2,1,0:T(8,128)(2,1)S(1)}, u32[]{:S(2)}, u32[]{:S(2)}) async-start(bf16[8,12,2,32,256]{4,3,2,1,0:T(8,128)(2,1)} %transform_planes.3), calls=%async_computation.4 | async-start | bytes 6291456 | tf_op jit(solution)/shard_map/all_to_all | solution.py:596
  238.1 2.8 collective-permute-start.5
  240.9 19.2 %collective-permute-done.2 = f32[1,8]{1,0:T(1,128)S(1)} collective-permute-done((f32[1,8]{1,0:T(1,128)S(1)}, f32[1,8]{1,0:T(1,128)S(1)}, u32[]{:S(2)}, u32[]{:S(2)}) %collective-permute-start.2) | collective-permute-done | bytes 64 | tf_op jit(solution)/shard_map/ppermute | solution.py:533
  260.1 4.5 %collective-permute-start.6 = (f32[1,8]{1,0:T(1,128)S(1)}, f32[1,8]{1,0:T(1,128)S(1)}, u32[]{:S(2)}, u32[]{:S(2)}) collective-permute-start(f32[1,8]{1,0:T(1,128)S(1)} %get-tuple-element.53), channel_id=1, source_target_pairs={{0,10},{2,8},{4,14},{6,12},{8,2},{10,0},{12,6},{14,4},{1,11},{3,9}... | collective-permute-start | bytes 104 | tf_op jit(solution)/shard_map/ppermute | solution.py:533
  264.6 22.0 %collective-permute-done.3 = f32[1,8]{1,0:T(1,128)S(1)} collective-permute-done((f32[1,8]{1,0:T(1,128)S(1)}, f32[1,8]{1,0:T(1,128)S(1)}, u32[]{:S(2)}, u32[]{:S(2)}) %collective-permute-start.3) | collective-permute-done | bytes 64 | tf_op jit(solution)/shard_map/ppermute | solution.py:533
  291.0 14.4 %collective-permute-done.5 = f32[1,8]{1,0:T(1,128)S(1)} collective-permute-done((f32[1,8]{1,0:T(1,128)S(1)}, f32[1,8]{1,0:T(1,128)S(1)}, u32[]{:S(2)}, u32[]{:S(2)}) %collective-permute-start.5) | collective-permute-done | bytes 64 | tf_op jit(solution)/shard_map/ppermute | solution.py:533
  306.9 5.1 %collective-permute-done.10.refs_3_ = bf16[8,12,2,32,256]{4,3,2,1,0:T(8,128)(2,1)S(1)} collective-permute-done((bf16[8,12,2,32,256]{4,3,2,1,0:T(8,128)(2,1)S(1)}, bf16[8,12,2,32,256]{4,3,2,1,0:T(8,128)(2,1)S(1)}, u32[]{:S(2)}, u32[]{:S(2)}) %collective-permute-start.10) | collective-permute-done | bytes 3145760 | tf_op jit(solution)/shard_map/ppermute | solution.py:600
  313.2 12.6 %transform_first.1 = f32[2,128,32,256]{3,2,1,0:T(8,128)} custom-call(s32[1]{0:T(128)} %bitcast.core_ref, bf16[8,4,2,32,256]{4,3,2,1,0:T(8,128)(2,1)S(1)} %copy-done.3, bf16[8,12,2,32,256]{4,3,2,1,0:T(8,128)(2,1)S(1)} %all-to-all-done.4.refs_1_, bf16[8,4,2,32,256]{4,3,2,1,0:T(8,128)(2,1)} %collective-permute-done.9.refs_2_, ...), custom_call_target="tpu_custom_call" | custom-call | tf_op jit(solution)/shard_map/transform_first/pallas_call | solution.py:603
  (70 shorter events, 23.8 us)
Async XLA Ops:
  37.0 62.6 %all-to-all-start.2 = ((bf16[8,1280,128]{2,1,0:T(8,128)(2,1)}), bf16[8,1280,128]{2,1,0:T(8,128)(2,1)S(1)}, u32[]{:S(2)}, u32[]{:S(2)}) async-start(bf16[8,1280,128]{2,1,0:T(8,128)(2,1)} %get-tuple-element.33), calls=%async_computation.2 | async-start | bytes 5242880 | tf_op jit(solution)/shard_map/all_to_all | solution.py:708
  40.8 4.2 %copy-start.7 = (s32[8]{0:T(128)}, s32[8]{0:T(128)S(1)}, u32[]{:S(2)}) copy-start(s32[8]{0:T(128)S(1)} %slice_reduce_fusion.2.totals_ref) | copy-start | bytes 100
  62.5 41.4 %copy-start.12 = (f32[64,2]{0,1:T(2,128)S(1)}, f32[64,2]{0,1:T(2,128)}, u32[]{:S(2)}) copy-start(f32[64,2]{0,1:T(2,128)} %param.22) | copy-start | bytes 1540
  62.5 41.5 %copy-start.10 = (bf16[4,128,128]{2,1,0:T(8,128)(2,1)S(1)}, bf16[4,128,128]{2,1,0:T(8,128)(2,1)}, u32[]{:S(2)}) copy-start(bf16[4,128,128]{2,1,0:T(8,128)(2,1)} %param.15) | copy-start | bytes 393220
  62.5 42.8 %copy-start.6 = (s32[136,128]{1,0:T(8,128)S(1)}, s32[136,128]{1,0:T(8,128)}, u32[]{:S(2)}) copy-start(s32[136,128]{1,0:T(8,128)} %decode.1) | copy-start | bytes 208900
  62.5 42.8 %copy-start.8 = (s32[8]{0:T(128)S(1)}, s32[8]{0:T(128)}, u32[]{:S(2)}) copy-start(s32[8]{0:T(128)} %copy-done.7) | copy-start | bytes 100
  99.5 49.2 %all-to-all-start.1 = ((bf16[8,768,128]{2,1,0:T(8,128)(2,1)}), bf16[8,768,128]{2,1,0:T(8,128)(2,1)}, u32[]{:S(2)}, u32[]{:S(2)}) async-start(bf16[8,768,128]{2,1,0:T(8,128)(2,1)} %get-tuple-element.32), calls=%async_computation.1 | async-start | bytes 3145728 | tf_op jit(solution)/shard_map/all_to_all | solution.py:708
  105.3 1.7 copy-start.4
  143.0 5.7 %copy-start = (f32[32776,128]{1,0:T(8,128)}, f32[32776,128]{1,0:T(8,128)S(1)}, u32[]{:S(2)}) copy-start(f32[32776,128]{1,0:T(8,128)S(1)} %get-tuple-element.34.rest_0_) | copy-start | bytes 50343940
  148.7 5.8 %copy-start.1 = (f32[32776,128]{1,0:T(8,128)S(1)}, f32[32776,128]{1,0:T(8,128)}, u32[]{:S(2)}) copy-start(f32[32776,128]{1,0:T(8,128)} %copy-done) | copy-start | bytes 50343940
  166.7 37.1 %collective-permute-start = (f32[12288,128]{1,0:T(8,128)}, f32[12288,128]{1,0:T(8,128)}, u32[]{:S(2)}, u32[]{:S(2)}) collective-permute-start(f32[12288,128]{1,0:T(8,128)} %get-tuple-element.36), channel_id=1, source_target_pairs={{0,1},{1,0},{2,3},{3,2},{4,5},{5,4},{6,7},{7,6},{8,9},{9,8},{10,11... | collective-permute-start | bytes 18874376 | tf_op jit(solution)/shard_map/ppermute | solution.py:550
  167.2 11.6 %collective-permute-start.1 = (f32[4096,128]{1,0:T(8,128)S(1)}, f32[4096,128]{1,0:T(8,128)S(1)}, u32[]{:S(2)}, u32[]{:S(2)}) collective-permute-start(f32[4096,128]{1,0:T(8,128)S(1)} %get-tuple-element.37), channel_id=1, source_target_pairs={{0,1},{1,0},{2,3},{3,2},{4,5},{5,4},{6,7},{7,6},{8,9},{9,8},{10,11... | collective-permute-start | bytes 6291464 | tf_op jit(solution)/shard_map/ppermute | solution.py:550
  189.0 40.8 %all-to-all-start.3 = ((bf16[8,4,2,32,256]{4,3,2,1,0:T(8,128)(2,1)}), bf16[8,4,2,32,256]{4,3,2,1,0:T(8,128)(2,1)S(1)}, u32[]{:S(2)}, u32[]{:S(2)}) async-start(bf16[8,4,2,32,256]{4,3,2,1,0:T(8,128)(2,1)} %transform_planes.2), calls=%async_computation.3 | async-start | bytes 2097152 | tf_op jit(solution)/shard_map/all_to_all | solution.py:596
  226.3 80.0 %copy-start.11 = (s32[8]{0:T(128)S(1)}, s32[8]{0:T(128)}, u32[]{:S(2)}) copy-start(s32[8]{0:T(128)} %counts_ref.3) | copy-start | bytes 100
  230.7 75.5 %all-to-all-start.4 = ((bf16[8,12,2,32,256]{4,3,2,1,0:T(8,128)(2,1)}), bf16[8,12,2,32,256]{4,3,2,1,0:T(8,128)(2,1)S(1)}, u32[]{:S(2)}, u32[]{:S(2)}) async-start(bf16[8,12,2,32,256]{4,3,2,1,0:T(8,128)(2,1)} %transform_planes.3), calls=%async_computation.4 | async-start | bytes 6291456 | tf_op jit(solution)/shard_map/all_to_all | solution.py:596
  234.4 71.8 %collective-permute-start.9 = (bf16[8,4,2,32,256]{4,3,2,1,0:T(8,128)(2,1)}, bf16[8,4,2,32,256]{4,3,2,1,0:T(8,128)(2,1)}, u32[]{:S(2)}, u32[]{:S(2)}) collective-permute-start(bf16[8,4,2,32,256]{4,3,2,1,0:T(8,128)(2,1)} %copy-done.2), channel_id=1, source_target_pairs={{0,1},{1,0},{2,3},{3,2},{4,5},{5,4},{6,7},{7,6},{8,9},{9,8},{10,11... | collective-permute-start | bytes 3145736 | tf_op jit(solution)/shard_map/ppermute | solution.py:598
  234.5 25.6 %collective-permute-start.2 = (f32[1,8]{1,0:T(1,128)S(1)}, f32[1,8]{1,0:T(1,128)S(1)}, u32[]{:S(2)}, u32[]{:S(2)}) collective-permute-start(f32[1,8]{1,0:T(1,128)S(1)} %get-tuple-element.50), channel_id=1, source_target_pairs={{0,2},{2,0},{4,6},{6,4},{8,10},{10,8},{12,14},{14,12},{1,3},{3,1},... | collective-permute-start | bytes 104 | tf_op jit(solution)/shard_map/ppermute | solution.py:533
  236.5 50.1 %collective-permute-start.3 = (f32[1,8]{1,0:T(1,128)S(1)}, f32[1,8]{1,0:T(1,128)S(1)}, u32[]{:S(2)}, u32[]{:S(2)}) collective-permute-start(f32[1,8]{1,0:T(1,128)S(1)} %get-tuple-element.56), channel_id=1, source_target_pairs={{0,4},{2,6},{4,0},{6,2},{8,12},{10,14},{12,8},{14,10},{1,5},{3,7},... | collective-permute-start | bytes 104 | tf_op jit(solution)/shard_map/ppermute | solution.py:533
  238.0 51.1 %collective-permute-start.4 = (f32[1,8]{1,0:T(1,128)S(1)}, f32[1,8]{1,0:T(1,128)S(1)}, u32[]{:S(2)}, u32[]{:S(2)}) collective-permute-start(f32[1,8]{1,0:T(1,128)S(1)} %get-tuple-element.55), channel_id=1, source_target_pairs={{0,6},{2,4},{4,2},{6,0},{8,14},{10,12},{12,10},{14,8},{1,7},{3,5},... | collective-permute-start | bytes 104 | tf_op jit(solution)/shard_map/ppermute | solution.py:533
  238.1 67.3 %collective-permute-start.5 = (f32[1,8]{1,0:T(1,128)S(1)}, f32[1,8]{1,0:T(1,128)S(1)}, u32[]{:S(2)}, u32[]{:S(2)}) collective-permute-start(f32[1,8]{1,0:T(1,128)S(1)} %get-tuple-element.54), channel_id=1, source_target_pairs={{0,8},{2,10},{4,12},{6,14},{8,0},{10,2},{12,4},{14,6},{1,9},{3,11}... | collective-permute-start | bytes 104 | tf_op jit(solution)/shard_map/ppermute | solution.py:533
  260.1 46.1 %collective-permute-start.6 = (f32[1,8]{1,0:T(1,128)S(1)}, f32[1,8]{1,0:T(1,128)S(1)}, u32[]{:S(2)}, u32[]{:S(2)}) collective-permute-start(f32[1,8]{1,0:T(1,128)S(1)} %get-tuple-element.53), channel_id=1, source_target_pairs={{0,10},{2,8},{4,14},{6,12},{8,2},{10,0},{12,6},{14,4},{1,11},{3,9}... | collective-permute-start | bytes 104 | tf_op jit(solution)/shard_map/ppermute | solution.py:533
  286.6 19.6 %collective-permute-start.7 = (f32[1,8]{1,0:T(1,128)S(1)}, f32[1,8]{1,0:T(1,128)S(1)}, u32[]{:S(2)}, u32[]{:S(2)}) collective-permute-start(f32[1,8]{1,0:T(1,128)S(1)} %get-tuple-element.52), channel_id=1, source_target_pairs={{0,12},{2,14},{4,8},{6,10},{8,4},{10,6},{12,0},{14,2},{1,13},{3,15... | collective-permute-start | bytes 104 | tf_op jit(solution)/shard_map/ppermute | solution.py:533
  289.1 17.1 %collective-permute-start.8 = (f32[1,8]{1,0:T(1,128)S(1)}, f32[1,8]{1,0:T(1,128)S(1)}, u32[]{:S(2)}, u32[]{:S(2)}) collective-permute-start(f32[1,8]{1,0:T(1,128)S(1)} %get-tuple-element.51), channel_id=1, source_target_pairs={{0,14},{2,12},{4,10},{6,8},{8,6},{10,4},{12,2},{14,0},{1,15},{3,13... | collective-permute-start | bytes 104 | tf_op jit(solution)/shard_map/ppermute | solution.py:533
  306.3 5.7 %collective-permute-start.10 = (bf16[8,12,2,32,256]{4,3,2,1,0:T(8,128)(2,1)S(1)}, bf16[8,12,2,32,256]{4,3,2,1,0:T(8,128)(2,1)S(1)}, u32[]{:S(2)}, u32[]{:S(2)}) collective-permute-start(bf16[8,12,2,32,256]{4,3,2,1,0:T(8,128)(2,1)S(1)} %all-to-all-done.4.refs_1_), channel_id=1, source_target_pairs={{0,1},{1,0},{2,3},{3,2},{4,5},{5,4},{6,7},{7,6},{8,9},{9,8},{10,11... | collective-permute-start | bytes 9437192 | tf_op jit(solution)/shard_map/ppermute | solution.py:600
  (4 other events, 4.9 us)

commit v16 on v15

--- a/solution.py
+++ b/solution.py
@@ -13,7 +13,7 @@
 GROUP = 16
 UNUSED = 100
 STEP = 256
-PAIR = 1
+PAIR = 2
 MIB = 1024 * 1024
 
 SMEM_SPEC = pl.BlockSpec(memory_space=pltpu.SMEM)
@@ -213,7 +213,6 @@
     square_ref, sum_ref, out_refs, (staged_ref, steps_ref, sems) = rest[0], rest[1], rest[2:-3], rest[-3:]
     slabs, _, tile = word_ref.shape
     step = staged_ref.shape[0] // PAIR
-    steps_each = tile // step
     blocks = sum_ref.shape[0] - 8
     features = image_ref.shape[2]
     kinds = forward_ref.shape[1] // features
@@ -232,18 +231,19 @@
 
     def list_source(source, count):
         def list_step(i, count):
-            steps_ref[count] = source * steps_each + i
+            steps_ref[2 * count] = source
+            steps_ref[2 * count + 1] = i * step
             return count + 1
 
         return lax.fori_loop(0, (live_of(source) + step - 1) // step, list_step, count)
 
     steps_ref[0] = 0
+    steps_ref[1] = 0
     count = lax.fori_loop(0, slabs, list_source, 0)
 
     def compare(number, slot):
-        which_step = steps_ref[jnp.minimum(number, jnp.maximum(count - 1, 0))]
-        source, at = which_step // steps_each, (which_step % steps_each) * step
-        at = pl.multiple_of(at, step)
+        spot = 2 * jnp.minimum(number, jnp.maximum(count - 1, 0))
+        source, at = steps_ref[spot], pl.multiple_of(steps_ref[spot + 1], step)
         live = jnp.where(number < count, live_of(source) - at, 0)
         word = word_ref[source, :, pl.ds(at, step)]
         kind = (word >> local_bits) & 3
@@ -297,8 +297,8 @@
             sum_ref[pl.ds(places[j], 1), :] = held[j] + new[j]
 
     def base_of(number):
-        earlier = steps_ref[jnp.clip(number, 0, jnp.maximum(count - 1, 0))]
-        base = (earlier // steps_each) * cap + offset + (earlier % steps_each) * step
+        spot = 2 * jnp.clip(number, 0, jnp.maximum(count - 1, 0))
+        base = steps_ref[spot] * cap + offset + steps_ref[spot + 1]
         return jnp.where((number >= 0) & (number < count), base, slabs * cap)
 
     @pl.loop(0, (count + PAIR - 1) // PAIR + 1)
@@ -729,7 +729,7 @@
             out_specs=(VMEM_SPEC, VMEM_SPEC) + (ANY_SPEC,) * len(lengths),
             scratch_shapes=[
                 pltpu.VMEM((PAIR * min(tile, STEP), features), jnp.float32),
-                pltpu.SMEM((slabs * tile // min(tile, STEP) + 1,), jnp.int32),
+                pltpu.SMEM((2 * (slabs * tile // min(tile, STEP) + 1),), jnp.int32),
                 pltpu.SemaphoreType.DMA((max(1, len(lengths)),)),
             ],
             input_output_aliases=aliases,

time: 329 us -> 319 us (0.970)
  Pallas kernels: 131 us -> 102 us
  waiting for transfers between devices: 114 us -> 131 us
    pallas_call x2, Pallas kernels: 46.7 us -> 23.9 us  [gradient_of_slab(): pl.pallas_call(functools.partial(slab_kernel, side, local_bits, list_leng...]
    all_to_all x2, waiting for transfers between devices: 37 us -> 54.4 us  [gradient_of_slab(): lax.all_to_all(packed[part], 'slab', split_axis=0, concat_axis=0, tiled=T...]
    pallas_call x1, Pallas kernels: 17.5 us -> 11.3 us  [gradient_of_slab(): pl.pallas_call(functools.partial(gather_kernel, slabs, cap), out_shape=tu...]
  transfers between devices with their start and end apart: 15 -> 15, of which waited for: 8 -> 9; matrix products, arithmetic and copies ran while one was open for 1% -> 1% of each run, Pallas kernels for 27% -> 19%
where the time goes in v16:
time: 319 us; the launch traced here: 314 us
  waiting for transfers between devices  131 us (41%)
  Pallas kernels  102 us (32%)
  starting transfers between devices  40.5 us (13%)
  local copies, waits for them, and re-layouts  20.3 us (6%)
  blocking collectives  16.1 us (5%)
    ppermute x7, waiting for transfers between devices, sum_over_slabs(): lax.ppermute(row(i), 'slab', [(slab, slab ^ i) for slab in range(slabs)])  56.4 us
    all_to_all x2, waiting for transfers between devices, gradient_of_slab(): lax.all_to_all(packed[part], 'slab', split_axis=0, concat_axis=0, tiled=T...  54.4 us
    pallas_call x2, Pallas kernels, to_field(): pl.pallas_call(planes_kernel, grid=(quads, per_row // yblocks), out_shape...  31.3 us
    pallas_call x2, Pallas kernels, gradient_of_slab(): pl.pallas_call(functools.partial(slab_kernel, side, local_bits, list_leng...  23.9 us
    unnamed x28, local copies, waits for them, and re-layouts  18.2 us
    all_to_all x2, starting transfers between devices, to_field(): got = lax.all_to_all(sent, 'slab', split_axis=0, concat_axis=0, tiled=True)  16.6 us
    pallas_call x1, Pallas kernels, gradient_of_slab(): pl.pallas_call(functools.partial(pack_kernel, slabs, cap, list_length), o...  16.5 us
    all_to_all x1, blocking collectives, gradient_of_slab(): lax.all_to_all(meta.reshape(slabs, stride), 'slab', split_axis=0, concat_...  16.1 us
  transfers between devices with their start and end apart: 15, of which 9 were waited for; matrix products, arithmetic and copies ran while one was open for 1% of the time, Pallas kernels for 19%

profile of v16, /device:TPU:0, one launch (start us, length us, event | category | flops | bytes accessed | tf_op | source)
XLA Modules:
  0.0 313.5 jit_solution(2737044590450124160)
XLA Ops:
  1.8 3.7 %route.1 = (s32[64,128]{1,0:T(8,128)}, s32[64,128]{1,0:T(8,128)}, s32[8,128]{1,0:T(8,128)}) custom-call(s32[64,128]{1,0:T(8,128)} %bitcast.50, s32[8,1024]{1,0:T(8,128)} %local_ref.1, s32[8,1024]{1,0:T(8,128)} %kind_ref.1, s32[8]{0:T(128)} %counts_ref.3), custom_call_target="tpu_custom_call" | custom-call | tf_op jit(solution)/shard_map/route/pallas_call | solution.py:632
  5.6 16.5 %pack.1 = (s32[17408]{0:T(1024)}, bf16[8,1280,128]{2,1,0:T(8,128)(2,1)}, bf16[8,768,128]{2,1,0:T(8,128)(2,1)}) custom-call(s32[8192]{0:T(1024)} %bitcast.48, s32[8192]{0:T(1024)} %bitcast.49, s32[8]{0:T(128)} %counts_ref.3, s32[8,128]{1,0:T(8,128)} %get-tuple-element.27.totals_ref, s32[8]{0:T(128)} %shift-left_or_fusion.code_ref, bf16[8192,128]{1,0:T(8,128)(2,1)} %bitcast.37), custom_call_target="tpu_custom_call" | custom-call | tf_op jit(solution)/shard_map/pack/pallas_call | solution.py:645
  22.1 16.1 %all_to_all.32 = s32[8,1,2176]{2,1,0:T(1,128)S(1)} all-to-all(s32[8,1,2176]{2,1,0:T(1,128)} %bitcast.47), channel_id=1, replica_groups=mesh['groups'=2,'slab'=8,'dom'=2] {'slab'}, dimensions={0} | all-to-all | bytes 139264 | tf_op jit(solution)/shard_map/all_to_all | solution.py:660
  38.2 3.6 %all-to-all-start.2 = ((bf16[8,1280,128]{2,1,0:T(8,128)(2,1)}), bf16[8,1280,128]{2,1,0:T(8,128)(2,1)S(1)}, u32[]{:S(2)}, u32[]{:S(2)}) async-start(bf16[8,1280,128]{2,1,0:T(8,128)(2,1)} %get-tuple-element.33), calls=%async_computation.2 | async-start | bytes 5242880 | tf_op jit(solution)/shard_map/all_to_all | solution.py:708
  46.2 11.3 %read_voxels.1 = (bf16[8,1280,128]{2,1,0:T(8,128)(2,1)}, bf16[8,768,128]{2,1,0:T(8,128)(2,1)}) custom-call(s32[17408]{0:T(1024)} %bitcast.32, s32[8]{0:T(128)} %copy-done.7, bf16[32768,128]{1,0:T(8,128)(2,1)} %volume_ref.1), custom_call_target="tpu_custom_call" | custom-call | bytes 104857600 | tf_op jit(solution)/shard_map/read_voxels/pallas_call | solution.py:679
  57.5 42.0 %all-to-all-done.2.image_ref = bf16[8,1280,128]{2,1,0:T(8,128)(2,1)S(1)} async-done(((bf16[8,1280,128]{2,1,0:T(8,128)(2,1)}), bf16[8,1280,128]{2,1,0:T(8,128)(2,1)S(1)}, u32[]{:S(2)}, u32[]{:S(2)}) %all-to-all-start.2) | async-done | bytes 2621472 | tf_op jit(solution)/shard_map/all_to_all | solution.py:708
  99.5 4.3 %all-to-all-start.1 = ((bf16[8,768,128]{2,1,0:T(8,128)(2,1)}), bf16[8,768,128]{2,1,0:T(8,128)(2,1)}, u32[]{:S(2)}, u32[]{:S(2)}) async-start(bf16[8,768,128]{2,1,0:T(8,128)(2,1)} %get-tuple-element.32), calls=%async_computation.1 | async-start | bytes 3145728 | tf_op jit(solution)/shard_map/all_to_all | solution.py:708
  107.0 15.3 %compare_and_add.2 = (f32[8,8,128]{2,1,0:T(8,128)S(1)}, f32[32776,128]{1,0:T(8,128)S(1)}) custom-call(s32[8]{0:T(128)S(1)} %copy-done.8, f32[64]{0:T(128)S(1)} %get-tuple-element.49.defocus_ref, f32[64]{0:T(128)S(1)} %get-tuple-element.48.phase_ref, f32[64]{0:T(128)S(1)} %mul.17.scale_ref, s32[17408]{0:T(1024)S(1)} %bitcast.33, s32[1]{0:T(128)} %bitcast.core_ref, ...), custom_call_target="tpu_custom_call" | custom-call | bytes 16777216 | tf_op jit(solution)/shard_map/compare_and_add/pallas_call | solution.py:719
  122.3 5.7 %copy-done = f32[32776,128]{1,0:T(8,128)} copy-done((f32[32776,128]{1,0:T(8,128)}, f32[32776,128]{1,0:T(8,128)S(1)}, u32[]{:S(2)}) %copy-start) | copy-done | bytes 16781336
  128.1 12.4 %all-to-all-done.1.image_ref = bf16[8,768,128]{2,1,0:T(8,128)(2,1)} async-done(((bf16[8,768,128]{2,1,0:T(8,128)(2,1)}), bf16[8,768,128]{2,1,0:T(8,128)(2,1)}, u32[]{:S(2)}, u32[]{:S(2)}) %all-to-all-start.1) | async-done | bytes 1572896 | tf_op jit(solution)/shard_map/all_to_all | solution.py:708
  140.4 5.8 %copy-done.1 = f32[32776,128]{1,0:T(8,128)S(1)} copy-done((f32[32776,128]{1,0:T(8,128)S(1)}, f32[32776,128]{1,0:T(8,128)}, u32[]{:S(2)}) %copy-start.1) | copy-done | bytes 16781336
  147.6 8.6 %compare_and_add.3 = (f32[8,8,128]{2,1,0:T(8,128)S(1)}, f32[32776,128]{1,0:T(8,128)S(1)}, f32[16384,128]{1,0:T(8,128)}, f32[4096,128]{1,0:T(8,128)S(1)}, f32[12288,128]{1,0:T(8,128)}) custom-call(s32[8]{0:T(128)S(1)} %copy-done.8, f32[64]{0:T(128)S(1)} %get-tuple-element.49.defocus_ref, ...), custom_call_target="tpu_custom_call", output_to_operand_aliasing={{1}: (11, {})} | custom-call | bytes 16777216 | tf_op jit(solution)/shard_map/compare_and_add/pallas_call | solution.py:719
  156.8 11.3 %collective-permute-done.1 = f32[4096,128]{1,0:T(8,128)S(1)} collective-permute-done((f32[4096,128]{1,0:T(8,128)S(1)}, f32[4096,128]{1,0:T(8,128)S(1)}, u32[]{:S(2)}, u32[]{:S(2)}) %collective-permute-start.1) | collective-permute-done | bytes 2097184 | tf_op jit(solution)/shard_map/ppermute | solution.py:550
  169.4 8.8 %transform_planes.2 = bf16[8,4,2,32,256]{4,3,2,1,0:T(8,128)(2,1)} custom-call(f32[16,32,32,128]{3,2,1,0:T(8,128)} %bitcast.35, f32[4,32,32,128]{3,2,1,0:T(8,128)} %bitcast.38, bf16[384,256]{1,0:T(8,128)(2,1)} %constant.67.clone.zblock_ref, f32[2,8,128]{2,1,0:T(8,128)} %constant.68.clone.turn_ref, bf16[512,512]{1,0:T(8,128)(2,1)} %constant.69.clone.wide_ref, ...), custom_call_target="tpu_custom_call" | custom-call | flops 536870912 | bytes 8388608 | tf_op jit(solution)/shard_map/transform_planes/pallas_call | solution.py:569
  178.2 13.0 %all-to-all-start.3 = ((bf16[8,4,2,32,256]{4,3,2,1,0:T(8,128)(2,1)}), bf16[8,4,2,32,256]{4,3,2,1,0:T(8,128)(2,1)S(1)}, u32[]{:S(2)}, u32[]{:S(2)}) async-start(bf16[8,4,2,32,256]{4,3,2,1,0:T(8,128)(2,1)} %transform_planes.2), calls=%async_computation.3 | async-start | bytes 2097152 | tf_op jit(solution)/shard_map/all_to_all | solution.py:596
  191.2 22.5 %transform_planes.3 = bf16[8,12,2,32,256]{4,3,2,1,0:T(8,128)(2,1)} custom-call(f32[16,32,32,128]{3,2,1,0:T(8,128)} %bitcast.36, f32[12,32,32,128]{3,2,1,0:T(8,128)} %bitcast.19.theirs_ref, bf16[384,256]{1,0:T(8,128)(2,1)} %constant.67.clone.zblock_ref, f32[2,8,128]{2,1,0:T(8,128)} %constant.68.clone.turn_ref, bf16[512,512]{1,0:T(8,128)(2,1)} %constant.69.clone.wide_ref, ...), custom_call_target="tpu_custom_call" | custom-call | flops 1610612736 | bytes 25165824 | tf_op jit(solution)/shard_map/transform_planes/pallas_call | solution.py:569
  213.8 3.7 %all-to-all-done.3.refs_0_ = bf16[8,4,2,32,256]{4,3,2,1,0:T(8,128)(2,1)S(1)} async-done(((bf16[8,4,2,32,256]{4,3,2,1,0:T(8,128)(2,1)}), bf16[8,4,2,32,256]{4,3,2,1,0:T(8,128)(2,1)S(1)}, u32[]{:S(2)}, u32[]{:S(2)}) %all-to-all-start.3) | async-done | bytes 1048608 | tf_op jit(solution)/shard_map/all_to_all | solution.py:596
  218.4 3.6 %all-to-all-start.4 = ((bf16[8,12,2,32,256]{4,3,2,1,0:T(8,128)(2,1)}), bf16[8,12,2,32,256]{4,3,2,1,0:T(8,128)(2,1)S(1)}, u32[]{:S(2)}, u32[]{:S(2)}) async-start(bf16[8,12,2,32,256]{4,3,2,1,0:T(8,128)(2,1)} %transform_planes.3), calls=%async_computation.4 | async-start | bytes 6291456 | tf_op jit(solution)/shard_map/all_to_all | solution.py:596
  228.5 19.2 %collective-permute-done.2 = f32[1,8]{1,0:T(1,128)S(1)} collective-permute-done((f32[1,8]{1,0:T(1,128)S(1)}, f32[1,8]{1,0:T(1,128)S(1)}, u32[]{:S(2)}, u32[]{:S(2)}) %collective-permute-start.2) | collective-permute-done | bytes 64 | tf_op jit(solution)/shard_map/ppermute | solution.py:533
  247.8 4.5 %collective-permute-start.6 = (f32[1,8]{1,0:T(1,128)S(1)}, f32[1,8]{1,0:T(1,128)S(1)}, u32[]{:S(2)}, u32[]{:S(2)}) collective-permute-start(f32[1,8]{1,0:T(1,128)S(1)} %get-tuple-element.53), channel_id=1, source_target_pairs={{0,10},{2,8},{4,14},{6,12},{8,2},{10,0},{12,6},{14,4},{1,11},{3,9}... | collective-permute-start | bytes 104 | tf_op jit(solution)/shard_map/ppermute | solution.py:533
  252.3 22.0 %collective-permute-done.3 = f32[1,8]{1,0:T(1,128)S(1)} collective-permute-done((f32[1,8]{1,0:T(1,128)S(1)}, f32[1,8]{1,0:T(1,128)S(1)}, u32[]{:S(2)}, u32[]{:S(2)}) %collective-permute-start.3) | collective-permute-done | bytes 64 | tf_op jit(solution)/shard_map/ppermute | solution.py:533
  278.7 14.4 %collective-permute-done.5 = f32[1,8]{1,0:T(1,128)S(1)} collective-permute-done((f32[1,8]{1,0:T(1,128)S(1)}, f32[1,8]{1,0:T(1,128)S(1)}, u32[]{:S(2)}, u32[]{:S(2)}) %collective-permute-start.5) | collective-permute-done | bytes 64 | tf_op jit(solution)/shard_map/ppermute | solution.py:533
  294.5 5.1 %collective-permute-done.10.refs_3_ = bf16[8,12,2,32,256]{4,3,2,1,0:T(8,128)(2,1)S(1)} collective-permute-done((bf16[8,12,2,32,256]{4,3,2,1,0:T(8,128)(2,1)S(1)}, bf16[8,12,2,32,256]{4,3,2,1,0:T(8,128)(2,1)S(1)}, u32[]{:S(2)}, u32[]{:S(2)}) %collective-permute-start.10) | collective-permute-done | bytes 3145760 | tf_op jit(solution)/shard_map/ppermute | solution.py:600
  300.9 12.6 %transform_first.1 = f32[2,128,32,256]{3,2,1,0:T(8,128)} custom-call(s32[1]{0:T(128)} %bitcast.core_ref, bf16[8,4,2,32,256]{4,3,2,1,0:T(8,128)(2,1)S(1)} %copy-done.3, bf16[8,12,2,32,256]{4,3,2,1,0:T(8,128)(2,1)S(1)} %all-to-all-done.4.refs_1_, bf16[8,4,2,32,256]{4,3,2,1,0:T(8,128)(2,1)} %collective-permute-done.9.refs_2_, ...), custom_call_target="tpu_custom_call" | custom-call | tf_op jit(solution)/shard_map/transform_first/pallas_call | solution.py:603
  (70 shorter events, 26.4 us)
Async XLA Ops:
  38.2 61.3 %all-to-all-start.2 = ((bf16[8,1280,128]{2,1,0:T(8,128)(2,1)}), bf16[8,1280,128]{2,1,0:T(8,128)(2,1)S(1)}, u32[]{:S(2)}, u32[]{:S(2)}) async-start(bf16[8,1280,128]{2,1,0:T(8,128)(2,1)} %get-tuple-element.33), calls=%async_computation.2 | async-start | bytes 5242880 | tf_op jit(solution)/shard_map/all_to_all | solution.py:708
  42.0 4.2 %copy-start.7 = (s32[8]{0:T(128)}, s32[8]{0:T(128)S(1)}, u32[]{:S(2)}) copy-start(s32[8]{0:T(128)S(1)} %slice_reduce_fusion.2.totals_ref) | copy-start | bytes 100
  57.5 46.3 %copy-start.12 = (f32[64,2]{0,1:T(2,128)S(1)}, f32[64,2]{0,1:T(2,128)}, u32[]{:S(2)}) copy-start(f32[64,2]{0,1:T(2,128)} %param.22) | copy-start | bytes 1540
  57.5 46.4 %copy-start.10 = (bf16[4,128,128]{2,1,0:T(8,128)(2,1)S(1)}, bf16[4,128,128]{2,1,0:T(8,128)(2,1)}, u32[]{:S(2)}) copy-start(bf16[4,128,128]{2,1,0:T(8,128)(2,1)} %param.15) | copy-start | bytes 393220
  57.5 47.8 %copy-start.6 = (s32[136,128]{1,0:T(8,128)S(1)}, s32[136,128]{1,0:T(8,128)}, u32[]{:S(2)}) copy-start(s32[136,128]{1,0:T(8,128)} %decode.1) | copy-start | bytes 208900
  57.5 47.8 %copy-start.8 = (s32[8]{0:T(128)S(1)}, s32[8]{0:T(128)}, u32[]{:S(2)}) copy-start(s32[8]{0:T(128)} %copy-done.7) | copy-start | bytes 100
  99.5 40.9 %all-to-all-start.1 = ((bf16[8,768,128]{2,1,0:T(8,128)(2,1)}), bf16[8,768,128]{2,1,0:T(8,128)(2,1)}, u32[]{:S(2)}, u32[]{:S(2)}) async-start(bf16[8,768,128]{2,1,0:T(8,128)(2,1)} %get-tuple-element.32), calls=%async_computation.1 | async-start | bytes 3145728 | tf_op jit(solution)/shard_map/all_to_all | solution.py:708
  105.3 1.7 copy-start.4
  122.3 5.7 %copy-start = (f32[32776,128]{1,0:T(8,128)}, f32[32776,128]{1,0:T(8,128)S(1)}, u32[]{:S(2)}) copy-start(f32[32776,128]{1,0:T(8,128)S(1)} %get-tuple-element.34.rest_0_) | copy-start | bytes 50343940
  140.4 5.8 %copy-start.1 = (f32[32776,128]{1,0:T(8,128)S(1)}, f32[32776,128]{1,0:T(8,128)}, u32[]{:S(2)}) copy-start(f32[32776,128]{1,0:T(8,128)} %copy-done) | copy-start | bytes 50343940
  156.2 35.0 %collective-permute-start = (f32[12288,128]{1,0:T(8,128)}, f32[12288,128]{1,0:T(8,128)}, u32[]{:S(2)}, u32[]{:S(2)}) collective-permute-start(f32[12288,128]{1,0:T(8,128)} %get-tuple-element.36), channel_id=1, source_target_pairs={{0,1},{1,0},{2,3},{3,2},{4,5},{5,4},{6,7},{7,6},{8,9},{9,8},{10,11... | collective-permute-start | bytes 18874376 | tf_op jit(solution)/shard_map/ppermute | solution.py:550
  156.3 11.8 %collective-permute-start.1 = (f32[4096,128]{1,0:T(8,128)S(1)}, f32[4096,128]{1,0:T(8,128)S(1)}, u32[]{:S(2)}, u32[]{:S(2)}) collective-permute-start(f32[4096,128]{1,0:T(8,128)S(1)} %get-tuple-element.37), channel_id=1, source_target_pairs={{0,1},{1,0},{2,3},{3,2},{4,5},{5,4},{6,7},{7,6},{8,9},{9,8},{10,11... | collective-permute-start | bytes 6291464 | tf_op jit(solution)/shard_map/ppermute | solution.py:550
  178.2 39.2 %all-to-all-start.3 = ((bf16[8,4,2,32,256]{4,3,2,1,0:T(8,128)(2,1)}), bf16[8,4,2,32,256]{4,3,2,1,0:T(8,128)(2,1)S(1)}, u32[]{:S(2)}, u32[]{:S(2)}) async-start(bf16[8,4,2,32,256]{4,3,2,1,0:T(8,128)(2,1)} %transform_planes.2), calls=%async_computation.3 | async-start | bytes 2097152 | tf_op jit(solution)/shard_map/all_to_all | solution.py:596
  213.8 80.2 %copy-start.11 = (s32[8]{0:T(128)S(1)}, s32[8]{0:T(128)}, u32[]{:S(2)}) copy-start(s32[8]{0:T(128)} %counts_ref.3) | copy-start | bytes 100
  218.4 75.5 %all-to-all-start.4 = ((bf16[8,12,2,32,256]{4,3,2,1,0:T(8,128)(2,1)}), bf16[8,12,2,32,256]{4,3,2,1,0:T(8,128)(2,1)S(1)}, u32[]{:S(2)}, u32[]{:S(2)}) async-start(bf16[8,12,2,32,256]{4,3,2,1,0:T(8,128)(2,1)} %transform_planes.3), calls=%async_computation.4 | async-start | bytes 6291456 | tf_op jit(solution)/shard_map/all_to_all | solution.py:596
  222.1 71.9 %collective-permute-start.9 = (bf16[8,4,2,32,256]{4,3,2,1,0:T(8,128)(2,1)}, bf16[8,4,2,32,256]{4,3,2,1,0:T(8,128)(2,1)}, u32[]{:S(2)}, u32[]{:S(2)}) collective-permute-start(bf16[8,4,2,32,256]{4,3,2,1,0:T(8,128)(2,1)} %copy-done.2), channel_id=1, source_target_pairs={{0,1},{1,0},{2,3},{3,2},{4,5},{5,4},{6,7},{7,6},{8,9},{9,8},{10,11... | collective-permute-start | bytes 3145736 | tf_op jit(solution)/shard_map/ppermute | solution.py:598
  222.2 25.6 %collective-permute-start.2 = (f32[1,8]{1,0:T(1,128)S(1)}, f32[1,8]{1,0:T(1,128)S(1)}, u32[]{:S(2)}, u32[]{:S(2)}) collective-permute-start(f32[1,8]{1,0:T(1,128)S(1)} %get-tuple-element.50), channel_id=1, source_target_pairs={{0,2},{2,0},{4,6},{6,4},{8,10},{10,8},{12,14},{14,12},{1,3},{3,1},... | collective-permute-start | bytes 104 | tf_op jit(solution)/shard_map/ppermute | solution.py:533
  224.1 50.1 %collective-permute-start.3 = (f32[1,8]{1,0:T(1,128)S(1)}, f32[1,8]{1,0:T(1,128)S(1)}, u32[]{:S(2)}, u32[]{:S(2)}) collective-permute-start(f32[1,8]{1,0:T(1,128)S(1)} %get-tuple-element.56), channel_id=1, source_target_pairs={{0,4},{2,6},{4,0},{6,2},{8,12},{10,14},{12,8},{14,10},{1,5},{3,7},... | collective-permute-start | bytes 104 | tf_op jit(solution)/shard_map/ppermute | solution.py:533
  225.6 51.2 %collective-permute-start.4 = (f32[1,8]{1,0:T(1,128)S(1)}, f32[1,8]{1,0:T(1,128)S(1)}, u32[]{:S(2)}, u32[]{:S(2)}) collective-permute-start(f32[1,8]{1,0:T(1,128)S(1)} %get-tuple-element.55), channel_id=1, source_target_pairs={{0,6},{2,4},{4,2},{6,0},{8,14},{10,12},{12,10},{14,8},{1,7},{3,5},... | collective-permute-start | bytes 104 | tf_op jit(solution)/shard_map/ppermute | solution.py:533
  225.8 67.3 %collective-permute-start.5 = (f32[1,8]{1,0:T(1,128)S(1)}, f32[1,8]{1,0:T(1,128)S(1)}, u32[]{:S(2)}, u32[]{:S(2)}) collective-permute-start(f32[1,8]{1,0:T(1,128)S(1)} %get-tuple-element.54), channel_id=1, source_target_pairs={{0,8},{2,10},{4,12},{6,14},{8,0},{10,2},{12,4},{14,6},{1,9},{3,11}... | collective-permute-start | bytes 104 | tf_op jit(solution)/shard_map/ppermute | solution.py:533
  247.8 46.1 %collective-permute-start.6 = (f32[1,8]{1,0:T(1,128)S(1)}, f32[1,8]{1,0:T(1,128)S(1)}, u32[]{:S(2)}, u32[]{:S(2)}) collective-permute-start(f32[1,8]{1,0:T(1,128)S(1)} %get-tuple-element.53), channel_id=1, source_target_pairs={{0,10},{2,8},{4,14},{6,12},{8,2},{10,0},{12,6},{14,4},{1,11},{3,9}... | collective-permute-start | bytes 104 | tf_op jit(solution)/shard_map/ppermute | solution.py:533
  274.3 19.6 %collective-permute-start.7 = (f32[1,8]{1,0:T(1,128)S(1)}, f32[1,8]{1,0:T(1,128)S(1)}, u32[]{:S(2)}, u32[]{:S(2)}) collective-permute-start(f32[1,8]{1,0:T(1,128)S(1)} %get-tuple-element.52), channel_id=1, source_target_pairs={{0,12},{2,14},{4,8},{6,10},{8,4},{10,6},{12,0},{14,2},{1,13},{3,15... | collective-permute-start | bytes 104 | tf_op jit(solution)/shard_map/ppermute | solution.py:533
  276.8 17.1 %collective-permute-start.8 = (f32[1,8]{1,0:T(1,128)S(1)}, f32[1,8]{1,0:T(1,128)S(1)}, u32[]{:S(2)}, u32[]{:S(2)}) collective-permute-start(f32[1,8]{1,0:T(1,128)S(1)} %get-tuple-element.51), channel_id=1, source_target_pairs={{0,14},{2,12},{4,10},{6,8},{8,6},{10,4},{12,2},{14,0},{1,15},{3,13... | collective-permute-start | bytes 104 | tf_op jit(solution)/shard_map/ppermute | solution.py:533
  293.9 5.7 %collective-permute-start.10 = (bf16[8,12,2,32,256]{4,3,2,1,0:T(8,128)(2,1)S(1)}, bf16[8,12,2,32,256]{4,3,2,1,0:T(8,128)(2,1)S(1)}, u32[]{:S(2)}, u32[]{:S(2)}) collective-permute-start(bf16[8,12,2,32,256]{4,3,2,1,0:T(8,128)(2,1)S(1)} %all-to-all-done.4.refs_1_), channel_id=1, source_target_pairs={{0,1},{1,0},{2,3},{3,2},{4,5},{5,4},{6,7},{7,6},{8,9},{9,8},{10,11... | collective-permute-start | bytes 9437192 | tf_op jit(solution)/shard_map/ppermute | solution.py:600
  (4 other events, 4.9 us)
